TPU v7x, 256 devices: a whole 4x4x8 slice. The times are simulated.
256 devices in a mesh: lat: 8 (over x, y_lo), lon: 32 (over z, y_hi, core).
Axes of the slice: x: 4, y: 4 (y_hi: 2, y_lo: 2; y = y_hi * 2 + y_lo), z: 8, core: 2. Of those that a mesh axis runs over, the one named last changes fastest.
Arguments:
- field_in: bfloat16 [4, 48, 768, 192], P(None, 'lat', 'lon'), may hold values from -6 to 6
- cotangent: bfloat16 [4, 48, 768, 192], P(None, 'lat', 'lon'), may hold values from -6 to 6
- ln1_gain: float32 [192], replicated, may hold values from 0.1 to 1.9
- w_qkv: bfloat16 [192, 576], replicated, may hold values from -0.4375 to 0.4375
- w_proj: bfloat16 [192, 192], replicated, may hold values from -0.4375 to 0.4375
- ln2_gain: float32 [192], replicated, may hold values from 0.1 to 1.9
- w_up: bfloat16 [192, 768], replicated, may hold values from -0.4375 to 0.4375
- w_down: bfloat16 [768, 192], replicated, may hold values from -0.21875 to 0.21875
- bias_table: float32 [2, 8, 6, 3312], P(None, 'lat'), may hold values from -330 to 330
- region_ids: int32 [4, 48, 768], P(None, 'lat', 'lon'), may hold values from 0 to 2
- keep_flags: int32 [2, 8, 64], P(None, 'lat', 'lon'), may hold values 0 or 1
Outputs:
- block_out: bfloat16 [4, 48, 768, 192], P(None, 'lat', 'lon')
- grad_field: bfloat16 [4, 48, 768, 192], P(None, 'lat', 'lon')
- grad_bias: float32 [2, 8, 6, 3312], P(None, 'lat')
All inputs are finite; a program needn't handle non-finite values. No bound on the sum of `keep_flags` on one device may be relied on, other than what follows from the above.
Results may differ from a plain program's by a relative error of at most 0.013.
Values may be sent and summed in bfloat16 or wider, within the bound.
No kernel may reach another device: no remote copies, remote signals or barrier semaphores. Data moves between devices by JAX's collectives and lax.ppermute only.
A program may use at most 128 MiB of HBM per device.

v0:
```python
import math

import jax
import jax.numpy as jnp
from jax import lax
from jax.sharding import PartitionSpec as P

WZ = 2
WLAT = 6
WLON = 12


epsilon = 1e-05
keep_share = 0.8
gelu_coef = 0.044715
highest = lax.Precision.HIGHEST


def passed_along(block, axis, distance):
    devices = range(lax.axis_size(axis))
    route = [((i - distance) % len(devices), i) for i in devices]
    return lax.ppermute(block, axis, route)


def norm_parts(values, ln_gain):
    row_mean = jnp.mean(values, axis=-1, keepdims=True)
    centred = values - row_mean
    variance = jnp.mean(centred * centred, axis=-1, keepdims=True)
    inverse = lax.rsqrt(variance + epsilon)
    normed = centred * inverse
    return (normed * ln_gain, normed, inverse)


def norm_back(grad_in, ln_gain, normed, inverse):
    scaled = grad_in * ln_gain
    first_mean = jnp.mean(scaled, axis=-1, keepdims=True)
    second_mean = jnp.mean(scaled * normed, axis=-1, keepdims=True)
    return (scaled - first_mean - normed * second_mean) * inverse


def gelu_parts(values):
    factor = math.sqrt(2.0 / math.pi)
    tangent = jnp.tanh(factor * (values + gelu_coef * values * values * values))
    result = 0.5 * values * (1.0 + tangent)
    derivative = 0.5 * (1.0 + tangent) + 0.5 * values * (1.0 - tangent * tangent) * factor * (
        1.0 + 3.0 * gelu_coef * values * values
    )
    return (result, derivative)


def roll_frame(values, direction):
    lon_half = WLON // 2
    lat_half = WLAT // 2
    level_half = WZ // 2
    if direction < 0:
        border = values[:, :, :lon_half]
    else:
        border = values[:, :, -lon_half:]
    arrived = passed_along(border, "lon", direction)
    if direction < 0:
        values = jnp.concatenate([values[:, :, lon_half:], arrived], axis=2)
        border = values[:, :lat_half]
    else:
        values = jnp.concatenate([arrived, values[:, :, :-lon_half]], axis=2)
        border = values[:, -lat_half:]
    arrived = passed_along(border, "lat", direction)
    if direction < 0:
        values = jnp.concatenate([values[:, lat_half:], arrived], axis=1)
        return jnp.roll(values, -level_half, axis=0)
    values = jnp.concatenate([arrived, values[:, :-lat_half]], axis=1)
    return jnp.roll(values, level_half, axis=0)


def to_windows(values):
    levels, lat_rows, lon_cols, channels = values.shape
    shaped = values.reshape(
        levels // WZ, WZ, lat_rows // WLAT, WLAT, lon_cols // WLON, WLON, channels
    )
    shaped = shaped.transpose(0, 2, 4, 1, 3, 5, 6)
    return shaped.reshape(
        levels // WZ, lat_rows // WLAT, lon_cols // WLON, WZ * WLAT * WLON, channels
    )


def from_windows(values):
    level_win, lat_win, lon_win, positions, channels = values.shape
    shaped = values.reshape(level_win, lat_win, lon_win, WZ, WLAT, WLON, channels)
    shaped = shaped.transpose(0, 3, 1, 4, 2, 5, 6)
    return shaped.reshape(level_win * WZ, lat_win * WLAT, lon_win * WLON, channels)


def lon_table():
    offsets = jnp.arange(WLON, dtype=jnp.int32)
    spread = 2 * WLON - 1
    target = offsets[:, None, None] - offsets[None, :, None] + WLON - 1
    return (jnp.arange(spread, dtype=jnp.int32)[None, None, :] == target).astype(jnp.float32)


def expand_bias(table):
    leading = table.shape[:-1]
    shaped = table.reshape(leading + (WZ, WZ, WLAT, WLAT, 2 * WLON - 1))
    expanded = jnp.einsum("...abcdr,oqr->...acobdq", shaped, lon_table(), precision=highest)
    return expanded.reshape(leading + (WZ * WLAT * WLON, WZ * WLAT * WLON))


def fold_bias(grads):
    leading = grads.shape[:-2]
    shaped = grads.reshape(leading + (WZ, WLAT, WLON, WZ, WLAT, WLON))
    folded = jnp.einsum("...acobdq,oqr->...abcdr", shaped, lon_table(), precision=highest)
    return folded.reshape(leading + (WZ * WZ * WLAT * WLAT * (2 * WLON - 1),))


def window_labels(region_ids, lat_start, lat_total):
    levels, lat_rows, lon_cols = region_ids.shape
    level_pos = jnp.arange(levels, dtype=jnp.int32)[:, None, None]
    lat_pos = lat_start + jnp.arange(lat_rows, dtype=jnp.int32)[None, :, None]
    wrapped = 2 * (level_pos >= levels - WZ // 2).astype(jnp.int32) + (
        lat_pos >= lat_total - WLAT // 2
    ).astype(jnp.int32)
    labels = 4 * region_ids + wrapped
    return to_windows(labels[..., None])[..., 0]


def pair_mask(labels):
    return labels[..., :, None] == labels[..., None, :]


def head_slice(packed, part_idx, head_idx, head_dim, channels):
    offset = part_idx * channels + head_idx * head_dim
    return packed[..., offset : offset + head_dim]


def head_probs(query_h, key_h, bias_full, allowed, head_idx):
    scores = jnp.einsum("abcpd,abcqd->abcpq", query_h, key_h, preferred_element_type=jnp.float32)
    scores = scores / math.sqrt(query_h.shape[-1]) + bias_full[:, :, head_idx][:, :, None]
    scores = jnp.where(allowed, scores, -jnp.inf)
    top_score = jnp.max(scores, axis=-1, keepdims=True)
    weights = jnp.exp(scores - top_score)
    return weights / jnp.sum(weights, axis=-1, keepdims=True)


def attention_forward(windows_in, w_qkv, w_proj, bias_full, allowed, factor):
    channels = windows_in.shape[-1]
    heads = bias_full.shape[2]
    head_dim = channels // heads
    qkv = jnp.dot(windows_in, w_qkv, preferred_element_type=jnp.float32).astype(jnp.bfloat16)
    pieces = []
    for head_idx in range(heads):
        query_h = head_slice(qkv, 0, head_idx, head_dim, channels)
        key_h = head_slice(qkv, 1, head_idx, head_dim, channels)
        value_h = head_slice(qkv, 2, head_idx, head_dim, channels)
        probs = head_probs(query_h, key_h, bias_full, allowed, head_idx)
        pieces.append(
            jnp.einsum(
                "abcpq,abcqd->abcpd",
                probs.astype(jnp.bfloat16),
                value_h,
                preferred_element_type=jnp.float32,
            ).astype(jnp.bfloat16)
        )
    attended = jnp.concatenate(pieces, axis=-1)
    projected = jnp.dot(attended, w_proj, preferred_element_type=jnp.float32)
    return (qkv, (projected * factor).astype(jnp.bfloat16))


def attention_backward(grad_win, qkv, w_qkv, w_proj, bias_full, allowed, factor):
    channels = grad_win.shape[-1]
    heads = bias_full.shape[2]
    head_dim = channels // heads
    root = math.sqrt(head_dim)
    grad_branch = (grad_win.astype(jnp.float32) * factor).astype(jnp.bfloat16)
    grad_att = jnp.dot(grad_branch, w_proj.T, preferred_element_type=jnp.float32).astype(
        jnp.bfloat16
    )
    grad_query, grad_key, grad_value, bias_parts = ([], [], [], [])
    for head_idx in range(heads):
        query_h = head_slice(qkv, 0, head_idx, head_dim, channels)
        key_h = head_slice(qkv, 1, head_idx, head_dim, channels)
        value_h = head_slice(qkv, 2, head_idx, head_dim, channels)
        grad_head = head_slice(grad_att, 0, head_idx, head_dim, channels)
        probs = head_probs(query_h, key_h, bias_full, allowed, head_idx)
        probs_low = probs.astype(jnp.bfloat16)
        grad_probs = jnp.einsum(
            "abcpd,abcqd->abcpq", grad_head, value_h, preferred_element_type=jnp.float32
        )
        grad_scores = probs * (grad_probs - jnp.sum(probs * grad_probs, axis=-1, keepdims=True))
        grad_low = grad_scores.astype(jnp.bfloat16)
        grad_query.append(
            (
                jnp.einsum(
                    "abcpq,abcqd->abcpd", grad_low, key_h, preferred_element_type=jnp.float32
                )
                / root
            ).astype(jnp.bfloat16)
        )
        grad_key.append(
            (
                jnp.einsum(
                    "abcpq,abcpd->abcqd", grad_low, query_h, preferred_element_type=jnp.float32
                )
                / root
            ).astype(jnp.bfloat16)
        )
        grad_value.append(
            jnp.einsum(
                "abcpq,abcpd->abcqd", probs_low, grad_head, preferred_element_type=jnp.float32
            ).astype(jnp.bfloat16)
        )
        folded = fold_bias(jnp.sum(grad_scores, axis=2))
        folded = lax.psum(folded, "lon")
        bias_parts.append(folded)
    grad_table = jnp.stack(bias_parts, axis=2)
    grad_qkv = jnp.concatenate(grad_query + grad_key + grad_value, axis=-1)
    grad_in = jnp.dot(grad_qkv, w_qkv.T, preferred_element_type=jnp.float32).astype(jnp.bfloat16)
    return (grad_in, grad_table)


def mlp_both(y_sum, grad_out, ln2_gain, w_up, w_down):
    normed2, plain2, inverse2 = norm_parts(y_sum, ln2_gain)
    up_proj = jnp.dot(normed2.astype(jnp.bfloat16), w_up, preferred_element_type=jnp.float32)
    act_val, act_slope = gelu_parts(up_proj)
    result = (
        y_sum + jnp.dot(act_val.astype(jnp.bfloat16), w_down, preferred_element_type=jnp.float32)
    ).astype(jnp.bfloat16)
    grad_act = jnp.dot(grad_out, w_down.T, preferred_element_type=jnp.float32)
    grad_up = (grad_act * act_slope).astype(jnp.bfloat16)
    grad_hidden = jnp.dot(grad_up, w_up.T, preferred_element_type=jnp.float32)
    grad_sum = grad_out.astype(jnp.float32) + norm_back(grad_hidden, ln2_gain, plain2, inverse2)
    return (result, grad_sum)


def body(
    field_in,
    cotangent,
    ln1_gain,
    w_qkv,
    w_proj,
    ln2_gain,
    w_up,
    w_down,
    bias_table,
    region_ids,
    keep_flags,
):
    lat_rows = field_in.shape[1]
    lat_start = lax.axis_index("lat") * lat_rows
    lat_total = lax.axis_size("lat") * lat_rows
    bias_full = expand_bias(bias_table)
    allowed = pair_mask(window_labels(region_ids, lat_start, lat_total))
    factor = (keep_flags.astype(jnp.float32) / keep_share)[..., None, None]
    normed1, plain1, inverse1 = norm_parts(field_in.astype(jnp.float32), ln1_gain)
    shifted = roll_frame(normed1.astype(jnp.bfloat16), -1)
    qkv, branch = attention_forward(to_windows(shifted), w_qkv, w_proj, bias_full, allowed, factor)
    returned = roll_frame(from_windows(branch), 1)
    y_sum = field_in.astype(jnp.float32) + returned.astype(jnp.float32)
    result, grad_sum = mlp_both(y_sum, cotangent, ln2_gain, w_up, w_down)
    grad_shift = roll_frame(grad_sum.astype(jnp.bfloat16), -1)
    grad_win, grad_table = attention_backward(
        to_windows(grad_shift), qkv, w_qkv, w_proj, bias_full, allowed, factor
    )
    grad_h1 = roll_frame(from_windows(grad_win), 1)
    grad_field = (
        grad_sum + norm_back(grad_h1.astype(jnp.float32), ln1_gain, plain1, inverse1)
    ).astype(jnp.bfloat16)
    return (result, grad_field, grad_table)


def solution(mesh):
    placed = (
        P(None, "lat", "lon", None),
        P(None, "lat", "lon", None),
        P(),
        P(),
        P(),
        P(),
        P(),
        P(),
        P(None, "lat", None, None),
        P(None, "lat", "lon"),
        P(None, "lat", "lon"),
    )
    return jax.shard_map(
        body,
        mesh=mesh,
        in_specs=placed,
        out_specs=(
            P(None, "lat", "lon", None),
            P(None, "lat", "lon", None),
            P(None, "lat", None, None),
        ),
        check_vma=False,
    )
```

profile of v0, /device:TPU:1, one launch (start us, length us, event | category | flops | bytes accessed | tf_op | source)
XLA Modules:
  0.0 502.7 jit_solution(11137616695451651610)
XLA Ops:
  10.9 3.3 collective-permute-start
  16.3 8.9 %convolution_bitcast_fusion = f32[2,1,6,2,6,12,2,6,12]{8,7,4,6,3,2,0,5,1:T(8,128)} fusion(f32[2,6,2,2,6,6,23,1]{6,5,4,3,2,1,0,7:T(8,128)S(1)} %reshape.689, s32[12,12]{1,0:T(8,128)S(1)} %subtract_add_fusion), kind=kOutput, calls=%fused_computation.6 | convolution fusion | flops 68680944 | bytes 1154880 | tf_op jit(solution)/shard_map/...abcdr,oqr->...acobdq/dot_general | solution.py:102
  25.1 12.1 %copy.212 = f32[2,1,6,2,6,12,2,6,12]{8,7,6,5,4,3,2,0,1:T(8,128)} copy(f32[2,1,6,2,6,12,2,6,12]{8,7,4,6,3,2,0,5,1:T(8,128)} %convolution_bitcast_fusion) | data formatting | bytes 1990656 | tf_op jit(solution)/shard_map/...abcdr,oqr->...acobdq/transpose | solution.py:102
  37.3 9.3 %reshape.638 = f32[2,1,6,144,144]{4,3,2,0,1:T(8,128)S(1)} reshape(f32[2,1,6,2,6,12,2,6,12]{8,7,6,5,4,3,2,0,1:T(8,128)} %copy.212) | data formatting | bytes 1990656 | tf_op jit(solution)/shard_map/reshape | solution.py:103
  75.9 3.5 collective-permute-start.2
  79.5 4.6 collective-permute-done.2
  84.3 6.3 %collective-permute-done.3 = bf16[4,3,24,192]{3,2,1,0:T(8,128)(2,1)S(1)} collective-permute-done((bf16[4,3,24,192]{3,2,1,0:T(8,128)(2,1)S(1)}, bf16[4,3,24,192]{3,2,1,0:T(8,128)(2,1)S(1)}, u32[]{:S(2)}, u32[]{:S(2)}) %collective-permute-start.3) | collective-permute-done | bytes 110624 | tf_op jit(solution)/shard_map/ppermute | solution.py:22
  92.9 3.9 fusion.207
  98.3 7.9 %collective-permute-start.4 = (bf16[4,6,6,192]{3,2,1,0:T(8,128)(2,1)S(1)}, bf16[4,6,6,192]{3,2,1,0:T(8,128)(2,1)S(1)}, u32[]{:S(2)}, u32[]{:S(2)}) collective-permute-start(bf16[4,6,6,192]{3,2,1,0:T(8,128)(2,1)S(1)} %slice.279), channel_id=1, source_target_pairs={{1,0},{2,1},{3,2},{4,3},{5,4},{6,5},{7,6},{8,7},{9,8},{10,9},{11,1... | collective-permute-start | bytes 165896 | tf_op jit(solution)/shard_map/ppermute | solution.py:22
  107.8 3.5 collective-permute-done.5
  120.2 5.0 copy.318
  125.3 3.5 convolution_bitcast_fusion.1
  134.7 4.8 copy.315
  139.5 3.5 convolution_bitcast_fusion.2
  147.1 3.2 reshape.705
  150.3 4.8 copy.312
  155.2 3.5 convolution_bitcast_fusion.3
  168.4 5.2 %copy.309 = f32[2,2,6,12,2,6,12]{6,5,3,4,2,1,0:T(8,128)} copy(f32[2,2,6,12,2,6,12]{3,2,1,6,5,4,0:T(8,128)} %reshape.704) | data formatting | bytes 331776 | tf_op jit(solution)/shard_map/reshape.179
  173.6 3.5 convolution_bitcast_fusion.4
  185.5 4.8 copy.306
  190.3 3.5 convolution_bitcast_fusion.5
  198.4 5.0 copy.303
  203.4 3.5 convolution_bitcast_fusion.6
  240.1 248.2 %all-reduce.3.cloned.1.call-done = (f32[2,1,1,3312]{3,0,2,1:T(2,128)}, f32[2,1,1,3312]{3,0,2,1:T(2,128)}, f32[2,1,1,3312]{3,0,2,1:T(2,128)}, f32[2,1,1,3312]{3,0...) async-done(((f32[2,1,1,3312]{3,0,2,1:T(2,128)}, f32[2,1,1,3312]{3,0,2,1:T(2,128)}, f32[2,1,1,3312]{3,0,2,1:T(2,128)}, f32[2,1,1,3312]{3,0,2,1:T(2,128)}, ...) | async-done | bytes 158992 | tf_op jit(solution)/shard_map/psum | solution.py:210
  (249 shorter events, 122.3 us)
Async XLA Ops:
  7.2 84.0 %copy-start = (bf16[192,768]{1,0:T(8,128)(2,1)S(1)}, bf16[192,768]{1,0:T(8,128)(2,1)}, u32[]{:S(2)}) copy-start(bf16[192,768]{1,0:T(8,128)(2,1)} %param.17) | copy-start | bytes 884740
  7.2 481.1 %all-reduce.3.cloned.1.call-start = ((), (), s32[]{:S(2)}) async-start(), calls=%async_computation | async-start | bytes 319488 | tf_op jit(solution)/shard_map/psum | solution.py:210
  10.9 36.9 %collective-permute-start = (bf16[4,6,6,192]{3,2,1,0:T(8,128)(2,1)S(1)}, bf16[4,6,6,192]{3,2,1,0:T(8,128)(2,1)S(1)}, u32[]{:S(2)}, u32[]{:S(2)}) collective-permute-start(bf16[4,6,6,192]{3,2,1,0:T(8,128)(2,1)S(1)} %slice.245), channel_id=1, source_target_pairs={{1,0},{2,1},{3,2},{4,3},{5,4},{6,5},{7,6},{8,7},{9,8},{10,9},{11,1... | collective-permute-start | bytes 165896 | tf_op jit(solution)/shard_map/ppermute | solution.py:22
  47.9 6.4 %collective-permute-start.1 = (bf16[4,3,24,192]{3,2,1,0:T(8,128)(2,1)S(1)}, bf16[4,3,24,192]{3,2,1,0:T(8,128)(2,1)S(1)}, u32[]{:S(2)}, u32[]{:S(2)}) collective-permute-start(bf16[4,3,24,192]{3,2,1,0:T(8,128)(2,1)S(1)} %get-tuple-element.43), channel_id=1, source_target_pairs={{32,0},{64,32},{96,64},{128,96},{160,128},{192,160},{224,192},{0,2... | collective-permute-start | bytes 331784 | tf_op jit(solution)/shard_map/ppermute | solution.py:22
  49.9 24.2 %copy-start.45 = (f32[2,1,2]{2,1,0:T(1,128)}, f32[2,1,2]{2,1,0:T(1,128)S(1)}, u32[]{:S(2)}) copy-start(f32[2,1,2]{2,1,0:T(1,128)S(1)} %convert_multiply_fusion.1) | copy-start | bytes 52
  58.5 8.0 %copy-start.7 = (f32[2,2,144,144]{2,3,1,0:T(8,128)}, f32[2,2,144,144]{2,3,1,0:T(8,128)S(1)}, u32[]{:S(2)}) copy-start(f32[2,2,144,144]{2,3,1,0:T(8,128)S(1)} %compare_select_fusion.3) | copy-start | bytes 995332
  64.3 7.6 %copy-start.40 = (f32[2,2,144]{2,1,0:T(2,128)}, f32[2,2,144]{2,1,0:T(2,128)S(1)}, u32[]{:S(2)}) copy-start(f32[2,2,144]{2,1,0:T(2,128)S(1)} %get-tuple-element.54) | copy-start | bytes 6916
  74.1 16.5 %copy-start.2 = (bf16[4,6,24,192]{3,2,1,0:T(8,128)(2,1)S(1)}, bf16[4,6,24,192]{3,2,1,0:T(8,128)(2,1)}, u32[]{:S(2)}) copy-start(bf16[4,6,24,192]{3,2,1,0:T(8,128)(2,1)} %param.11) | copy-start | bytes 663556
  75.9 15.3 %copy-start.47 = (f32[192]{0:T(256)S(1)}, f32[192]{0:T(256)}, u32[]{:S(2)}) copy-start(f32[192]{0:T(256)} %param.16) | copy-start | bytes 2308
  75.9 8.2 %collective-permute-start.2 = (bf16[4,6,6,192]{3,2,1,0:T(8,128)(2,1)S(1)}, bf16[4,6,6,192]{3,2,1,0:T(8,128)(2,1)S(1)}, u32[]{:S(2)}, u32[]{:S(2)}) collective-permute-start(bf16[4,6,6,192]{3,2,1,0:T(8,128)(2,1)S(1)} %slice.274), channel_id=1, source_target_pairs={{31,0},{0,1},{1,2},{2,3},{3,4},{4,5},{5,6},{6,7},{7,8},{8,9},{9,10... | collective-permute-start | bytes 165896 | tf_op jit(solution)/shard_map/ppermute | solution.py:22
  84.2 6.4 %collective-permute-start.3 = (bf16[4,3,24,192]{3,2,1,0:T(8,128)(2,1)S(1)}, bf16[4,3,24,192]{3,2,1,0:T(8,128)(2,1)S(1)}, u32[]{:S(2)}, u32[]{:S(2)}) collective-permute-start(bf16[4,3,24,192]{3,2,1,0:T(8,128)(2,1)S(1)} %fusion.159), channel_id=1, source_target_pairs={{224,0},{0,32},{32,64},{64,96},{96,128},{128,160},{160,192},{192,2... | collective-permute-start | bytes 331784 | tf_op jit(solution)/shard_map/ppermute | solution.py:22
  96.8 14.5 %copy-start.27 = (f32[4,6,24]{2,1,0:T(8,128)}, f32[4,6,24]{2,1,0:T(8,128)S(1)}, u32[]{:S(2)}) copy-start(f32[4,6,24]{2,1,0:T(8,128)S(1)} %get-tuple-element.69) | copy-start | bytes 6916
  96.8 14.5 %copy-start.29 = (f32[4,6,24]{2,1,0:T(8,128)}, f32[4,6,24]{2,1,0:T(8,128)S(1)}, u32[]{:S(2)}) copy-start(f32[4,6,24]{2,1,0:T(8,128)S(1)} %get-tuple-element.70) | copy-start | bytes 6916
  98.3 8.8 %collective-permute-start.4 = (bf16[4,6,6,192]{3,2,1,0:T(8,128)(2,1)S(1)}, bf16[4,6,6,192]{3,2,1,0:T(8,128)(2,1)S(1)}, u32[]{:S(2)}, u32[]{:S(2)}) collective-permute-start(bf16[4,6,6,192]{3,2,1,0:T(8,128)(2,1)S(1)} %slice.279), channel_id=1, source_target_pairs={{1,0},{2,1},{3,2},{4,3},{5,4},{6,5},{7,6},{8,7},{9,8},{10,9},{11,1... | collective-permute-start | bytes 165896 | tf_op jit(solution)/shard_map/ppermute | solution.py:22
  107.2 4.1 collective-permute-start.5
  203.4 7.9 %copy-start.14 = (bf16[2,2,144,144]{2,3,1,0:T(8,128)(2,1)S(1)}, bf16[2,2,144,144]{2,3,1,0:T(8,128)(2,1)}, u32[]{:S(2)}) copy-start(bf16[2,2,144,144]{2,3,1,0:T(8,128)(2,1)} %get-tuple-element.35) | copy-start | bytes 497668
  236.6 3.3 collective-permute-start.6
  236.7 256.8 %copy-start.26 = (f32[4,6,24]{2,1,0:T(8,128)S(1)}, f32[4,6,24]{2,1,0:T(8,128)}, u32[]{:S(2)}) copy-start(f32[4,6,24]{2,1,0:T(8,128)} %copy-done.25) | copy-start | bytes 6916
  236.7 256.8 %copy-start.44 = (f32[192]{0:T(256)S(1)}, f32[192]{0:T(256)}, u32[]{:S(2)}) copy-start(f32[192]{0:T(256)} %param.13) | copy-start | bytes 2308
  239.3 254.8 %copy-start.4 = (f32[4,6,24,192]{3,2,1,0:T(8,128)S(1)}, f32[4,6,24,192]{3,2,1,0:T(8,128)}, u32[]{:S(2)}) copy-start(f32[4,6,24,192]{3,2,1,0:T(8,128)} %get-tuple-element.56) | copy-start | bytes 1327108
  239.3 254.8 %copy-start.17 = (bf16[4,6,24,192]{3,2,1,0:T(8,128)(2,1)S(1)}, bf16[4,6,24,192]{3,2,1,0:T(8,128)(2,1)}, u32[]{:S(2)}) copy-start(bf16[4,6,24,192]{3,2,1,0:T(8,128)(2,1)} %param.12) | copy-start | bytes 663556
  239.3 254.9 %copy-start.28 = (f32[4,6,24]{2,1,0:T(8,128)S(1)}, f32[4,6,24]{2,1,0:T(8,128)}, u32[]{:S(2)}) copy-start(f32[4,6,24]{2,1,0:T(8,128)} %copy-done.27) | copy-start | bytes 6916
  239.3 254.9 %copy-start.30 = (f32[4,6,24]{2,1,0:T(8,128)S(1)}, f32[4,6,24]{2,1,0:T(8,128)}, u32[]{:S(2)}) copy-start(f32[4,6,24]{2,1,0:T(8,128)} %copy-done.29) | copy-start | bytes 6916
  240.0 253.6 %collective-permute-start.7 = (bf16[4,3,24,192]{3,2,1,0:T(8,128)(2,1)S(1)}, bf16[4,3,24,192]{3,2,1,0:T(8,128)(2,1)S(1)}, u32[]{:S(2)}, u32[]{:S(2)}) collective-permute-start(bf16[4,3,24,192]{3,2,1,0:T(8,128)(2,1)S(1)} %fusion.157), channel_id=1, source_target_pairs={{224,0},{0,32},{32,64},{64,96},{96,128},{128,160},{160,192},{192,2... | collective-permute-start | bytes 331784 | tf_op jit(solution)/shard_map/ppermute | solution.py:22
  (35 other events, 115.8 us)
Sparse Core Ops, SparseCore 0:
  236.8 251.3 all-reduce.2
where the time goes:
time: 511 us; the launch traced here: 503 us
  waiting for transfers between devices  264 us (52%)
  local copies, waits for them, and re-layouts  97.5 us (19%)
  matrix products  86.3 us (17%)
  other arithmetic  22.1 us (4%)
  starting transfers between devices  17.6 us (3%)
  between operations  15.1 us (3%)
    psum x1, waiting for transfers between devices, attention_backward(): folded = lax.psum(folded, 'lon')  248 us
    another operation x13, local copies, waits for them, and re-layouts  47.4 us
    dot_general x6, matrix products, fold_bias(): jnp.einsum('...acobdq,oqr->...abcdr', shaped, lon_table(), precision=high...  20.8 us
    ppermute x8, starting transfers between devices, passed_along(): return lax.ppermute(block, axis, route)  17.5 us
    ppermute x8, waiting for transfers between devices, passed_along(): return lax.ppermute(block, axis, route)  15.9 us
    dot_general x6, matrix products, attention_backward(): jnp.einsum('abcpq,abcpd->abcqd', probs_low, grad_head, preferred_element_...  13.4 us
    transpose x1, local copies, waits for them, and re-layouts, expand_bias(): jnp.einsum('...abcdr,oqr->...acobdq', shaped, lon_table(), precision=high...  12.1 us
    dot_general x6, matrix products, attention_forward(): jnp.einsum('abcpq,abcqd->abcpd', probs.astype(jnp.bfloat16), value_h, pre...  10.7 us
  transfers between devices with their start and end apart: 9, of which 6 were waited for; matrix products, arithmetic and copies ran while one was open for 9% of the time, Pallas kernels for 0%

commit v1 on v0

v1 whole, which is shorter than its diff:
```python
import math

import jax
import jax.numpy as jnp
import numpy as np
from jax import lax
from jax.experimental import pallas as pl
from jax.experimental.pallas import tpu as pltpu
from jax.sharding import PartitionSpec as P

C = 192
HEADS = 6
HD = 32
FF = 768
WZ = 2
WLAT = 6
WLON = 12
SPREAD = 2 * WLON - 1
POS = WZ * WLAT * WLON
PAIR = WZ * WLAT
TAB = PAIR * SPREAD
ROWS = HEADS * POS

epsilon = 1e-05
keep_share = 0.8
gelu_coef = 0.044715
bf16 = jnp.bfloat16
f32 = jnp.float32


def shifted(block, lat_step, lon_step):
    lats, lons = lax.axis_size("lat"), lax.axis_size("lon")
    route = []
    for a in range(lats):
        for b in range(lons):
            target = ((a + lat_step) % lats) * lons + (b + lon_step) % lons
            route.append((a * lons + b, target))
    return lax.ppermute(block, ("lat", "lon"), route)


def swapped(block, distance):
    lons = lax.axis_size("lon")
    return lax.ppermute(block, "lon", [(i, i ^ distance) for i in range(lons)])


def mm(a, b):
    return lax.dot_general(a, b, (((1,), (0,)), ((), ())), preferred_element_type=f32)


def mm_nt(a, b):
    return lax.dot_general(a, b, (((1,), (1,)), ((), ())), preferred_element_type=f32)


def norm_parts(values, gain):
    row_mean = jnp.mean(values, axis=-1, keepdims=True)
    centred = values - row_mean
    variance = jnp.mean(centred * centred, axis=-1, keepdims=True)
    inverse = lax.rsqrt(variance + epsilon)
    normed = centred * inverse
    return normed * gain, normed, inverse


def norm_back(grad_in, gain, normed, inverse):
    scaled = grad_in * gain
    first_mean = jnp.mean(scaled, axis=-1, keepdims=True)
    second_mean = jnp.mean(scaled * normed, axis=-1, keepdims=True)
    return (scaled - first_mean - normed * second_mean) * inverse


def gelu_parts(values):
    factor = math.sqrt(2.0 / math.pi)
    square = values * values
    tangent = jnp.tanh(factor * (values + gelu_coef * values * square))
    half = 0.5 * (1.0 + tangent)
    result = values * half
    derivative = half + 0.5 * values * (1.0 - tangent * tangent) * (
        factor + (3.0 * gelu_coef * factor) * square
    )
    return result, derivative


def head_blocks(wide):
    return jnp.concatenate(
        [wide[h * HD : (h + 1) * HD, h * POS : (h + 1) * POS] for h in range(HEADS)], axis=0
    )


def spread_heads(rows, head_mask):
    return jnp.concatenate([rows * head_mask[h : h + 1, :] for h in range(HEADS)], axis=0)


def block_kernel(
    field_ref,
    cot_ref,
    lon_ref,
    lat_ref,
    diag_ref,
    gain1_ref,
    wqkv_t_ref,
    wproj_ref,
    gain2_ref,
    wup_ref,
    wdown_ref,
    table_ref,
    label_row_ref,
    label_col_ref,
    factor_ref,
    perm_ref,
    perm_t_ref,
    head_mask_ref,
    own_out,
    lon_out,
    lat_out,
    diag_out,
    fold_out,
    frame,
    bias,
):
    half = WLAT // 2
    cols = 2 * WLON
    edge = WLON // 2
    inner = cols - edge
    root = 1.0 / math.sqrt(HD)
    for t, own in enumerate((field_ref, cot_ref)):
        for level in range(4):
            z = (level + 1) % 4
            for i in range(half):
                row = (level * WLAT + i) * cols
                frame[t, row : row + cols, :] = jnp.concatenate(
                    [own[z, half + i].astype(f32)[edge:, :], lon_ref[t, z, i].astype(f32)], axis=0
                )
                row = (level * WLAT + half + i) * cols
                frame[t, row : row + cols, :] = jnp.concatenate(
                    [lat_ref[t, z, i].astype(f32), diag_ref[t, z, i].astype(f32)], axis=0
                )
    gain1 = gain1_ref[...]
    gain2 = gain2_ref[...]
    wq_t = wqkv_t_ref[0:C, :]
    wk_t = wqkv_t_ref[C : 2 * C, :]
    wv_t = wqkv_t_ref[2 * C : 3 * C, :]
    head_mask = head_mask_ref[...]
    perm = perm_ref[...]
    perm_t = perm_t_ref[...]
    for n in range(2):
        for o in range(WLON):
            start = PAIR * (WLON - 1 - o)
            bias[:, PAIR * o : PAIR * (o + 1), :] = table_ref[n, :, :, start : start + POS]
        bias_t = bias[...].reshape(ROWS, POS).T
        x = mm(perm, frame[0, n * 2 * POS : (n + 1) * 2 * POS, :].astype(bf16))
        cot = mm(perm, frame[1, n * 2 * POS : (n + 1) * 2 * POS, :].astype(bf16))
        scaled1, normed1, inverse1 = norm_parts(x, gain1)
        h1 = scaled1.astype(bf16)
        q_all = mm_nt(h1, wq_t).astype(bf16)
        k_all = mm_nt(h1, wk_t).astype(bf16)
        v_all = mm_nt(h1, wv_t).astype(bf16)
        saved = []
        branches = []
        for c in range(2):
            w = 2 * n + c
            rows = slice(c * POS, (c + 1) * POS)
            v_t = mm_nt(wv_t, h1[rows]).astype(bf16)
            q_wide = spread_heads(q_all[rows], head_mask)
            scores = mm_nt(k_all[rows], q_wide) * root + bias_t
            allowed = label_col_ref[:, w : w + 1] == label_row_ref[w]
            scores = jnp.where(allowed, scores, -1e30)
            weights = jnp.exp(scores - jnp.max(scores, axis=0, keepdims=True))
            probs = weights * (1.0 / jnp.sum(weights, axis=0, keepdims=True))
            probs_low = probs.astype(bf16)
            attended = head_blocks(mm(v_t, probs_low)).T.astype(bf16)
            factor = factor_ref[w]
            branches.append((mm(attended, wproj_ref[...]) * factor).astype(bf16).astype(f32))
            saved.append((q_wide, probs, probs_low))
        y_sum = x + jnp.concatenate(branches, axis=0)
        scaled2, normed2, inverse2 = norm_parts(y_sum, gain2)
        act, slope = gelu_parts(mm(scaled2.astype(bf16), wup_ref[...]))
        result = (y_sum + mm(act.astype(bf16), wdown_ref[...])).astype(bf16)
        grad_up = (mm_nt(cot.astype(bf16), wdown_ref[...]) * slope).astype(bf16)
        grad_sum = cot + norm_back(mm_nt(grad_up, wup_ref[...]), gain2, normed2, inverse2)
        grad_low_in = grad_sum.astype(bf16).astype(f32)
        folded = None
        grad_h1 = []
        for c in range(2):
            w = 2 * n + c
            rows = slice(c * POS, (c + 1) * POS)
            q_wide, probs, probs_low = saved[c]
            k_t = mm_nt(wk_t, h1[rows]).astype(bf16)
            grad_branch = (grad_low_in[rows] * factor_ref[w]).astype(bf16)
            grad_att = mm_nt(grad_branch, wproj_ref[...]).astype(bf16)
            g_wide = spread_heads(grad_att, head_mask)
            grad_probs = mm_nt(v_all[rows], g_wide)
            inner_sum = jnp.sum(probs * grad_probs, axis=0, keepdims=True)
            grad_scores = probs * (grad_probs - inner_sum)
            folded = grad_scores if folded is None else folded + grad_scores
            grad_low = grad_scores.astype(bf16)
            grad_q = (head_blocks(mm(k_t, grad_low)).T * root).astype(bf16)
            grad_k = (mm(grad_low, q_wide) * root).astype(bf16)
            grad_v = mm(probs_low, g_wide).astype(bf16)
            grad_h1.append(mm(grad_q, wq_t) + mm(grad_k, wk_t) + mm(grad_v, wv_t))
        grad_h1 = jnp.concatenate(grad_h1, axis=0).astype(bf16).astype(f32)
        grad_field = (grad_sum + norm_back(grad_h1, gain1, normed1, inverse1)).astype(bf16)
        bias[...] = folded.T.reshape(HEADS, POS, POS)
        total = None
        for o in range(WLON):
            left = PAIR * (WLON - 1 - o)
            right = TAB - POS - left
            parts = [bias[:, PAIR * o : PAIR * (o + 1), :]]
            if left:
                parts = [jnp.zeros((HEADS, PAIR, left), f32)] + parts
            if right:
                parts = parts + [jnp.zeros((HEADS, PAIR, right), f32)]
            piece = jnp.concatenate(parts, axis=2)
            total = piece if total is None else total + piece
        fold_out[n] = total
        for t, value in enumerate((result, grad_field)):
            natural = mm(perm_t, value)
            for dz in range(WZ):
                z = (2 * n + dz + 1) % 4
                for i in range(half):
                    row = (dz * WLAT + i) * cols
                    slab = natural[row : row + cols]
                    own_out[t, z, i] = slab[:inner].astype(bf16)
                    lon_out[t, z, i] = slab[inner:].astype(bf16)
                    row = (dz * WLAT + half + i) * cols
                    slab = natural[row : row + cols]
                    lat_out[t, z, i] = slab[:inner].astype(bf16)
                    diag_out[t, z, i] = slab[inner:].astype(bf16)


def finish_kernel(own_ref, lon_ref, lat_ref, diag_ref, out_ref, grad_ref):
    half = WLAT // 2
    for t, target in enumerate((out_ref, grad_ref)):
        for z in range(4):
            for i in range(half):
                target[z, i] = jnp.concatenate(
                    [diag_ref[t, z, i].astype(f32), lat_ref[t, z, i].astype(f32)], axis=0
                ).astype(bf16)
                target[z, half + i] = jnp.concatenate(
                    [lon_ref[t, z, i].astype(f32), own_ref[t, z, i].astype(f32)], axis=0
                ).astype(bf16)


def window_order():
    perm = np.zeros((2 * POS, 2 * POS), np.float32)
    for c in range(2):
        for j in range(WLON):
            for d in range(PAIR):
                perm[c * POS + j * PAIR + d, d * 2 * WLON + c * WLON + j] = 1.0
    return perm


def lon_sum(value):
    lons = lax.axis_size("lon")
    group = min(4, lons)
    others = lons // group
    me = lax.axis_index("lon") % group
    low = value.astype(bf16)
    if group < 4:
        low = low.reshape((group, 4 // group) + low.shape[1:])

    def quarter(d):
        return lax.dynamic_index_in_dim(low, me ^ d, 0, keepdims=False)

    def tree(parts):
        while len(parts) > 1:
            parts = [parts[i] + parts[i + 1] for i in range(0, len(parts), 2)]
        return parts[0]

    parts = [quarter(0)] + [swapped(quarter(d), d) for d in range(1, group)]
    mine = tree([p.astype(f32) for p in parts]).astype(bf16)
    parts = [mine] + [swapped(mine, d * group) for d in range(1, others)]
    mine = tree([p.astype(f32) for p in parts]).astype(bf16)
    parts = [mine] + [swapped(mine, d) for d in range(1, group)]
    bit = 1
    while bit < group:
        flip = (me & bit) != 0
        parts = [jnp.where(flip, parts[i ^ bit], parts[i]) for i in range(group)]
        bit *= 2
    return jnp.stack(parts, axis=0).astype(f32)


def body(
    field_in,
    cotangent,
    ln1_gain,
    w_qkv,
    w_proj,
    ln2_gain,
    w_up,
    w_down,
    bias_table,
    region_ids,
    keep_flags,
):
    levels, lat_rows, lon_cols, channels = field_in.shape
    half = WLAT // 2
    edge = WLON // 2
    both = (field_in, cotangent)
    lon_part = shifted(jnp.stack([v[:, half:, :edge] for v in both]), 0, -1)
    lat_part = shifted(jnp.stack([v[:, :half, edge:] for v in both]), -1, 0)
    diag_part = shifted(jnp.stack([v[:, :half, :edge] for v in both]), -1, -1)

    lat_start = lax.axis_index("lat") * lat_rows
    lat_total = lax.axis_size("lat") * lat_rows
    level_pos = jnp.arange(levels, dtype=jnp.int32)[:, None, None]
    lat_pos = lat_start + jnp.arange(lat_rows, dtype=jnp.int32)[None, :, None]
    labels = 4 * region_ids + (
        2 * (level_pos >= levels - WZ // 2).astype(jnp.int32)
        + (lat_pos >= lat_total - half).astype(jnp.int32)
    )
    labels = labels.reshape(2, WZ, WLAT, 2, WLON).transpose(0, 3, 4, 1, 2).reshape(4, POS)
    label_row = jnp.tile(labels, (1, HEADS)).reshape(4, 1, ROWS)
    label_col = labels.T
    factor = (keep_flags.astype(f32) / keep_share).reshape(4)

    table = bias_table.reshape(2, HEADS, WZ, WZ, WLAT, WLAT, SPREAD)[..., ::-1]
    table = table.transpose(0, 1, 2, 4, 6, 3, 5).reshape(2, HEADS, PAIR, TAB)

    perm = window_order()
    head_mask = np.repeat(np.eye(HEADS, dtype=np.float32), HD, axis=1)
    vmem = pl.BlockSpec(memory_space=pltpu.VMEM)
    smem = pl.BlockSpec(memory_space=pltpu.SMEM)
    inner = lon_cols - edge
    own, lon_back, lat_back, diag_back, fold = pl.pallas_call(
        block_kernel,
        out_shape=(
            jax.ShapeDtypeStruct((2, 4, half, inner, C), bf16),
            jax.ShapeDtypeStruct((2, 4, half, edge, C), bf16),
            jax.ShapeDtypeStruct((2, 4, half, inner, C), bf16),
            jax.ShapeDtypeStruct((2, 4, half, edge, C), bf16),
            jax.ShapeDtypeStruct((2, HEADS, PAIR, TAB), f32),
        ),
        in_specs=[vmem] * 14 + [smem] + [vmem] * 3,
        out_specs=(vmem,) * 5,
        scratch_shapes=[
            pltpu.VMEM((2, 4 * WLAT * lon_cols, C), f32),
            pltpu.VMEM((HEADS, POS, POS), f32),
        ],
        compiler_params=pltpu.CompilerParams(vmem_limit_bytes=48 * 1024 * 1024),
        name="block",
    )(
        field_in,
        cotangent,
        lon_part,
        lat_part,
        diag_part,
        ln1_gain.reshape(1, C),
        w_qkv.T,
        w_proj,
        ln2_gain.reshape(1, C),
        w_up,
        w_down,
        table,
        label_row,
        label_col,
        factor,
        jnp.asarray(perm, bf16),
        jnp.asarray(perm.T, bf16),
        jnp.asarray(head_mask, bf16),
    )
    lon_back = shifted(lon_back, 0, 1)
    lat_back = shifted(lat_back, 1, 0)
    diag_back = shifted(diag_back, 1, 1)
    grads = lon_sum(fold.reshape(4, HEADS // 2 * PAIR, TAB))
    grads = grads.reshape(2, HEADS, WZ, WLAT, SPREAD, WZ, WLAT)[:, :, :, :, ::-1]
    grads = grads.transpose(0, 1, 2, 5, 3, 6, 4).reshape(2, 1, HEADS, PAIR * TAB)
    result, grad_field = pl.pallas_call(
        finish_kernel,
        out_shape=(jax.ShapeDtypeStruct(field_in.shape, bf16),) * 2,
        in_specs=[vmem] * 4,
        out_specs=(vmem,) * 2,
        name="finish",
    )(own, lon_back, lat_back, diag_back)
    return (result, grad_field, grads)


def solution(mesh):
    placed = (
        P(None, "lat", "lon", None),
        P(None, "lat", "lon", None),
        P(),
        P(),
        P(),
        P(),
        P(),
        P(),
        P(None, "lat", None, None),
        P(None, "lat", "lon"),
        P(None, "lat", "lon"),
    )
    return jax.shard_map(
        body,
        mesh=mesh,
        in_specs=placed,
        out_specs=(
            P(None, "lat", "lon", None),
            P(None, "lat", "lon", None),
            P(None, "lat", None, None),
        ),
        check_vma=False,
    )
```

time: 511 us -> 94.4 us (0.18); the launches traced: 503 us -> 93.9 us
  waiting for transfers between devices: 264 us -> 4.62 us
  matrix products: 86.3 us -> 0 us
  local copies, waits for them, and re-layouts: 97.5 us -> 34.5 us
  starting transfers between devices: 17.6 us -> 38.1 us
  other arithmetic: 22.1 us -> 2.52 us
  between operations: 15.1 us -> 1.01 us
  Pallas kernels: 0 us -> 13.2 us
    psum x1 -> x0, waiting for transfers between devices: 248 us -> none  [attention_backward(): folded = lax.psum(folded, 'lon')]
    dot_general x50 -> x0, matrix products: 86.3 us -> none  [the longest x6 20.8 us: fold_bias(): jnp.einsum('...acobdq,oqr->...abcdr', shaped, lon_table(), precision=high...]
    another operation x22 -> x6, local copies, waits for them, and re-layouts: 56 us -> 2.32 us  [the longest x1 1.06 us: body(): lat_part = shifted(jnp.stack([v[:, :half, edge:] for v in both]), -1, 0)]
    ppermute x8 -> x19, starting transfers between devices: 17.5 us -> 38.1 us  [the longest x13 21.6 us: swapped(): return lax.ppermute(block, 'lon', [(i, i ^ distance) for i in range(lons)])]
    pallas_call x0 -> x2, Pallas kernels: none -> 13.2 us  [the longest x1 11.2 us: body(): pl.pallas_call(block_kernel, out_shape=(jax.ShapeDtypeStruct((2, 4, half,...]
    ppermute x8 -> x19, waiting for transfers between devices: 15.9 us -> 4.62 us  [the longest x13 4.6 us: swapped(): return lax.ppermute(block, 'lon', [(i, i ^ distance) for i in range(lons)])]
    reduce_sum x11 -> x0, other arithmetic: 10.9 us -> none  [the longest x6 7.53 us: attention_backward(): folded = fold_bias(jnp.sum(grad_scores, axis=2))]
    transpose x8 -> x1, local copies, waits for them, and re-layouts: 14.5 us -> 4.87 us  [body(): grads.transpose(0, 1, 2, 5, 3, 6, 4).reshape(2, 1, HEADS, PAIR * TAB)]
  transfers between devices with their start and end apart: 9 -> 19, of which waited for: 6 -> 4; matrix products, arithmetic and copies ran while one was open for 9% -> 37% of each run, Pallas kernels for 0% -> 0%
where the time goes in v1:
time: 94.4 us; the launch traced here: 93.9 us
  starting transfers between devices  38.1 us (40%)
  local copies, waits for them, and re-layouts  34.5 us (37%)
  Pallas kernels  13.2 us (14%)
  waiting for transfers between devices  4.62 us (5%)
  other arithmetic  2.52 us (3%)
  between operations  1.01 us (1%)
    ppermute x13, starting transfers between devices, swapped(): return lax.ppermute(block, 'lon', [(i, i ^ distance) for i in range(lons)])  21.6 us
    ppermute x6, starting transfers between devices, shifted(): return lax.ppermute(block, ('lat', 'lon'), route)  16.6 us
    pallas_call x1, Pallas kernels, body(): pl.pallas_call(block_kernel, out_shape=(jax.ShapeDtypeStruct((2, 4, half,...  11.2 us
    unnamed x33, local copies, waits for them, and re-layouts  10 us
    reshape x2, local copies, waits for them, and re-layouts, body(): table = table.transpose(0, 1, 2, 4, 6, 3, 5).reshape(2, HEADS, PAIR, TAB)  9.76 us
    transpose x1, local copies, waits for them, and re-layouts, body(): grads.transpose(0, 1, 2, 5, 3, 6, 4).reshape(2, 1, HEADS, PAIR * TAB)  4.87 us
    ppermute x13, waiting for transfers between devices, swapped(): return lax.ppermute(block, 'lon', [(i, i ^ distance) for i in range(lons)])  4.6 us
    convert_element_type x1, local copies, waits for them, and re-layouts, lon_sum(): return jnp.stack(parts, axis=0).astype(f32)  4.07 us
  transfers between devices with their start and end apart: 19, of which 4 were waited for; matrix products, arithmetic and copies ran while one was open for 37% of the time, Pallas kernels for 0%

profile of v1, /device:TPU:1, one launch (start us, length us, event | category | flops | bytes accessed | tf_op | source)
XLA Modules:
  0.0 93.9 jit_solution(7969221017915046144)
XLA Ops:
  1.6 3.3 %collective-permute-start = (bf16[2,4,3,6,192]{4,3,2,1,0:T(8,128)(2,1)S(1)}, bf16[2,4,3,6,192]{4,3,2,1,0:T(8,128)(2,1)S(1)}, u32[]{:S(2)}, u32[]{:S(2)}) collective-permute-start(bf16[2,4,3,6,192]{4,3,2,1,0:T(8,128)(2,1)S(1)} %pad_maximum_fusion.1), channel_id=1, source_target_pairs={{0,31},{1,0},{2,1},{3,2},{4,3},{5,4},{6,5},{7,6},{8,7},{9,8},{10,9... | collective-permute-start | bytes 165896 | tf_op jit(solution)/shard_map/ppermute | solution.py:38
  5.0 8.7 %collective-permute-start.2 = (bf16[2,4,3,6,192]{4,3,2,1,0:T(8,128)(2,1)S(1)}, bf16[2,4,3,6,192]{4,3,2,1,0:T(8,128)(2,1)S(1)}, u32[]{:S(2)}, u32[]{:S(2)}) collective-permute-start(bf16[2,4,3,6,192]{4,3,2,1,0:T(8,128)(2,1)S(1)} %pad_maximum_fusion.2), channel_id=1, source_target_pairs={{0,255},{1,224},{2,225},{3,226},{4,227},{5,228},{6,229},{7,230},{8... | collective-permute-start | bytes 165896 | tf_op jit(solution)/shard_map/ppermute | solution.py:38
  13.7 1.1 %slice_bitcast_fusion = (bf16[1,4,3,18,192]{4,3,2,1,0:T(8,128)(2,1)S(1)}, bf16[1,4,3,18,192]{4,3,2,1,0:T(8,128)(2,1)S(1)}) fusion(bf16[4,6,24,192]{3,2,1,0:T(8,128)(2,1)} %cot_ref.1, bf16[4,6,24,192]{3,2,1,0:T(8,128)(2,1)} %field_ref.1), kind=kLoop, calls=%fused_computation.2 | loop fusion | bytes 331776 | tf_op jit(solution)/shard_map/stack | solution.py:299
  15.5 1.1 %collective-permute-start.1 = (bf16[2,4,3,18,192]{4,3,2,1,0:T(8,128)(2,1)}, bf16[2,4,3,18,192]{4,3,2,1,0:T(8,128)(2,1)S(1)}, u32[]{:S(2)}, u32[]{:S(2)}) collective-permute-start(bf16[2,4,3,18,192]{4,3,2,1,0:T(8,128)(2,1)} %pad_maximum_fusion), channel_id=1, source_target_pairs={{0,224},{1,225},{2,226},{3,227},{4,228},{5,229},{6,230},{7,231},{8... | collective-permute-start | bytes 497672 | tf_op jit(solution)/shard_map/ppermute | solution.py:38
  18.9 1.0 %copy.24 = f32[2,1,6,3312]{3,0,2,1:T(2,128)S(1)} copy(f32[2,1,6,3312]{3,1,2,0:T(1,128)} %param.22) | data formatting | bytes 317952 | tf_op args[8]
  19.9 1.1 %copy.23 = bf16[192,576]{0,1:T(8,128)(2,1)S(1)} copy(bf16[192,576]{1,0:T(8,128)(2,1)} %param.17) | data formatting | bytes 442368 | tf_op args[3]
  22.0 2.2 %rev.6 = f32[2,6,2,2,6,6,23]{6,5,4,3,2,0,1:T(8,128)} reverse(f32[2,6,2,2,6,6,23]{6,5,4,3,2,0,1:T(8,128)S(1)} %reshape.92), dimensions={6} | reverse | bytes 317952 | tf_op jit(solution)/shard_map/rev | solution.py:315
  24.3 6.0 %copy.33 = f32[2,6,2,6,23,2,6]{6,5,4,3,2,1,0:T(2,128)} copy(f32[2,6,2,6,23,2,6]{4,6,3,5,2,0,1:T(8,128)} %bitcast.45) | data formatting | bytes 317952 | tf_op jit(solution)/shard_map/reshape | solution.py:316
  30.2 3.8 %reshape.99.table_ref = f32[2,6,12,276]{3,2,1,0:T(8,128)S(1)} reshape(f32[2,6,2,6,23,2,6]{6,5,4,3,2,1,0:T(2,128)} %copy.33) | data formatting | bytes 317952 | tf_op jit(solution)/shard_map/reshape | solution.py:316
  34.2 11.2 %block.1 = (bf16[2,4,3,18,192]{4,3,2,1,0:T(8,128)(2,1)S(1)}, bf16[2,4,3,6,192]{4,3,2,1,0:T(8,128)(2,1)S(1)}, bf16[2,4,3,18,192]{4,3,2,1,0:T(8,128)(2,1)S(1)}, bf...) custom-call(bf16[4,6,24,192]{3,2,1,0:T(8,128)(2,1)S(1)} %copy-done, bf16[4,6,24,192]{3,2,1,0:T(8,128)(2,1)S(1)} %copy-done.1, ...), custom_call_target="tpu_custom_call" | custom-call | tf_op jit(solution)/shard_map/block/pallas_call | solution.py:323
  46.6 3.3 %collective-permute-start.7 = (bf16[36,276]{1,0:T(8,128)(2,1)S(1)}, bf16[36,276]{1,0:T(8,128)(2,1)S(1)}, u32[]{:S(2)}, u32[]{:S(2)}) collective-permute-start(bf16[36,276]{1,0:T(8,128)(2,1)S(1)} %get-tuple-element.30), channel_id=1, source_target_pairs={{0,2},{1,3},{2,0},{3,1},{4,6},{5,7},{6,4},{7,5},{8,10},{9,11},{10,... | collective-permute-start | bytes 59624 | tf_op jit(solution)/shard_map/ppermute | solution.py:43
  49.9 1.9 %collective-permute-done.8 = bf16[36,276]{1,0:T(8,128)(2,1)S(1)} collective-permute-done((bf16[36,276]{1,0:T(8,128)(2,1)S(1)}, bf16[36,276]{1,0:T(8,128)(2,1)S(1)}, u32[]{:S(2)}, u32[]{:S(2)}) %collective-permute-start.8) | collective-permute-done | bytes 19904 | tf_op jit(solution)/shard_map/ppermute | solution.py:43
  53.5 2.5 %collective-permute-start.13 = (bf16[36,276]{1,0:T(8,128)(2,1)S(1)}, bf16[36,276]{1,0:T(8,128)(2,1)S(1)}, u32[]{:S(2)}, u32[]{:S(2)}) collective-permute-start(bf16[36,276]{1,0:T(8,128)(2,1)S(1)} %fusion.1), channel_id=1, source_target_pairs={{0,20},{1,21},{2,22},{3,23},{4,16},{5,17},{6,18},{7,19},{8,28},{9,... | collective-permute-start | bytes 59624 | tf_op jit(solution)/shard_map/ppermute | solution.py:43
  56.1 4.3 %collective-permute-start.12 = (bf16[36,276]{1,0:T(8,128)(2,1)S(1)}, bf16[36,276]{1,0:T(8,128)(2,1)S(1)}, u32[]{:S(2)}, u32[]{:S(2)}) collective-permute-start(bf16[36,276]{1,0:T(8,128)(2,1)S(1)} %fusion.1), channel_id=1, source_target_pairs={{0,16},{1,17},{2,18},{3,19},{4,20},{5,21},{6,22},{7,23},{8,24},{9,... | collective-permute-start | bytes 59624 | tf_op jit(solution)/shard_map/ppermute | solution.py:43
  60.5 3.4 %collective-permute-start.9 = (bf16[36,276]{1,0:T(8,128)(2,1)S(1)}, bf16[36,276]{1,0:T(8,128)(2,1)S(1)}, u32[]{:S(2)}, u32[]{:S(2)}) collective-permute-start(bf16[36,276]{1,0:T(8,128)(2,1)S(1)} %fusion.1), channel_id=1, source_target_pairs={{0,4},{1,5},{2,6},{3,7},{4,0},{5,1},{6,2},{7,3},{8,12},{9,13},{10,... | collective-permute-start | bytes 59624 | tf_op jit(solution)/shard_map/ppermute | solution.py:43
  63.9 1.6 %collective-permute-done.11 = bf16[36,276]{1,0:T(8,128)(2,1)S(1)} collective-permute-done((bf16[36,276]{1,0:T(8,128)(2,1)S(1)}, bf16[36,276]{1,0:T(8,128)(2,1)S(1)}, u32[]{:S(2)}, u32[]{:S(2)}) %collective-permute-start.11) | collective-permute-done | bytes 19904 | tf_op jit(solution)/shard_map/ppermute | solution.py:43
  65.5 3.0 %collective-permute-start.18 = (bf16[36,276]{1,0:T(8,128)(2,1)S(1)}, bf16[36,276]{1,0:T(8,128)(2,1)S(1)}, u32[]{:S(2)}, u32[]{:S(2)}) collective-permute-start(bf16[36,276]{1,0:T(8,128)(2,1)S(1)} %add_convert_fusion), channel_id=1, source_target_pairs={{0,1},{1,0},{2,3},{3,2},{4,5},{5,4},{6,7},{7,6},{8,9},{9,8},{10,11... | collective-permute-start | bytes 59624 | tf_op jit(solution)/shard_map/ppermute | solution.py:43
  68.5 2.6 %collective-permute-start.17 = (bf16[36,276]{1,0:T(8,128)(2,1)S(1)}, bf16[36,276]{1,0:T(8,128)(2,1)S(1)}, u32[]{:S(2)}, u32[]{:S(2)}) collective-permute-start(bf16[36,276]{1,0:T(8,128)(2,1)S(1)} %add_convert_fusion), channel_id=1, source_target_pairs={{0,2},{1,3},{2,0},{3,1},{4,6},{5,7},{6,4},{7,5},{8,10},{9,11},{10,... | collective-permute-start | bytes 59624 | tf_op jit(solution)/shard_map/ppermute | solution.py:43
  71.7 2.6 %collective-permute-start.3 = (bf16[2,4,3,6,192]{4,3,2,1,0:T(8,128)(2,1)S(1)}, bf16[2,4,3,6,192]{4,3,2,1,0:T(8,128)(2,1)S(1)}, u32[]{:S(2)}, u32[]{:S(2)}) collective-permute-start(bf16[2,4,3,6,192]{4,3,2,1,0:T(8,128)(2,1)S(1)} %get-tuple-element.11), channel_id=1, source_target_pairs={{0,1},{1,2},{2,3},{3,4},{4,5},{5,6},{6,7},{7,8},{8,9},{9,10},{10,1... | collective-permute-start | bytes 165896 | tf_op jit(solution)/shard_map/ppermute | solution.py:38
  75.9 4.1 %reshape.98 = f32[2,6,2,6,23,2,6]{6,5,4,3,2,1,0:T(2,128)} reshape(f32[4,36,276]{2,1,0:T(8,128)S(1)} %maximum_convert_fusion) | data formatting | bytes 317952 | tf_op jit(solution)/shard_map/convert_element_type | solution.py:278
  80.0 4.9 %reverse_bitcast_fusion = f32[2,6,2,2,6,6,23]{5,3,6,4,2,1,0:T(2,128)} fusion(f32[2,6,2,6,23,2,6]{6,5,4,3,2,1,0:T(2,128)} %reshape.98), kind=kLoop, calls=%fused_computation | loop fusion | bytes 317952 | tf_op jit(solution)/shard_map/transpose | solution.py:365
  84.9 4.8 %copy.34 = f32[2,6,2,2,6,6,23]{6,5,4,3,2,1,0:T(8,128)S(1)} copy(f32[2,6,2,2,6,6,23]{5,3,6,4,2,1,0:T(2,128)} %reverse_bitcast_fusion) | data formatting | bytes 317952
  89.7 1.4 %reshape.100 = f32[2,1,6,3312]{3,1,2,0:T(1,128)} reshape(f32[2,6,2,2,6,6,23]{6,5,4,3,2,1,0:T(8,128)S(1)} %copy.34) | data formatting | bytes 317952
  91.9 2.0 %finish.1 = (bf16[4,6,24,192]{3,2,1,0:T(8,128)(2,1)}, bf16[4,6,24,192]{3,2,1,0:T(8,128)(2,1)}) custom-call(bf16[2,4,3,18,192]{4,3,2,1,0:T(8,128)(2,1)} %copy-done.3, bf16[2,4,3,6,192]{4,3,2,1,0:T(8,128)(2,1)} %copy-done.12, bf16[2,4,3,18,192]{4,3,2,1,0:T(8,128)(2,1)} %copy-done.10, bf16[2,4,3,6,192]{4,3,2,1,0:T(8,128)(2,1)} %copy-done.13), custom_call_target="tpu_custom_call" | custom-call | tf_op jit(solution)/shard_map/finish/pallas_call | solution.py:366
  (79 shorter events, 11.3 us)
Async XLA Ops:
  0.6 20.3 %copy-start.11 = (bf16[768,192]{0,1:T(8,128)(2,1)S(1)}, bf16[768,192]{0,1:T(8,128)(2,1)}, u32[]{:S(2)}) copy-start(bf16[768,192]{0,1:T(8,128)(2,1)} %param.21) | copy-start | bytes 884740
  1.6 32.4 %collective-permute-start = (bf16[2,4,3,6,192]{4,3,2,1,0:T(8,128)(2,1)S(1)}, bf16[2,4,3,6,192]{4,3,2,1,0:T(8,128)(2,1)S(1)}, u32[]{:S(2)}, u32[]{:S(2)}) collective-permute-start(bf16[2,4,3,6,192]{4,3,2,1,0:T(8,128)(2,1)S(1)} %pad_maximum_fusion.1), channel_id=1, source_target_pairs={{0,31},{1,0},{2,1},{3,2},{4,3},{5,4},{6,5},{7,6},{8,7},{9,8},{10,9... | collective-permute-start | bytes 165896 | tf_op jit(solution)/shard_map/ppermute | solution.py:38
  5.0 29.1 %collective-permute-start.2 = (bf16[2,4,3,6,192]{4,3,2,1,0:T(8,128)(2,1)S(1)}, bf16[2,4,3,6,192]{4,3,2,1,0:T(8,128)(2,1)S(1)}, u32[]{:S(2)}, u32[]{:S(2)}) collective-permute-start(bf16[2,4,3,6,192]{4,3,2,1,0:T(8,128)(2,1)S(1)} %pad_maximum_fusion.2), channel_id=1, source_target_pairs={{0,255},{1,224},{2,225},{3,226},{4,227},{5,228},{6,229},{7,230},{8... | collective-permute-start | bytes 165896 | tf_op jit(solution)/shard_map/ppermute | solution.py:38
  15.5 18.5 %collective-permute-start.1 = (bf16[2,4,3,18,192]{4,3,2,1,0:T(8,128)(2,1)}, bf16[2,4,3,18,192]{4,3,2,1,0:T(8,128)(2,1)S(1)}, u32[]{:S(2)}, u32[]{:S(2)}) collective-permute-start(bf16[2,4,3,18,192]{4,3,2,1,0:T(8,128)(2,1)} %pad_maximum_fusion), channel_id=1, source_target_pairs={{0,224},{1,225},{2,226},{3,227},{4,228},{5,229},{6,230},{7,231},{8... | collective-permute-start | bytes 497672 | tf_op jit(solution)/shard_map/ppermute | solution.py:38
  24.2 9.9 %copy-start.4 = (bf16[288,288]{1,0:T(8,128)(2,1)S(1)}, bf16[288,288]{1,0:T(8,128)(2,1)}, u32[]{:S(2)}) copy-start(bf16[288,288]{1,0:T(8,128)(2,1)} %constant.56.clone.perm_t_ref) | copy-start | bytes 497668
  24.2 9.9 %copy-start.5 = (bf16[288,288]{1,0:T(8,128)(2,1)S(1)}, bf16[288,288]{1,0:T(8,128)(2,1)}, u32[]{:S(2)}) copy-start(bf16[288,288]{1,0:T(8,128)(2,1)} %constant.55.clone.perm_ref) | copy-start | bytes 497668
  24.2 9.9 %copy-start.6 = (bf16[192,192]{1,0:T(8,128)(2,1)S(1)}, bf16[192,192]{1,0:T(8,128)(2,1)}, u32[]{:S(2)}) copy-start(bf16[192,192]{1,0:T(8,128)(2,1)} %wproj_ref.1) | copy-start | bytes 221188
  24.2 9.9 %copy-start.7 = (bf16[6,192]{1,0:T(8,128)(2,1)S(1)}, bf16[6,192]{1,0:T(8,128)(2,1)}, u32[]{:S(2)}) copy-start(bf16[6,192]{1,0:T(8,128)(2,1)} %constant.57.clone.head_mask_ref) | copy-start | bytes 6916
  46.2 3.7 %collective-permute-start.6 = (bf16[36,276]{1,0:T(8,128)(2,1)S(1)}, bf16[36,276]{1,0:T(8,128)(2,1)S(1)}, u32[]{:S(2)}, u32[]{:S(2)}) collective-permute-start(bf16[36,276]{1,0:T(8,128)(2,1)S(1)} %get-tuple-element.28), channel_id=1, source_target_pairs={{0,1},{1,0},{2,3},{3,2},{4,5},{5,4},{6,7},{7,6},{8,9},{9,8},{10,11... | collective-permute-start | bytes 59624 | tf_op jit(solution)/shard_map/ppermute | solution.py:43
  46.5 5.2 %collective-permute-start.8 = (bf16[36,276]{1,0:T(8,128)(2,1)S(1)}, bf16[36,276]{1,0:T(8,128)(2,1)S(1)}, u32[]{:S(2)}, u32[]{:S(2)}) collective-permute-start(bf16[36,276]{1,0:T(8,128)(2,1)S(1)} %get-tuple-element.29), channel_id=1, source_target_pairs={{0,3},{1,2},{2,1},{3,0},{4,7},{5,6},{6,5},{7,4},{8,11},{9,10},{10,... | collective-permute-start | bytes 59624 | tf_op jit(solution)/shard_map/ppermute | solution.py:43
  46.6 5.5 %collective-permute-start.7 = (bf16[36,276]{1,0:T(8,128)(2,1)S(1)}, bf16[36,276]{1,0:T(8,128)(2,1)S(1)}, u32[]{:S(2)}, u32[]{:S(2)}) collective-permute-start(bf16[36,276]{1,0:T(8,128)(2,1)S(1)} %get-tuple-element.30), channel_id=1, source_target_pairs={{0,2},{1,3},{2,0},{3,1},{4,6},{5,7},{6,4},{7,5},{8,10},{9,11},{10,... | collective-permute-start | bytes 59624 | tf_op jit(solution)/shard_map/ppermute | solution.py:43
  52.2 8.3 %collective-permute-start.15 = (bf16[36,276]{1,0:T(8,128)(2,1)S(1)}, bf16[36,276]{1,0:T(8,128)(2,1)S(1)}, u32[]{:S(2)}, u32[]{:S(2)}) collective-permute-start(bf16[36,276]{1,0:T(8,128)(2,1)S(1)} %fusion.1), channel_id=1, source_target_pairs={{0,28},{1,29},{2,30},{3,31},{4,24},{5,25},{6,26},{7,27},{8,20},{9,... | collective-permute-start | bytes 59624 | tf_op jit(solution)/shard_map/ppermute | solution.py:43
  53.0 7.5 %collective-permute-start.14 = (bf16[36,276]{1,0:T(8,128)(2,1)S(1)}, bf16[36,276]{1,0:T(8,128)(2,1)S(1)}, u32[]{:S(2)}, u32[]{:S(2)}) collective-permute-start(bf16[36,276]{1,0:T(8,128)(2,1)S(1)} %fusion.1), channel_id=1, source_target_pairs={{0,24},{1,25},{2,26},{3,27},{4,28},{5,29},{6,30},{7,31},{8,16},{9,... | collective-permute-start | bytes 59624 | tf_op jit(solution)/shard_map/ppermute | solution.py:43
  53.5 10.3 %collective-permute-start.13 = (bf16[36,276]{1,0:T(8,128)(2,1)S(1)}, bf16[36,276]{1,0:T(8,128)(2,1)S(1)}, u32[]{:S(2)}, u32[]{:S(2)}) collective-permute-start(bf16[36,276]{1,0:T(8,128)(2,1)S(1)} %fusion.1), channel_id=1, source_target_pairs={{0,20},{1,21},{2,22},{3,23},{4,16},{5,17},{6,18},{7,19},{8,28},{9,... | collective-permute-start | bytes 59624 | tf_op jit(solution)/shard_map/ppermute | solution.py:43
  56.1 7.8 %collective-permute-start.12 = (bf16[36,276]{1,0:T(8,128)(2,1)S(1)}, bf16[36,276]{1,0:T(8,128)(2,1)S(1)}, u32[]{:S(2)}, u32[]{:S(2)}) collective-permute-start(bf16[36,276]{1,0:T(8,128)(2,1)S(1)} %fusion.1), channel_id=1, source_target_pairs={{0,16},{1,17},{2,18},{3,19},{4,20},{5,21},{6,22},{7,23},{8,24},{9,... | collective-permute-start | bytes 59624 | tf_op jit(solution)/shard_map/ppermute | solution.py:43
  60.3 5.2 %collective-permute-start.11 = (bf16[36,276]{1,0:T(8,128)(2,1)S(1)}, bf16[36,276]{1,0:T(8,128)(2,1)S(1)}, u32[]{:S(2)}, u32[]{:S(2)}) collective-permute-start(bf16[36,276]{1,0:T(8,128)(2,1)S(1)} %fusion.1), channel_id=1, source_target_pairs={{0,12},{1,13},{2,14},{3,15},{4,8},{5,9},{6,10},{7,11},{8,4},{9,5},... | collective-permute-start | bytes 59624 | tf_op jit(solution)/shard_map/ppermute | solution.py:43
  60.5 5.0 %collective-permute-start.10 = (bf16[36,276]{1,0:T(8,128)(2,1)S(1)}, bf16[36,276]{1,0:T(8,128)(2,1)S(1)}, u32[]{:S(2)}, u32[]{:S(2)}) collective-permute-start(bf16[36,276]{1,0:T(8,128)(2,1)S(1)} %fusion.1), channel_id=1, source_target_pairs={{0,8},{1,9},{2,10},{3,11},{4,12},{5,13},{6,14},{7,15},{8,0},{9,1},... | collective-permute-start | bytes 59624 | tf_op jit(solution)/shard_map/ppermute | solution.py:43
  60.5 5.0 %collective-permute-start.9 = (bf16[36,276]{1,0:T(8,128)(2,1)S(1)}, bf16[36,276]{1,0:T(8,128)(2,1)S(1)}, u32[]{:S(2)}, u32[]{:S(2)}) collective-permute-start(bf16[36,276]{1,0:T(8,128)(2,1)S(1)} %fusion.1), channel_id=1, source_target_pairs={{0,4},{1,5},{2,6},{3,7},{4,0},{5,1},{6,2},{7,3},{8,12},{9,13},{10,... | collective-permute-start | bytes 59624 | tf_op jit(solution)/shard_map/ppermute | solution.py:43
  65.5 9.4 %collective-permute-start.18 = (bf16[36,276]{1,0:T(8,128)(2,1)S(1)}, bf16[36,276]{1,0:T(8,128)(2,1)S(1)}, u32[]{:S(2)}, u32[]{:S(2)}) collective-permute-start(bf16[36,276]{1,0:T(8,128)(2,1)S(1)} %add_convert_fusion), channel_id=1, source_target_pairs={{0,1},{1,0},{2,3},{3,2},{4,5},{5,4},{6,7},{7,6},{8,9},{9,8},{10,11... | collective-permute-start | bytes 59624 | tf_op jit(solution)/shard_map/ppermute | solution.py:43
  68.5 6.7 %collective-permute-start.17 = (bf16[36,276]{1,0:T(8,128)(2,1)S(1)}, bf16[36,276]{1,0:T(8,128)(2,1)S(1)}, u32[]{:S(2)}, u32[]{:S(2)}) collective-permute-start(bf16[36,276]{1,0:T(8,128)(2,1)S(1)} %add_convert_fusion), channel_id=1, source_target_pairs={{0,2},{1,3},{2,0},{3,1},{4,6},{5,7},{6,4},{7,5},{8,10},{9,11},{10,... | collective-permute-start | bytes 59624 | tf_op jit(solution)/shard_map/ppermute | solution.py:43
  71.1 4.8 %collective-permute-start.16 = (bf16[36,276]{1,0:T(8,128)(2,1)S(1)}, bf16[36,276]{1,0:T(8,128)(2,1)S(1)}, u32[]{:S(2)}, u32[]{:S(2)}) collective-permute-start(bf16[36,276]{1,0:T(8,128)(2,1)S(1)} %add_convert_fusion), channel_id=1, source_target_pairs={{0,3},{1,2},{2,1},{3,0},{4,7},{5,6},{6,5},{7,4},{8,11},{9,10},{10,... | collective-permute-start | bytes 59624 | tf_op jit(solution)/shard_map/ppermute | solution.py:43
  71.7 19.4 %collective-permute-start.3 = (bf16[2,4,3,6,192]{4,3,2,1,0:T(8,128)(2,1)S(1)}, bf16[2,4,3,6,192]{4,3,2,1,0:T(8,128)(2,1)S(1)}, u32[]{:S(2)}, u32[]{:S(2)}) collective-permute-start(bf16[2,4,3,6,192]{4,3,2,1,0:T(8,128)(2,1)S(1)} %get-tuple-element.11), channel_id=1, source_target_pairs={{0,1},{1,2},{2,3},{3,4},{4,5},{5,6},{6,7},{7,8},{8,9},{9,10},{10,1... | collective-permute-start | bytes 165896 | tf_op jit(solution)/shard_map/ppermute | solution.py:38
  74.3 16.8 %collective-permute-start.5 = (bf16[2,4,3,6,192]{4,3,2,1,0:T(8,128)(2,1)S(1)}, bf16[2,4,3,6,192]{4,3,2,1,0:T(8,128)(2,1)S(1)}, u32[]{:S(2)}, u32[]{:S(2)}) collective-permute-start(bf16[2,4,3,6,192]{4,3,2,1,0:T(8,128)(2,1)S(1)} %get-tuple-element.13), channel_id=1, source_target_pairs={{0,33},{1,34},{2,35},{3,36},{4,37},{5,38},{6,39},{7,40},{8,41},{9,... | collective-permute-start | bytes 165896 | tf_op jit(solution)/shard_map/ppermute | solution.py:38
  74.9 16.2 %collective-permute-start.4 = (bf16[2,4,3,18,192]{4,3,2,1,0:T(8,128)(2,1)S(1)}, bf16[2,4,3,18,192]{4,3,2,1,0:T(8,128)(2,1)S(1)}, u32[]{:S(2)}, u32[]{:S(2)}) collective-permute-start(bf16[2,4,3,18,192]{4,3,2,1,0:T(8,128)(2,1)S(1)} %get-tuple-element.12), channel_id=1, source_target_pairs={{0,32},{1,33},{2,34},{3,35},{4,36},{5,37},{6,38},{7,39},{8,40},{9,... | collective-permute-start | bytes 497672 | tf_op jit(solution)/shard_map/ppermute | solution.py:38
  (9 other events, 52.3 us)

commit v2 on v1

--- a/solution.py
+++ b/solution.py
@@ -20,6 +20,8 @@
 PAIR = WZ * WLAT
 TAB = PAIR * SPREAD
 ROWS = HEADS * POS
+SLOTS = 16
+CHUNK = 8
 
 epsilon = 1e-05
 keep_share = 0.8
@@ -36,11 +38,6 @@
             target = ((a + lat_step) % lats) * lons + (b + lon_step) % lons
             route.append((a * lons + b, target))
     return lax.ppermute(block, ("lat", "lon"), route)
-
-
-def swapped(block, distance):
-    lons = lax.axis_size("lon")
-    return lax.ppermute(block, "lon", [(i, i ^ distance) for i in range(lons)])
 
 
 def mm(a, b):
@@ -100,21 +97,23 @@
     wproj_ref,
     gain2_ref,
     wup_ref,
-    wdown_ref,
-    table_ref,
+    wdown_t_ref,
+    bias_ref,
     label_row_ref,
     label_col_ref,
     factor_ref,
     perm_ref,
     perm_t_ref,
     head_mask_ref,
+    table_perm_ref,
+    chunk_perm_ref,
     own_out,
     lon_out,
     lat_out,
     diag_out,
     fold_out,
     frame,
-    bias,
+    wide,
 ):
     half = WLAT // 2
     cols = 2 * WLON
@@ -133,6 +132,9 @@
                 frame[t, row : row + cols, :] = jnp.concatenate(
                     [lat_ref[t, z, i].astype(f32), diag_ref[t, z, i].astype(f32)], axis=0
                 )
+    spare = fold_out.shape[0] - 2 * PAIR
+    if spare:
+        fold_out[2 * PAIR :] = jnp.zeros((spare, CHUNK, TAB), bf16)
     gain1 = gain1_ref[...]
     gain2 = gain2_ref[...]
     wq_t = wqkv_t_ref[0:C, :]
@@ -142,10 +144,6 @@
     perm = perm_ref[...]
     perm_t = perm_t_ref[...]
     for n in range(2):
-        for o in range(WLON):
-            start = PAIR * (WLON - 1 - o)
-            bias[:, PAIR * o : PAIR * (o + 1), :] = table_ref[n, :, :, start : start + POS]
-        bias_t = bias[...].reshape(ROWS, POS).T
         x = mm(perm, frame[0, n * 2 * POS : (n + 1) * 2 * POS, :].astype(bf16))
         cot = mm(perm, frame[1, n * 2 * POS : (n + 1) * 2 * POS, :].astype(bf16))
         scaled1, normed1, inverse1 = norm_parts(x, gain1)
@@ -160,7 +158,7 @@
             rows = slice(c * POS, (c + 1) * POS)
             v_t = mm_nt(wv_t, h1[rows]).astype(bf16)
             q_wide = spread_heads(q_all[rows], head_mask)
-            scores = mm_nt(k_all[rows], q_wide) * root + bias_t
+            scores = mm_nt(k_all[rows], q_wide) * root + bias_ref[n]
             allowed = label_col_ref[:, w : w + 1] == label_row_ref[w]
             scores = jnp.where(allowed, scores, -1e30)
             weights = jnp.exp(scores - jnp.max(scores, axis=0, keepdims=True))
@@ -173,8 +171,8 @@
         y_sum = x + jnp.concatenate(branches, axis=0)
         scaled2, normed2, inverse2 = norm_parts(y_sum, gain2)
         act, slope = gelu_parts(mm(scaled2.astype(bf16), wup_ref[...]))
-        result = (y_sum + mm(act.astype(bf16), wdown_ref[...])).astype(bf16)
-        grad_up = (mm_nt(cot.astype(bf16), wdown_ref[...]) * slope).astype(bf16)
+        result = (y_sum + mm_nt(act.astype(bf16), wdown_t_ref[...])).astype(bf16)
+        grad_up = (mm(cot.astype(bf16), wdown_t_ref[...]) * slope).astype(bf16)
         grad_sum = cot + norm_back(mm_nt(grad_up, wup_ref[...]), gain2, normed2, inverse2)
         grad_low_in = grad_sum.astype(bf16).astype(f32)
         folded = None
@@ -198,19 +196,23 @@
             grad_h1.append(mm(grad_q, wq_t) + mm(grad_k, wk_t) + mm(grad_v, wv_t))
         grad_h1 = jnp.concatenate(grad_h1, axis=0).astype(bf16).astype(f32)
         grad_field = (grad_sum + norm_back(grad_h1, gain1, normed1, inverse1)).astype(bf16)
-        bias[...] = folded.T.reshape(HEADS, POS, POS)
+        wide[...] = folded.T.reshape(HEADS, POS, POS)
         total = None
         for o in range(WLON):
             left = PAIR * (WLON - 1 - o)
             right = TAB - POS - left
-            parts = [bias[:, PAIR * o : PAIR * (o + 1), :]]
+            parts = [wide[:, PAIR * o : PAIR * (o + 1), :]]
             if left:
                 parts = [jnp.zeros((HEADS, PAIR, left), f32)] + parts
             if right:
                 parts = parts + [jnp.zeros((HEADS, PAIR, right), f32)]
             piece = jnp.concatenate(parts, axis=2)
             total = piece if total is None else total + piece
-        fold_out[n] = total
+        total = jnp.concatenate([total, jnp.zeros((HEADS, SLOTS - PAIR, TAB), f32)], axis=1)
+        total = total.reshape(HEADS * SLOTS, TAB).astype(bf16)
+        total = mm_nt(total, table_perm_ref[...]).astype(bf16)
+        total = mm(chunk_perm_ref[...], total).reshape(PAIR, CHUNK, TAB).astype(bf16)
+        fold_out[n * PAIR : (n + 1) * PAIR] = total
         for t, value in enumerate((result, grad_field)):
             natural = mm(perm_t, value)
             for dz in range(WZ):
@@ -226,6 +228,50 @@
                     diag_out[t, z, i] = slab[inner:].astype(bf16)
 
 
+def expand_kernel(table_ref, table_perm_ref, row_perm_ref, bias_out, flat, rows, wide):
+    part = PAIR // WZ * SPREAD
+    for k in range(2 * HEADS):
+        flat[k : k + 1, :] = table_ref[k]
+    rows[...] = jnp.zeros_like(rows)
+    for a in range(WZ):
+        for c in range(WLAT):
+            pieces = []
+            for b in range(WZ):
+                start = ((a * WZ + b) * WLAT + c) * part
+                pieces.append(flat[:, start : start + part])
+            row = (a * WLAT + c) * SLOTS
+            rows[row : row + 2 * HEADS, :] = jnp.concatenate(pieces, axis=1)
+    left = rows[...]
+    perm = table_perm_ref[...]
+    total = None
+    for _ in range(3):
+        low = left.astype(bf16)
+        left = left - low.astype(f32)
+        term = mm(row_perm_ref[...], mm(low, perm).astype(bf16))
+        total = term if total is None else total + term
+    total = total.reshape(2 * HEADS, SLOTS, TAB)
+    for o in range(WLON):
+        start = PAIR * (WLON - 1 - o)
+        wide[:, PAIR * o : PAIR * (o + 1), :] = total[:, :PAIR, start : start + POS]
+    for n in range(2):
+        bias_out[n] = wide[n * HEADS : (n + 1) * HEADS].reshape(ROWS, POS).T
+
+
+def unpack_kernel(grad_ref, table_out, flat):
+    part = PAIR // WZ * SPREAD
+    for n in range(2):
+        for a in range(WZ):
+            for c in range(WLAT):
+                chunk = grad_ref[n * PAIR + a * WLAT + c].astype(f32)[:HEADS]
+                for b in range(WZ):
+                    start = ((a * WZ + b) * WLAT + c) * part
+                    flat[n * HEADS : (n + 1) * HEADS, start : start + part] = chunk[
+                        :, b * part : (b + 1) * part
+                    ]
+    for k in range(2 * HEADS):
+        table_out[k] = flat[k : k + 1, :]
+
+
 def finish_kernel(own_ref, lon_ref, lat_ref, diag_ref, out_ref, grad_ref):
     half = WLAT // 2
     for t, target in enumerate((out_ref, grad_ref)):
@@ -248,34 +294,37 @@
     return perm
 
 
-def lon_sum(value):
+def table_order():
+    perm = np.zeros((TAB, TAB), np.float32)
+    for d in range(PAIR):
+        for r in range(SPREAD):
+            perm[d * SPREAD + r, (SPREAD - 1 - r) * PAIR + d] = 1.0
+    return perm
+
+
+def chunk_order():
+    perm = np.zeros((PAIR * CHUNK, HEADS * SLOTS), np.float32)
+    for h in range(HEADS):
+        for k in range(PAIR):
+            perm[k * CHUNK + h, h * SLOTS + k] = 1.0
+    return perm
+
+
+def row_order():
+    perm = np.zeros((2 * HEADS * SLOTS, PAIR * SLOTS), np.float32)
+    for h in range(2 * HEADS):
+        for k in range(PAIR):
+            perm[h * SLOTS + k, k * SLOTS + h] = 1.0
+    return perm
+
+
+def lon_sum(chunks):
     lons = lax.axis_size("lon")
-    group = min(4, lons)
-    others = lons // group
-    me = lax.axis_index("lon") % group
-    low = value.astype(bf16)
-    if group < 4:
-        low = low.reshape((group, 4 // group) + low.shape[1:])
-
-    def quarter(d):
-        return lax.dynamic_index_in_dim(low, me ^ d, 0, keepdims=False)
-
-    def tree(parts):
-        while len(parts) > 1:
-            parts = [parts[i] + parts[i + 1] for i in range(0, len(parts), 2)]
-        return parts[0]
-
-    parts = [quarter(0)] + [swapped(quarter(d), d) for d in range(1, group)]
-    mine = tree([p.astype(f32) for p in parts]).astype(bf16)
-    parts = [mine] + [swapped(mine, d * group) for d in range(1, others)]
-    mine = tree([p.astype(f32) for p in parts]).astype(bf16)
-    parts = [mine] + [swapped(mine, d) for d in range(1, group)]
-    bit = 1
-    while bit < group:
-        flip = (me & bit) != 0
-        parts = [jnp.where(flip, parts[i ^ bit], parts[i]) for i in range(group)]
-        bit *= 2
-    return jnp.stack(parts, axis=0).astype(f32)
+    shares = chunks.reshape((lons, -1) + chunks.shape[1:])
+    shares = lax.all_to_all(shares, "lon", 0, 0)
+    share = jnp.sum(shares.astype(f32), axis=0).astype(bf16)
+    shares = lax.all_to_all(jnp.broadcast_to(share, shares.shape), "lon", 0, 0)
+    return shares.reshape(chunks.shape)
 
 
 def body(
@@ -312,14 +361,31 @@
     label_col = labels.T
     factor = (keep_flags.astype(f32) / keep_share).reshape(4)
 
-    table = bias_table.reshape(2, HEADS, WZ, WZ, WLAT, WLAT, SPREAD)[..., ::-1]
-    table = table.transpose(0, 1, 2, 4, 6, 3, 5).reshape(2, HEADS, PAIR, TAB)
-
     perm = window_order()
     head_mask = np.repeat(np.eye(HEADS, dtype=np.float32), HD, axis=1)
     vmem = pl.BlockSpec(memory_space=pltpu.VMEM)
     smem = pl.BlockSpec(memory_space=pltpu.SMEM)
     inner = lon_cols - edge
+    table_perm = jnp.asarray(table_order(), bf16)
+    bias_wide = pl.pallas_call(
+        expand_kernel,
+        out_shape=jax.ShapeDtypeStruct((2, POS, ROWS), f32),
+        in_specs=[vmem] * 3,
+        out_specs=vmem,
+        scratch_shapes=[
+            pltpu.VMEM((2 * HEADS, PAIR * TAB), f32),
+            pltpu.VMEM((PAIR * SLOTS, TAB), f32),
+            pltpu.VMEM((2 * HEADS, POS, POS), f32),
+        ],
+        compiler_params=pltpu.CompilerParams(vmem_limit_bytes=32 * 1024 * 1024),
+        name="expand",
+    )(
+        bias_table.reshape(2 * HEADS, 1, PAIR * TAB),
+        table_perm,
+        jnp.asarray(row_order(), bf16),
+    )
+    lons = lax.axis_size("lon")
+    chunks = -(-2 * PAIR // lons) * lons
     own, lon_back, lat_back, diag_back, fold = pl.pallas_call(
         block_kernel,
         out_shape=(
@@ -327,9 +393,9 @@
             jax.ShapeDtypeStruct((2, 4, half, edge, C), bf16),
             jax.ShapeDtypeStruct((2, 4, half, inner, C), bf16),
             jax.ShapeDtypeStruct((2, 4, half, edge, C), bf16),
-            jax.ShapeDtypeStruct((2, HEADS, PAIR, TAB), f32),
+            jax.ShapeDtypeStruct((chunks, CHUNK, TAB), bf16),
         ),
-        in_specs=[vmem] * 14 + [smem] + [vmem] * 3,
+        in_specs=[vmem] * 14 + [smem] + [vmem] * 5,
         out_specs=(vmem,) * 5,
         scratch_shapes=[
             pltpu.VMEM((2, 4 * WLAT * lon_cols, C), f32),
@@ -348,21 +414,29 @@
         w_proj,
         ln2_gain.reshape(1, C),
         w_up,
-        w_down,
-        table,
+        w_down.T,
+        bias_wide,
         label_row,
         label_col,
         factor,
         jnp.asarray(perm, bf16),
         jnp.asarray(perm.T, bf16),
         jnp.asarray(head_mask, bf16),
+        table_perm,
+        jnp.asarray(chunk_order(), bf16),
     )
     lon_back = shifted(lon_back, 0, 1)
     lat_back = shifted(lat_back, 1, 0)
     diag_back = shifted(diag_back, 1, 1)
-    grads = lon_sum(fold.reshape(4, HEADS // 2 * PAIR, TAB))
-    grads = grads.reshape(2, HEADS, WZ, WLAT, SPREAD, WZ, WLAT)[:, :, :, :, ::-1]
-    grads = grads.transpose(0, 1, 2, 5, 3, 6, 4).reshape(2, 1, HEADS, PAIR * TAB)
+    grads = pl.pallas_call(
+        unpack_kernel,
+        out_shape=jax.ShapeDtypeStruct((2 * HEADS, 1, PAIR * TAB), f32),
+        in_specs=[vmem],
+        out_specs=vmem,
+        scratch_shapes=[pltpu.VMEM((2 * HEADS, PAIR * TAB), f32)],
+        name="unpack",
+    )(lon_sum(fold))
+    grads = grads.reshape(2, 1, HEADS, PAIR * TAB)
     result, grad_field = pl.pallas_call(
         finish_kernel,
         out_shape=(jax.ShapeDtypeStruct(field_in.shape, bf16),) * 2,

time: 94.4 us -> 77 us (0.82)
  local copies, waits for them, and re-layouts: 34.5 us -> 6.27 us
  starting transfers between devices: 38.1 us -> 21.7 us
  blocking collectives: 0 us -> 16.3 us
  waiting for transfers between devices: 4.62 us -> 13.6 us
  Pallas kernels: 13.2 us -> 17.6 us
  other arithmetic: 2.52 us -> 0.34 us
    ppermute x13 -> x0, starting transfers between devices: 21.6 us -> none  [swapped(): return lax.ppermute(block, 'lon', [(i, i ^ distance) for i in range(lons)])]
    all_to_all x0 -> x1, blocking collectives: none -> 16.3 us  [lon_sum(): shares = lax.all_to_all(shares, 'lon', 0, 0)]
    ppermute x6, waiting for transfers between devices: 0.02 us -> 13.6 us  [shifted(): return lax.ppermute(block, ('lat', 'lon'), route)]
    reshape x3 -> x0, local copies, waits for them, and re-layouts: 10.6 us -> none  [the longest x2 9.76 us: body(): table = table.transpose(0, 1, 2, 4, 6, 3, 5).reshape(2, HEADS, PAIR, TAB)]
    unnamed x33 -> x45, local copies, waits for them, and re-layouts: 10 us -> 3.91 us
    transpose x1 -> x0, local copies, waits for them, and re-layouts: 4.87 us -> none  [body(): grads.transpose(0, 1, 2, 5, 3, 6, 4).reshape(2, 1, HEADS, PAIR * TAB)]
    ppermute x13 -> x0, waiting for transfers between devices: 4.6 us -> none  [swapped(): return lax.ppermute(block, 'lon', [(i, i ^ distance) for i in range(lons)])]
    all_to_all x0 -> x1, starting transfers between devices: none -> 4.13 us  [lon_sum(): shares = lax.all_to_all(jnp.broadcast_to(share, shares.shape), 'lon', 0, 0)]
  transfers between devices with their start and end apart: 19 -> 7, of which waited for: 4 -> 3; matrix products, arithmetic and copies ran while one was open for 37% -> 1% of each run, Pallas kernels for 0% -> 5%
where the time goes in v2:
time: 77 us; the launch traced here: 76.6 us
  starting transfers between devices  21.7 us (28%)
  Pallas kernels  17.6 us (23%)
  blocking collectives  16.3 us (21%)
  waiting for transfers between devices  13.6 us (18%)
  local copies, waits for them, and re-layouts  6.27 us (8%)
  between operations  0.9 us (1%)
    ppermute x6, starting transfers between devices, shifted(): return lax.ppermute(block, ('lat', 'lon'), route)  17.5 us
    all_to_all x1, blocking collectives, lon_sum(): shares = lax.all_to_all(shares, 'lon', 0, 0)  16.3 us
    ppermute x6, waiting for transfers between devices, shifted(): return lax.ppermute(block, ('lat', 'lon'), route)  13.6 us
    pallas_call x1, Pallas kernels, body(): pl.pallas_call(block_kernel, out_shape=(jax.ShapeDtypeStruct((2, 4, half,...  11.8 us
    all_to_all x1, starting transfers between devices, lon_sum(): shares = lax.all_to_all(jnp.broadcast_to(share, shares.shape), 'lon', 0, 0)  4.13 us
    unnamed x45, local copies, waits for them, and re-layouts  3.91 us
    pallas_call x1, Pallas kernels, body(): pl.pallas_call(expand_kernel, out_shape=jax.ShapeDtypeStruct((2, POS, ROW...  2.04 us
    pallas_call x1, Pallas kernels, body(): pl.pallas_call(finish_kernel, out_shape=(jax.ShapeDtypeStruct(field_in.sh...  2.01 us
  transfers between devices with their start and end apart: 7, of which 3 were waited for; matrix products, arithmetic and copies ran while one was open for 1% of the time, Pallas kernels for 5%

profile of v2, /device:TPU:1, one launch (start us, length us, event | category | flops | bytes accessed | tf_op | source)
XLA Modules:
  0.0 76.6 jit_solution(7222444224855440927)
XLA Ops:
  0.6 0.9 %slice_bitcast_fusion.2 = (bf16[1,4,3,6,192]{4,3,2,1,0:T(8,128)(2,1)S(1)}, bf16[1,4,3,6,192]{4,3,2,1,0:T(8,128)(2,1)S(1)}, bf16[1,4,3,6,192]{4,3,2,1,0:T(8,128)(2,1)S(1)}, bf16[1,4,3,6,192]{4,3,2,1,0:T(8,128)(2,1)S(1)}) fusion(bf16[4,6,24,192]{3,2,1,0:T(8,128)(2,1)} %cot_ref.1, bf16[4,6,24,192]{3,2,1,0:T(8,128)(2,1)} %field_ref.1), kind=kLoop, calls=%fused_computation.5 | loop fusion | bytes 221184 | tf_op jit(solution)/shard_map/stack | solution.py:349
  1.6 3.3 %collective-permute-start = (bf16[2,4,3,6,192]{4,3,2,1,0:T(8,128)(2,1)S(1)}, bf16[2,4,3,6,192]{4,3,2,1,0:T(8,128)(2,1)S(1)}, u32[]{:S(2)}, u32[]{:S(2)}) collective-permute-start(bf16[2,4,3,6,192]{4,3,2,1,0:T(8,128)(2,1)S(1)} %pad_maximum_fusion.1), channel_id=1, source_target_pairs={{0,31},{1,0},{2,1},{3,2},{4,3},{5,4},{6,5},{7,6},{8,7},{9,8},{10,9... | collective-permute-start | bytes 165896 | tf_op jit(solution)/shard_map/ppermute | solution.py:40
  5.0 8.7 %collective-permute-start.2 = (bf16[2,4,3,6,192]{4,3,2,1,0:T(8,128)(2,1)S(1)}, bf16[2,4,3,6,192]{4,3,2,1,0:T(8,128)(2,1)S(1)}, u32[]{:S(2)}, u32[]{:S(2)}) collective-permute-start(bf16[2,4,3,6,192]{4,3,2,1,0:T(8,128)(2,1)S(1)} %pad_maximum_fusion.2), channel_id=1, source_target_pairs={{0,255},{1,224},{2,225},{3,226},{4,227},{5,228},{6,229},{7,230},{8... | collective-permute-start | bytes 165896 | tf_op jit(solution)/shard_map/ppermute | solution.py:40
  13.9 1.3 %collective-permute-start.1 = (bf16[2,4,3,18,192]{4,3,2,1,0:T(8,128)(2,1)S(1)}, bf16[2,4,3,18,192]{4,3,2,1,0:T(8,128)(2,1)S(1)}, u32[]{:S(2)}, u32[]{:S(2)}) collective-permute-start(bf16[2,4,3,18,192]{4,3,2,1,0:T(8,128)(2,1)S(1)} %pad_maximum_fusion), channel_id=1, source_target_pairs={{0,224},{1,225},{2,226},{3,227},{4,228},{5,229},{6,230},{7,231},{8... | collective-permute-start | bytes 497672 | tf_op jit(solution)/shard_map/ppermute | solution.py:40
  15.6 0.1 copy.28
  16.1 0.2 copy.27
  16.3 0.7 copy-done.2
  17.2 2.0 %expand.1.bias_ref = f32[2,144,864]{2,1,0:T(8,128)S(1)} custom-call(f32[12,1,3312]{2,1,0:T(1,128)S(1)} %bitcast.30, bf16[276,276]{1,0:T(8,128)(2,1)S(1)} %copy-done.2, bf16[192,192]{1,0:T(8,128)(2,1)S(1)} %copy-done.9), custom_call_target="tpu_custom_call" | custom-call | tf_op jit(solution)/shard_map/expand/pallas_call | solution.py:370
  19.3 3.3 %collective-permute-done.1.lat_ref = bf16[2,4,3,18,192]{4,3,2,1,0:T(8,128)(2,1)S(1)} collective-permute-done((bf16[2,4,3,18,192]{4,3,2,1,0:T(8,128)(2,1)S(1)}, bf16[2,4,3,18,192]{4,3,2,1,0:T(8,128)(2,1)S(1)}, u32[]{:S(2)}, u32[]{:S(2)}) %collective-permute-start.1) | collective-permute-done | bytes 165920 | tf_op jit(solution)/shard_map/ppermute | solution.py:40
  22.6 0.6 copy-done.12
  23.3 11.8 %block.1 = (bf16[2,4,3,18,192]{4,3,2,1,0:T(8,128)(2,1)S(1)}, bf16[2,4,3,6,192]{4,3,2,1,0:T(8,128)(2,1)S(1)}, bf16[2,4,3,18,192]{4,3,2,1,0:T(8,128)(2,1)S(1)}, bf...) custom-call(bf16[4,6,24,192]{3,2,1,0:T(8,128)(2,1)S(1)} %copy-done, bf16[4,6,24,192]{3,2,1,0:T(8,128)(2,1)S(1)} %copy-done.1, ...), custom_call_target="tpu_custom_call" | custom-call | tf_op jit(solution)/shard_map/block/pallas_call | solution.py:389
  35.1 0.7 copy-done.5
  35.8 16.3 %all_to_all.10 = bf16[32,1,8,276]{3,2,1,0:T(8,128)(2,1)S(1)} all-to-all(bf16[32,1,8,276]{3,2,1,0:T(8,128)(2,1)S(1)} %bitcast.29), channel_id=1, replica_groups=mesh['lat'=8,'lon'=32] {'lon'}, dimensions={0} | all-to-all | bytes 282624 | tf_op jit(solution)/shard_map/all_to_all | solution.py:324
  52.1 0.7 broadcast_in_dim.2
  52.8 4.1 %all-to-all-start.1 = ((bf16[32,1,8,276]{3,2,1,0:T(8,128)(2,1)}), bf16[32,1,8,276]{3,2,1,0:T(8,128)(2,1)S(1)}, u32[]{:S(2)}, u32[]{:S(2)}) async-start(bf16[32,1,8,276]{3,2,1,0:T(8,128)(2,1)} %broadcast_in_dim.2), calls=%async_computation.1 | async-start | bytes 393216 | tf_op jit(solution)/shard_map/all_to_all | solution.py:326
  56.9 0.1 collective-permute-start.4
  57.1 4.0 %collective-permute-start.3 = (bf16[2,4,3,6,192]{4,3,2,1,0:T(8,128)(2,1)S(1)}, bf16[2,4,3,6,192]{4,3,2,1,0:T(8,128)(2,1)S(1)}, u32[]{:S(2)}, u32[]{:S(2)}) collective-permute-start(bf16[2,4,3,6,192]{4,3,2,1,0:T(8,128)(2,1)S(1)} %get-tuple-element.11), channel_id=1, source_target_pairs={{0,1},{1,2},{2,3},{3,4},{4,5},{5,6},{6,7},{7,8},{8,9},{9,10},{10,1... | collective-permute-start | bytes 165896 | tf_op jit(solution)/shard_map/ppermute | solution.py:40
  61.1 6.4 %collective-permute-done.3.lon_ref = bf16[2,4,3,6,192]{4,3,2,1,0:T(8,128)(2,1)S(1)} collective-permute-done((bf16[2,4,3,6,192]{4,3,2,1,0:T(8,128)(2,1)S(1)}, bf16[2,4,3,6,192]{4,3,2,1,0:T(8,128)(2,1)S(1)}, u32[]{:S(2)}, u32[]{:S(2)}) %collective-permute-start.3) | collective-permute-done | bytes 55328 | tf_op jit(solution)/shard_map/ppermute | solution.py:40
  67.5 3.9 %collective-permute-done.5.diag_ref = bf16[2,4,3,6,192]{4,3,2,1,0:T(8,128)(2,1)S(1)} collective-permute-done((bf16[2,4,3,6,192]{4,3,2,1,0:T(8,128)(2,1)S(1)}, bf16[2,4,3,6,192]{4,3,2,1,0:T(8,128)(2,1)S(1)}, u32[]{:S(2)}, u32[]{:S(2)}) %collective-permute-start.5) | collective-permute-done | bytes 55328 | tf_op jit(solution)/shard_map/ppermute | solution.py:40
  71.4 0.6 copy-done.19
  72.1 0.1 copy-done.16
  72.2 2.0 %finish.1 = (bf16[4,6,24,192]{3,2,1,0:T(8,128)(2,1)}, bf16[4,6,24,192]{3,2,1,0:T(8,128)(2,1)}) custom-call(bf16[2,4,3,18,192]{4,3,2,1,0:T(8,128)(2,1)} %copy-done.5, bf16[2,4,3,6,192]{4,3,2,1,0:T(8,128)(2,1)} %copy-done.18, bf16[2,4,3,18,192]{4,3,2,1,0:T(8,128)(2,1)} %copy-done.16, bf16[2,4,3,6,192]{4,3,2,1,0:T(8,128)(2,1)} %copy-done.19), custom_call_target="tpu_custom_call" | custom-call | tf_op jit(solution)/shard_map/finish/pallas_call | solution.py:440
  74.2 0.7 copy-done.15
  74.9 1.8 %unpack.1 = f32[12,1,3312]{2,1,0:T(1,128)} custom-call(bf16[32,8,276]{2,1,0:T(8,128)(2,1)} %bitcast.33), custom_call_target="tpu_custom_call" | custom-call | tf_op jit(solution)/shard_map/unpack/pallas_call | solution.py:431
  (59 shorter events, 1.2 us)
Async XLA Ops:
  0.6 13.1 %copy-start.1 = (bf16[4,6,24,192]{3,2,1,0:T(8,128)(2,1)S(1)}, bf16[4,6,24,192]{3,2,1,0:T(8,128)(2,1)}, u32[]{:S(2)}) copy-start(bf16[4,6,24,192]{3,2,1,0:T(8,128)(2,1)} %cot_ref.1) | copy-start | bytes 663556
  1.6 12.1 %copy-start = (bf16[4,6,24,192]{3,2,1,0:T(8,128)(2,1)S(1)}, bf16[4,6,24,192]{3,2,1,0:T(8,128)(2,1)}, u32[]{:S(2)}) copy-start(bf16[4,6,24,192]{3,2,1,0:T(8,128)(2,1)} %field_ref.1) | copy-start | bytes 663556
  1.6 17.7 %collective-permute-start = (bf16[2,4,3,6,192]{4,3,2,1,0:T(8,128)(2,1)S(1)}, bf16[2,4,3,6,192]{4,3,2,1,0:T(8,128)(2,1)S(1)}, u32[]{:S(2)}, u32[]{:S(2)}) collective-permute-start(bf16[2,4,3,6,192]{4,3,2,1,0:T(8,128)(2,1)S(1)} %pad_maximum_fusion.1), channel_id=1, source_target_pairs={{0,31},{1,0},{2,1},{3,2},{4,3},{5,4},{6,5},{7,6},{8,7},{9,8},{10,9... | collective-permute-start | bytes 165896 | tf_op jit(solution)/shard_map/ppermute | solution.py:40
  5.0 14.3 %collective-permute-start.2 = (bf16[2,4,3,6,192]{4,3,2,1,0:T(8,128)(2,1)S(1)}, bf16[2,4,3,6,192]{4,3,2,1,0:T(8,128)(2,1)S(1)}, u32[]{:S(2)}, u32[]{:S(2)}) collective-permute-start(bf16[2,4,3,6,192]{4,3,2,1,0:T(8,128)(2,1)S(1)} %pad_maximum_fusion.2), channel_id=1, source_target_pairs={{0,255},{1,224},{2,225},{3,226},{4,227},{5,228},{6,229},{7,230},{8... | collective-permute-start | bytes 165896 | tf_op jit(solution)/shard_map/ppermute | solution.py:40
  13.8 1.5 %copy-start.20 = (s32[4,6,24]{2,0,1:T(4,128)S(1)}, s32[4,6,24]{2,0,1:T(4,128)}, u32[]{:S(2)}) copy-start(s32[4,6,24]{2,0,1:T(4,128)} %param.26) | copy-start | bytes 6916
  13.8 1.6 %copy-start.21 = (s32[2,1,2]{2,1,0:T(1,128)S(1)}, s32[2,1,2]{2,1,0:T(1,128)}, u32[]{:S(2)}) copy-start(s32[2,1,2]{2,1,0:T(1,128)} %param.27) | copy-start | bytes 52
  13.9 2.2 %copy-start.17 = (bf16[192,576]{1,0:T(8,128)(2,1)S(1)}, bf16[192,576]{1,0:T(8,128)(2,1)}, u32[]{:S(2)}) copy-start(bf16[192,576]{1,0:T(8,128)(2,1)} %param.20) | copy-start | bytes 663556
  13.9 8.7 %collective-permute-start.1 = (bf16[2,4,3,18,192]{4,3,2,1,0:T(8,128)(2,1)S(1)}, bf16[2,4,3,18,192]{4,3,2,1,0:T(8,128)(2,1)S(1)}, u32[]{:S(2)}, u32[]{:S(2)}) collective-permute-start(bf16[2,4,3,18,192]{4,3,2,1,0:T(8,128)(2,1)S(1)} %pad_maximum_fusion), channel_id=1, source_target_pairs={{0,224},{1,225},{2,226},{3,227},{4,228},{5,229},{6,230},{7,231},{8... | collective-permute-start | bytes 497672 | tf_op jit(solution)/shard_map/ppermute | solution.py:40
  16.1 0.9 %copy-start.2 = (bf16[276,276]{1,0:T(8,128)(2,1)S(1)}, bf16[276,276]{1,0:T(8,128)(2,1)}, u32[]{:S(2)}) copy-start(bf16[276,276]{1,0:T(8,128)(2,1)} %constant.36.clone.table_perm_ref) | copy-start | bytes 457060
  16.1 1.0 %copy-start.8 = (f32[2,1,6,3312]{3,1,2,0:T(1,128)S(1)}, f32[2,1,6,3312]{3,1,2,0:T(1,128)}, u32[]{:S(2)}) copy-start(f32[2,1,6,3312]{3,1,2,0:T(1,128)} %param.25) | copy-start | bytes 476932
  16.1 1.1 %copy-start.9 = (bf16[192,192]{1,0:T(8,128)(2,1)S(1)}, bf16[192,192]{1,0:T(8,128)(2,1)}, u32[]{:S(2)}) copy-start(bf16[192,192]{1,0:T(8,128)(2,1)} %constant.37.clone.row_perm_ref) | copy-start | bytes 221188
  17.2 5.4 %copy-start.3 = (bf16[192,768]{1,0:T(8,128)(2,1)S(1)}, bf16[192,768]{1,0:T(8,128)(2,1)}, u32[]{:S(2)}) copy-start(bf16[192,768]{1,0:T(8,128)(2,1)} %wup_ref.1) | copy-start | bytes 884740
  17.2 5.4 %copy-start.4 = (bf16[768,192]{0,1:T(8,128)(2,1)S(1)}, bf16[768,192]{0,1:T(8,128)(2,1)}, u32[]{:S(2)}) copy-start(bf16[768,192]{0,1:T(8,128)(2,1)} %param.24) | copy-start | bytes 884740
  17.2 5.4 %copy-start.6 = (bf16[288,288]{1,0:T(8,128)(2,1)S(1)}, bf16[288,288]{1,0:T(8,128)(2,1)}, u32[]{:S(2)}) copy-start(bf16[288,288]{1,0:T(8,128)(2,1)} %constant.39.clone.perm_t_ref) | copy-start | bytes 497668
  17.2 5.4 %copy-start.7 = (bf16[288,288]{1,0:T(8,128)(2,1)S(1)}, bf16[288,288]{1,0:T(8,128)(2,1)}, u32[]{:S(2)}) copy-start(bf16[288,288]{1,0:T(8,128)(2,1)} %constant.38.clone.perm_ref) | copy-start | bytes 497668
  17.2 5.4 %copy-start.10 = (bf16[192,192]{1,0:T(8,128)(2,1)S(1)}, bf16[192,192]{1,0:T(8,128)(2,1)}, u32[]{:S(2)}) copy-start(bf16[192,192]{1,0:T(8,128)(2,1)} %wproj_ref.1) | copy-start | bytes 221188
  17.2 5.4 %copy-start.11 = (bf16[96,96]{1,0:T(8,128)(2,1)S(1)}, bf16[96,96]{1,0:T(8,128)(2,1)}, u32[]{:S(2)}) copy-start(bf16[96,96]{1,0:T(8,128)(2,1)} %constant.41.clone.chunk_perm_ref) | copy-start | bytes 55300
  17.2 5.4 %copy-start.14 = (f32[192]{0:T(256)S(1)}, f32[192]{0:T(256)}, u32[]{:S(2)}) copy-start(f32[192]{0:T(256)} %param.22) | copy-start | bytes 2308
  52.8 21.4 %all-to-all-start.1 = ((bf16[32,1,8,276]{3,2,1,0:T(8,128)(2,1)}), bf16[32,1,8,276]{3,2,1,0:T(8,128)(2,1)S(1)}, u32[]{:S(2)}, u32[]{:S(2)}) async-start(bf16[32,1,8,276]{3,2,1,0:T(8,128)(2,1)} %broadcast_in_dim.2), calls=%async_computation.1 | async-start | bytes 393216 | tf_op jit(solution)/shard_map/all_to_all | solution.py:326
  56.9 14.5 %collective-permute-start.4 = (bf16[2,4,3,18,192]{4,3,2,1,0:T(8,128)(2,1)S(1)}, bf16[2,4,3,18,192]{4,3,2,1,0:T(8,128)(2,1)S(1)}, u32[]{:S(2)}, u32[]{:S(2)}) collective-permute-start(bf16[2,4,3,18,192]{4,3,2,1,0:T(8,128)(2,1)S(1)} %get-tuple-element.12), channel_id=1, source_target_pairs={{0,32},{1,33},{2,34},{3,35},{4,36},{5,37},{6,38},{7,39},{8,40},{9,... | collective-permute-start | bytes 497672 | tf_op jit(solution)/shard_map/ppermute | solution.py:40
  57.1 10.5 %collective-permute-start.3 = (bf16[2,4,3,6,192]{4,3,2,1,0:T(8,128)(2,1)S(1)}, bf16[2,4,3,6,192]{4,3,2,1,0:T(8,128)(2,1)S(1)}, u32[]{:S(2)}, u32[]{:S(2)}) collective-permute-start(bf16[2,4,3,6,192]{4,3,2,1,0:T(8,128)(2,1)S(1)} %get-tuple-element.11), channel_id=1, source_target_pairs={{0,1},{1,2},{2,3},{3,4},{4,5},{5,6},{6,7},{7,8},{8,9},{9,10},{10,1... | collective-permute-start | bytes 165896 | tf_op jit(solution)/shard_map/ppermute | solution.py:40
  61.1 10.3 %collective-permute-start.5 = (bf16[2,4,3,6,192]{4,3,2,1,0:T(8,128)(2,1)S(1)}, bf16[2,4,3,6,192]{4,3,2,1,0:T(8,128)(2,1)S(1)}, u32[]{:S(2)}, u32[]{:S(2)}) collective-permute-start(bf16[2,4,3,6,192]{4,3,2,1,0:T(8,128)(2,1)S(1)} %get-tuple-element.13), channel_id=1, source_target_pairs={{0,33},{1,34},{2,35},{3,36},{4,37},{5,38},{6,39},{7,40},{8,41},{9,... | collective-permute-start | bytes 165896 | tf_op jit(solution)/shard_map/ppermute | solution.py:40
  67.5 3.9 %copy-start.18 = (bf16[2,4,3,6,192]{4,3,2,1,0:T(8,128)(2,1)}, bf16[2,4,3,6,192]{4,3,2,1,0:T(8,128)(2,1)S(1)}, u32[]{:S(2)}) copy-start(bf16[2,4,3,6,192]{4,3,2,1,0:T(8,128)(2,1)S(1)} %collective-permute-done.3.lon_ref) | copy-start | bytes 165892
  71.4 0.7 copy-start.16
  (5 other events, 3.4 us)

commit v3 on v2

--- a/solution.py
+++ b/solution.py
@@ -21,7 +21,8 @@
 TAB = PAIR * SPREAD
 ROWS = HEADS * POS
 SLOTS = 16
-CHUNK = 8
+QUARTER = PAIR * HEADS // 2
+LANES = 128
 
 epsilon = 1e-05
 keep_share = 0.8
@@ -86,7 +87,42 @@
     return jnp.concatenate([rows * head_mask[h : h + 1, :] for h in range(HEADS)], axis=0)
 
 
-def block_kernel(
+def put(packed, t, row, slab):
+    third = packed.shape[0] // 3
+    size = slab.shape[0]
+    rest = C - LANES
+    packed[t * third + row : t * third + row + size, :] = slab[:, :LANES]
+    packed[2 * third + row : 2 * third + row + size, t * rest : (t + 1) * rest] = slab[:, LANES:]
+
+
+def get(packed, t, row, size):
+    third = packed.shape[0] // 3
+    rest = C - LANES
+    return (
+        packed[t * third + row : t * third + row + size, :],
+        packed[2 * third + row : 2 * third + row + size, t * rest : (t + 1) * rest],
+    )
+
+
+def pack_kernel(field_ref, cot_ref, lat_out, diag_out, lon_out, lat_buf, diag_buf, lon_buf):
+    half = WLAT // 2
+    edge = WLON // 2
+    inner = 2 * WLON - edge
+    for t, source in enumerate((field_ref, cot_ref)):
+        for z in range(4):
+            for i in range(half):
+                k = z * half + i
+                top = source[z, i].astype(f32)
+                low = source[z, half + i].astype(f32)
+                put(lat_buf, t, k * inner, top[edge:])
+                put(diag_buf, t, k * edge, top[:edge])
+                put(lon_buf, t, k * edge, low[:edge])
+    lat_out[...] = lat_buf[...].astype(bf16)
+    diag_out[...] = diag_buf[...].astype(bf16)
+    lon_out[...] = lon_buf[...].astype(bf16)
+
+
+def scores_kernel(
     field_ref,
     cot_ref,
     lon_ref,
@@ -103,15 +139,18 @@
     label_col_ref,
     factor_ref,
     perm_ref,
-    perm_t_ref,
     head_mask_ref,
     table_perm_ref,
     chunk_perm_ref,
-    own_out,
-    lon_out,
-    lat_out,
-    diag_out,
     fold_out,
+    x_out,
+    q_out,
+    kt_out,
+    probs_out,
+    grad_low_out,
+    grad_att_out,
+    grad_sum_out,
+    result_out,
     frame,
     wide,
 ):
@@ -120,21 +159,26 @@
     edge = WLON // 2
     inner = cols - edge
     root = 1.0 / math.sqrt(HD)
+    lon_part = lon_ref[...].astype(f32)
+    lat_part = lat_ref[...].astype(f32)
+    diag_part = diag_ref[...].astype(f32)
     for t, own in enumerate((field_ref, cot_ref)):
         for level in range(4):
             z = (level + 1) % 4
             for i in range(half):
+                k = z * half + i
                 row = (level * WLAT + i) * cols
-                frame[t, row : row + cols, :] = jnp.concatenate(
-                    [own[z, half + i].astype(f32)[edge:, :], lon_ref[t, z, i].astype(f32)], axis=0
-                )
+                frame[t, row : row + inner, :] = own[z, half + i].astype(f32)[edge:, :]
+                main, rest = get(lon_part, t, k * edge, edge)
+                frame[t, row + inner : row + cols, :LANES] = main
+                frame[t, row + inner : row + cols, LANES:] = rest
                 row = (level * WLAT + half + i) * cols
-                frame[t, row : row + cols, :] = jnp.concatenate(
-                    [lat_ref[t, z, i].astype(f32), diag_ref[t, z, i].astype(f32)], axis=0
-                )
-    spare = fold_out.shape[0] - 2 * PAIR
-    if spare:
-        fold_out[2 * PAIR :] = jnp.zeros((spare, CHUNK, TAB), bf16)
+                main, rest = get(lat_part, t, k * inner, inner)
+                frame[t, row : row + inner, :LANES] = main
+                frame[t, row : row + inner, LANES:] = rest
+                main, rest = get(diag_part, t, k * edge, edge)
+                frame[t, row + inner : row + cols, :LANES] = main
+                frame[t, row + inner : row + cols, LANES:] = rest
     gain1 = gain1_ref[...]
     gain2 = gain2_ref[...]
     wq_t = wqkv_t_ref[0:C, :]
@@ -142,21 +186,23 @@
     wv_t = wqkv_t_ref[2 * C : 3 * C, :]
     head_mask = head_mask_ref[...]
     perm = perm_ref[...]
-    perm_t = perm_t_ref[...]
     for n in range(2):
-        x = mm(perm, frame[0, n * 2 * POS : (n + 1) * 2 * POS, :].astype(bf16))
-        cot = mm(perm, frame[1, n * 2 * POS : (n + 1) * 2 * POS, :].astype(bf16))
-        scaled1, normed1, inverse1 = norm_parts(x, gain1)
-        h1 = scaled1.astype(bf16)
+        both = slice(n * 2 * POS, (n + 1) * 2 * POS)
+        x = mm(perm, frame[0, both, :].astype(bf16))
+        cot = mm(perm, frame[1, both, :].astype(bf16))
+        x_out[both, :] = x.astype(bf16)
+        h1 = norm_parts(x, gain1)[0].astype(bf16)
         q_all = mm_nt(h1, wq_t).astype(bf16)
         k_all = mm_nt(h1, wk_t).astype(bf16)
         v_all = mm_nt(h1, wv_t).astype(bf16)
+        q_out[both, :] = q_all
         saved = []
         branches = []
         for c in range(2):
             w = 2 * n + c
             rows = slice(c * POS, (c + 1) * POS)
             v_t = mm_nt(wv_t, h1[rows]).astype(bf16)
+            kt_out[w] = mm_nt(wk_t, h1[rows]).astype(bf16)
             q_wide = spread_heads(q_all[rows], head_mask)
             scores = mm_nt(k_all[rows], q_wide) * root + bias_ref[n]
             allowed = label_col_ref[:, w : w + 1] == label_row_ref[w]
@@ -164,38 +210,32 @@
             weights = jnp.exp(scores - jnp.max(scores, axis=0, keepdims=True))
             probs = weights * (1.0 / jnp.sum(weights, axis=0, keepdims=True))
             probs_low = probs.astype(bf16)
+            probs_out[w] = probs_low
             attended = head_blocks(mm(v_t, probs_low)).T.astype(bf16)
             factor = factor_ref[w]
             branches.append((mm(attended, wproj_ref[...]) * factor).astype(bf16).astype(f32))
-            saved.append((q_wide, probs, probs_low))
+            saved.append(probs)
         y_sum = x + jnp.concatenate(branches, axis=0)
         scaled2, normed2, inverse2 = norm_parts(y_sum, gain2)
         act, slope = gelu_parts(mm(scaled2.astype(bf16), wup_ref[...]))
-        result = (y_sum + mm_nt(act.astype(bf16), wdown_t_ref[...])).astype(bf16)
+        result_out[both, :] = (y_sum + mm_nt(act.astype(bf16), wdown_t_ref[...])).astype(bf16)
         grad_up = (mm(cot.astype(bf16), wdown_t_ref[...]) * slope).astype(bf16)
         grad_sum = cot + norm_back(mm_nt(grad_up, wup_ref[...]), gain2, normed2, inverse2)
+        grad_sum_out[both, :] = grad_sum
         grad_low_in = grad_sum.astype(bf16).astype(f32)
         folded = None
-        grad_h1 = []
         for c in range(2):
             w = 2 * n + c
             rows = slice(c * POS, (c + 1) * POS)
-            q_wide, probs, probs_low = saved[c]
-            k_t = mm_nt(wk_t, h1[rows]).astype(bf16)
+            probs = saved[c]
             grad_branch = (grad_low_in[rows] * factor_ref[w]).astype(bf16)
             grad_att = mm_nt(grad_branch, wproj_ref[...]).astype(bf16)
-            g_wide = spread_heads(grad_att, head_mask)
-            grad_probs = mm_nt(v_all[rows], g_wide)
+            grad_att_out[w * POS : (w + 1) * POS, :] = grad_att
+            grad_probs = mm_nt(v_all[rows], spread_heads(grad_att, head_mask))
             inner_sum = jnp.sum(probs * grad_probs, axis=0, keepdims=True)
             grad_scores = probs * (grad_probs - inner_sum)
             folded = grad_scores if folded is None else folded + grad_scores
-            grad_low = grad_scores.astype(bf16)
-            grad_q = (head_blocks(mm(k_t, grad_low)).T * root).astype(bf16)
-            grad_k = (mm(grad_low, q_wide) * root).astype(bf16)
-            grad_v = mm(probs_low, g_wide).astype(bf16)
-            grad_h1.append(mm(grad_q, wq_t) + mm(grad_k, wk_t) + mm(grad_v, wv_t))
-        grad_h1 = jnp.concatenate(grad_h1, axis=0).astype(bf16).astype(f32)
-        grad_field = (grad_sum + norm_back(grad_h1, gain1, normed1, inverse1)).astype(bf16)
+            grad_low_out[w] = grad_scores.astype(bf16)
         wide[...] = folded.T.reshape(HEADS, POS, POS)
         total = None
         for o in range(WLON):
@@ -211,21 +251,77 @@
         total = jnp.concatenate([total, jnp.zeros((HEADS, SLOTS - PAIR, TAB), f32)], axis=1)
         total = total.reshape(HEADS * SLOTS, TAB).astype(bf16)
         total = mm_nt(total, table_perm_ref[...]).astype(bf16)
-        total = mm(chunk_perm_ref[...], total).reshape(PAIR, CHUNK, TAB).astype(bf16)
-        fold_out[n * PAIR : (n + 1) * PAIR] = total
-        for t, value in enumerate((result, grad_field)):
+        total = mm(chunk_perm_ref[...], total)
+        fold_out[2 * n] = total[:QUARTER].astype(bf16)
+        fold_out[2 * n + 1] = total[QUARTER:].astype(bf16)
+
+
+def inputs_kernel(
+    x_ref,
+    q_ref,
+    kt_ref,
+    probs_ref,
+    grad_low_ref,
+    grad_att_ref,
+    grad_sum_ref,
+    result_ref,
+    gain1_ref,
+    wqkv_t_ref,
+    perm_t_ref,
+    head_mask_ref,
+    own_out,
+    lat_out,
+    diag_out,
+    lon_out,
+    lat_buf,
+    diag_buf,
+    lon_buf,
+):
+    half = WLAT // 2
+    cols = 2 * WLON
+    edge = WLON // 2
+    inner = cols - edge
+    root = 1.0 / math.sqrt(HD)
+    gain1 = gain1_ref[...]
+    wq_t = wqkv_t_ref[0:C, :]
+    wk_t = wqkv_t_ref[C : 2 * C, :]
+    wv_t = wqkv_t_ref[2 * C : 3 * C, :]
+    head_mask = head_mask_ref[...]
+    perm_t = perm_t_ref[...]
+    for n in range(2):
+        both = slice(n * 2 * POS, (n + 1) * 2 * POS)
+        _, normed1, inverse1 = norm_parts(x_ref[both, :].astype(f32), gain1)
+        grad_h1 = []
+        for c in range(2):
+            w = 2 * n + c
+            rows = slice(w * POS, (w + 1) * POS)
+            grad_low = grad_low_ref[w]
+            q_wide = spread_heads(q_ref[rows, :], head_mask)
+            g_wide = spread_heads(grad_att_ref[rows, :], head_mask)
+            grad_q = (head_blocks(mm(kt_ref[w], grad_low)).T * root).astype(bf16)
+            grad_k = (mm(grad_low, q_wide) * root).astype(bf16)
+            grad_v = mm(probs_ref[w], g_wide).astype(bf16)
+            grad_h1.append(mm(grad_q, wq_t) + mm(grad_k, wk_t) + mm(grad_v, wv_t))
+        grad_h1 = jnp.concatenate(grad_h1, axis=0).astype(bf16).astype(f32)
+        grad_sum = grad_sum_ref[both, :]
+        grad_field = (grad_sum + norm_back(grad_h1, gain1, normed1, inverse1)).astype(bf16)
+        for t, value in enumerate((result_ref[both, :], grad_field)):
             natural = mm(perm_t, value)
             for dz in range(WZ):
                 z = (2 * n + dz + 1) % 4
                 for i in range(half):
+                    k = z * half + i
                     row = (dz * WLAT + i) * cols
                     slab = natural[row : row + cols]
                     own_out[t, z, i] = slab[:inner].astype(bf16)
-                    lon_out[t, z, i] = slab[inner:].astype(bf16)
+                    put(lon_buf, t, k * edge, slab[inner:])
                     row = (dz * WLAT + half + i) * cols
                     slab = natural[row : row + cols]
-                    lat_out[t, z, i] = slab[:inner].astype(bf16)
-                    diag_out[t, z, i] = slab[inner:].astype(bf16)
+                    put(lat_buf, t, k * inner, slab[:inner])
+                    put(diag_buf, t, k * edge, slab[inner:])
+    lat_out[...] = lat_buf[...].astype(bf16)
+    diag_out[...] = diag_buf[...].astype(bf16)
+    lon_out[...] = lon_buf[...].astype(bf16)
 
 
 def expand_kernel(table_ref, table_perm_ref, row_perm_ref, bias_out, flat, rows, wide):
@@ -260,9 +356,11 @@
 def unpack_kernel(grad_ref, table_out, flat):
     part = PAIR // WZ * SPREAD
     for n in range(2):
+        halves = [grad_ref[2 * n + k].astype(f32) for k in range(2)]
         for a in range(WZ):
             for c in range(WLAT):
-                chunk = grad_ref[n * PAIR + a * WLAT + c].astype(f32)[:HEADS]
+                row = c * HEADS
+                chunk = halves[a][row : row + HEADS]
                 for b in range(WZ):
                     start = ((a * WZ + b) * WLAT + c) * part
                     flat[n * HEADS : (n + 1) * HEADS, start : start + part] = chunk[
@@ -272,17 +370,23 @@
         table_out[k] = flat[k : k + 1, :]
 
 
-def finish_kernel(own_ref, lon_ref, lat_ref, diag_ref, out_ref, grad_ref):
+def finish_kernel(own_ref, lat_ref, diag_ref, lon_ref, out_ref, grad_ref):
     half = WLAT // 2
+    edge = WLON // 2
+    inner = 2 * WLON - edge
+    lat_part = lat_ref[...].astype(f32)
+    diag_part = diag_ref[...].astype(f32)
+    lon_part = lon_ref[...].astype(f32)
     for t, target in enumerate((out_ref, grad_ref)):
         for z in range(4):
             for i in range(half):
-                target[z, i] = jnp.concatenate(
-                    [diag_ref[t, z, i].astype(f32), lat_ref[t, z, i].astype(f32)], axis=0
-                ).astype(bf16)
-                target[z, half + i] = jnp.concatenate(
-                    [lon_ref[t, z, i].astype(f32), own_ref[t, z, i].astype(f32)], axis=0
-                ).astype(bf16)
+                k = z * half + i
+                parts = (get(diag_part, t, k * edge, edge), get(lat_part, t, k * inner, inner))
+                slab = [jnp.concatenate([parts[0][j], parts[1][j]], axis=0) for j in range(2)]
+                target[z, i] = jnp.concatenate(slab, axis=1).astype(bf16)
+                slab = jnp.concatenate(get(lon_part, t, k * edge, edge), axis=1)
+                own = own_ref[t, z, i].astype(f32)
+                target[z, half + i] = jnp.concatenate([slab, own], axis=0).astype(bf16)
 
 
 def window_order():
@@ -303,10 +407,10 @@
 
 
 def chunk_order():
-    perm = np.zeros((PAIR * CHUNK, HEADS * SLOTS), np.float32)
+    perm = np.zeros((PAIR * HEADS, HEADS * SLOTS), np.float32)
     for h in range(HEADS):
         for k in range(PAIR):
-            perm[k * CHUNK + h, h * SLOTS + k] = 1.0
+            perm[k * HEADS + h, h * SLOTS + k] = 1.0
     return perm
 
 
@@ -318,13 +422,36 @@
     return perm
 
 
-def lon_sum(chunks):
+def lon_sum(quarters):
     lons = lax.axis_size("lon")
-    shares = chunks.reshape((lons, -1) + chunks.shape[1:])
-    shares = lax.all_to_all(shares, "lon", 0, 0)
-    share = jnp.sum(shares.astype(f32), axis=0).astype(bf16)
-    shares = lax.all_to_all(jnp.broadcast_to(share, shares.shape), "lon", 0, 0)
-    return shares.reshape(chunks.shape)
+    me = lax.axis_index("lon")
+    bits = [(me >> k) & 1 for k in range(2)]
+
+    def swapped(block, distance):
+        return lax.ppermute(block, "lon", [(i, i ^ distance) for i in range(lons)])
+
+    def pick(value, bit):
+        return lax.dynamic_index_in_dim(value, bit, 0, keepdims=False)
+
+    def add(a, b):
+        return (a.astype(f32) + b.astype(f32)).astype(bf16)
+
+    def gathered(value, distance, bit):
+        other = swapped(value, distance)
+        first = jnp.where(bit == 0, value, other)
+        second = jnp.where(bit == 0, other, value)
+        return jnp.stack([first, second])
+
+    pairs = quarters.reshape((2, 2) + quarters.shape[1:])
+    value = add(pick(pairs, bits[0]), swapped(pick(pairs, 1 - bits[0]), 1))
+    value = add(pick(value, bits[1]), swapped(pick(value, 1 - bits[1]), 2))
+    distance = 4
+    while distance < lons:
+        value = add(value, swapped(value, distance))
+        distance *= 2
+    value = gathered(value, 2, bits[1])
+    value = gathered(value, 1, bits[0])
+    return value.reshape(quarters.shape)
 
 
 def body(
@@ -343,10 +470,23 @@
     levels, lat_rows, lon_cols, channels = field_in.shape
     half = WLAT // 2
     edge = WLON // 2
-    both = (field_in, cotangent)
-    lon_part = shifted(jnp.stack([v[:, half:, :edge] for v in both]), 0, -1)
-    lat_part = shifted(jnp.stack([v[:, :half, edge:] for v in both]), -1, 0)
-    diag_part = shifted(jnp.stack([v[:, :half, :edge] for v in both]), -1, -1)
+    inner = lon_cols - edge
+    vmem = pl.BlockSpec(memory_space=pltpu.VMEM)
+    smem = pl.BlockSpec(memory_space=pltpu.SMEM)
+    sizes = [3 * levels * half * size for size in (inner, edge, edge)]
+    packed = tuple(jax.ShapeDtypeStruct((size, LANES), bf16) for size in sizes)
+    buffers = [pltpu.VMEM((size, LANES), f32) for size in sizes]
+    lat_part, diag_part, lon_part = pl.pallas_call(
+        pack_kernel,
+        out_shape=packed,
+        in_specs=[vmem] * 2,
+        out_specs=(vmem,) * 3,
+        scratch_shapes=buffers,
+        name="pack",
+    )(field_in, cotangent)
+    lat_part = shifted(lat_part, -1, 0)
+    diag_part = shifted(diag_part, -1, -1)
+    lon_part = shifted(lon_part, 0, -1)
 
     lat_start = lax.axis_index("lat") * lat_rows
     lat_total = lax.axis_size("lat") * lat_rows
@@ -363,9 +503,6 @@
 
     perm = window_order()
     head_mask = np.repeat(np.eye(HEADS, dtype=np.float32), HD, axis=1)
-    vmem = pl.BlockSpec(memory_space=pltpu.VMEM)
-    smem = pl.BlockSpec(memory_space=pltpu.SMEM)
-    inner = lon_cols - edge
     table_perm = jnp.asarray(table_order(), bf16)
     bias_wide = pl.pallas_call(
         expand_kernel,
@@ -384,33 +521,39 @@
         table_perm,
         jnp.asarray(row_order(), bf16),
     )
-    lons = lax.axis_size("lon")
-    chunks = -(-2 * PAIR // lons) * lons
-    own, lon_back, lat_back, diag_back, fold = pl.pallas_call(
-        block_kernel,
+    positions = levels * lat_rows * lon_cols
+    weights_t = w_qkv.T
+    gain1 = ln1_gain.reshape(1, C)
+    head_mask = jnp.asarray(head_mask, bf16)
+    fold, *saved = pl.pallas_call(
+        scores_kernel,
         out_shape=(
-            jax.ShapeDtypeStruct((2, 4, half, inner, C), bf16),
-            jax.ShapeDtypeStruct((2, 4, half, edge, C), bf16),
-            jax.ShapeDtypeStruct((2, 4, half, inner, C), bf16),
-            jax.ShapeDtypeStruct((2, 4, half, edge, C), bf16),
-            jax.ShapeDtypeStruct((chunks, CHUNK, TAB), bf16),
+            jax.ShapeDtypeStruct((4, QUARTER, TAB), bf16),
+            jax.ShapeDtypeStruct((positions, C), bf16),
+            jax.ShapeDtypeStruct((positions, C), bf16),
+            jax.ShapeDtypeStruct((4, C, POS), bf16),
+            jax.ShapeDtypeStruct((4, POS, ROWS), bf16),
+            jax.ShapeDtypeStruct((4, POS, ROWS), bf16),
+            jax.ShapeDtypeStruct((positions, C), bf16),
+            jax.ShapeDtypeStruct((positions, C), f32),
+            jax.ShapeDtypeStruct((positions, C), bf16),
         ),
-        in_specs=[vmem] * 14 + [smem] + [vmem] * 5,
-        out_specs=(vmem,) * 5,
+        in_specs=[vmem] * 14 + [smem] + [vmem] * 4,
+        out_specs=(vmem,) * 9,
         scratch_shapes=[
-            pltpu.VMEM((2, 4 * WLAT * lon_cols, C), f32),
+            pltpu.VMEM((2, positions, C), f32),
             pltpu.VMEM((HEADS, POS, POS), f32),
         ],
         compiler_params=pltpu.CompilerParams(vmem_limit_bytes=48 * 1024 * 1024),
-        name="block",
+        name="scores",
     )(
         field_in,
         cotangent,
         lon_part,
         lat_part,
         diag_part,
-        ln1_gain.reshape(1, C),
-        w_qkv.T,
+        gain1,
+        weights_t,
         w_proj,
         ln2_gain.reshape(1, C),
         w_up,
@@ -420,14 +563,25 @@
         label_col,
         factor,
         jnp.asarray(perm, bf16),
-        jnp.asarray(perm.T, bf16),
-        jnp.asarray(head_mask, bf16),
+        head_mask,
         table_perm,
         jnp.asarray(chunk_order(), bf16),
     )
-    lon_back = shifted(lon_back, 0, 1)
+    own, lat_back, diag_back, lon_back = pl.pallas_call(
+        inputs_kernel,
+        out_shape=(jax.ShapeDtypeStruct((2, levels, half, inner, C), bf16),) + packed,
+        in_specs=[vmem] * 12,
+        out_specs=(vmem,) * 4,
+        scratch_shapes=buffers,
+        compiler_params=pltpu.CompilerParams(vmem_limit_bytes=32 * 1024 * 1024),
+        cost_estimate=pl.CostEstimate(
+            flops=1_000_000_000, bytes_accessed=8_000_000, transcendentals=0
+        ),
+        name="inputs",
+    )(*saved, gain1, weights_t, jnp.asarray(perm.T, bf16), head_mask)
     lat_back = shifted(lat_back, 1, 0)
     diag_back = shifted(diag_back, 1, 1)
+    lon_back = shifted(lon_back, 0, 1)
     grads = pl.pallas_call(
         unpack_kernel,
         out_shape=jax.ShapeDtypeStruct((2 * HEADS, 1, PAIR * TAB), f32),
@@ -443,7 +597,7 @@
         in_specs=[vmem] * 4,
         out_specs=(vmem,) * 2,
         name="finish",
-    )(own, lon_back, lat_back, diag_back)
+    )(own, lat_back, diag_back, lon_back)
     return (result, grad_field, grads)
 
 

time: 77 us -> 84.5 us (1.097)
  blocking collectives: 16.3 us -> 0 us
  local copies, waits for them, and re-layouts: 6.27 us -> 14 us
  waiting for transfers between devices: 13.6 us -> 20.5 us
  Pallas kernels: 17.6 us -> 22.2 us
  starting transfers between devices: 21.7 us -> 24.4 us
  other arithmetic: 0.34 us -> 1.8 us
    ppermute x0 -> x7, waiting for transfers between devices: none -> 17.2 us  [swapped(): return lax.ppermute(block, 'lon', [(i, i ^ distance) for i in range(lons)])]
    all_to_all x1 -> x0, blocking collectives: 16.3 us -> none  [lon_sum(): shares = lax.all_to_all(shares, 'lon', 0, 0)]
    ppermute x6, waiting for transfers between devices: 13.6 us -> 3.27 us  [shifted(): return lax.ppermute(block, ('lat', 'lon'), route)]
    unnamed x45 -> x65, local copies, waits for them, and re-layouts: 3.91 us -> 13.4 us
    ppermute x6, starting transfers between devices: 17.5 us -> 22.4 us  [shifted(): return lax.ppermute(block, ('lat', 'lon'), route)]
    pallas_call x1 -> x3, Pallas kernels: 11.8 us -> 16.5 us  [the longest x1 11.7 us: body(): pl.pallas_call(scores_kernel, out_shape=(jax.ShapeDtypeStruct((4, QUARTER...]
    all_to_all x1 -> x0, starting transfers between devices: 4.13 us -> none  [lon_sum(): shares = lax.all_to_all(jnp.broadcast_to(share, shares.shape), 'lon', 0, 0)]
    ppermute x0 -> x7, starting transfers between devices: none -> 2.06 us  [swapped(): return lax.ppermute(block, 'lon', [(i, i ^ distance) for i in range(lons)])]
  transfers between devices with their start and end apart: 7 -> 13, of which waited for: 3 -> 6; matrix products, arithmetic and copies ran while one was open for 1% -> 1% of each run, Pallas kernels for 5% -> 8%
where the time goes in v3:
time: 84.5 us; the launch traced here: 84 us
  starting transfers between devices  24.4 us (29%)
  Pallas kernels  22.2 us (26%)
  waiting for transfers between devices  20.5 us (24%)
  local copies, waits for them, and re-layouts  14 us (17%)
  other arithmetic  1.8 us (2%)
  between operations  0.96 us (1%)
    ppermute x6, starting transfers between devices, shifted(): return lax.ppermute(block, ('lat', 'lon'), route)  22.4 us
    ppermute x7, waiting for transfers between devices, swapped(): return lax.ppermute(block, 'lon', [(i, i ^ distance) for i in range(lons)])  17.2 us
    unnamed x65, local copies, waits for them, and re-layouts  13.4 us
    pallas_call x1, Pallas kernels, body(): pl.pallas_call(scores_kernel, out_shape=(jax.ShapeDtypeStruct((4, QUARTER...  11.7 us
    ppermute x6, waiting for transfers between devices, shifted(): return lax.ppermute(block, ('lat', 'lon'), route)  3.27 us
    pallas_call x1, Pallas kernels, body(): pl.pallas_call(inputs_kernel, out_shape=(jax.ShapeDtypeStruct((2, levels,...  2.85 us
    ppermute x7, starting transfers between devices, swapped(): return lax.ppermute(block, 'lon', [(i, i ^ distance) for i in range(lons)])  2.06 us
    pallas_call x1, Pallas kernels, body(): pl.pallas_call(expand_kernel, out_shape=jax.ShapeDtypeStruct((2, POS, ROW...  2.04 us
  transfers between devices with their start and end apart: 13, of which 6 were waited for; matrix products, arithmetic and copies ran while one was open for 1% of the time, Pallas kernels for 8%

profile of v3, /device:TPU:1, one launch (start us, length us, event | category | flops | bytes accessed | tf_op | source)
XLA Modules:
  0.0 84.0 jit_solution(13792076218100233690)
XLA Ops:
  0.6 1.9 %pack.1 = (bf16[648,128]{1,0:T(8,128)(2,1)}, bf16[216,128]{1,0:T(8,128)(2,1)}, bf16[216,128]{1,0:T(8,128)(2,1)}) custom-call(bf16[4,6,24,192]{3,2,1,0:T(8,128)(2,1)} %field_ref.3, bf16[4,6,24,192]{3,2,1,0:T(8,128)(2,1)} %cot_ref.3), custom_call_target="tpu_custom_call" | custom-call | tf_op jit(solution)/shard_map/pack/pallas_call | solution.py:479
  2.5 3.2 %collective-permute-start = (bf16[216,128]{1,0:T(8,128)(2,1)}, bf16[216,128]{1,0:T(8,128)(2,1)S(1)}, u32[]{:S(2)}, u32[]{:S(2)}) collective-permute-start(bf16[216,128]{1,0:T(8,128)(2,1)} %get-tuple-element.21), channel_id=1, source_target_pairs={{0,31},{1,0},{2,1},{3,2},{4,3},{5,4},{6,5},{7,6},{8,7},{9,8},{10,9... | collective-permute-start | bytes 165896 | tf_op jit(solution)/shard_map/ppermute | solution.py:41
  5.8 1.8 %collective-permute-start.1 = (bf16[648,128]{1,0:T(8,128)(2,1)}, bf16[648,128]{1,0:T(8,128)(2,1)S(1)}, u32[]{:S(2)}, u32[]{:S(2)}) collective-permute-start(bf16[648,128]{1,0:T(8,128)(2,1)} %get-tuple-element.22), channel_id=1, source_target_pairs={{0,224},{1,225},{2,226},{3,227},{4,228},{5,229},{6,230},{7,231},{8... | collective-permute-start | bytes 497672 | tf_op jit(solution)/shard_map/ppermute | solution.py:41
  7.5 8.3 %collective-permute-start.2 = (bf16[216,128]{1,0:T(8,128)(2,1)}, bf16[216,128]{1,0:T(8,128)(2,1)S(1)}, u32[]{:S(2)}, u32[]{:S(2)}) collective-permute-start(bf16[216,128]{1,0:T(8,128)(2,1)} %get-tuple-element.23), channel_id=1, source_target_pairs={{0,255},{1,224},{2,225},{3,226},{4,227},{5,228},{6,229},{7,230},{8... | collective-permute-start | bytes 165896 | tf_op jit(solution)/shard_map/ppermute | solution.py:41
  18.1 2.0 %expand.1.bias_ref = f32[2,144,864]{2,1,0:T(8,128)S(1)} custom-call(f32[12,1,3312]{2,1,0:T(1,128)S(1)} %bitcast.34, bf16[276,276]{1,0:T(8,128)(2,1)S(1)} %copy-done.4, bf16[192,192]{1,0:T(8,128)(2,1)S(1)} %copy-done.17), custom_call_target="tpu_custom_call" | custom-call | tf_op jit(solution)/shard_map/expand/pallas_call | solution.py:507
  20.2 1.0 %copy-done = f32[2,144,864]{2,1,0:T(8,128)} copy-done((f32[2,144,864]{2,1,0:T(8,128)}, f32[2,144,864]{2,1,0:T(8,128)S(1)}, u32[]{:S(2)}) %copy-start) | copy-done | bytes 995352
  23.8 0.9 %copy-done.13 = bf16[648,128]{1,0:T(8,128)(2,1)S(1)} copy-done((bf16[648,128]{1,0:T(8,128)(2,1)S(1)}, bf16[648,128]{1,0:T(8,128)(2,1)}, u32[]{:S(2)}) %copy-start.13) | copy-done | bytes 165912
  26.3 11.7 %scores.1 = (bf16[4,36,276]{2,1,0:T(8,128)(2,1)S(1)}, bf16[576,192]{1,0:T(8,128)(2,1)S(1)}, bf16[576,192]{1,0:T(8,128)(2,1)S(1)}, bf16[4,192,144]{2,1,0:T(8,128)...) custom-call(bf16[4,6,24,192]{3,2,1,0:T(8,128)(2,1)S(1)} %copy-done.1, ...), custom_call_target="tpu_custom_call" | custom-call | tf_op jit(solution)/shard_map/scores/pallas_call | solution.py:528
  39.4 1.2 %collective-permute-done.6 = bf16[2,36,276]{2,1,0:T(8,128)(2,1)S(1)} collective-permute-done((bf16[2,36,276]{2,1,0:T(8,128)(2,1)S(1)}, bf16[2,36,276]{2,1,0:T(8,128)(2,1)S(1)}, u32[]{:S(2)}, u32[]{:S(2)}) %collective-permute-start.6) | collective-permute-done | bytes 39776 | tf_op jit(solution)/shard_map/ppermute | solution.py:431
  40.7 0.8 %fusion = bf16[2,36,276]{2,1,0:T(8,128)(2,1)S(1)} fusion(bf16[2,36,276]{2,1,0:T(8,128)(2,1)S(1)} %collective-permute-done.6, bf16[2,2,36,276]{3,2,1,0:T(8,128)(2,1)} %bitcast.36, s32[]{:T(128)S(6)} %select_n.40), kind=kLoop, calls=%fused_computation.2 | loop fusion | flops 79488 | bytes 119236 | tf_op jit(solution)/shard_map/convert_element_type | solution.py:437
  41.6 4.2 %collective-permute-done.7 = bf16[36,276]{1,0:T(8,128)(2,1)S(1)} collective-permute-done((bf16[36,276]{1,0:T(8,128)(2,1)S(1)}, bf16[36,276]{1,0:T(8,128)(2,1)S(1)}, u32[]{:S(2)}, u32[]{:S(2)}) %collective-permute-start.7) | collective-permute-done | bytes 19904 | tf_op jit(solution)/shard_map/ppermute | solution.py:431
  46.0 2.7 %collective-permute-done.8 = bf16[36,276]{1,0:T(8,128)(2,1)S(1)} collective-permute-done((bf16[36,276]{1,0:T(8,128)(2,1)S(1)}, bf16[36,276]{1,0:T(8,128)(2,1)S(1)}, u32[]{:S(2)}, u32[]{:S(2)}) %collective-permute-start.8) | collective-permute-done | bytes 19904 | tf_op jit(solution)/shard_map/ppermute | solution.py:431
  49.1 3.7 %collective-permute-done.9 = bf16[36,276]{1,0:T(8,128)(2,1)S(1)} collective-permute-done((bf16[36,276]{1,0:T(8,128)(2,1)S(1)}, bf16[36,276]{1,0:T(8,128)(2,1)S(1)}, u32[]{:S(2)}, u32[]{:S(2)}) %collective-permute-start.9) | collective-permute-done | bytes 19904 | tf_op jit(solution)/shard_map/ppermute | solution.py:431
  52.8 1.4 %collective-permute-start.10 = (bf16[36,276]{1,0:T(8,128)(2,1)S(1)}, bf16[36,276]{1,0:T(8,128)(2,1)S(1)}, u32[]{:S(2)}, u32[]{:S(2)}) collective-permute-start(bf16[36,276]{1,0:T(8,128)(2,1)S(1)} %add_convert_fusion.1), channel_id=1, source_target_pairs={{0,16},{1,17},{2,18},{3,19},{4,20},{5,21},{6,22},{7,23},{8,24},{9,... | collective-permute-start | bytes 59624 | tf_op jit(solution)/shard_map/ppermute | solution.py:431
  54.1 5.4 %collective-permute-done.10 = bf16[36,276]{1,0:T(8,128)(2,1)S(1)} collective-permute-done((bf16[36,276]{1,0:T(8,128)(2,1)S(1)}, bf16[36,276]{1,0:T(8,128)(2,1)S(1)}, u32[]{:S(2)}, u32[]{:S(2)}) %collective-permute-start.10) | collective-permute-done | bytes 19904 | tf_op jit(solution)/shard_map/ppermute | solution.py:431
  59.6 1.2 %copy-done.3 = bf16[4,144,864]{2,1,0:T(8,128)(2,1)S(1)} copy-done((bf16[4,144,864]{2,1,0:T(8,128)(2,1)S(1)}, bf16[4,144,864]{2,1,0:T(8,128)(2,1)}, u32[]{:S(2)}) %copy-start.3) | copy-done | bytes 995352
  60.8 1.0 %copy-done.8 = bf16[576,192]{1,0:T(8,128)(2,1)S(1)} copy-done((bf16[576,192]{1,0:T(8,128)(2,1)S(1)}, bf16[576,192]{1,0:T(8,128)(2,1)}, u32[]{:S(2)}) %copy-start.8) | copy-done | bytes 221208
  61.8 0.9 %copy-done.11 = bf16[288,288]{1,0:T(8,128)(2,1)S(1)} copy-done((bf16[288,288]{1,0:T(8,128)(2,1)S(1)}, bf16[288,288]{1,0:T(8,128)(2,1)}, u32[]{:S(2)}) %copy-start.11) | copy-done | bytes 165912
  62.7 2.8 %inputs.1 = (bf16[2,4,3,18,192]{4,3,2,1,0:T(8,128)(2,1)S(1)}, bf16[648,128]{1,0:T(8,128)(2,1)S(1)}, bf16[216,128]{1,0:T(8,128)(2,1)S(1)}, bf16[216,128]{1,0:T(8,128)(2,1)S(1)}) custom-call(bf16[576,192]{1,0:T(8,128)(2,1)S(1)} %get-tuple-element.24.x_ref, bf16[576,192]{1,0:T(8,128)(2,1)S(1)} %get-tuple-element.25.q_ref, ...), custom_call_target="tpu_custom_call" | custom-call | flops 1000000000 | bytes 8000000 | tf_op jit(solution)/shard_map/inputs/pallas_call | solution.py:570
  66.7 7.3 %collective-permute-start.4 = (bf16[216,128]{1,0:T(8,128)(2,1)S(1)}, bf16[216,128]{1,0:T(8,128)(2,1)S(1)}, u32[]{:S(2)}, u32[]{:S(2)}) collective-permute-start(bf16[216,128]{1,0:T(8,128)(2,1)S(1)} %get-tuple-element.34), channel_id=1, source_target_pairs={{0,33},{1,34},{2,35},{3,36},{4,37},{5,38},{6,39},{7,40},{8,41},{9,... | collective-permute-start | bytes 165896 | tf_op jit(solution)/shard_map/ppermute | solution.py:41
  74.0 1.5 %collective-permute-start.5 = (bf16[216,128]{1,0:T(8,128)(2,1)S(1)}, bf16[216,128]{1,0:T(8,128)(2,1)S(1)}, u32[]{:S(2)}, u32[]{:S(2)}) collective-permute-start(bf16[216,128]{1,0:T(8,128)(2,1)S(1)} %get-tuple-element.35), channel_id=1, source_target_pairs={{0,1},{1,2},{2,3},{3,4},{4,5},{5,6},{6,7},{7,8},{8,9},{9,10},{10,1... | collective-permute-start | bytes 165896 | tf_op jit(solution)/shard_map/ppermute | solution.py:41
  75.6 3.3 %collective-permute-done.4.diag_ref = bf16[216,128]{1,0:T(8,128)(2,1)S(1)} collective-permute-done((bf16[216,128]{1,0:T(8,128)(2,1)S(1)}, bf16[216,128]{1,0:T(8,128)(2,1)S(1)}, u32[]{:S(2)}, u32[]{:S(2)}) %collective-permute-start.4) | collective-permute-done | bytes 55328 | tf_op jit(solution)/shard_map/ppermute | solution.py:41
  79.5 2.0 %finish.1 = (bf16[4,6,24,192]{3,2,1,0:T(8,128)(2,1)}, bf16[4,6,24,192]{3,2,1,0:T(8,128)(2,1)}) custom-call(bf16[2,4,3,18,192]{4,3,2,1,0:T(8,128)(2,1)} %copy-done.9, bf16[648,128]{1,0:T(8,128)(2,1)} %copy-done.27, bf16[216,128]{1,0:T(8,128)(2,1)} %copy-done.28, bf16[216,128]{1,0:T(8,128)(2,1)} %copy-done.29), custom_call_target="tpu_custom_call" | custom-call | tf_op jit(solution)/shard_map/finish/pallas_call | solution.py:594
  82.2 1.7 %unpack.1 = f32[12,1,3312]{2,1,0:T(1,128)} custom-call(bf16[4,36,276]{2,1,0:T(8,128)(2,1)} %bitcast.40), custom_call_target="tpu_custom_call" | custom-call | tf_op jit(solution)/shard_map/unpack/pallas_call | solution.py:585
  (96 shorter events, 11.0 us)
Async XLA Ops:
  0.6 16.0 %copy-start.26 = (bf16[192,576]{1,0:T(8,128)(2,1)S(1)}, bf16[192,576]{1,0:T(8,128)(2,1)}, u32[]{:S(2)}) copy-start(bf16[192,576]{1,0:T(8,128)(2,1)} %param.20) | copy-start | bytes 663556
  2.5 13.3 %copy-start.30 = (s32[4,6,24]{2,0,1:T(4,128)S(1)}, s32[4,6,24]{2,0,1:T(4,128)}, u32[]{:S(2)}) copy-start(s32[4,6,24]{2,0,1:T(4,128)} %param.26) | copy-start | bytes 6916
  2.5 18.6 %collective-permute-start = (bf16[216,128]{1,0:T(8,128)(2,1)}, bf16[216,128]{1,0:T(8,128)(2,1)S(1)}, u32[]{:S(2)}, u32[]{:S(2)}) collective-permute-start(bf16[216,128]{1,0:T(8,128)(2,1)} %get-tuple-element.21), channel_id=1, source_target_pairs={{0,31},{1,0},{2,1},{3,2},{4,3},{5,4},{6,5},{7,6},{8,7},{9,8},{10,9... | collective-permute-start | bytes 165896 | tf_op jit(solution)/shard_map/ppermute | solution.py:41
  5.8 16.6 %collective-permute-start.1 = (bf16[648,128]{1,0:T(8,128)(2,1)}, bf16[648,128]{1,0:T(8,128)(2,1)S(1)}, u32[]{:S(2)}, u32[]{:S(2)}) collective-permute-start(bf16[648,128]{1,0:T(8,128)(2,1)} %get-tuple-element.22), channel_id=1, source_target_pairs={{0,224},{1,225},{2,226},{3,227},{4,228},{5,229},{6,230},{7,231},{8... | collective-permute-start | bytes 497672 | tf_op jit(solution)/shard_map/ppermute | solution.py:41
  7.5 14.3 %collective-permute-start.2 = (bf16[216,128]{1,0:T(8,128)(2,1)}, bf16[216,128]{1,0:T(8,128)(2,1)S(1)}, u32[]{:S(2)}, u32[]{:S(2)}) collective-permute-start(bf16[216,128]{1,0:T(8,128)(2,1)} %get-tuple-element.23), channel_id=1, source_target_pairs={{0,255},{1,224},{2,225},{3,226},{4,227},{5,228},{6,229},{7,230},{8... | collective-permute-start | bytes 165896 | tf_op jit(solution)/shard_map/ppermute | solution.py:41
  17.3 5.8 %copy-start.23 = (bf16[6,192]{1,0:T(8,128)(2,1)S(1)}, bf16[6,192]{1,0:T(8,128)(2,1)}, u32[]{:S(2)}) copy-start(bf16[6,192]{1,0:T(8,128)(2,1)} %constant.55.clone.head_mask_ref) | copy-start | bytes 6916
  17.3 5.8 %copy-start.25 = (f32[192]{0:T(256)S(1)}, f32[192]{0:T(256)}, u32[]{:S(2)}) copy-start(f32[192]{0:T(256)} %param.22) | copy-start | bytes 2308
  17.5 5.6 %copy-start.22 = (bf16[72,96]{1,0:T(8,128)(2,1)S(1)}, bf16[72,96]{1,0:T(8,128)(2,1)}, u32[]{:S(2)}) copy-start(bf16[72,96]{1,0:T(8,128)(2,1)} %constant.57.clone.chunk_perm_ref) | copy-start | bytes 41476
  18.1 5.0 %copy-start.1 = (bf16[4,6,24,192]{3,2,1,0:T(8,128)(2,1)S(1)}, bf16[4,6,24,192]{3,2,1,0:T(8,128)(2,1)}, u32[]{:S(2)}) copy-start(bf16[4,6,24,192]{3,2,1,0:T(8,128)(2,1)} %field_ref.3) | copy-start | bytes 663556
  18.1 5.0 %copy-start.2 = (bf16[4,6,24,192]{3,2,1,0:T(8,128)(2,1)S(1)}, bf16[4,6,24,192]{3,2,1,0:T(8,128)(2,1)}, u32[]{:S(2)}) copy-start(bf16[4,6,24,192]{3,2,1,0:T(8,128)(2,1)} %cot_ref.3) | copy-start | bytes 663556
  18.1 5.0 %copy-start.5 = (bf16[192,768]{1,0:T(8,128)(2,1)S(1)}, bf16[192,768]{1,0:T(8,128)(2,1)}, u32[]{:S(2)}) copy-start(bf16[192,768]{1,0:T(8,128)(2,1)} %wup_ref.1) | copy-start | bytes 884740
  18.1 5.1 %copy-start.6 = (bf16[768,192]{0,1:T(8,128)(2,1)S(1)}, bf16[768,192]{0,1:T(8,128)(2,1)}, u32[]{:S(2)}) copy-start(bf16[768,192]{0,1:T(8,128)(2,1)} %param.24) | copy-start | bytes 884740
  18.1 5.1 %copy-start.10 = (bf16[288,288]{1,0:T(8,128)(2,1)S(1)}, bf16[288,288]{1,0:T(8,128)(2,1)}, u32[]{:S(2)}) copy-start(bf16[288,288]{1,0:T(8,128)(2,1)} %constant.56.clone.perm_ref) | copy-start | bytes 497668
  18.1 5.1 %copy-start.16 = (bf16[192,192]{1,0:T(8,128)(2,1)S(1)}, bf16[192,192]{1,0:T(8,128)(2,1)}, u32[]{:S(2)}) copy-start(bf16[192,192]{1,0:T(8,128)(2,1)} %wproj_ref.1) | copy-start | bytes 221188
  39.4 1.2 %collective-permute-start.6 = (bf16[2,36,276]{2,1,0:T(8,128)(2,1)S(1)}, bf16[2,36,276]{2,1,0:T(8,128)(2,1)S(1)}, u32[]{:S(2)}, u32[]{:S(2)}) collective-permute-start(bf16[2,36,276]{2,1,0:T(8,128)(2,1)S(1)} %dynamic-slice_bitcast_fusion), channel_id=1, source_target_pairs={{0,1},{1,0},{2,3},{3,2},{4,5},{5,4},{6,7},{7,6},{8,9},{9,8},{10,11... | collective-permute-start | bytes 119240 | tf_op jit(solution)/shard_map/ppermute | solution.py:431
  41.5 4.3 %collective-permute-start.7 = (bf16[36,276]{1,0:T(8,128)(2,1)S(1)}, bf16[36,276]{1,0:T(8,128)(2,1)S(1)}, u32[]{:S(2)}, u32[]{:S(2)}) collective-permute-start(bf16[36,276]{1,0:T(8,128)(2,1)S(1)} %dynamic-slice_bitcast_fusion.1), channel_id=1, source_target_pairs={{0,2},{1,3},{2,0},{3,1},{4,6},{5,7},{6,4},{7,5},{8,10},{9,11},{10,... | collective-permute-start | bytes 59624 | tf_op jit(solution)/shard_map/ppermute | solution.py:431
  45.9 2.8 %collective-permute-start.8 = (bf16[36,276]{1,0:T(8,128)(2,1)S(1)}, bf16[36,276]{1,0:T(8,128)(2,1)S(1)}, u32[]{:S(2)}, u32[]{:S(2)}) collective-permute-start(bf16[36,276]{1,0:T(8,128)(2,1)S(1)} %fusion.1), channel_id=1, source_target_pairs={{0,4},{1,5},{2,6},{3,7},{4,0},{5,1},{6,2},{7,3},{8,12},{9,13},{10,... | collective-permute-start | bytes 59624 | tf_op jit(solution)/shard_map/ppermute | solution.py:431
  48.7 4.0 %collective-permute-start.9 = (bf16[36,276]{1,0:T(8,128)(2,1)S(1)}, bf16[36,276]{1,0:T(8,128)(2,1)S(1)}, u32[]{:S(2)}, u32[]{:S(2)}) collective-permute-start(bf16[36,276]{1,0:T(8,128)(2,1)S(1)} %add_convert_fusion.2), channel_id=1, source_target_pairs={{0,8},{1,9},{2,10},{3,11},{4,12},{5,13},{6,14},{7,15},{8,0},{9,1},... | collective-permute-start | bytes 59624 | tf_op jit(solution)/shard_map/ppermute | solution.py:431
  52.8 6.7 %collective-permute-start.10 = (bf16[36,276]{1,0:T(8,128)(2,1)S(1)}, bf16[36,276]{1,0:T(8,128)(2,1)S(1)}, u32[]{:S(2)}, u32[]{:S(2)}) collective-permute-start(bf16[36,276]{1,0:T(8,128)(2,1)S(1)} %add_convert_fusion.1), channel_id=1, source_target_pairs={{0,16},{1,17},{2,18},{3,19},{4,20},{5,21},{6,22},{7,23},{8,24},{9,... | collective-permute-start | bytes 59624 | tf_op jit(solution)/shard_map/ppermute | solution.py:431
  59.5 15.9 %collective-permute-start.11 = (bf16[36,276]{1,0:T(8,128)(2,1)S(1)}, bf16[36,276]{1,0:T(8,128)(2,1)S(1)}, u32[]{:S(2)}, u32[]{:S(2)}) collective-permute-start(bf16[36,276]{1,0:T(8,128)(2,1)S(1)} %add_convert_fusion), channel_id=1, source_target_pairs={{0,2},{1,3},{2,0},{3,1},{4,6},{5,7},{6,4},{7,5},{8,10},{9,11},{10,... | collective-permute-start | bytes 59624 | tf_op jit(solution)/shard_map/ppermute | solution.py:431
  66.3 12.5 %collective-permute-start.3 = (bf16[648,128]{1,0:T(8,128)(2,1)S(1)}, bf16[648,128]{1,0:T(8,128)(2,1)S(1)}, u32[]{:S(2)}, u32[]{:S(2)}) collective-permute-start(bf16[648,128]{1,0:T(8,128)(2,1)S(1)} %get-tuple-element.33), channel_id=1, source_target_pairs={{0,32},{1,33},{2,34},{3,35},{4,36},{5,37},{6,38},{7,39},{8,40},{9,... | collective-permute-start | bytes 497672 | tf_op jit(solution)/shard_map/ppermute | solution.py:41
  66.7 12.1 %collective-permute-start.4 = (bf16[216,128]{1,0:T(8,128)(2,1)S(1)}, bf16[216,128]{1,0:T(8,128)(2,1)S(1)}, u32[]{:S(2)}, u32[]{:S(2)}) collective-permute-start(bf16[216,128]{1,0:T(8,128)(2,1)S(1)} %get-tuple-element.34), channel_id=1, source_target_pairs={{0,33},{1,34},{2,35},{3,36},{4,37},{5,38},{6,39},{7,40},{8,41},{9,... | collective-permute-start | bytes 165896 | tf_op jit(solution)/shard_map/ppermute | solution.py:41
  74.0 4.9 %collective-permute-start.5 = (bf16[216,128]{1,0:T(8,128)(2,1)S(1)}, bf16[216,128]{1,0:T(8,128)(2,1)S(1)}, u32[]{:S(2)}, u32[]{:S(2)}) collective-permute-start(bf16[216,128]{1,0:T(8,128)(2,1)S(1)} %get-tuple-element.35), channel_id=1, source_target_pairs={{0,1},{1,2},{2,3},{3,4},{4,5},{5,6},{6,7},{7,8},{8,9},{9,10},{10,1... | collective-permute-start | bytes 165896 | tf_op jit(solution)/shard_map/ppermute | solution.py:41
  75.5 6.0 %collective-permute-start.12 = (bf16[2,36,276]{2,1,0:T(8,128)(2,1)S(1)}, bf16[2,36,276]{2,1,0:T(8,128)(2,1)S(1)}, u32[]{:S(2)}, u32[]{:S(2)}) collective-permute-start(bf16[2,36,276]{2,1,0:T(8,128)(2,1)S(1)} %pad_maximum_fusion.1), channel_id=1, source_target_pairs={{0,1},{1,0},{2,3},{3,2},{4,5},{5,4},{6,7},{7,6},{8,9},{9,8},{10,11... | collective-permute-start | bytes 119240 | tf_op jit(solution)/shard_map/ppermute | solution.py:431
  (21 other events, 16.8 us)

commit v4 on v3

--- a/solution.py
+++ b/solution.py
@@ -26,7 +26,9 @@
 
 epsilon = 1e-05
 keep_share = 0.8
+LOG2E = math.log2(math.e)
 gelu_coef = 0.044715
+VMEM_BYTES = 16 * 1024 * 1024
 bf16 = jnp.bfloat16
 f32 = jnp.float32
 
@@ -68,12 +70,10 @@
 def gelu_parts(values):
     factor = math.sqrt(2.0 / math.pi)
     square = values * values
-    tangent = jnp.tanh(factor * (values + gelu_coef * values * square))
-    half = 0.5 * (1.0 + tangent)
+    tangent = jnp.tanh(values * (factor + (gelu_coef * factor) * square))
+    half = 0.5 + 0.5 * tangent
     result = values * half
-    derivative = half + 0.5 * values * (1.0 - tangent * tangent) * (
-        factor + (3.0 * gelu_coef * factor) * square
-    )
+    derivative = half + result * (1.0 - tangent) * (factor + (3.0 * gelu_coef * factor) * square)
     return result, derivative
 
 
@@ -104,20 +104,26 @@
     )
 
 
-def pack_kernel(field_ref, cot_ref, lat_out, diag_out, lon_out, lat_buf, diag_buf, lon_buf):
+def pack_lat_kernel(field_ref, cot_ref, lat_out, lat_buf):
     half = WLAT // 2
     edge = WLON // 2
     inner = 2 * WLON - edge
     for t, source in enumerate((field_ref, cot_ref)):
         for z in range(4):
             for i in range(half):
-                k = z * half + i
-                top = source[z, i].astype(f32)
-                low = source[z, half + i].astype(f32)
-                put(lat_buf, t, k * inner, top[edge:])
-                put(diag_buf, t, k * edge, top[:edge])
-                put(lon_buf, t, k * edge, low[:edge])
+                put(lat_buf, t, (z * half + i) * inner, source[z, i].astype(f32)[edge:])
     lat_out[...] = lat_buf[...].astype(bf16)
+
+
+def pack_edge_kernel(field_ref, cot_ref, after_ref, diag_out, lon_out, diag_buf, lon_buf):
+    half = WLAT // 2
+    edge = WLON // 2
+    for t, source in enumerate((field_ref, cot_ref)):
+        for z in range(4):
+            for i in range(half):
+                row = (z * half + i) * edge
+                put(diag_buf, t, row, source[z, i].astype(f32)[:edge])
+                put(lon_buf, t, row, source[z, half + i].astype(f32)[:edge])
     diag_out[...] = diag_buf[...].astype(bf16)
     lon_out[...] = lon_buf[...].astype(bf16)
 
@@ -204,10 +210,10 @@
             v_t = mm_nt(wv_t, h1[rows]).astype(bf16)
             kt_out[w] = mm_nt(wk_t, h1[rows]).astype(bf16)
             q_wide = spread_heads(q_all[rows], head_mask)
-            scores = mm_nt(k_all[rows], q_wide) * root + bias_ref[n]
+            scores = mm_nt(k_all[rows], q_wide) * (root * LOG2E) + bias_ref[n]
             allowed = label_col_ref[:, w : w + 1] == label_row_ref[w]
             scores = jnp.where(allowed, scores, -1e30)
-            weights = jnp.exp(scores - jnp.max(scores, axis=0, keepdims=True))
+            weights = jnp.exp2(scores - jnp.max(scores, axis=0, keepdims=True))
             probs = weights * (1.0 / jnp.sum(weights, axis=0, keepdims=True))
             probs_low = probs.astype(bf16)
             probs_out[w] = probs_low
@@ -350,7 +356,7 @@
         start = PAIR * (WLON - 1 - o)
         wide[:, PAIR * o : PAIR * (o + 1), :] = total[:, :PAIR, start : start + POS]
     for n in range(2):
-        bias_out[n] = wide[n * HEADS : (n + 1) * HEADS].reshape(ROWS, POS).T
+        bias_out[n] = wide[n * HEADS : (n + 1) * HEADS].reshape(ROWS, POS).T * LOG2E
 
 
 def unpack_kernel(grad_ref, table_out, flat):
@@ -424,34 +430,21 @@
 
 def lon_sum(quarters):
     lons = lax.axis_size("lon")
-    me = lax.axis_index("lon")
-    bits = [(me >> k) & 1 for k in range(2)]
-
-    def swapped(block, distance):
-        return lax.ppermute(block, "lon", [(i, i ^ distance) for i in range(lons)])
-
-    def pick(value, bit):
-        return lax.dynamic_index_in_dim(value, bit, 0, keepdims=False)
-
-    def add(a, b):
-        return (a.astype(f32) + b.astype(f32)).astype(bf16)
-
-    def gathered(value, distance, bit):
-        other = swapped(value, distance)
-        first = jnp.where(bit == 0, value, other)
-        second = jnp.where(bit == 0, other, value)
-        return jnp.stack([first, second])
-
-    pairs = quarters.reshape((2, 2) + quarters.shape[1:])
-    value = add(pick(pairs, bits[0]), swapped(pick(pairs, 1 - bits[0]), 1))
-    value = add(pick(value, bits[1]), swapped(pick(value, 1 - bits[1]), 2))
-    distance = 4
-    while distance < lons:
-        value = add(value, swapped(value, distance))
-        distance *= 2
-    value = gathered(value, 2, bits[1])
-    value = gathered(value, 1, bits[0])
-    return value.reshape(quarters.shape)
+    near = [[4 * k + j for j in range(4)] for k in range(lons // 4)]
+    far = [[4 * k + j for k in range(lons // 4)] for j in range(4)]
+
+    def exchange(parts, groups):
+        return lax.all_to_all(parts, "lon", 0, 0, axis_index_groups=groups)
+
+    def total(parts):
+        return jnp.sum(parts.astype(f32), axis=0).astype(bf16)
+
+    def copies(part, count):
+        return jnp.broadcast_to(part, (count,) + part.shape)
+
+    quarter = total(exchange(quarters, near))
+    quarter = total(exchange(copies(quarter, lons // 4), far))
+    return exchange(copies(quarter, 4), near)
 
 
 def body(
@@ -476,14 +469,25 @@
     sizes = [3 * levels * half * size for size in (inner, edge, edge)]
     packed = tuple(jax.ShapeDtypeStruct((size, LANES), bf16) for size in sizes)
     buffers = [pltpu.VMEM((size, LANES), f32) for size in sizes]
-    lat_part, diag_part, lon_part = pl.pallas_call(
-        pack_kernel,
-        out_shape=packed,
+    params = pltpu.CompilerParams(vmem_limit_bytes=VMEM_BYTES)
+    lat_part = pl.pallas_call(
+        pack_lat_kernel,
+        out_shape=packed[0],
         in_specs=[vmem] * 2,
-        out_specs=(vmem,) * 3,
-        scratch_shapes=buffers,
-        name="pack",
+        out_specs=vmem,
+        scratch_shapes=buffers[:1],
+        compiler_params=params,
+        name="pack_lat",
     )(field_in, cotangent)
+    diag_part, lon_part = pl.pallas_call(
+        pack_edge_kernel,
+        out_shape=packed[1:],
+        in_specs=[vmem] * 2 + [pl.BlockSpec(memory_space=pl.ANY)],
+        out_specs=(vmem,) * 2,
+        scratch_shapes=buffers[1:],
+        compiler_params=params,
+        name="pack_edge",
+    )(field_in, cotangent, lat_part)
     lat_part = shifted(lat_part, -1, 0)
     diag_part = shifted(diag_part, -1, -1)
     lon_part = shifted(lon_part, 0, -1)
@@ -514,7 +518,7 @@
             pltpu.VMEM((PAIR * SLOTS, TAB), f32),
             pltpu.VMEM((2 * HEADS, POS, POS), f32),
         ],
-        compiler_params=pltpu.CompilerParams(vmem_limit_bytes=32 * 1024 * 1024),
+        compiler_params=params,
         name="expand",
     )(
         bias_table.reshape(2 * HEADS, 1, PAIR * TAB),
@@ -544,7 +548,7 @@
             pltpu.VMEM((2, positions, C), f32),
             pltpu.VMEM((HEADS, POS, POS), f32),
         ],
-        compiler_params=pltpu.CompilerParams(vmem_limit_bytes=48 * 1024 * 1024),
+        compiler_params=params,
         name="scores",
     )(
         field_in,
@@ -573,7 +577,7 @@
         in_specs=[vmem] * 12,
         out_specs=(vmem,) * 4,
         scratch_shapes=buffers,
-        compiler_params=pltpu.CompilerParams(vmem_limit_bytes=32 * 1024 * 1024),
+        compiler_params=params,
         cost_estimate=pl.CostEstimate(
             flops=1_000_000_000, bytes_accessed=8_000_000, transcendentals=0
         ),
@@ -588,6 +592,7 @@
         in_specs=[vmem],
         out_specs=vmem,
         scratch_shapes=[pltpu.VMEM((2 * HEADS, PAIR * TAB), f32)],
+        compiler_params=params,
         name="unpack",
     )(lon_sum(fold))
     grads = grads.reshape(2, 1, HEADS, PAIR * TAB)
@@ -596,6 +601,7 @@
         out_shape=(jax.ShapeDtypeStruct(field_in.shape, bf16),) * 2,
         in_specs=[vmem] * 4,
         out_specs=(vmem,) * 2,
+        compiler_params=params,
         name="finish",
     )(own, lat_back, diag_back, lon_back)
     return (result, grad_field, grads)

time: 84.5 us -> 78 us (0.923); the launches traced: 84 us -> 76.5 us
  waiting for transfers between devices: 20.5 us -> 1.53 us
  blocking collectives: 0 us -> 7.9 us
  local copies, waits for them, and re-layouts: 14 us -> 21.1 us
  Pallas kernels: 22.2 us -> 17.1 us
  starting transfers between devices: 24.4 us -> 26.9 us
    ppermute x7 -> x0, waiting for transfers between devices: 17.2 us -> none  [swapped(): return lax.ppermute(block, 'lon', [(i, i ^ distance) for i in range(lons)])]
    all_to_all x0 -> x2, starting transfers between devices: none -> 9.77 us  [exchange(): return lax.all_to_all(parts, 'lon', 0, 0, axis_index_groups=groups)]
    all_to_all x0 -> x1, blocking collectives: none -> 7.9 us  [exchange(): return lax.all_to_all(parts, 'lon', 0, 0, axis_index_groups=groups)]
    ppermute x6, starting transfers between devices: 22.4 us -> 17.1 us  [shifted(): return lax.ppermute(block, ('lat', 'lon'), route)]
    unnamed x65 -> x79, local copies, waits for them, and re-layouts: 13.4 us -> 18.5 us
    ppermute x7 -> x0, starting transfers between devices: 2.06 us -> none  [swapped(): return lax.ppermute(block, 'lon', [(i, i ^ distance) for i in range(lons)])]
    ppermute x6, waiting for transfers between devices: 3.27 us -> 1.52 us  [shifted(): return lax.ppermute(block, ('lat', 'lon'), route)]
    pallas_call x1 -> x2, Pallas kernels: 1.91 us -> 0.2 us  [the longest x1 0.1 us: body(): pl.pallas_call(pack_lat_kernel, out_shape=packed[0], in_specs=[vmem] * 2,...]
  transfers between devices with their start and end apart: 13 -> 8, of which waited for: 6 -> 1; matrix products, arithmetic and copies ran while one was open for 1% -> 4% of each run, Pallas kernels for 8% -> 8%
where the time goes in v4:
time: 78 us; the launch traced here: 76.5 us
  starting transfers between devices  26.9 us (34%)
  local copies, waits for them, and re-layouts  21.1 us (27%)
  Pallas kernels  17.1 us (22%)
  blocking collectives  7.9 us (10%)
  waiting for transfers between devices  1.53 us (2%)
  other arithmetic  1.19 us (2%)
  between operations  0.91 us (1%)
    unnamed x79, local copies, waits for them, and re-layouts  18.5 us
    ppermute x6, starting transfers between devices, shifted(): return lax.ppermute(block, ('lat', 'lon'), route)  17.1 us
    pallas_call x1, Pallas kernels, body(): pl.pallas_call(scores_kernel, out_shape=(jax.ShapeDtypeStruct((4, QUARTER...  10.2 us
    all_to_all x2, starting transfers between devices, exchange(): return lax.all_to_all(parts, 'lon', 0, 0, axis_index_groups=groups)  9.77 us
    all_to_all x1, blocking collectives, exchange(): return lax.all_to_all(parts, 'lon', 0, 0, axis_index_groups=groups)  7.9 us
    pallas_call x1, Pallas kernels, body(): pl.pallas_call(inputs_kernel, out_shape=(jax.ShapeDtypeStruct((2, levels,...  2.9 us
    pallas_call x1, Pallas kernels, body(): pl.pallas_call(expand_kernel, out_shape=jax.ShapeDtypeStruct((2, POS, ROW...  2.05 us
  transfers between devices with their start and end apart: 8, of which 1 were waited for; matrix products, arithmetic and copies ran while one was open for 4% of the time, Pallas kernels for 8%

profile of v4, /device:TPU:1, one launch (start us, length us, event | category | flops | bytes accessed | tf_op | source)
XLA Modules:
  0.0 76.5 jit_solution(17368754561500260586)
XLA Ops:
  0.6 1.0 %copy-done = bf16[4,6,24,192]{3,2,1,0:T(8,128)(2,1)S(1)} copy-done((bf16[4,6,24,192]{3,2,1,0:T(8,128)(2,1)S(1)}, bf16[4,6,24,192]{3,2,1,0:T(8,128)(2,1)}, u32[]{:S(2)}) %copy-start) | copy-done | bytes 221208
  1.6 1.0 %copy-done.2 = bf16[4,6,24,192]{3,2,1,0:T(8,128)(2,1)S(1)} copy-done((bf16[4,6,24,192]{3,2,1,0:T(8,128)(2,1)S(1)}, bf16[4,6,24,192]{3,2,1,0:T(8,128)(2,1)}, u32[]{:S(2)}) %copy-start.2) | copy-done | bytes 221208
  2.7 4.4 %collective-permute-start.1 = (bf16[648,128]{1,0:T(8,128)(2,1)S(1)}, bf16[648,128]{1,0:T(8,128)(2,1)S(1)}, u32[]{:S(2)}, u32[]{:S(2)}) collective-permute-start(bf16[648,128]{1,0:T(8,128)(2,1)S(1)} %pack_lat.1.after_ref), channel_id=1, source_target_pairs={{0,224},{1,225},{2,226},{3,227},{4,228},{5,229},{6,230},{7,231},{8... | collective-permute-start | bytes 497672 | tf_op jit(solution)/shard_map/ppermute | solution.py:43
  7.2 1.0 %collective-permute-start = (bf16[216,128]{1,0:T(8,128)(2,1)S(1)}, bf16[216,128]{1,0:T(8,128)(2,1)S(1)}, u32[]{:S(2)}, u32[]{:S(2)}) collective-permute-start(bf16[216,128]{1,0:T(8,128)(2,1)S(1)} %get-tuple-element.20), channel_id=1, source_target_pairs={{0,31},{1,0},{2,1},{3,2},{4,3},{5,4},{6,5},{7,6},{8,7},{9,8},{10,9... | collective-permute-start | bytes 165896 | tf_op jit(solution)/shard_map/ppermute | solution.py:43
  8.2 7.1 %collective-permute-start.2 = (bf16[216,128]{1,0:T(8,128)(2,1)S(1)}, bf16[216,128]{1,0:T(8,128)(2,1)S(1)}, u32[]{:S(2)}, u32[]{:S(2)}) collective-permute-start(bf16[216,128]{1,0:T(8,128)(2,1)S(1)} %get-tuple-element.21), channel_id=1, source_target_pairs={{0,255},{1,224},{2,225},{3,226},{4,227},{5,228},{6,229},{7,230},{8... | collective-permute-start | bytes 165896 | tf_op jit(solution)/shard_map/ppermute | solution.py:43
  17.8 2.0 %expand.1.bias_ref = f32[2,144,864]{2,1,0:T(8,128)S(1)} custom-call(f32[12,1,3312]{2,1,0:T(1,128)S(1)} %bitcast.14, bf16[276,276]{1,0:T(8,128)(2,1)S(1)} %copy-done.4, bf16[192,192]{1,0:T(8,128)(2,1)S(1)} %copy-done.23), custom_call_target="tpu_custom_call" | custom-call | tf_op jit(solution)/shard_map/expand/pallas_call | solution.py:511
  22.5 0.9 %copy-done.20 = bf16[648,128]{1,0:T(8,128)(2,1)S(1)} copy-done((bf16[648,128]{1,0:T(8,128)(2,1)S(1)}, bf16[648,128]{1,0:T(8,128)(2,1)}, u32[]{:S(2)}) %copy-start.20) | copy-done | bytes 165912
  23.4 0.8 %copy-done.25 = bf16[216,128]{1,0:T(8,128)(2,1)S(1)} copy-done((bf16[216,128]{1,0:T(8,128)(2,1)S(1)}, bf16[216,128]{1,0:T(8,128)(2,1)}, u32[]{:S(2)}) %copy-start.25) | copy-done | bytes 55320
  25.8 10.2 %scores.1 = (bf16[4,36,276]{2,1,0:T(8,128)(2,1)S(1)}, bf16[576,192]{1,0:T(8,128)(2,1)S(1)}, bf16[576,192]{1,0:T(8,128)(2,1)S(1)}, bf16[4,192,144]{2,1,0:T(8,128)...) custom-call(bf16[4,6,24,192]{3,2,1,0:T(8,128)(2,1)S(1)} %copy-done.1, ...), custom_call_target="tpu_custom_call" | custom-call | tf_op jit(solution)/shard_map/scores/pallas_call | solution.py:532
  38.9 7.9 %all_to_all.15 = bf16[4,36,276]{2,1,0:T(8,128)(2,1)S(1)} all-to-all(bf16[4,36,276]{2,1,0:T(8,128)(2,1)S(1)} %get-tuple-element.36), channel_id=1, replica_groups={{0,1,2,3},{4,5,6,7},{8,9,10,11},{12,13,14,15},{16,17,18,19},{20,21,22,2..., dimensions={0} | all-to-all | bytes 158976 | tf_op jit(solution)/shard_map/all_to_all | solution.py:437
  47.5 4.3 %all-to-all-start.1 = ((bf16[8,36,276]{2,1,0:T(8,128)(2,1)}), bf16[8,36,276]{2,1,0:T(8,128)(2,1)}, u32[]{:S(2)}, u32[]{:S(2)}) async-start(bf16[8,36,276]{2,1,0:T(8,128)(2,1)} %broadcast_in_dim.8), calls=%async_computation.1 | async-start | bytes 491520 | tf_op jit(solution)/shard_map/all_to_all | solution.py:437
  52.5 1.0 %copy-done.6 = bf16[4,192,144]{2,1,0:T(8,128)(2,1)S(1)} copy-done((bf16[4,192,144]{2,1,0:T(8,128)(2,1)S(1)}, bf16[4,192,144]{2,1,0:T(8,128)(2,1)}, u32[]{:S(2)}) %copy-start.6) | copy-done | bytes 221208
  53.5 1.0 %copy-done.10 = bf16[576,192]{1,0:T(8,128)(2,1)S(1)} copy-done((bf16[576,192]{1,0:T(8,128)(2,1)S(1)}, bf16[576,192]{1,0:T(8,128)(2,1)}, u32[]{:S(2)}) %copy-start.10) | copy-done | bytes 221208
  54.4 1.0 %copy-done.12 = bf16[576,192]{1,0:T(8,128)(2,1)S(1)} copy-done((bf16[576,192]{1,0:T(8,128)(2,1)S(1)}, bf16[576,192]{1,0:T(8,128)(2,1)}, u32[]{:S(2)}) %copy-start.12) | copy-done | bytes 221208
  55.4 1.0 %copy-done.14 = bf16[576,192]{1,0:T(8,128)(2,1)S(1)} copy-done((bf16[576,192]{1,0:T(8,128)(2,1)S(1)}, bf16[576,192]{1,0:T(8,128)(2,1)}, u32[]{:S(2)}) %copy-start.14) | copy-done | bytes 221208
  56.3 0.9 %copy-done.18 = bf16[288,288]{1,0:T(8,128)(2,1)S(1)} copy-done((bf16[288,288]{1,0:T(8,128)(2,1)S(1)}, bf16[288,288]{1,0:T(8,128)(2,1)}, u32[]{:S(2)}) %copy-start.18) | copy-done | bytes 165912
  57.3 2.9 %inputs.1 = (bf16[2,4,3,18,192]{4,3,2,1,0:T(8,128)(2,1)S(1)}, bf16[648,128]{1,0:T(8,128)(2,1)S(1)}, bf16[216,128]{1,0:T(8,128)(2,1)S(1)}, bf16[216,128]{1,0:T(8,128)(2,1)S(1)}) custom-call(bf16[576,192]{1,0:T(8,128)(2,1)S(1)} %get-tuple-element.22.x_ref, bf16[576,192]{1,0:T(8,128)(2,1)S(1)} %copy-done.10, bf16[4,192,144]{2,1,0:T(8,128)(2,1)S(1)} %copy-done.6, ...), custom_call_target="tpu_custom_call" | custom-call | flops 1000000000 | bytes 8000000 | tf_op jit(solution)/shard_map/inputs/pallas_call | solution.py:574
  61.9 1.0 %reduce_sum.25 = bf16[36,276]{1,0:T(8,128)(2,1)S(1)} reduce(bf16[8,36,276]{2,1,0:T(8,128)(2,1)} %all-to-all-done.1, bf16[]{:T(256)} %constant.36.clone.1), dimensions={0}, to_apply=%region_1.0 | reduce | flops 69552 | bytes 178850 | tf_op jit(solution)/shard_map/reduce_sum | solution.py:440
  63.6 5.5 %all-to-all-start.2 = ((bf16[4,36,276]{2,1,0:T(8,128)(2,1)}), bf16[4,36,276]{2,1,0:T(8,128)(2,1)S(1)}, u32[]{:S(2)}, u32[]{:S(2)}) async-start(bf16[4,36,276]{2,1,0:T(8,128)(2,1)} %broadcast_in_dim.9), calls=%async_computation.2 | async-start | bytes 245760 | tf_op jit(solution)/shard_map/all_to_all | solution.py:437
  69.1 3.0 %collective-permute-start.4 = (bf16[216,128]{1,0:T(8,128)(2,1)S(1)}, bf16[216,128]{1,0:T(8,128)(2,1)S(1)}, u32[]{:S(2)}, u32[]{:S(2)}) collective-permute-start(bf16[216,128]{1,0:T(8,128)(2,1)S(1)} %copy-done.35), channel_id=1, source_target_pairs={{0,33},{1,34},{2,35},{3,36},{4,37},{5,38},{6,39},{7,40},{8,41},{9,... | collective-permute-start | bytes 165896 | tf_op jit(solution)/shard_map/ppermute | solution.py:43
  72.1 1.2 %collective-permute-start.5 = (bf16[216,128]{1,0:T(8,128)(2,1)S(1)}, bf16[216,128]{1,0:T(8,128)(2,1)S(1)}, u32[]{:S(2)}, u32[]{:S(2)}) collective-permute-start(bf16[216,128]{1,0:T(8,128)(2,1)S(1)} %get-tuple-element.33), channel_id=1, source_target_pairs={{0,1},{1,2},{2,3},{3,4},{4,5},{5,6},{6,7},{7,8},{8,9},{9,10},{10,1... | collective-permute-start | bytes 165896 | tf_op jit(solution)/shard_map/ppermute | solution.py:43
  73.3 1.5 %collective-permute-done.4.diag_ref = bf16[216,128]{1,0:T(8,128)(2,1)S(1)} collective-permute-done((bf16[216,128]{1,0:T(8,128)(2,1)S(1)}, bf16[216,128]{1,0:T(8,128)(2,1)S(1)}, u32[]{:S(2)}, u32[]{:S(2)}) %collective-permute-start.4) | collective-permute-done | bytes 55328 | tf_op jit(solution)/shard_map/ppermute | solution.py:43
  74.8 0.9 %finish.1 = (bf16[4,6,24,192]{3,2,1,0:T(8,128)(2,1)}, bf16[4,6,24,192]{3,2,1,0:T(8,128)(2,1)}) custom-call(bf16[2,4,3,18,192]{4,3,2,1,0:T(8,128)(2,1)S(1)} %copy-done.16, bf16[648,128]{1,0:T(8,128)(2,1)S(1)} %collective-permute-done.3.lat_ref, bf16[216,128]{1,0:T(8,128)(2,1)S(1)} %collective-permute-done.4.diag_ref, ...), custom_call_target="tpu_custom_call" | custom-call | tf_op jit(solution)/shard_map/finish/pallas_call | solution.py:599
  75.7 0.8 %unpack.1 = f32[12,1,3312]{2,1,0:T(1,128)} custom-call(bf16[4,36,276]{2,1,0:T(8,128)(2,1)S(1)} %all-to-all-done.2.grad_ref), custom_call_target="tpu_custom_call" | custom-call | tf_op jit(solution)/shard_map/unpack/pallas_call | solution.py:589
  (95 shorter events, 13.4 us)
Async XLA Ops:
  0.6 1.0 %copy-start = (bf16[4,6,24,192]{3,2,1,0:T(8,128)(2,1)S(1)}, bf16[4,6,24,192]{3,2,1,0:T(8,128)(2,1)}, u32[]{:S(2)}) copy-start(bf16[4,6,24,192]{3,2,1,0:T(8,128)(2,1)} %field_ref.5) | copy-start | bytes 663556
  2.7 18.5 %collective-permute-start.1 = (bf16[648,128]{1,0:T(8,128)(2,1)S(1)}, bf16[648,128]{1,0:T(8,128)(2,1)S(1)}, u32[]{:S(2)}, u32[]{:S(2)}) collective-permute-start(bf16[648,128]{1,0:T(8,128)(2,1)S(1)} %pack_lat.1.after_ref), channel_id=1, source_target_pairs={{0,224},{1,225},{2,226},{3,227},{4,228},{5,229},{6,230},{7,231},{8... | collective-permute-start | bytes 497672 | tf_op jit(solution)/shard_map/ppermute | solution.py:43
  7.1 8.3 %copy-start.37 = (s32[4,6,24]{2,0,1:T(4,128)S(1)}, s32[4,6,24]{2,0,1:T(4,128)}, u32[]{:S(2)}) copy-start(s32[4,6,24]{2,0,1:T(4,128)} %param.26) | copy-start | bytes 6916
  7.1 8.4 %copy-start.38 = (s32[2,1,2]{2,1,0:T(1,128)S(1)}, s32[2,1,2]{2,1,0:T(1,128)}, u32[]{:S(2)}) copy-start(s32[2,1,2]{2,1,0:T(1,128)} %param.27) | copy-start | bytes 52
  7.2 9.5 %copy-start.36 = (bf16[192,576]{1,0:T(8,128)(2,1)S(1)}, bf16[192,576]{1,0:T(8,128)(2,1)}, u32[]{:S(2)}) copy-start(bf16[192,576]{1,0:T(8,128)(2,1)} %param.20) | copy-start | bytes 663556
  7.2 12.7 %collective-permute-start = (bf16[216,128]{1,0:T(8,128)(2,1)S(1)}, bf16[216,128]{1,0:T(8,128)(2,1)S(1)}, u32[]{:S(2)}, u32[]{:S(2)}) collective-permute-start(bf16[216,128]{1,0:T(8,128)(2,1)S(1)} %get-tuple-element.20), channel_id=1, source_target_pairs={{0,31},{1,0},{2,1},{3,2},{4,3},{5,4},{6,5},{7,6},{8,7},{9,8},{10,9... | collective-permute-start | bytes 165896 | tf_op jit(solution)/shard_map/ppermute | solution.py:43
  8.2 12.3 %collective-permute-start.2 = (bf16[216,128]{1,0:T(8,128)(2,1)S(1)}, bf16[216,128]{1,0:T(8,128)(2,1)S(1)}, u32[]{:S(2)}, u32[]{:S(2)}) collective-permute-start(bf16[216,128]{1,0:T(8,128)(2,1)S(1)} %get-tuple-element.21), channel_id=1, source_target_pairs={{0,255},{1,224},{2,225},{3,226},{4,227},{5,228},{6,229},{7,230},{8... | collective-permute-start | bytes 165896 | tf_op jit(solution)/shard_map/ppermute | solution.py:43
  16.7 1.0 %copy-start.21 = (f32[2,1,6,3312]{3,1,2,0:T(1,128)S(1)}, f32[2,1,6,3312]{3,1,2,0:T(1,128)}, u32[]{:S(2)}) copy-start(f32[2,1,6,3312]{3,1,2,0:T(1,128)} %param.25) | copy-start | bytes 476932
  16.7 1.1 %copy-start.23 = (bf16[192,192]{1,0:T(8,128)(2,1)S(1)}, bf16[192,192]{1,0:T(8,128)(2,1)}, u32[]{:S(2)}) copy-start(bf16[192,192]{1,0:T(8,128)(2,1)} %constant.38.clone.row_perm_ref) | copy-start | bytes 221188
  17.8 4.0 %copy-start.1 = (bf16[4,6,24,192]{3,2,1,0:T(8,128)(2,1)S(1)}, bf16[4,6,24,192]{3,2,1,0:T(8,128)(2,1)}, u32[]{:S(2)}) copy-start(bf16[4,6,24,192]{3,2,1,0:T(8,128)(2,1)} %field_ref.5) | copy-start | bytes 663556
  17.8 4.0 %copy-start.3 = (bf16[4,6,24,192]{3,2,1,0:T(8,128)(2,1)S(1)}, bf16[4,6,24,192]{3,2,1,0:T(8,128)(2,1)}, u32[]{:S(2)}) copy-start(bf16[4,6,24,192]{3,2,1,0:T(8,128)(2,1)} %cot_ref.5) | copy-start | bytes 663556
  17.8 4.1 %copy-start.7 = (bf16[192,768]{1,0:T(8,128)(2,1)S(1)}, bf16[192,768]{1,0:T(8,128)(2,1)}, u32[]{:S(2)}) copy-start(bf16[192,768]{1,0:T(8,128)(2,1)} %wup_ref.1) | copy-start | bytes 884740
  17.8 4.1 %copy-start.8 = (bf16[768,192]{0,1:T(8,128)(2,1)S(1)}, bf16[768,192]{0,1:T(8,128)(2,1)}, u32[]{:S(2)}) copy-start(bf16[768,192]{0,1:T(8,128)(2,1)} %param.24) | copy-start | bytes 884740
  17.8 4.1 %copy-start.17 = (bf16[288,288]{1,0:T(8,128)(2,1)S(1)}, bf16[288,288]{1,0:T(8,128)(2,1)}, u32[]{:S(2)}) copy-start(bf16[288,288]{1,0:T(8,128)(2,1)} %constant.40.clone.perm_ref) | copy-start | bytes 497668
  17.8 4.1 %copy-start.22 = (bf16[192,192]{1,0:T(8,128)(2,1)S(1)}, bf16[192,192]{1,0:T(8,128)(2,1)}, u32[]{:S(2)}) copy-start(bf16[192,192]{1,0:T(8,128)(2,1)} %wproj_ref.1) | copy-start | bytes 221188
  17.8 4.1 %copy-start.32 = (f32[192]{0:T(256)S(1)}, f32[192]{0:T(256)}, u32[]{:S(2)}) copy-start(f32[192]{0:T(256)} %param.22) | copy-start | bytes 2308
  47.5 14.4 %all-to-all-start.1 = ((bf16[8,36,276]{2,1,0:T(8,128)(2,1)}), bf16[8,36,276]{2,1,0:T(8,128)(2,1)}, u32[]{:S(2)}, u32[]{:S(2)}) async-start(bf16[8,36,276]{2,1,0:T(8,128)(2,1)} %broadcast_in_dim.8), calls=%async_computation.1 | async-start | bytes 491520 | tf_op jit(solution)/shard_map/all_to_all | solution.py:437
  52.5 1.0 %copy-start.6 = (bf16[4,192,144]{2,1,0:T(8,128)(2,1)S(1)}, bf16[4,192,144]{2,1,0:T(8,128)(2,1)}, u32[]{:S(2)}) copy-start(bf16[4,192,144]{2,1,0:T(8,128)(2,1)} %copy-done.5) | copy-start | bytes 663556
  61.5 13.3 %copy-start.16 = (bf16[2,4,3,18,192]{4,3,2,1,0:T(8,128)(2,1)S(1)}, bf16[2,4,3,18,192]{4,3,2,1,0:T(8,128)(2,1)}, u32[]{:S(2)}) copy-start(bf16[2,4,3,18,192]{4,3,2,1,0:T(8,128)(2,1)} %copy-done.15) | copy-start | bytes 497668
  61.5 13.3 %collective-permute-start.3 = (bf16[648,128]{1,0:T(8,128)(2,1)S(1)}, bf16[648,128]{1,0:T(8,128)(2,1)S(1)}, u32[]{:S(2)}, u32[]{:S(2)}) collective-permute-start(bf16[648,128]{1,0:T(8,128)(2,1)S(1)} %get-tuple-element.31), channel_id=1, source_target_pairs={{0,32},{1,33},{2,34},{3,35},{4,36},{5,37},{6,38},{7,39},{8,40},{9,... | collective-permute-start | bytes 497672 | tf_op jit(solution)/shard_map/ppermute | solution.py:43
  63.6 5.5 %copy-start.35 = (bf16[216,128]{1,0:T(8,128)(2,1)S(1)}, bf16[216,128]{1,0:T(8,128)(2,1)}, u32[]{:S(2)}) copy-start(bf16[216,128]{1,0:T(8,128)(2,1)} %copy-done.34) | copy-start | bytes 165892
  63.6 12.1 %all-to-all-start.2 = ((bf16[4,36,276]{2,1,0:T(8,128)(2,1)}), bf16[4,36,276]{2,1,0:T(8,128)(2,1)S(1)}, u32[]{:S(2)}, u32[]{:S(2)}) async-start(bf16[4,36,276]{2,1,0:T(8,128)(2,1)} %broadcast_in_dim.9), calls=%async_computation.2 | async-start | bytes 245760 | tf_op jit(solution)/shard_map/all_to_all | solution.py:437
  69.1 5.7 %collective-permute-start.4 = (bf16[216,128]{1,0:T(8,128)(2,1)S(1)}, bf16[216,128]{1,0:T(8,128)(2,1)S(1)}, u32[]{:S(2)}, u32[]{:S(2)}) collective-permute-start(bf16[216,128]{1,0:T(8,128)(2,1)S(1)} %copy-done.35), channel_id=1, source_target_pairs={{0,33},{1,34},{2,35},{3,36},{4,37},{5,38},{6,39},{7,40},{8,41},{9,... | collective-permute-start | bytes 165896 | tf_op jit(solution)/shard_map/ppermute | solution.py:43
  72.1 2.7 %collective-permute-start.5 = (bf16[216,128]{1,0:T(8,128)(2,1)S(1)}, bf16[216,128]{1,0:T(8,128)(2,1)S(1)}, u32[]{:S(2)}, u32[]{:S(2)}) collective-permute-start(bf16[216,128]{1,0:T(8,128)(2,1)S(1)} %get-tuple-element.33), channel_id=1, source_target_pairs={{0,1},{1,2},{2,3},{3,4},{4,5},{5,6},{6,7},{7,8},{8,9},{9,10},{10,1... | collective-permute-start | bytes 165896 | tf_op jit(solution)/shard_map/ppermute | solution.py:43
  (23 other events, 17.9 us)

commit v5 on v4

--- a/solution.py
+++ b/solution.py
@@ -104,14 +104,22 @@
     )
 
 
-def pack_lat_kernel(field_ref, cot_ref, lat_out, lat_buf):
+def pack_lat_kernel(field_ref, cot_ref, lat_out, lat_buf, rows, arrived):
     half = WLAT // 2
     edge = WLON // 2
     inner = 2 * WLON - edge
-    for t, source in enumerate((field_ref, cot_ref)):
+    sources = (field_ref, cot_ref)
+    copies = [
+        pltpu.make_async_copy(sources[t].at[:, pl.ds(0, half)], rows.at[t], arrived.at[t])
+        for t in range(2)
+    ]
+    for copy in copies:
+        copy.start()
+    for t in range(2):
+        copies[t].wait()
         for z in range(4):
             for i in range(half):
-                put(lat_buf, t, (z * half + i) * inner, source[z, i].astype(f32)[edge:])
+                put(lat_buf, t, (z * half + i) * inner, rows[t, z, i].astype(f32)[edge:])
     lat_out[...] = lat_buf[...].astype(bf16)
 
 
@@ -143,18 +151,15 @@
     bias_ref,
     label_row_ref,
     label_col_ref,
-    factor_ref,
+    keep_ref,
     perm_ref,
     head_mask_ref,
     table_perm_ref,
     chunk_perm_ref,
     fold_out,
     x_out,
-    q_out,
-    kt_out,
     probs_out,
     grad_low_out,
-    grad_att_out,
     grad_sum_out,
     result_out,
     frame,
@@ -201,24 +206,22 @@
         q_all = mm_nt(h1, wq_t).astype(bf16)
         k_all = mm_nt(h1, wk_t).astype(bf16)
         v_all = mm_nt(h1, wv_t).astype(bf16)
-        q_out[both, :] = q_all
         saved = []
         branches = []
         for c in range(2):
             w = 2 * n + c
             rows = slice(c * POS, (c + 1) * POS)
             v_t = mm_nt(wv_t, h1[rows]).astype(bf16)
-            kt_out[w] = mm_nt(wk_t, h1[rows]).astype(bf16)
             q_wide = spread_heads(q_all[rows], head_mask)
             scores = mm_nt(k_all[rows], q_wide) * (root * LOG2E) + bias_ref[n]
-            allowed = label_col_ref[:, w : w + 1] == label_row_ref[w]
+            allowed = label_col_ref[:, w : w + 1] == label_row_ref[w : w + 1, :]
             scores = jnp.where(allowed, scores, -1e30)
             weights = jnp.exp2(scores - jnp.max(scores, axis=0, keepdims=True))
             probs = weights * (1.0 / jnp.sum(weights, axis=0, keepdims=True))
             probs_low = probs.astype(bf16)
             probs_out[w] = probs_low
             attended = head_blocks(mm(v_t, probs_low)).T.astype(bf16)
-            factor = factor_ref[w]
+            factor = keep_ref[n, 0, c].astype(f32) * (1.0 / keep_share)
             branches.append((mm(attended, wproj_ref[...]) * factor).astype(bf16).astype(f32))
             saved.append(probs)
         y_sum = x + jnp.concatenate(branches, axis=0)
@@ -234,9 +237,9 @@
             w = 2 * n + c
             rows = slice(c * POS, (c + 1) * POS)
             probs = saved[c]
-            grad_branch = (grad_low_in[rows] * factor_ref[w]).astype(bf16)
+            factor = keep_ref[n, 0, c].astype(f32) * (1.0 / keep_share)
+            grad_branch = (grad_low_in[rows] * factor).astype(bf16)
             grad_att = mm_nt(grad_branch, wproj_ref[...]).astype(bf16)
-            grad_att_out[w * POS : (w + 1) * POS, :] = grad_att
             grad_probs = mm_nt(v_all[rows], spread_heads(grad_att, head_mask))
             inner_sum = jnp.sum(probs * grad_probs, axis=0, keepdims=True)
             grad_scores = probs * (grad_probs - inner_sum)
@@ -264,15 +267,14 @@
 
 def inputs_kernel(
     x_ref,
-    q_ref,
-    kt_ref,
     probs_ref,
     grad_low_ref,
-    grad_att_ref,
     grad_sum_ref,
     result_ref,
     gain1_ref,
     wqkv_t_ref,
+    wproj_ref,
+    keep_ref,
     perm_t_ref,
     head_mask_ref,
     own_out,
@@ -296,20 +298,27 @@
     perm_t = perm_t_ref[...]
     for n in range(2):
         both = slice(n * 2 * POS, (n + 1) * 2 * POS)
-        _, normed1, inverse1 = norm_parts(x_ref[both, :].astype(f32), gain1)
+        scaled1, normed1, inverse1 = norm_parts(x_ref[both, :].astype(f32), gain1)
+        h1 = scaled1.astype(bf16)
+        q_all = mm_nt(h1, wq_t).astype(bf16)
+        grad_sum = grad_sum_ref[both, :]
+        grad_low_in = grad_sum.astype(bf16).astype(f32)
         grad_h1 = []
         for c in range(2):
             w = 2 * n + c
-            rows = slice(w * POS, (w + 1) * POS)
+            rows = slice(c * POS, (c + 1) * POS)
             grad_low = grad_low_ref[w]
-            q_wide = spread_heads(q_ref[rows, :], head_mask)
-            g_wide = spread_heads(grad_att_ref[rows, :], head_mask)
-            grad_q = (head_blocks(mm(kt_ref[w], grad_low)).T * root).astype(bf16)
+            k_t = mm_nt(wk_t, h1[rows]).astype(bf16)
+            factor = keep_ref[n, 0, c].astype(f32) * (1.0 / keep_share)
+            grad_branch = (grad_low_in[rows] * factor).astype(bf16)
+            grad_att = mm_nt(grad_branch, wproj_ref[...]).astype(bf16)
+            q_wide = spread_heads(q_all[rows], head_mask)
+            g_wide = spread_heads(grad_att, head_mask)
+            grad_q = (head_blocks(mm(k_t, grad_low)).T * root).astype(bf16)
             grad_k = (mm(grad_low, q_wide) * root).astype(bf16)
             grad_v = mm(probs_ref[w], g_wide).astype(bf16)
             grad_h1.append(mm(grad_q, wq_t) + mm(grad_k, wk_t) + mm(grad_v, wv_t))
         grad_h1 = jnp.concatenate(grad_h1, axis=0).astype(bf16).astype(f32)
-        grad_sum = grad_sum_ref[both, :]
         grad_field = (grad_sum + norm_back(grad_h1, gain1, normed1, inverse1)).astype(bf16)
         for t, value in enumerate((result_ref[both, :], grad_field)):
             natural = mm(perm_t, value)
@@ -330,7 +339,45 @@
     lon_out[...] = lon_buf[...].astype(bf16)
 
 
-def expand_kernel(table_ref, table_perm_ref, row_perm_ref, bias_out, flat, rows, wide):
+def prepare_kernel(
+    table_ref,
+    table_perm_ref,
+    row_perm_ref,
+    region_ref,
+    wqkv_ref,
+    bias_out,
+    label_row_out,
+    label_col_out,
+    wqkv_t_out,
+    flat,
+    rows,
+    wide,
+    marks,
+):
+    wqkv_t_out[...] = wqkv_ref[...].astype(f32).T.astype(bf16)
+    last = lax.axis_index("lat") == lax.axis_size("lat") - 1
+    level = lax.broadcasted_iota(jnp.int32, (4, 2 * WLON), 0)
+    for i in range(WLAT):
+        wrapped = 2 * (level >= 4 - WZ // 2).astype(jnp.int32)
+        if i >= WLAT // 2:
+            wrapped = wrapped + last.astype(jnp.int32)
+        marks[4 * i : 4 * (i + 1), :] = (4 * region_ref[i] + wrapped).astype(f32)
+    place = lax.broadcasted_iota(jnp.int32, (POS, 4 * WLAT), 0)
+    lane = lax.broadcasted_iota(jnp.int32, (POS, 4 * WLAT), 1)
+    lon = (place * 43691) >> 19
+    pair = place - PAIR * lon
+    upper = (pair >= WLAT).astype(jnp.int32)
+    source = 4 * (pair - WLAT * upper) + upper
+    columns = []
+    for n in range(2):
+        chosen = mm((lane == source + WZ * n).astype(f32).astype(bf16), marks[...].astype(bf16))
+        for c in range(2):
+            own = jnp.where(lane == lon + WLON * c, chosen, 0.0)
+            columns.append(jnp.sum(own, axis=1, keepdims=True))
+    label_col_out[...] = jnp.concatenate(columns, axis=1)
+    spread = jnp.concatenate([jnp.broadcast_to(v, (POS, LANES)) for v in columns], axis=1).T
+    labels = jnp.concatenate([spread[k * LANES : k * LANES + 1] for k in range(4)], axis=0)
+    label_row_out[...] = jnp.concatenate([labels] * HEADS, axis=1)
     part = PAIR // WZ * SPREAD
     for k in range(2 * HEADS):
         flat[k : k + 1, :] = table_ref[k]
@@ -376,6 +423,15 @@
         table_out[k] = flat[k : k + 1, :]
 
 
+def add_kernel(parts_ref, copies_out):
+    total = parts_ref[0].astype(f32)
+    for k in range(1, parts_ref.shape[0]):
+        total = total + parts_ref[k].astype(f32)
+    total = total.astype(bf16)
+    for k in range(copies_out.shape[0]):
+        copies_out[k] = total
+
+
 def finish_kernel(own_ref, lat_ref, diag_ref, lon_ref, out_ref, grad_ref):
     half = WLAT // 2
     edge = WLON // 2
@@ -436,15 +492,20 @@
     def exchange(parts, groups):
         return lax.all_to_all(parts, "lon", 0, 0, axis_index_groups=groups)
 
-    def total(parts):
-        return jnp.sum(parts.astype(f32), axis=0).astype(bf16)
-
-    def copies(part, count):
-        return jnp.broadcast_to(part, (count,) + part.shape)
-
-    quarter = total(exchange(quarters, near))
-    quarter = total(exchange(copies(quarter, lons // 4), far))
-    return exchange(copies(quarter, 4), near)
+    def added(parts, copies):
+        vmem = pl.BlockSpec(memory_space=pltpu.VMEM)
+        return pl.pallas_call(
+            add_kernel,
+            out_shape=jax.ShapeDtypeStruct((copies,) + parts.shape[1:], bf16),
+            in_specs=[vmem],
+            out_specs=vmem,
+            compiler_params=pltpu.CompilerParams(vmem_limit_bytes=VMEM_BYTES),
+            name="add",
+        )(parts)
+
+    parts = exchange(quarters, near)
+    parts = exchange(added(parts, lons // 4), far)
+    return exchange(added(parts, 4), near)
 
 
 def body(
@@ -473,9 +534,10 @@
     lat_part = pl.pallas_call(
         pack_lat_kernel,
         out_shape=packed[0],
-        in_specs=[vmem] * 2,
+        in_specs=[pl.BlockSpec(memory_space=pltpu.HBM)] * 2,
         out_specs=vmem,
-        scratch_shapes=buffers[:1],
+        scratch_shapes=buffers[:1]
+        + [pltpu.VMEM((2, levels, half, lon_cols, C), bf16), pltpu.SemaphoreType.DMA((2,))],
         compiler_params=params,
         name="pack_lat",
     )(field_in, cotangent)
@@ -492,41 +554,35 @@
     diag_part = shifted(diag_part, -1, -1)
     lon_part = shifted(lon_part, 0, -1)
 
-    lat_start = lax.axis_index("lat") * lat_rows
-    lat_total = lax.axis_size("lat") * lat_rows
-    level_pos = jnp.arange(levels, dtype=jnp.int32)[:, None, None]
-    lat_pos = lat_start + jnp.arange(lat_rows, dtype=jnp.int32)[None, :, None]
-    labels = 4 * region_ids + (
-        2 * (level_pos >= levels - WZ // 2).astype(jnp.int32)
-        + (lat_pos >= lat_total - half).astype(jnp.int32)
-    )
-    labels = labels.reshape(2, WZ, WLAT, 2, WLON).transpose(0, 3, 4, 1, 2).reshape(4, POS)
-    label_row = jnp.tile(labels, (1, HEADS)).reshape(4, 1, ROWS)
-    label_col = labels.T
-    factor = (keep_flags.astype(f32) / keep_share).reshape(4)
-
     perm = window_order()
     head_mask = np.repeat(np.eye(HEADS, dtype=np.float32), HD, axis=1)
     table_perm = jnp.asarray(table_order(), bf16)
-    bias_wide = pl.pallas_call(
-        expand_kernel,
-        out_shape=jax.ShapeDtypeStruct((2, POS, ROWS), f32),
-        in_specs=[vmem] * 3,
-        out_specs=vmem,
+    bias_wide, label_row, label_col, weights_t = pl.pallas_call(
+        prepare_kernel,
+        out_shape=(
+            jax.ShapeDtypeStruct((2, POS, ROWS), f32),
+            jax.ShapeDtypeStruct((4, ROWS), f32),
+            jax.ShapeDtypeStruct((POS, 4), f32),
+            jax.ShapeDtypeStruct((3 * C, C), bf16),
+        ),
+        in_specs=[vmem] * 5,
+        out_specs=(vmem,) * 4,
         scratch_shapes=[
             pltpu.VMEM((2 * HEADS, PAIR * TAB), f32),
             pltpu.VMEM((PAIR * SLOTS, TAB), f32),
             pltpu.VMEM((2 * HEADS, POS, POS), f32),
+            pltpu.VMEM((4 * WLAT, 2 * WLON), f32),
         ],
         compiler_params=params,
-        name="expand",
+        name="prepare",
     )(
         bias_table.reshape(2 * HEADS, 1, PAIR * TAB),
         table_perm,
         jnp.asarray(row_order(), bf16),
+        region_ids.transpose(1, 0, 2),
+        w_qkv,
     )
     positions = levels * lat_rows * lon_cols
-    weights_t = w_qkv.T
     gain1 = ln1_gain.reshape(1, C)
     head_mask = jnp.asarray(head_mask, bf16)
     fold, *saved = pl.pallas_call(
@@ -534,16 +590,13 @@
         out_shape=(
             jax.ShapeDtypeStruct((4, QUARTER, TAB), bf16),
             jax.ShapeDtypeStruct((positions, C), bf16),
-            jax.ShapeDtypeStruct((positions, C), bf16),
-            jax.ShapeDtypeStruct((4, C, POS), bf16),
             jax.ShapeDtypeStruct((4, POS, ROWS), bf16),
             jax.ShapeDtypeStruct((4, POS, ROWS), bf16),
-            jax.ShapeDtypeStruct((positions, C), bf16),
             jax.ShapeDtypeStruct((positions, C), f32),
             jax.ShapeDtypeStruct((positions, C), bf16),
         ),
         in_specs=[vmem] * 14 + [smem] + [vmem] * 4,
-        out_specs=(vmem,) * 9,
+        out_specs=(vmem,) * 6,
         scratch_shapes=[
             pltpu.VMEM((2, positions, C), f32),
             pltpu.VMEM((HEADS, POS, POS), f32),
@@ -565,7 +618,7 @@
         bias_wide,
         label_row,
         label_col,
-        factor,
+        keep_flags,
         jnp.asarray(perm, bf16),
         head_mask,
         table_perm,
@@ -574,7 +627,7 @@
     own, lat_back, diag_back, lon_back = pl.pallas_call(
         inputs_kernel,
         out_shape=(jax.ShapeDtypeStruct((2, levels, half, inner, C), bf16),) + packed,
-        in_specs=[vmem] * 12,
+        in_specs=[vmem] * 8 + [smem] + [vmem] * 2,
         out_specs=(vmem,) * 4,
         scratch_shapes=buffers,
         compiler_params=params,
@@ -582,7 +635,7 @@
             flops=1_000_000_000, bytes_accessed=8_000_000, transcendentals=0
         ),
         name="inputs",
-    )(*saved, gain1, weights_t, jnp.asarray(perm.T, bf16), head_mask)
+    )(*saved, gain1, weights_t, w_proj, keep_flags, jnp.asarray(perm.T, bf16), head_mask)
     lat_back = shifted(lat_back, 1, 0)
     diag_back = shifted(diag_back, 1, 1)
     lon_back = shifted(lon_back, 0, 1)

time: 78 us -> 69.7 us (0.89)
  local copies, waits for them, and re-layouts: 21.1 us -> 7.9 us
  Pallas kernels: 17.1 us -> 20.8 us
  waiting for transfers between devices: 1.53 us -> 4.07 us
  other arithmetic: 1.19 us -> 0 us
    unnamed x79 -> x58, local copies, waits for them, and re-layouts: 18.5 us -> 7.9 us
    pallas_call x2 -> x4, Pallas kernels: 2.15 us -> 4.25 us  [the longest x1 2.6 us: body(): pl.pallas_call(prepare_kernel, out_shape=(jax.ShapeDtypeStruct((2, POS, R...]
    pallas_call x1, Pallas kernels: 2.9 us -> 4.44 us  [body(): pl.pallas_call(inputs_kernel, out_shape=(jax.ShapeDtypeStruct((2, levels,...]
    broadcast_in_dim x2 -> x0, local copies, waits for them, and re-layouts: 1.38 us -> none  [copies(): return jnp.broadcast_to(part, (count,) + part.shape)]
    all_to_all x2, waiting for transfers between devices: 0.01 us -> 1.38 us  [exchange(): return lax.all_to_all(parts, 'lon', 0, 0, axis_index_groups=groups)]
    ppermute x6, starting transfers between devices: 17.1 us -> 15.8 us  [shifted(): return lax.ppermute(block, ('lat', 'lon'), route)]
    ppermute x6, waiting for transfers between devices: 1.52 us -> 2.69 us  [shifted(): return lax.ppermute(block, ('lat', 'lon'), route)]
    reduce_sum x2 -> x0, other arithmetic: 1.02 us -> none  [total(): return jnp.sum(parts.astype(f32), axis=0).astype(bf16)]
  transfers between devices with their start and end apart: 8 -> 8, of which waited for: 1 -> 2; matrix products, arithmetic and copies ran while one was open for 4% -> 0% of each run, Pallas kernels for 8% -> 13%
where the time goes in v5:
time: 69.7 us; the launch traced here: 68.3 us
  starting transfers between devices  26.2 us (38%)
  Pallas kernels  20.8 us (30%)
  blocking collectives  8.52 us (12%)
  local copies, waits for them, and re-layouts  7.9 us (11%)
  waiting for transfers between devices  4.07 us (6%)
  between operations  0.9 us (1%)
    ppermute x6, starting transfers between devices, shifted(): return lax.ppermute(block, ('lat', 'lon'), route)  15.8 us
    all_to_all x2, starting transfers between devices, exchange(): return lax.all_to_all(parts, 'lon', 0, 0, axis_index_groups=groups)  10.4 us
    pallas_call x1, Pallas kernels, body(): pl.pallas_call(scores_kernel, out_shape=(jax.ShapeDtypeStruct((4, QUARTER...  10.2 us
    all_to_all x1, blocking collectives, exchange(): return lax.all_to_all(parts, 'lon', 0, 0, axis_index_groups=groups)  8.52 us
    unnamed x58, local copies, waits for them, and re-layouts  7.9 us
    pallas_call x1, Pallas kernels, body(): pl.pallas_call(inputs_kernel, out_shape=(jax.ShapeDtypeStruct((2, levels,...  4.44 us
    ppermute x6, waiting for transfers between devices, shifted(): return lax.ppermute(block, ('lat', 'lon'), route)  2.69 us
    pallas_call x1, Pallas kernels, body(): pl.pallas_call(prepare_kernel, out_shape=(jax.ShapeDtypeStruct((2, POS, R...  2.6 us
  transfers between devices with their start and end apart: 8, of which 2 were waited for; matrix products, arithmetic and copies ran while one was open for 0% of the time, Pallas kernels for 13%

profile of v5, /device:TPU:1, one launch (start us, length us, event | category | flops | bytes accessed | tf_op | source)
XLA Modules:
  0.0 68.3 jit_solution(8253583645909650899)
XLA Ops:
  0.6 1.0 %copy-done = bf16[4,6,24,192]{3,2,1,0:T(8,128)(2,1)S(1)} copy-done((bf16[4,6,24,192]{3,2,1,0:T(8,128)(2,1)S(1)}, bf16[4,6,24,192]{3,2,1,0:T(8,128)(2,1)}, u32[]{:S(2)}) %copy-start) | copy-done | bytes 221208
  1.6 1.0 %copy-done.2 = bf16[4,6,24,192]{3,2,1,0:T(8,128)(2,1)S(1)} copy-done((bf16[4,6,24,192]{3,2,1,0:T(8,128)(2,1)S(1)}, bf16[4,6,24,192]{3,2,1,0:T(8,128)(2,1)}, u32[]{:S(2)}) %copy-start.2) | copy-done | bytes 221208
  2.9 4.4 %collective-permute-start.1 = (bf16[648,128]{1,0:T(8,128)(2,1)S(1)}, bf16[648,128]{1,0:T(8,128)(2,1)S(1)}, u32[]{:S(2)}, u32[]{:S(2)}) collective-permute-start(bf16[648,128]{1,0:T(8,128)(2,1)S(1)} %pack_lat.1.after_ref), channel_id=1, source_target_pairs={{0,224},{1,225},{2,226},{3,227},{4,228},{5,229},{6,230},{7,231},{8... | collective-permute-start | bytes 497672 | tf_op jit(solution)/shard_map/ppermute | solution.py:43
  7.4 1.0 %collective-permute-start = (bf16[216,128]{1,0:T(8,128)(2,1)S(1)}, bf16[216,128]{1,0:T(8,128)(2,1)S(1)}, u32[]{:S(2)}, u32[]{:S(2)}) collective-permute-start(bf16[216,128]{1,0:T(8,128)(2,1)S(1)} %get-tuple-element.21), channel_id=1, source_target_pairs={{0,31},{1,0},{2,1},{3,2},{4,3},{5,4},{6,5},{7,6},{8,7},{9,8},{10,9... | collective-permute-start | bytes 165896 | tf_op jit(solution)/shard_map/ppermute | solution.py:43
  8.4 7.1 %collective-permute-start.2 = (bf16[216,128]{1,0:T(8,128)(2,1)S(1)}, bf16[216,128]{1,0:T(8,128)(2,1)S(1)}, u32[]{:S(2)}, u32[]{:S(2)}) collective-permute-start(bf16[216,128]{1,0:T(8,128)(2,1)S(1)} %get-tuple-element.22), channel_id=1, source_target_pairs={{0,255},{1,224},{2,225},{3,226},{4,227},{5,228},{6,229},{7,230},{8... | collective-permute-start | bytes 165896 | tf_op jit(solution)/shard_map/ppermute | solution.py:43
  15.6 2.6 %prepare.1 = (f32[2,144,864]{2,1,0:T(8,128)S(1)}, f32[4,864]{1,0:T(4,128)S(1)}, f32[144,4]{1,0:T(8,128)S(1)}, bf16[576,192]{1,0:T(8,128)(2,1)S(1)}) custom-call(f32[12,1,3312]{2,1,0:T(1,128)S(1)} %bitcast.7, bf16[276,276]{1,0:T(8,128)(2,1)S(1)} %copy-done.4, bf16[192,192]{1,0:T(8,128)(2,1)S(1)} %copy-done.18, s32[6,4,24]{2,1,0:T(4,128)S(1)} %bitcast.8, ...), custom_call_target="tpu_custom_call" | custom-call | tf_op jit(solution)/shard_map/prepare/pallas_call | solution.py:560
  18.9 10.2 %scores.1 = (bf16[4,36,276]{2,1,0:T(8,128)(2,1)S(1)}, bf16[576,192]{1,0:T(8,128)(2,1)S(1)}, bf16[4,144,864]{2,1,0:T(8,128)(2,1)S(1)}, bf16[4,144,864]{2,1,0:T(8,...) custom-call(bf16[4,6,24,192]{3,2,1,0:T(8,128)(2,1)S(1)} %copy-done.1, ...), custom_call_target="tpu_custom_call" | custom-call | tf_op jit(solution)/shard_map/scores/pallas_call | solution.py:588
  29.2 0.7 %copy-done.6 = bf16[576,192]{1,0:T(8,128)(2,1)} copy-done((bf16[576,192]{1,0:T(8,128)(2,1)}, bf16[576,192]{1,0:T(8,128)(2,1)S(1)}, u32[]{:S(2)}) %copy-start.6) | copy-done | bytes 221208
  29.9 0.7 %copy-done.8 = bf16[576,192]{1,0:T(8,128)(2,1)} copy-done((bf16[576,192]{1,0:T(8,128)(2,1)}, bf16[576,192]{1,0:T(8,128)(2,1)S(1)}, u32[]{:S(2)}) %copy-start.8) | copy-done | bytes 221208
  30.6 8.5 %all_to_all.15.parts_ref = bf16[4,36,276]{2,1,0:T(8,128)(2,1)S(1)} all-to-all(bf16[4,36,276]{2,1,0:T(8,128)(2,1)S(1)} %get-tuple-element.38), channel_id=1, replica_groups={{0,1,2,3},{4,5,6,7},{8,9,10,11},{12,13,14,15},{16,17,18,19},{20,21,22,2..., dimensions={0} | all-to-all | bytes 158976 | tf_op jit(solution)/shard_map/all_to_all | solution.py:493
  39.1 0.7 %add.2 = bf16[8,36,276]{2,1,0:T(8,128)(2,1)} custom-call(bf16[4,36,276]{2,1,0:T(8,128)(2,1)S(1)} %all_to_all.15.parts_ref), custom_call_target="tpu_custom_call" | custom-call | tf_op jit(solution)/shard_map/add/pallas_call | solution.py:497
  39.8 4.2 %all-to-all-start.1 = ((bf16[8,36,276]{2,1,0:T(8,128)(2,1)}), bf16[8,36,276]{2,1,0:T(8,128)(2,1)S(1)}, u32[]{:S(2)}, u32[]{:S(2)}) async-start(bf16[8,36,276]{2,1,0:T(8,128)(2,1)} %add.2), calls=%async_computation.1 | async-start | bytes 491520 | tf_op jit(solution)/shard_map/all_to_all | solution.py:493
  44.0 1.0 %copy-done.7 = bf16[576,192]{1,0:T(8,128)(2,1)S(1)} copy-done((bf16[576,192]{1,0:T(8,128)(2,1)S(1)}, bf16[576,192]{1,0:T(8,128)(2,1)}, u32[]{:S(2)}) %copy-start.7) | copy-done | bytes 221208
  45.0 1.0 %copy-done.9 = bf16[576,192]{1,0:T(8,128)(2,1)S(1)} copy-done((bf16[576,192]{1,0:T(8,128)(2,1)S(1)}, bf16[576,192]{1,0:T(8,128)(2,1)}, u32[]{:S(2)}) %copy-start.9) | copy-done | bytes 221208
  45.9 4.4 %inputs.1 = (bf16[2,4,3,18,192]{4,3,2,1,0:T(8,128)(2,1)S(1)}, bf16[648,128]{1,0:T(8,128)(2,1)}, bf16[216,128]{1,0:T(8,128)(2,1)S(1)}, bf16[216,128]{1,0:T(8,128)(2,1)S(1)}) custom-call(bf16[576,192]{1,0:T(8,128)(2,1)S(1)} %copy-done.7, bf16[4,144,864]{2,1,0:T(8,128)(2,1)S(1)} %get-tuple-element.28.probs_ref, ...), custom_call_target="tpu_custom_call" | custom-call | flops 1000000000 | bytes 8000000 | tf_op jit(solution)/shard_map/inputs/pallas_call | solution.py:627
  50.4 0.7 %copy-done.10 = bf16[2,4,3,18,192]{4,3,2,1,0:T(8,128)(2,1)} copy-done((bf16[2,4,3,18,192]{4,3,2,1,0:T(8,128)(2,1)}, bf16[2,4,3,18,192]{4,3,2,1,0:T(8,128)(2,1)S(1)}, u32[]{:S(2)}) %copy-start.10) | copy-done | bytes 165912
  52.3 1.4 %all-to-all-done.1.parts_ref = bf16[8,36,276]{2,1,0:T(8,128)(2,1)S(1)} async-done(((bf16[8,36,276]{2,1,0:T(8,128)(2,1)}), bf16[8,36,276]{2,1,0:T(8,128)(2,1)S(1)}, u32[]{:S(2)}, u32[]{:S(2)}) %all-to-all-start.1) | async-done | bytes 159008 | tf_op jit(solution)/shard_map/all_to_all | solution.py:493
  53.7 0.7 %add.3 = bf16[4,36,276]{2,1,0:T(8,128)(2,1)} custom-call(bf16[8,36,276]{2,1,0:T(8,128)(2,1)S(1)} %all-to-all-done.1.parts_ref), custom_call_target="tpu_custom_call" | custom-call | tf_op jit(solution)/shard_map/add/pallas_call | solution.py:497
  54.4 6.2 %all-to-all-start.2 = ((bf16[4,36,276]{2,1,0:T(8,128)(2,1)}), bf16[4,36,276]{2,1,0:T(8,128)(2,1)S(1)}, u32[]{:S(2)}, u32[]{:S(2)}) async-start(bf16[4,36,276]{2,1,0:T(8,128)(2,1)} %add.3), calls=%async_computation.2 | async-start | bytes 245760 | tf_op jit(solution)/shard_map/all_to_all | solution.py:493
  60.6 2.1 %collective-permute-start.4 = (bf16[216,128]{1,0:T(8,128)(2,1)S(1)}, bf16[216,128]{1,0:T(8,128)(2,1)S(1)}, u32[]{:S(2)}, u32[]{:S(2)}) collective-permute-start(bf16[216,128]{1,0:T(8,128)(2,1)S(1)} %copy-done.28), channel_id=1, source_target_pairs={{0,33},{1,34},{2,35},{3,36},{4,37},{5,38},{6,39},{7,40},{8,41},{9,... | collective-permute-start | bytes 165896 | tf_op jit(solution)/shard_map/ppermute | solution.py:43
  62.7 1.2 %collective-permute-start.5 = (bf16[216,128]{1,0:T(8,128)(2,1)S(1)}, bf16[216,128]{1,0:T(8,128)(2,1)S(1)}, u32[]{:S(2)}, u32[]{:S(2)}) collective-permute-start(bf16[216,128]{1,0:T(8,128)(2,1)S(1)} %copy-done.26), channel_id=1, source_target_pairs={{0,1},{1,2},{2,3},{3,4},{4,5},{5,6},{6,7},{7,8},{8,9},{9,10},{10,1... | collective-permute-start | bytes 165896 | tf_op jit(solution)/shard_map/ppermute | solution.py:43
  63.9 2.7 %collective-permute-done.4.diag_ref = bf16[216,128]{1,0:T(8,128)(2,1)S(1)} collective-permute-done((bf16[216,128]{1,0:T(8,128)(2,1)S(1)}, bf16[216,128]{1,0:T(8,128)(2,1)S(1)}, u32[]{:S(2)}, u32[]{:S(2)}) %collective-permute-start.4) | collective-permute-done | bytes 55328 | tf_op jit(solution)/shard_map/ppermute | solution.py:43
  66.6 0.9 %finish.1 = (bf16[4,6,24,192]{3,2,1,0:T(8,128)(2,1)}, bf16[4,6,24,192]{3,2,1,0:T(8,128)(2,1)}) custom-call(bf16[2,4,3,18,192]{4,3,2,1,0:T(8,128)(2,1)S(1)} %copy-done.11, bf16[648,128]{1,0:T(8,128)(2,1)S(1)} %collective-permute-done.3.lat_ref, bf16[216,128]{1,0:T(8,128)(2,1)S(1)} %collective-permute-done.4.diag_ref, ...), custom_call_target="tpu_custom_call" | custom-call | tf_op jit(solution)/shard_map/finish/pallas_call | solution.py:652
  67.5 0.8 %unpack.1 = f32[12,1,3312]{2,1,0:T(1,128)} custom-call(bf16[4,36,276]{2,1,0:T(8,128)(2,1)S(1)} %all-to-all-done.2.grad_ref), custom_call_target="tpu_custom_call" | custom-call | tf_op jit(solution)/shard_map/unpack/pallas_call | solution.py:642
  (60 shorter events, 2.3 us)
Async XLA Ops:
  2.6 12.9 %copy-start.14 = (bf16[192,576]{1,0:T(8,128)(2,1)S(1)}, bf16[192,576]{1,0:T(8,128)(2,1)}, u32[]{:S(2)}) copy-start(bf16[192,576]{1,0:T(8,128)(2,1)} %wqkv_ref.1) | copy-start | bytes 663556
  2.6 12.9 %copy-start.17 = (f32[2,1,6,3312]{3,1,2,0:T(1,128)S(1)}, f32[2,1,6,3312]{3,1,2,0:T(1,128)}, u32[]{:S(2)}) copy-start(f32[2,1,6,3312]{3,1,2,0:T(1,128)} %param.25) | copy-start | bytes 476932
  2.6 12.9 %copy-start.18 = (bf16[192,192]{1,0:T(8,128)(2,1)S(1)}, bf16[192,192]{1,0:T(8,128)(2,1)}, u32[]{:S(2)}) copy-start(bf16[192,192]{1,0:T(8,128)(2,1)} %constant.13.clone.row_perm_ref) | copy-start | bytes 221188
  2.6 12.9 %copy-start.21 = (s32[4,6,24]{2,0,1:T(4,128)S(1)}, s32[4,6,24]{2,0,1:T(4,128)}, u32[]{:S(2)}) copy-start(s32[4,6,24]{2,0,1:T(4,128)} %param.26) | copy-start | bytes 6916
  2.6 15.7 %copy-start.16 = (bf16[288,288]{1,0:T(8,128)(2,1)S(1)}, bf16[288,288]{1,0:T(8,128)(2,1)}, u32[]{:S(2)}) copy-start(bf16[288,288]{1,0:T(8,128)(2,1)} %constant.15.clone.perm_ref) | copy-start | bytes 497668
  2.6 15.7 %copy-start.19 = (bf16[72,96]{1,0:T(8,128)(2,1)S(1)}, bf16[72,96]{1,0:T(8,128)(2,1)}, u32[]{:S(2)}) copy-start(bf16[72,96]{1,0:T(8,128)(2,1)} %constant.16.clone.chunk_perm_ref) | copy-start | bytes 41476
  2.8 12.7 %copy-start.4 = (bf16[276,276]{1,0:T(8,128)(2,1)S(1)}, bf16[276,276]{1,0:T(8,128)(2,1)}, u32[]{:S(2)}) copy-start(bf16[276,276]{1,0:T(8,128)(2,1)} %constant.12.clone.table_perm_ref) | copy-start | bytes 457060
  2.9 15.3 %collective-permute-start.1 = (bf16[648,128]{1,0:T(8,128)(2,1)S(1)}, bf16[648,128]{1,0:T(8,128)(2,1)S(1)}, u32[]{:S(2)}, u32[]{:S(2)}) collective-permute-start(bf16[648,128]{1,0:T(8,128)(2,1)S(1)} %pack_lat.1.after_ref), channel_id=1, source_target_pairs={{0,224},{1,225},{2,226},{3,227},{4,228},{5,229},{6,230},{7,231},{8... | collective-permute-start | bytes 497672 | tf_op jit(solution)/shard_map/ppermute | solution.py:43
  7.3 11.0 %copy-start.12 = (bf16[192,768]{1,0:T(8,128)(2,1)S(1)}, bf16[192,768]{1,0:T(8,128)(2,1)}, u32[]{:S(2)}) copy-start(bf16[192,768]{1,0:T(8,128)(2,1)} %wup_ref.1) | copy-start | bytes 884740
  7.3 11.0 %copy-start.13 = (bf16[768,192]{0,1:T(8,128)(2,1)S(1)}, bf16[768,192]{0,1:T(8,128)(2,1)}, u32[]{:S(2)}) copy-start(bf16[768,192]{0,1:T(8,128)(2,1)} %param.24) | copy-start | bytes 884740
  7.4 10.8 %collective-permute-start = (bf16[216,128]{1,0:T(8,128)(2,1)S(1)}, bf16[216,128]{1,0:T(8,128)(2,1)S(1)}, u32[]{:S(2)}, u32[]{:S(2)}) collective-permute-start(bf16[216,128]{1,0:T(8,128)(2,1)S(1)} %get-tuple-element.21), channel_id=1, source_target_pairs={{0,31},{1,0},{2,1},{3,2},{4,3},{5,4},{6,5},{7,6},{8,7},{9,8},{10,9... | collective-permute-start | bytes 165896 | tf_op jit(solution)/shard_map/ppermute | solution.py:43
  8.4 9.8 %collective-permute-start.2 = (bf16[216,128]{1,0:T(8,128)(2,1)S(1)}, bf16[216,128]{1,0:T(8,128)(2,1)S(1)}, u32[]{:S(2)}, u32[]{:S(2)}) collective-permute-start(bf16[216,128]{1,0:T(8,128)(2,1)S(1)} %get-tuple-element.22), channel_id=1, source_target_pairs={{0,255},{1,224},{2,225},{3,226},{4,227},{5,228},{6,229},{7,230},{8... | collective-permute-start | bytes 165896 | tf_op jit(solution)/shard_map/ppermute | solution.py:43
  15.5 2.8 %copy-start.1 = (bf16[4,6,24,192]{3,2,1,0:T(8,128)(2,1)S(1)}, bf16[4,6,24,192]{3,2,1,0:T(8,128)(2,1)}, u32[]{:S(2)}) copy-start(bf16[4,6,24,192]{3,2,1,0:T(8,128)(2,1)} %field_ref.5) | copy-start | bytes 663556
  15.5 2.8 %copy-start.3 = (bf16[4,6,24,192]{3,2,1,0:T(8,128)(2,1)S(1)}, bf16[4,6,24,192]{3,2,1,0:T(8,128)(2,1)}, u32[]{:S(2)}) copy-start(bf16[4,6,24,192]{3,2,1,0:T(8,128)(2,1)} %cot_ref.5) | copy-start | bytes 663556
  15.5 2.8 %copy-start.5 = (bf16[192,192]{1,0:T(8,128)(2,1)S(1)}, bf16[192,192]{1,0:T(8,128)(2,1)}, u32[]{:S(2)}) copy-start(bf16[192,192]{1,0:T(8,128)(2,1)} %wproj_ref.3) | copy-start | bytes 221188
  39.8 4.2 %copy-start.15 = (bf16[288,288]{1,0:T(8,128)(2,1)S(1)}, bf16[288,288]{1,0:T(8,128)(2,1)}, u32[]{:S(2)}) copy-start(bf16[288,288]{1,0:T(8,128)(2,1)} %constant.17.clone.perm_t_ref) | copy-start | bytes 497668
  39.8 13.9 %all-to-all-start.1 = ((bf16[8,36,276]{2,1,0:T(8,128)(2,1)}), bf16[8,36,276]{2,1,0:T(8,128)(2,1)S(1)}, u32[]{:S(2)}, u32[]{:S(2)}) async-start(bf16[8,36,276]{2,1,0:T(8,128)(2,1)} %add.2), calls=%async_computation.1 | async-start | bytes 491520 | tf_op jit(solution)/shard_map/all_to_all | solution.py:493
  52.3 14.3 %copy-start.11 = (bf16[2,4,3,18,192]{4,3,2,1,0:T(8,128)(2,1)S(1)}, bf16[2,4,3,18,192]{4,3,2,1,0:T(8,128)(2,1)}, u32[]{:S(2)}) copy-start(bf16[2,4,3,18,192]{4,3,2,1,0:T(8,128)(2,1)} %copy-done.10) | copy-start | bytes 497668
  52.3 14.3 %collective-permute-start.3 = (bf16[648,128]{1,0:T(8,128)(2,1)}, bf16[648,128]{1,0:T(8,128)(2,1)S(1)}, u32[]{:S(2)}, u32[]{:S(2)}) collective-permute-start(bf16[648,128]{1,0:T(8,128)(2,1)} %get-tuple-element.33), channel_id=1, source_target_pairs={{0,32},{1,33},{2,34},{3,35},{4,36},{5,37},{6,38},{7,39},{8,40},{9,... | collective-permute-start | bytes 497672 | tf_op jit(solution)/shard_map/ppermute | solution.py:43
  54.4 6.2 %copy-start.28 = (bf16[216,128]{1,0:T(8,128)(2,1)S(1)}, bf16[216,128]{1,0:T(8,128)(2,1)}, u32[]{:S(2)}) copy-start(bf16[216,128]{1,0:T(8,128)(2,1)} %copy-done.27) | copy-start | bytes 165892
  54.4 8.3 %copy-start.26 = (bf16[216,128]{1,0:T(8,128)(2,1)S(1)}, bf16[216,128]{1,0:T(8,128)(2,1)}, u32[]{:S(2)}) copy-start(bf16[216,128]{1,0:T(8,128)(2,1)} %copy-done.25) | copy-start | bytes 165892
  54.4 13.1 %all-to-all-start.2 = ((bf16[4,36,276]{2,1,0:T(8,128)(2,1)}), bf16[4,36,276]{2,1,0:T(8,128)(2,1)S(1)}, u32[]{:S(2)}, u32[]{:S(2)}) async-start(bf16[4,36,276]{2,1,0:T(8,128)(2,1)} %add.3), calls=%async_computation.2 | async-start | bytes 245760 | tf_op jit(solution)/shard_map/all_to_all | solution.py:493
  60.6 6.0 %collective-permute-start.4 = (bf16[216,128]{1,0:T(8,128)(2,1)S(1)}, bf16[216,128]{1,0:T(8,128)(2,1)S(1)}, u32[]{:S(2)}, u32[]{:S(2)}) collective-permute-start(bf16[216,128]{1,0:T(8,128)(2,1)S(1)} %copy-done.28), channel_id=1, source_target_pairs={{0,33},{1,34},{2,35},{3,36},{4,37},{5,38},{6,39},{7,40},{8,41},{9,... | collective-permute-start | bytes 165896 | tf_op jit(solution)/shard_map/ppermute | solution.py:43
  62.7 3.9 %collective-permute-start.5 = (bf16[216,128]{1,0:T(8,128)(2,1)S(1)}, bf16[216,128]{1,0:T(8,128)(2,1)S(1)}, u32[]{:S(2)}, u32[]{:S(2)}) collective-permute-start(bf16[216,128]{1,0:T(8,128)(2,1)S(1)} %copy-done.26), channel_id=1, source_target_pairs={{0,1},{1,2},{2,3},{3,4},{4,5},{5,6},{6,7},{7,8},{8,9},{9,10},{10,1... | collective-permute-start | bytes 165896 | tf_op jit(solution)/shard_map/ppermute | solution.py:43
  (13 other events, 14.1 us)

commit v6 on v5

--- a/solution.py
+++ b/solution.py
@@ -136,7 +136,7 @@
     lon_out[...] = lon_buf[...].astype(bf16)
 
 
-def scores_kernel(
+def block_kernel(
     field_ref,
     cot_ref,
     lon_ref,
@@ -156,14 +156,17 @@
     head_mask_ref,
     table_perm_ref,
     chunk_perm_ref,
+    perm_t_ref,
     fold_out,
-    x_out,
-    probs_out,
-    grad_low_out,
-    grad_sum_out,
-    result_out,
+    own_out,
+    lat_out,
+    diag_out,
+    lon_out,
     frame,
     wide,
+    lat_buf,
+    diag_buf,
+    lon_buf,
 ):
     half = WLAT // 2
     cols = 2 * WLON
@@ -197,12 +200,13 @@
     wv_t = wqkv_t_ref[2 * C : 3 * C, :]
     head_mask = head_mask_ref[...]
     perm = perm_ref[...]
+    perm_t = perm_t_ref[...]
     for n in range(2):
         both = slice(n * 2 * POS, (n + 1) * 2 * POS)
         x = mm(perm, frame[0, both, :].astype(bf16))
         cot = mm(perm, frame[1, both, :].astype(bf16))
-        x_out[both, :] = x.astype(bf16)
-        h1 = norm_parts(x, gain1)[0].astype(bf16)
+        scaled1, normed1, inverse1 = norm_parts(x, gain1)
+        h1 = scaled1.astype(bf16)
         q_all = mm_nt(h1, wq_t).astype(bf16)
         k_all = mm_nt(h1, wk_t).astype(bf16)
         v_all = mm_nt(h1, wv_t).astype(bf16)
@@ -219,32 +223,36 @@
             weights = jnp.exp2(scores - jnp.max(scores, axis=0, keepdims=True))
             probs = weights * (1.0 / jnp.sum(weights, axis=0, keepdims=True))
             probs_low = probs.astype(bf16)
-            probs_out[w] = probs_low
             attended = head_blocks(mm(v_t, probs_low)).T.astype(bf16)
             factor = keep_ref[n, 0, c].astype(f32) * (1.0 / keep_share)
             branches.append((mm(attended, wproj_ref[...]) * factor).astype(bf16).astype(f32))
-            saved.append(probs)
+            saved.append((q_wide, probs, probs_low))
         y_sum = x + jnp.concatenate(branches, axis=0)
         scaled2, normed2, inverse2 = norm_parts(y_sum, gain2)
         act, slope = gelu_parts(mm(scaled2.astype(bf16), wup_ref[...]))
-        result_out[both, :] = (y_sum + mm_nt(act.astype(bf16), wdown_t_ref[...])).astype(bf16)
+        result = (y_sum + mm_nt(act.astype(bf16), wdown_t_ref[...])).astype(bf16)
         grad_up = (mm(cot.astype(bf16), wdown_t_ref[...]) * slope).astype(bf16)
         grad_sum = cot + norm_back(mm_nt(grad_up, wup_ref[...]), gain2, normed2, inverse2)
-        grad_sum_out[both, :] = grad_sum
         grad_low_in = grad_sum.astype(bf16).astype(f32)
         folded = None
+        grad_h1 = []
         for c in range(2):
-            w = 2 * n + c
             rows = slice(c * POS, (c + 1) * POS)
-            probs = saved[c]
+            q_wide, probs, probs_low = saved[c]
             factor = keep_ref[n, 0, c].astype(f32) * (1.0 / keep_share)
             grad_branch = (grad_low_in[rows] * factor).astype(bf16)
             grad_att = mm_nt(grad_branch, wproj_ref[...]).astype(bf16)
-            grad_probs = mm_nt(v_all[rows], spread_heads(grad_att, head_mask))
+            g_wide = spread_heads(grad_att, head_mask)
+            grad_probs = mm_nt(v_all[rows], g_wide)
             inner_sum = jnp.sum(probs * grad_probs, axis=0, keepdims=True)
             grad_scores = probs * (grad_probs - inner_sum)
             folded = grad_scores if folded is None else folded + grad_scores
-            grad_low_out[w] = grad_scores.astype(bf16)
+            grad_low = grad_scores.astype(bf16)
+            k_t = mm_nt(wk_t, h1[rows]).astype(bf16)
+            grad_q = (head_blocks(mm(k_t, grad_low)).T * root).astype(bf16)
+            grad_k = (mm(grad_low, q_wide) * root).astype(bf16)
+            grad_v = mm(probs_low, g_wide).astype(bf16)
+            grad_h1.append(mm(grad_q, wq_t) + mm(grad_k, wk_t) + mm(grad_v, wv_t))
         wide[...] = folded.T.reshape(HEADS, POS, POS)
         total = None
         for o in range(WLON):
@@ -263,64 +271,9 @@
         total = mm(chunk_perm_ref[...], total)
         fold_out[2 * n] = total[:QUARTER].astype(bf16)
         fold_out[2 * n + 1] = total[QUARTER:].astype(bf16)
-
-
-def inputs_kernel(
-    x_ref,
-    probs_ref,
-    grad_low_ref,
-    grad_sum_ref,
-    result_ref,
-    gain1_ref,
-    wqkv_t_ref,
-    wproj_ref,
-    keep_ref,
-    perm_t_ref,
-    head_mask_ref,
-    own_out,
-    lat_out,
-    diag_out,
-    lon_out,
-    lat_buf,
-    diag_buf,
-    lon_buf,
-):
-    half = WLAT // 2
-    cols = 2 * WLON
-    edge = WLON // 2
-    inner = cols - edge
-    root = 1.0 / math.sqrt(HD)
-    gain1 = gain1_ref[...]
-    wq_t = wqkv_t_ref[0:C, :]
-    wk_t = wqkv_t_ref[C : 2 * C, :]
-    wv_t = wqkv_t_ref[2 * C : 3 * C, :]
-    head_mask = head_mask_ref[...]
-    perm_t = perm_t_ref[...]
-    for n in range(2):
-        both = slice(n * 2 * POS, (n + 1) * 2 * POS)
-        scaled1, normed1, inverse1 = norm_parts(x_ref[both, :].astype(f32), gain1)
-        h1 = scaled1.astype(bf16)
-        q_all = mm_nt(h1, wq_t).astype(bf16)
-        grad_sum = grad_sum_ref[both, :]
-        grad_low_in = grad_sum.astype(bf16).astype(f32)
-        grad_h1 = []
-        for c in range(2):
-            w = 2 * n + c
-            rows = slice(c * POS, (c + 1) * POS)
-            grad_low = grad_low_ref[w]
-            k_t = mm_nt(wk_t, h1[rows]).astype(bf16)
-            factor = keep_ref[n, 0, c].astype(f32) * (1.0 / keep_share)
-            grad_branch = (grad_low_in[rows] * factor).astype(bf16)
-            grad_att = mm_nt(grad_branch, wproj_ref[...]).astype(bf16)
-            q_wide = spread_heads(q_all[rows], head_mask)
-            g_wide = spread_heads(grad_att, head_mask)
-            grad_q = (head_blocks(mm(k_t, grad_low)).T * root).astype(bf16)
-            grad_k = (mm(grad_low, q_wide) * root).astype(bf16)
-            grad_v = mm(probs_ref[w], g_wide).astype(bf16)
-            grad_h1.append(mm(grad_q, wq_t) + mm(grad_k, wk_t) + mm(grad_v, wv_t))
         grad_h1 = jnp.concatenate(grad_h1, axis=0).astype(bf16).astype(f32)
         grad_field = (grad_sum + norm_back(grad_h1, gain1, normed1, inverse1)).astype(bf16)
-        for t, value in enumerate((result_ref[both, :], grad_field)):
+        for t, value in enumerate((result, grad_field)):
             natural = mm(perm_t, value)
             for dz in range(WZ):
                 z = (2 * n + dz + 1) % 4
@@ -484,7 +437,7 @@
     return perm
 
 
-def lon_sum(quarters):
+def lon_sum(quarters, after):
     lons = lax.axis_size("lon")
     near = [[4 * k + j for j in range(4)] for k in range(lons // 4)]
     far = [[4 * k + j for k in range(lons // 4)] for j in range(4)]
@@ -503,9 +456,10 @@
             name="add",
         )(parts)
 
-    parts = exchange(quarters, near)
-    parts = exchange(added(parts, lons // 4), far)
-    return exchange(added(parts, 4), near)
+    parts = added(exchange(quarters, near), lons // 4)
+    parts, after = lax.optimization_barrier((parts, after))
+    parts = exchange(parts, far)
+    return exchange(added(parts, 4), near), after
 
 
 def body(
@@ -585,24 +539,22 @@
     positions = levels * lat_rows * lon_cols
     gain1 = ln1_gain.reshape(1, C)
     head_mask = jnp.asarray(head_mask, bf16)
-    fold, *saved = pl.pallas_call(
-        scores_kernel,
+    fold, own, *strips = pl.pallas_call(
+        block_kernel,
         out_shape=(
             jax.ShapeDtypeStruct((4, QUARTER, TAB), bf16),
-            jax.ShapeDtypeStruct((positions, C), bf16),
-            jax.ShapeDtypeStruct((4, POS, ROWS), bf16),
-            jax.ShapeDtypeStruct((4, POS, ROWS), bf16),
-            jax.ShapeDtypeStruct((positions, C), f32),
-            jax.ShapeDtypeStruct((positions, C), bf16),
-        ),
-        in_specs=[vmem] * 14 + [smem] + [vmem] * 4,
-        out_specs=(vmem,) * 6,
+            jax.ShapeDtypeStruct((2, levels, half, inner, C), bf16),
+        )
+        + packed,
+        in_specs=[vmem] * 14 + [smem] + [vmem] * 5,
+        out_specs=(vmem,) * 5,
         scratch_shapes=[
             pltpu.VMEM((2, positions, C), f32),
             pltpu.VMEM((HEADS, POS, POS), f32),
-        ],
+        ]
+        + buffers,
         compiler_params=params,
-        name="scores",
+        name="block",
     )(
         field_in,
         cotangent,
@@ -623,19 +575,9 @@
         head_mask,
         table_perm,
         jnp.asarray(chunk_order(), bf16),
+        jnp.asarray(perm.T, bf16),
     )
-    own, lat_back, diag_back, lon_back = pl.pallas_call(
-        inputs_kernel,
-        out_shape=(jax.ShapeDtypeStruct((2, levels, half, inner, C), bf16),) + packed,
-        in_specs=[vmem] * 8 + [smem] + [vmem] * 2,
-        out_specs=(vmem,) * 4,
-        scratch_shapes=buffers,
-        compiler_params=params,
-        cost_estimate=pl.CostEstimate(
-            flops=1_000_000_000, bytes_accessed=8_000_000, transcendentals=0
-        ),
-        name="inputs",
-    )(*saved, gain1, weights_t, w_proj, keep_flags, jnp.asarray(perm.T, bf16), head_mask)
+    grads, (lat_back, diag_back, lon_back) = lon_sum(fold, strips)
     lat_back = shifted(lat_back, 1, 0)
     diag_back = shifted(diag_back, 1, 1)
     lon_back = shifted(lon_back, 0, 1)
@@ -647,7 +589,7 @@
         scratch_shapes=[pltpu.VMEM((2 * HEADS, PAIR * TAB), f32)],
         compiler_params=params,
         name="unpack",
-    )(lon_sum(fold))
+    )(grads)
     grads = grads.reshape(2, 1, HEADS, PAIR * TAB)
     result, grad_field = pl.pallas_call(
         finish_kernel,

time: 69.7 us -> 72 us (1.033)
  the two profiles are of different devices: /device:TPU:1 before, /device:TPU:6 now
where the time goes in v6:
time: 72 us; the launch traced here: 71.4 us
  starting transfers between devices  24.4 us (34%)
  Pallas kernels  18 us (25%)
  waiting for transfers between devices  13.3 us (18%)
  blocking collectives  8.43 us (12%)
  local copies, waits for them, and re-layouts  6.41 us (9%)
  between operations  0.8 us (1%)
    ppermute x6, starting transfers between devices, shifted(): return lax.ppermute(block, ('lat', 'lon'), route)  17.1 us
    pallas_call x1, Pallas kernels, body(): pl.pallas_call(block_kernel, out_shape=(jax.ShapeDtypeStruct((4, QUARTER,...  12 us
    all_to_all x2, waiting for transfers between devices, exchange(): return lax.all_to_all(parts, 'lon', 0, 0, axis_index_groups=groups)  8.79 us
    all_to_all x1, blocking collectives, exchange(): return lax.all_to_all(parts, 'lon', 0, 0, axis_index_groups=groups)  8.43 us
    all_to_all x2, starting transfers between devices, exchange(): return lax.all_to_all(parts, 'lon', 0, 0, axis_index_groups=groups)  7.28 us
    unnamed x38, local copies, waits for them, and re-layouts  6.41 us
    ppermute x6, waiting for transfers between devices, shifted(): return lax.ppermute(block, ('lat', 'lon'), route)  4.53 us
    pallas_call x1, Pallas kernels, body(): pl.pallas_call(prepare_kernel, out_shape=(jax.ShapeDtypeStruct((2, POS, R...  2.6 us
  transfers between devices with their start and end apart: 8, of which 3 were waited for; matrix products, arithmetic and copies ran while one was open for 0% of the time, Pallas kernels for 6%

profile of v6, /device:TPU:6, one launch (start us, length us, event | category | flops | bytes accessed | tf_op | source)
XLA Modules:
  0.0 71.4 jit_solution(16515571483137827962)
XLA Ops:
  0.6 1.0 %copy-done = bf16[4,6,24,192]{3,2,1,0:T(8,128)(2,1)S(1)} copy-done((bf16[4,6,24,192]{3,2,1,0:T(8,128)(2,1)S(1)}, bf16[4,6,24,192]{3,2,1,0:T(8,128)(2,1)}, u32[]{:S(2)}) %copy-start) | copy-done | bytes 221208
  1.6 1.0 %copy-done.2 = bf16[4,6,24,192]{3,2,1,0:T(8,128)(2,1)S(1)} copy-done((bf16[4,6,24,192]{3,2,1,0:T(8,128)(2,1)S(1)}, bf16[4,6,24,192]{3,2,1,0:T(8,128)(2,1)}, u32[]{:S(2)}) %copy-start.2) | copy-done | bytes 221208
  2.8 1.9 %collective-permute-start.1 = (bf16[648,128]{1,0:T(8,128)(2,1)S(1)}, bf16[648,128]{1,0:T(8,128)(2,1)S(1)}, u32[]{:S(2)}, u32[]{:S(2)}) collective-permute-start(bf16[648,128]{1,0:T(8,128)(2,1)S(1)} %pack_lat.1.after_ref), channel_id=1, source_target_pairs={{0,224},{1,225},{2,226},{3,227},{4,228},{5,229},{6,230},{7,231},{8... | collective-permute-start | bytes 497672 | tf_op jit(solution)/shard_map/ppermute | solution.py:43
  4.9 7.4 %collective-permute-start = (bf16[216,128]{1,0:T(8,128)(2,1)S(1)}, bf16[216,128]{1,0:T(8,128)(2,1)S(1)}, u32[]{:S(2)}, u32[]{:S(2)}) collective-permute-start(bf16[216,128]{1,0:T(8,128)(2,1)S(1)} %get-tuple-element.20), channel_id=1, source_target_pairs={{0,31},{1,0},{2,1},{3,2},{4,3},{5,4},{6,5},{7,6},{8,7},{9,8},{10,9... | collective-permute-start | bytes 165896 | tf_op jit(solution)/shard_map/ppermute | solution.py:43
  12.5 0.9 %copy-done.11 = bf16[192,192]{1,0:T(8,128)(2,1)S(1)} copy-done((bf16[192,192]{1,0:T(8,128)(2,1)S(1)}, bf16[192,192]{1,0:T(8,128)(2,1)}, u32[]{:S(2)}) %copy-start.11) | copy-done | bytes 73752
  13.4 0.7 copy-done.14
  14.1 2.6 %prepare.1 = (f32[2,144,864]{2,1,0:T(8,128)S(1)}, f32[4,864]{1,0:T(4,128)S(1)}, f32[144,4]{1,0:T(8,128)S(1)}, bf16[576,192]{1,0:T(8,128)(2,1)S(1)}) custom-call(f32[12,1,3312]{2,1,0:T(1,128)S(1)} %bitcast.7, bf16[276,276]{1,0:T(8,128)(2,1)S(1)} %copy-done.4, bf16[192,192]{1,0:T(8,128)(2,1)S(1)} %copy-done.11, s32[6,4,24]{2,1,0:T(4,128)S(1)} %bitcast.8, ...), custom_call_target="tpu_custom_call" | custom-call | tf_op jit(solution)/shard_map/prepare/pallas_call | solution.py:514
  17.5 0.9 %copy-done.12 = bf16[192,192]{1,0:T(8,128)(2,1)S(1)} copy-done((bf16[192,192]{1,0:T(8,128)(2,1)S(1)}, bf16[192,192]{1,0:T(8,128)(2,1)}, u32[]{:S(2)}) %copy-start.12) | copy-done | bytes 73752
  18.4 0.7 copy-done.15
  19.0 0.7 copy-done.18
  19.7 12.0 %block.1 = (bf16[4,36,276]{2,1,0:T(8,128)(2,1)S(1)}, bf16[2,4,3,18,192]{4,3,2,1,0:T(8,128)(2,1)S(1)}, bf16[648,128]{1,0:T(8,128)(2,1)S(1)}, bf16[216,128]{1,0:T(8,128)(2,1)S(1)}, bf16[216,128]{1,0:T(8,128)(2,1)S(1)}) custom-call(bf16[4,6,24,192]{3,2,1,0:T(8,128)(2,1)S(1)} %copy-done.1, bf16[4,6,24,192]{3,2,1,0:T(8,128)(2,1)S(1)} %copy-done.3, ...), custom_call_target="tpu_custom_call" | custom-call | tf_op jit(solution)/shard_map/block/pallas_call | solution.py:542
  31.7 8.4 %all_to_all.15.parts_ref = bf16[4,36,276]{2,1,0:T(8,128)(2,1)S(1)} all-to-all(bf16[4,36,276]{2,1,0:T(8,128)(2,1)S(1)} %get-tuple-element.27), channel_id=1, replica_groups={{0,1,2,3},{4,5,6,7},{8,9,10,11},{12,13,14,15},{16,17,18,19},{20,21,22,2..., dimensions={0} | all-to-all | bytes 158976 | tf_op jit(solution)/shard_map/all_to_all | solution.py:446
  40.1 0.7 %add.2 = bf16[8,36,276]{2,1,0:T(8,128)(2,1)} custom-call(bf16[4,36,276]{2,1,0:T(8,128)(2,1)S(1)} %all_to_all.15.parts_ref), custom_call_target="tpu_custom_call" | custom-call | tf_op jit(solution)/shard_map/add/pallas_call | solution.py:450
  40.8 4.0 %all-to-all-start.1 = ((bf16[8,36,276]{2,1,0:T(8,128)(2,1)}), bf16[8,36,276]{2,1,0:T(8,128)(2,1)S(1)}, u32[]{:S(2)}, u32[]{:S(2)}) async-start(bf16[8,36,276]{2,1,0:T(8,128)(2,1)} %add.2), calls=%async_computation.1 | async-start | bytes 491520 | tf_op jit(solution)/shard_map/all_to_all | solution.py:446
  44.8 2.4 %collective-permute-start.3 = (bf16[648,128]{1,0:T(8,128)(2,1)S(1)}, bf16[648,128]{1,0:T(8,128)(2,1)S(1)}, u32[]{:S(2)}, u32[]{:S(2)}) collective-permute-start(bf16[648,128]{1,0:T(8,128)(2,1)S(1)} %get-tuple-element.31), channel_id=1, source_target_pairs={{0,32},{1,33},{2,34},{3,35},{4,36},{5,37},{6,38},{7,39},{8,40},{9,... | collective-permute-start | bytes 497672 | tf_op jit(solution)/shard_map/ppermute | solution.py:43
  47.2 8.8 %all-to-all-done.1.parts_ref = bf16[8,36,276]{2,1,0:T(8,128)(2,1)S(1)} async-done(((bf16[8,36,276]{2,1,0:T(8,128)(2,1)}), bf16[8,36,276]{2,1,0:T(8,128)(2,1)S(1)}, u32[]{:S(2)}, u32[]{:S(2)}) %all-to-all-start.1) | async-done | bytes 159008 | tf_op jit(solution)/shard_map/all_to_all | solution.py:446
  56.0 0.7 add.3
  56.7 3.3 %all-to-all-start.2 = ((bf16[4,36,276]{2,1,0:T(8,128)(2,1)}), bf16[4,36,276]{2,1,0:T(8,128)(2,1)S(1)}, u32[]{:S(2)}, u32[]{:S(2)}) async-start(bf16[4,36,276]{2,1,0:T(8,128)(2,1)} %add.3), calls=%async_computation.2 | async-start | bytes 245760 | tf_op jit(solution)/shard_map/all_to_all | solution.py:446
  60.0 2.5 %collective-permute-start.4 = (bf16[216,128]{1,0:T(8,128)(2,1)S(1)}, bf16[216,128]{1,0:T(8,128)(2,1)S(1)}, u32[]{:S(2)}, u32[]{:S(2)}) collective-permute-start(bf16[216,128]{1,0:T(8,128)(2,1)S(1)} %get-tuple-element.32), channel_id=1, source_target_pairs={{0,33},{1,34},{2,35},{3,36},{4,37},{5,38},{6,39},{7,40},{8,41},{9,... | collective-permute-start | bytes 165896 | tf_op jit(solution)/shard_map/ppermute | solution.py:43
  62.5 2.7 %collective-permute-start.5 = (bf16[216,128]{1,0:T(8,128)(2,1)S(1)}, bf16[216,128]{1,0:T(8,128)(2,1)S(1)}, u32[]{:S(2)}, u32[]{:S(2)}) collective-permute-start(bf16[216,128]{1,0:T(8,128)(2,1)S(1)} %get-tuple-element.33), channel_id=1, source_target_pairs={{0,1},{1,2},{2,3},{3,4},{4,5},{5,6},{6,7},{7,8},{8,9},{9,10},{10,1... | collective-permute-start | bytes 165896 | tf_op jit(solution)/shard_map/ppermute | solution.py:43
  65.1 2.7 %collective-permute-done.4.diag_ref = bf16[216,128]{1,0:T(8,128)(2,1)S(1)} collective-permute-done((bf16[216,128]{1,0:T(8,128)(2,1)S(1)}, bf16[216,128]{1,0:T(8,128)(2,1)S(1)}, u32[]{:S(2)}, u32[]{:S(2)}) %collective-permute-start.4) | collective-permute-done | bytes 55328 | tf_op jit(solution)/shard_map/ppermute | solution.py:43
  67.9 1.8 %collective-permute-done.5.lon_ref = bf16[216,128]{1,0:T(8,128)(2,1)S(1)} collective-permute-done((bf16[216,128]{1,0:T(8,128)(2,1)S(1)}, bf16[216,128]{1,0:T(8,128)(2,1)S(1)}, u32[]{:S(2)}, u32[]{:S(2)}) %collective-permute-start.5) | collective-permute-done | bytes 55328 | tf_op jit(solution)/shard_map/ppermute | solution.py:43
  69.7 0.9 %finish.1 = (bf16[4,6,24,192]{3,2,1,0:T(8,128)(2,1)}, bf16[4,6,24,192]{3,2,1,0:T(8,128)(2,1)}) custom-call(bf16[2,4,3,18,192]{4,3,2,1,0:T(8,128)(2,1)S(1)} %get-tuple-element.26.own_ref, bf16[648,128]{1,0:T(8,128)(2,1)S(1)} %collective-permute-done.3.lat_ref, bf16[216,128]{1,0:T(8,128)(2,1)S(1)} %collective-permute-done.4.diag_ref, ...), custom_call_target="tpu_custom_call" | custom-call | tf_op jit(solution)/shard_map/finish/pallas_call | solution.py:594
  70.6 0.8 %unpack.1 = f32[12,1,3312]{2,1,0:T(1,128)} custom-call(bf16[4,36,276]{2,1,0:T(8,128)(2,1)S(1)} %all-to-all-done.2.grad_ref), custom_call_target="tpu_custom_call" | custom-call | tf_op jit(solution)/shard_map/unpack/pallas_call | solution.py:584
  (39 shorter events, 1.2 us)
Async XLA Ops:
  0.6 1.0 %copy-start = (bf16[4,6,24,192]{3,2,1,0:T(8,128)(2,1)S(1)}, bf16[4,6,24,192]{3,2,1,0:T(8,128)(2,1)}, u32[]{:S(2)}) copy-start(bf16[4,6,24,192]{3,2,1,0:T(8,128)(2,1)} %field_ref.5) | copy-start | bytes 663556
  1.6 1.0 %copy-start.2 = (bf16[4,6,24,192]{3,2,1,0:T(8,128)(2,1)S(1)}, bf16[4,6,24,192]{3,2,1,0:T(8,128)(2,1)}, u32[]{:S(2)}) copy-start(bf16[4,6,24,192]{3,2,1,0:T(8,128)(2,1)} %cot_ref.5) | copy-start | bytes 663556
  2.6 10.0 %copy-start.7 = (bf16[192,576]{1,0:T(8,128)(2,1)S(1)}, bf16[192,576]{1,0:T(8,128)(2,1)}, u32[]{:S(2)}) copy-start(bf16[192,576]{1,0:T(8,128)(2,1)} %wqkv_ref.1) | copy-start | bytes 663556
  2.6 10.0 %copy-start.10 = (f32[2,1,6,3312]{3,1,2,0:T(1,128)S(1)}, f32[2,1,6,3312]{3,1,2,0:T(1,128)}, u32[]{:S(2)}) copy-start(f32[2,1,6,3312]{3,1,2,0:T(1,128)} %param.25) | copy-start | bytes 476932
  2.6 14.2 %copy-start.8 = (bf16[288,288]{1,0:T(8,128)(2,1)S(1)}, bf16[288,288]{1,0:T(8,128)(2,1)}, u32[]{:S(2)}) copy-start(bf16[288,288]{1,0:T(8,128)(2,1)} %constant.17.clone.perm_t_ref) | copy-start | bytes 497668
  2.6 14.2 %copy-start.9 = (bf16[288,288]{1,0:T(8,128)(2,1)S(1)}, bf16[288,288]{1,0:T(8,128)(2,1)}, u32[]{:S(2)}) copy-start(bf16[288,288]{1,0:T(8,128)(2,1)} %constant.15.clone.perm_ref) | copy-start | bytes 497668
  2.8 9.7 %copy-start.4 = (bf16[276,276]{1,0:T(8,128)(2,1)S(1)}, bf16[276,276]{1,0:T(8,128)(2,1)}, u32[]{:S(2)}) copy-start(bf16[276,276]{1,0:T(8,128)(2,1)} %constant.12.clone.table_perm_ref) | copy-start | bytes 457060
  2.8 13.9 %collective-permute-start.1 = (bf16[648,128]{1,0:T(8,128)(2,1)S(1)}, bf16[648,128]{1,0:T(8,128)(2,1)S(1)}, u32[]{:S(2)}, u32[]{:S(2)}) collective-permute-start(bf16[648,128]{1,0:T(8,128)(2,1)S(1)} %pack_lat.1.after_ref), channel_id=1, source_target_pairs={{0,224},{1,225},{2,226},{3,227},{4,228},{5,229},{6,230},{7,231},{8... | collective-permute-start | bytes 497672 | tf_op jit(solution)/shard_map/ppermute | solution.py:43
  4.8 12.1 %copy-start.5 = (bf16[192,768]{1,0:T(8,128)(2,1)S(1)}, bf16[192,768]{1,0:T(8,128)(2,1)}, u32[]{:S(2)}) copy-start(bf16[192,768]{1,0:T(8,128)(2,1)} %wup_ref.1) | copy-start | bytes 884740
  4.8 12.1 %copy-start.6 = (bf16[768,192]{0,1:T(8,128)(2,1)S(1)}, bf16[768,192]{0,1:T(8,128)(2,1)}, u32[]{:S(2)}) copy-start(bf16[768,192]{0,1:T(8,128)(2,1)} %param.24) | copy-start | bytes 884740
  4.9 11.9 %collective-permute-start = (bf16[216,128]{1,0:T(8,128)(2,1)S(1)}, bf16[216,128]{1,0:T(8,128)(2,1)S(1)}, u32[]{:S(2)}, u32[]{:S(2)}) collective-permute-start(bf16[216,128]{1,0:T(8,128)(2,1)S(1)} %get-tuple-element.20), channel_id=1, source_target_pairs={{0,31},{1,0},{2,1},{3,2},{4,3},{5,4},{6,5},{7,6},{8,7},{9,8},{10,9... | collective-permute-start | bytes 165896 | tf_op jit(solution)/shard_map/ppermute | solution.py:43
  12.3 4.5 %collective-permute-start.2 = (bf16[216,128]{1,0:T(8,128)(2,1)S(1)}, bf16[216,128]{1,0:T(8,128)(2,1)S(1)}, u32[]{:S(2)}, u32[]{:S(2)}) collective-permute-start(bf16[216,128]{1,0:T(8,128)(2,1)S(1)} %get-tuple-element.21), channel_id=1, source_target_pairs={{0,255},{1,224},{2,225},{3,226},{4,227},{5,228},{6,229},{7,230},{8... | collective-permute-start | bytes 165896 | tf_op jit(solution)/shard_map/ppermute | solution.py:43
  12.5 0.9 %copy-start.11 = (bf16[192,192]{1,0:T(8,128)(2,1)S(1)}, bf16[192,192]{1,0:T(8,128)(2,1)}, u32[]{:S(2)}) copy-start(bf16[192,192]{1,0:T(8,128)(2,1)} %constant.13.clone.row_perm_ref) | copy-start | bytes 221188
  13.4 0.7 copy-start.14
  14.1 2.7 %copy-start.1 = (bf16[4,6,24,192]{3,2,1,0:T(8,128)(2,1)S(1)}, bf16[4,6,24,192]{3,2,1,0:T(8,128)(2,1)}, u32[]{:S(2)}) copy-start(bf16[4,6,24,192]{3,2,1,0:T(8,128)(2,1)} %field_ref.5) | copy-start | bytes 663556
  14.1 2.7 %copy-start.3 = (bf16[4,6,24,192]{3,2,1,0:T(8,128)(2,1)S(1)}, bf16[4,6,24,192]{3,2,1,0:T(8,128)(2,1)}, u32[]{:S(2)}) copy-start(bf16[4,6,24,192]{3,2,1,0:T(8,128)(2,1)} %cot_ref.5) | copy-start | bytes 663556
  14.1 2.7 %copy-start.13 = (bf16[72,96]{1,0:T(8,128)(2,1)S(1)}, bf16[72,96]{1,0:T(8,128)(2,1)}, u32[]{:S(2)}) copy-start(bf16[72,96]{1,0:T(8,128)(2,1)} %constant.16.clone.chunk_perm_ref) | copy-start | bytes 41476
  14.1 2.7 %copy-start.17 = (f32[192]{0:T(256)S(1)}, f32[192]{0:T(256)}, u32[]{:S(2)}) copy-start(f32[192]{0:T(256)} %param.22) | copy-start | bytes 2308
  17.5 0.9 %copy-start.12 = (bf16[192,192]{1,0:T(8,128)(2,1)S(1)}, bf16[192,192]{1,0:T(8,128)(2,1)}, u32[]{:S(2)}) copy-start(bf16[192,192]{1,0:T(8,128)(2,1)} %wproj_ref.1) | copy-start | bytes 221188
  40.8 15.1 %all-to-all-start.1 = ((bf16[8,36,276]{2,1,0:T(8,128)(2,1)}), bf16[8,36,276]{2,1,0:T(8,128)(2,1)S(1)}, u32[]{:S(2)}, u32[]{:S(2)}) async-start(bf16[8,36,276]{2,1,0:T(8,128)(2,1)} %add.2), calls=%async_computation.1 | async-start | bytes 491520 | tf_op jit(solution)/shard_map/all_to_all | solution.py:446
  44.8 24.9 %collective-permute-start.3 = (bf16[648,128]{1,0:T(8,128)(2,1)S(1)}, bf16[648,128]{1,0:T(8,128)(2,1)S(1)}, u32[]{:S(2)}, u32[]{:S(2)}) collective-permute-start(bf16[648,128]{1,0:T(8,128)(2,1)S(1)} %get-tuple-element.31), channel_id=1, source_target_pairs={{0,32},{1,33},{2,34},{3,35},{4,36},{5,37},{6,38},{7,39},{8,40},{9,... | collective-permute-start | bytes 497672 | tf_op jit(solution)/shard_map/ppermute | solution.py:43
  56.7 13.9 %all-to-all-start.2 = ((bf16[4,36,276]{2,1,0:T(8,128)(2,1)}), bf16[4,36,276]{2,1,0:T(8,128)(2,1)S(1)}, u32[]{:S(2)}, u32[]{:S(2)}) async-start(bf16[4,36,276]{2,1,0:T(8,128)(2,1)} %add.3), calls=%async_computation.2 | async-start | bytes 245760 | tf_op jit(solution)/shard_map/all_to_all | solution.py:446
  60.0 7.9 %collective-permute-start.4 = (bf16[216,128]{1,0:T(8,128)(2,1)S(1)}, bf16[216,128]{1,0:T(8,128)(2,1)S(1)}, u32[]{:S(2)}, u32[]{:S(2)}) collective-permute-start(bf16[216,128]{1,0:T(8,128)(2,1)S(1)} %get-tuple-element.32), channel_id=1, source_target_pairs={{0,33},{1,34},{2,35},{3,36},{4,37},{5,38},{6,39},{7,40},{8,41},{9,... | collective-permute-start | bytes 165896 | tf_op jit(solution)/shard_map/ppermute | solution.py:43
  62.5 7.2 %collective-permute-start.5 = (bf16[216,128]{1,0:T(8,128)(2,1)S(1)}, bf16[216,128]{1,0:T(8,128)(2,1)S(1)}, u32[]{:S(2)}, u32[]{:S(2)}) collective-permute-start(bf16[216,128]{1,0:T(8,128)(2,1)S(1)} %get-tuple-element.33), channel_id=1, source_target_pairs={{0,1},{1,2},{2,3},{3,4},{4,5},{5,6},{6,7},{7,8},{8,9},{9,10},{10,1... | collective-permute-start | bytes 165896 | tf_op jit(solution)/shard_map/ppermute | solution.py:43
  (3 other events, 2.0 us)

commit v7 on v6

--- a/solution.py
+++ b/solution.py
@@ -2,7 +2,6 @@
 
 import jax
 import jax.numpy as jnp
-import numpy as np
 from jax import lax
 from jax.experimental import pallas as pl
 from jax.experimental.pallas import tpu as pltpu
@@ -22,6 +21,8 @@
 ROWS = HEADS * POS
 SLOTS = 16
 QUARTER = PAIR * HEADS // 2
+REST = 20
+DENSE = 80
 LANES = 128
 
 epsilon = 1e-05
@@ -85,6 +86,60 @@
 
 def spread_heads(rows, head_mask):
     return jnp.concatenate([rows * head_mask[h : h + 1, :] for h in range(HEADS)], axis=0)
+
+
+def quotient(values, divisor):
+    return (values * (2**20 // divisor + 1)) >> 20
+
+
+def one_hot(rows, columns, target):
+    row = lax.broadcasted_iota(jnp.int32, (rows, columns), 0)
+    column = lax.broadcasted_iota(jnp.int32, (rows, columns), 1)
+    return (column == target(row)).astype(f32).astype(bf16)
+
+
+def window_order():
+    def target(row):
+        c = (row >= POS).astype(jnp.int32)
+        row = row - POS * c
+        j = quotient(row, PAIR)
+        return (row - PAIR * j) * (2 * WLON) + c * WLON + j
+
+    return one_hot(2 * POS, 2 * POS, target)
+
+
+def natural_order():
+    def target(row):
+        pair = quotient(row, 2 * WLON)
+        lon = row - 2 * WLON * pair
+        c = (lon >= WLON).astype(jnp.int32)
+        return c * POS + (lon - WLON * c) * PAIR + pair
+
+    return one_hot(2 * POS, 2 * POS, target)
+
+
+def table_order():
+    def target(row):
+        pair = quotient(row, SPREAD)
+        return (SPREAD - 1 - (row - SPREAD * pair)) * PAIR + pair
+
+    return one_hot(TAB, TAB, target)
+
+
+def chunk_order():
+    def target(row):
+        pair = quotient(row, HEADS)
+        return (row - HEADS * pair) * SLOTS + pair
+
+    return one_hot(PAIR * HEADS, HEADS * SLOTS, target)
+
+
+def row_order():
+    def target(row):
+        head = quotient(row, SLOTS)
+        return (row - SLOTS * head) * SLOTS + head
+
+    return one_hot(2 * HEADS * SLOTS, PAIR * SLOTS, target)
 
 
 def put(packed, t, row, slab):
@@ -152,11 +207,6 @@
     label_row_ref,
     label_col_ref,
     keep_ref,
-    perm_ref,
-    head_mask_ref,
-    table_perm_ref,
-    chunk_perm_ref,
-    perm_t_ref,
     fold_out,
     own_out,
     lat_out,
@@ -164,6 +214,7 @@
     lon_out,
     frame,
     wide,
+    dense,
     lat_buf,
     diag_buf,
     lon_buf,
@@ -198,9 +249,14 @@
     wq_t = wqkv_t_ref[0:C, :]
     wk_t = wqkv_t_ref[C : 2 * C, :]
     wv_t = wqkv_t_ref[2 * C : 3 * C, :]
-    head_mask = head_mask_ref[...]
-    perm = perm_ref[...]
-    perm_t = perm_t_ref[...]
+    head = lax.broadcasted_iota(jnp.int32, (HEADS, C), 0)
+    head_mask = (lax.broadcasted_iota(jnp.int32, (HEADS, C), 1) >> 5) == head
+    head_mask = head_mask.astype(f32).astype(bf16)
+    perm = window_order()
+    perm_t = natural_order()
+    table_perm = table_order()
+    chunk_perm = chunk_order()
+    dense[...] = jnp.zeros_like(dense)
     for n in range(2):
         both = slice(n * 2 * POS, (n + 1) * 2 * POS)
         x = mm(perm, frame[0, both, :].astype(bf16))
@@ -267,10 +323,15 @@
             total = piece if total is None else total + piece
         total = jnp.concatenate([total, jnp.zeros((HEADS, SLOTS - PAIR, TAB), f32)], axis=1)
         total = total.reshape(HEADS * SLOTS, TAB).astype(bf16)
-        total = mm_nt(total, table_perm_ref[...]).astype(bf16)
-        total = mm(chunk_perm_ref[...], total)
-        fold_out[2 * n] = total[:QUARTER].astype(bf16)
-        fold_out[2 * n + 1] = total[QUARTER:].astype(bf16)
+        total = mm_nt(total, table_perm).astype(bf16)
+        total = mm(chunk_perm, total)
+        for k in range(2):
+            part = total[k * QUARTER : (k + 1) * QUARTER]
+            dense[:QUARTER, :] = part[:, :LANES]
+            dense[QUARTER : 2 * QUARTER, :] = part[:, LANES : 2 * LANES]
+            rest = [part[HEADS * g : HEADS * (g + 1), 2 * LANES :] for g in range(WLAT)]
+            dense[2 * QUARTER : 2 * QUARTER + HEADS, : WLAT * REST] = jnp.concatenate(rest, axis=1)
+            fold_out[2 * n + k] = dense[...].astype(bf16)
         grad_h1 = jnp.concatenate(grad_h1, axis=0).astype(bf16).astype(f32)
         grad_field = (grad_sum + norm_back(grad_h1, gain1, normed1, inverse1)).astype(bf16)
         for t, value in enumerate((result, grad_field)):
@@ -294,8 +355,6 @@
 
 def prepare_kernel(
     table_ref,
-    table_perm_ref,
-    row_perm_ref,
     region_ref,
     wqkv_ref,
     bias_out,
@@ -317,7 +376,7 @@
         marks[4 * i : 4 * (i + 1), :] = (4 * region_ref[i] + wrapped).astype(f32)
     place = lax.broadcasted_iota(jnp.int32, (POS, 4 * WLAT), 0)
     lane = lax.broadcasted_iota(jnp.int32, (POS, 4 * WLAT), 1)
-    lon = (place * 43691) >> 19
+    lon = quotient(place, PAIR)
     pair = place - PAIR * lon
     upper = (pair >= WLAT).astype(jnp.int32)
     source = 4 * (pair - WLAT * upper) + upper
@@ -344,12 +403,13 @@
             row = (a * WLAT + c) * SLOTS
             rows[row : row + 2 * HEADS, :] = jnp.concatenate(pieces, axis=1)
     left = rows[...]
-    perm = table_perm_ref[...]
+    perm = table_order()
+    row_perm = row_order()
     total = None
     for _ in range(3):
         low = left.astype(bf16)
         left = left - low.astype(f32)
-        term = mm(row_perm_ref[...], mm(low, perm).astype(bf16))
+        term = mm(row_perm, mm(low, perm).astype(bf16))
         total = term if total is None else total + term
     total = total.reshape(2 * HEADS, SLOTS, TAB)
     for o in range(WLON):
@@ -362,7 +422,14 @@
 def unpack_kernel(grad_ref, table_out, flat):
     part = PAIR // WZ * SPREAD
     for n in range(2):
-        halves = [grad_ref[2 * n + k].astype(f32) for k in range(2)]
+        halves = []
+        for k in range(2):
+            dense = grad_ref[2 * n + k].astype(f32)
+            rest = dense[2 * QUARTER : 2 * QUARTER + HEADS]
+            rest = [rest[:, g * REST : (g + 1) * REST] for g in range(WLAT)]
+            rest = jnp.concatenate(rest, axis=0)
+            parts = [dense[:QUARTER], dense[QUARTER : 2 * QUARTER], rest]
+            halves.append(jnp.concatenate(parts, axis=1))
         for a in range(WZ):
             for c in range(WLAT):
                 row = c * HEADS
@@ -404,40 +471,7 @@
                 target[z, half + i] = jnp.concatenate([slab, own], axis=0).astype(bf16)
 
 
-def window_order():
-    perm = np.zeros((2 * POS, 2 * POS), np.float32)
-    for c in range(2):
-        for j in range(WLON):
-            for d in range(PAIR):
-                perm[c * POS + j * PAIR + d, d * 2 * WLON + c * WLON + j] = 1.0
-    return perm
-
-
-def table_order():
-    perm = np.zeros((TAB, TAB), np.float32)
-    for d in range(PAIR):
-        for r in range(SPREAD):
-            perm[d * SPREAD + r, (SPREAD - 1 - r) * PAIR + d] = 1.0
-    return perm
-
-
-def chunk_order():
-    perm = np.zeros((PAIR * HEADS, HEADS * SLOTS), np.float32)
-    for h in range(HEADS):
-        for k in range(PAIR):
-            perm[k * HEADS + h, h * SLOTS + k] = 1.0
-    return perm
-
-
-def row_order():
-    perm = np.zeros((2 * HEADS * SLOTS, PAIR * SLOTS), np.float32)
-    for h in range(2 * HEADS):
-        for k in range(PAIR):
-            perm[h * SLOTS + k, k * SLOTS + h] = 1.0
-    return perm
-
-
-def lon_sum(quarters, after):
+def lon_sum(quarters, strips):
     lons = lax.axis_size("lon")
     near = [[4 * k + j for j in range(4)] for k in range(lons // 4)]
     far = [[4 * k + j for k in range(lons // 4)] for j in range(4)]
@@ -457,9 +491,12 @@
         )(parts)
 
     parts = added(exchange(quarters, near), lons // 4)
-    parts, after = lax.optimization_barrier((parts, after))
+    parts, strips = lax.optimization_barrier((parts, strips))
+    steps = ((1, 0), (1, 1), (0, 1))
+    strips = [shifted(strip, *step) for strip, step in zip(strips, steps)]
     parts = exchange(parts, far)
-    return exchange(added(parts, 4), near), after
+    parts, strips = lax.optimization_barrier((added(parts, 4), strips))
+    return exchange(parts, near), strips
 
 
 def body(
@@ -508,9 +545,6 @@
     diag_part = shifted(diag_part, -1, -1)
     lon_part = shifted(lon_part, 0, -1)
 
-    perm = window_order()
-    head_mask = np.repeat(np.eye(HEADS, dtype=np.float32), HD, axis=1)
-    table_perm = jnp.asarray(table_order(), bf16)
     bias_wide, label_row, label_col, weights_t = pl.pallas_call(
         prepare_kernel,
         out_shape=(
@@ -519,7 +553,7 @@
             jax.ShapeDtypeStruct((POS, 4), f32),
             jax.ShapeDtypeStruct((3 * C, C), bf16),
         ),
-        in_specs=[vmem] * 5,
+        in_specs=[vmem] * 3,
         out_specs=(vmem,) * 4,
         scratch_shapes=[
             pltpu.VMEM((2 * HEADS, PAIR * TAB), f32),
@@ -531,26 +565,24 @@
         name="prepare",
     )(
         bias_table.reshape(2 * HEADS, 1, PAIR * TAB),
-        table_perm,
-        jnp.asarray(row_order(), bf16),
         region_ids.transpose(1, 0, 2),
         w_qkv,
     )
     positions = levels * lat_rows * lon_cols
     gain1 = ln1_gain.reshape(1, C)
-    head_mask = jnp.asarray(head_mask, bf16)
     fold, own, *strips = pl.pallas_call(
         block_kernel,
         out_shape=(
-            jax.ShapeDtypeStruct((4, QUARTER, TAB), bf16),
+            jax.ShapeDtypeStruct((4, DENSE, LANES), bf16),
             jax.ShapeDtypeStruct((2, levels, half, inner, C), bf16),
         )
         + packed,
-        in_specs=[vmem] * 14 + [smem] + [vmem] * 5,
+        in_specs=[vmem] * 14 + [smem],
         out_specs=(vmem,) * 5,
         scratch_shapes=[
             pltpu.VMEM((2, positions, C), f32),
             pltpu.VMEM((HEADS, POS, POS), f32),
+            pltpu.VMEM((DENSE, LANES), f32),
         ]
         + buffers,
         compiler_params=params,
@@ -571,16 +603,8 @@
         label_row,
         label_col,
         keep_flags,
-        jnp.asarray(perm, bf16),
-        head_mask,
-        table_perm,
-        jnp.asarray(chunk_order(), bf16),
-        jnp.asarray(perm.T, bf16),
     )
     grads, (lat_back, diag_back, lon_back) = lon_sum(fold, strips)
-    lat_back = shifted(lat_back, 1, 0)
-    diag_back = shifted(diag_back, 1, 1)
-    lon_back = shifted(lon_back, 0, 1)
     grads = pl.pallas_call(
         unpack_kernel,
         out_shape=jax.ShapeDtypeStruct((2 * HEADS, 1, PAIR * TAB), f32),

time: 72 us -> 64.6 us (0.90)
  the two profiles are of different devices: /device:TPU:6 before, /device:TPU:1 now
where the time goes in v7:
time: 64.6 us; the launch traced here: 64.3 us
  starting transfers between devices  23.3 us (36%)
  Pallas kernels  18.1 us (28%)
  waiting for transfers between devices  11.2 us (17%)
  blocking collectives  8.35 us (13%)
  local copies, waits for them, and re-layouts  2.56 us (4%)
  between operations  0.79 us (1%)
    ppermute x6, starting transfers between devices, shifted(): return lax.ppermute(block, ('lat', 'lon'), route)  14.1 us
    pallas_call x1, Pallas kernels, body(): pl.pallas_call(block_kernel, out_shape=(jax.ShapeDtypeStruct((4, DENSE, L...  12 us
    all_to_all x2, waiting for transfers between devices, exchange(): return lax.all_to_all(parts, 'lon', 0, 0, axis_index_groups=groups)  10.7 us
    all_to_all x2, starting transfers between devices, exchange(): return lax.all_to_all(parts, 'lon', 0, 0, axis_index_groups=groups)  9.15 us
    all_to_all x1, blocking collectives, exchange(): return lax.all_to_all(parts, 'lon', 0, 0, axis_index_groups=groups)  8.35 us
    pallas_call x1, Pallas kernels, body(): pl.pallas_call(prepare_kernel, out_shape=(jax.ShapeDtypeStruct((2, POS, R...  2.6 us
    unnamed x26, local copies, waits for them, and re-layouts  2.56 us
    pallas_call x2, Pallas kernels, added(): pl.pallas_call(add_kernel, out_shape=jax.ShapeDtypeStruct((copies,) + par...  1.34 us
  transfers between devices with their start and end apart: 8, of which 3 were waited for; matrix products, arithmetic and copies ran while one was open for 0% of the time, Pallas kernels for 7%

profile of v7, /device:TPU:1, one launch (start us, length us, event | category | flops | bytes accessed | tf_op | source)
XLA Modules:
  0.0 64.3 jit_solution(1095739156951117169)
XLA Ops:
  0.6 1.0 %copy-done = bf16[4,6,24,192]{3,2,1,0:T(8,128)(2,1)S(1)} copy-done((bf16[4,6,24,192]{3,2,1,0:T(8,128)(2,1)S(1)}, bf16[4,6,24,192]{3,2,1,0:T(8,128)(2,1)}, u32[]{:S(2)}) %copy-start) | copy-done | bytes 221208
  1.6 1.0 %copy-done.2 = bf16[4,6,24,192]{3,2,1,0:T(8,128)(2,1)S(1)} copy-done((bf16[4,6,24,192]{3,2,1,0:T(8,128)(2,1)S(1)}, bf16[4,6,24,192]{3,2,1,0:T(8,128)(2,1)}, u32[]{:S(2)}) %copy-start.2) | copy-done | bytes 221208
  2.6 0.2 pack_lat.1.after_ref
  2.8 0.0 copy-start.9
  2.8 4.4 %collective-permute-start.1 = (bf16[648,128]{1,0:T(8,128)(2,1)S(1)}, bf16[648,128]{1,0:T(8,128)(2,1)S(1)}, u32[]{:S(2)}, u32[]{:S(2)}) collective-permute-start(bf16[648,128]{1,0:T(8,128)(2,1)S(1)} %pack_lat.1.after_ref), channel_id=1, source_target_pairs={{0,224},{1,225},{2,226},{3,227},{4,228},{5,229},{6,230},{7,231},{8... | collective-permute-start | bytes 497672 | tf_op jit(solution)/shard_map/ppermute | solution.py:44
  7.2 0.1 pack_edge.1
  7.3 0.0 copy-start.1
  7.3 1.0 %collective-permute-start = (bf16[216,128]{1,0:T(8,128)(2,1)S(1)}, bf16[216,128]{1,0:T(8,128)(2,1)S(1)}, u32[]{:S(2)}, u32[]{:S(2)}) collective-permute-start(bf16[216,128]{1,0:T(8,128)(2,1)S(1)} %get-tuple-element.24), channel_id=1, source_target_pairs={{0,31},{1,0},{2,1},{3,2},{4,3},{5,4},{6,5},{7,6},{8,7},{9,8},{10,9... | collective-permute-start | bytes 165896 | tf_op jit(solution)/shard_map/ppermute | solution.py:44
  8.4 7.1 %collective-permute-start.2 = (bf16[216,128]{1,0:T(8,128)(2,1)S(1)}, bf16[216,128]{1,0:T(8,128)(2,1)S(1)}, u32[]{:S(2)}, u32[]{:S(2)}) collective-permute-start(bf16[216,128]{1,0:T(8,128)(2,1)S(1)} %get-tuple-element.25), channel_id=1, source_target_pairs={{0,255},{1,224},{2,225},{3,226},{4,227},{5,228},{6,229},{7,230},{8... | collective-permute-start | bytes 165896 | tf_op jit(solution)/shard_map/ppermute | solution.py:44
  15.5 2.6 %prepare.1 = (f32[2,144,864]{2,1,0:T(8,128)S(1)}, f32[4,864]{1,0:T(4,128)S(1)}, f32[144,4]{1,0:T(8,128)S(1)}, bf16[576,192]{1,0:T(8,128)(2,1)S(1)}) custom-call(f32[12,1,3312]{2,1,0:T(1,128)S(1)} %bitcast.7, s32[6,4,24]{2,1,0:T(4,128)S(1)} %bitcast.8, bf16[192,576]{1,0:T(8,128)(2,1)S(1)} %copy-done.6), custom_call_target="tpu_custom_call" | custom-call | tf_op jit(solution)/shard_map/prepare/pallas_call | solution.py:548
  18.2 0.6 copy-done.10
  18.8 12.0 %block.1 = (bf16[4,80,128]{2,1,0:T(8,128)(2,1)S(1)}, bf16[2,4,3,18,192]{4,3,2,1,0:T(8,128)(2,1)S(1)}, bf16[648,128]{1,0:T(8,128)(2,1)S(1)}, bf16[216,128]{1,0:T(8,128)(2,1)S(1)}, bf16[216,128]{1,0:T(8,128)(2,1)S(1)}) custom-call(bf16[4,6,24,192]{3,2,1,0:T(8,128)(2,1)S(1)} %copy-done.1, bf16[4,6,24,192]{3,2,1,0:T(8,128)(2,1)S(1)} %copy-done.3, ...), custom_call_target="tpu_custom_call" | custom-call | tf_op jit(solution)/shard_map/block/pallas_call | solution.py:573
  30.8 8.4 %all_to_all.15.parts_ref = bf16[4,80,128]{2,1,0:T(8,128)(2,1)S(1)} all-to-all(bf16[4,80,128]{2,1,0:T(8,128)(2,1)S(1)} %get-tuple-element.31), channel_id=1, replica_groups={{0,1,2,3},{4,5,6,7},{8,9,10,11},{12,13,14,15},{16,17,18,19},{20,21,22,2..., dimensions={0} | all-to-all | bytes 163840 | tf_op jit(solution)/shard_map/all_to_all | solution.py:480
  39.1 0.7 %add.2 = bf16[8,80,128]{2,1,0:T(8,128)(2,1)} custom-call(bf16[4,80,128]{2,1,0:T(8,128)(2,1)S(1)} %all_to_all.15.parts_ref), custom_call_target="tpu_custom_call" | custom-call | tf_op jit(solution)/shard_map/add/pallas_call | solution.py:484
  39.8 4.0 %all-to-all-start.1 = ((bf16[8,80,128]{2,1,0:T(8,128)(2,1)}), bf16[8,80,128]{2,1,0:T(8,128)(2,1)S(1)}, u32[]{:S(2)}, u32[]{:S(2)}) async-start(bf16[8,80,128]{2,1,0:T(8,128)(2,1)} %add.2), calls=%async_computation.1 | async-start | bytes 327680 | tf_op jit(solution)/shard_map/all_to_all | solution.py:480
  43.9 1.0 %collective-permute-start.4 = (bf16[216,128]{1,0:T(8,128)(2,1)S(1)}, bf16[216,128]{1,0:T(8,128)(2,1)S(1)}, u32[]{:S(2)}, u32[]{:S(2)}) collective-permute-start(bf16[216,128]{1,0:T(8,128)(2,1)S(1)} %get-tuple-element.37), channel_id=1, source_target_pairs={{0,33},{1,34},{2,35},{3,36},{4,37},{5,38},{6,39},{7,40},{8,41},{9,... | collective-permute-start | bytes 165896 | tf_op jit(solution)/shard_map/ppermute | solution.py:44
  44.8 0.6 collective-permute-start.5
  45.5 6.8 %all-to-all-done.1.parts_ref = bf16[8,80,128]{2,1,0:T(8,128)(2,1)S(1)} async-done(((bf16[8,80,128]{2,1,0:T(8,128)(2,1)}), bf16[8,80,128]{2,1,0:T(8,128)(2,1)S(1)}, u32[]{:S(2)}, u32[]{:S(2)}) %all-to-all-start.1) | async-done | bytes 163872 | tf_op jit(solution)/shard_map/all_to_all | solution.py:480
  52.2 0.7 %add.3 = bf16[4,80,128]{2,1,0:T(8,128)(2,1)} custom-call(bf16[8,80,128]{2,1,0:T(8,128)(2,1)S(1)} %all-to-all-done.1.parts_ref), custom_call_target="tpu_custom_call" | custom-call | tf_op jit(solution)/shard_map/add/pallas_call | solution.py:484
  52.9 0.5 collective-permute-done.4.diag_ref
  53.4 5.1 %all-to-all-start.2 = ((bf16[4,80,128]{2,1,0:T(8,128)(2,1)}), bf16[4,80,128]{2,1,0:T(8,128)(2,1)S(1)}, u32[]{:S(2)}, u32[]{:S(2)}) async-start(bf16[4,80,128]{2,1,0:T(8,128)(2,1)} %add.3), calls=%async_computation.2 | async-start | bytes 163840 | tf_op jit(solution)/shard_map/all_to_all | solution.py:480
  58.5 0.9 %finish.1 = (bf16[4,6,24,192]{3,2,1,0:T(8,128)(2,1)}, bf16[4,6,24,192]{3,2,1,0:T(8,128)(2,1)}) custom-call(bf16[2,4,3,18,192]{4,3,2,1,0:T(8,128)(2,1)S(1)} %get-tuple-element.30.own_ref, bf16[648,128]{1,0:T(8,128)(2,1)S(1)} %collective-permute-done.3.lat_ref, bf16[216,128]{1,0:T(8,128)(2,1)S(1)} %collective-permute-done.4.diag_ref, ...), custom_call_target="tpu_custom_call" | custom-call | tf_op jit(solution)/shard_map/finish/pallas_call | solution.py:618
  59.4 3.9 %all-to-all-done.2.grad_ref = bf16[4,80,128]{2,1,0:T(8,128)(2,1)S(1)} async-done(((bf16[4,80,128]{2,1,0:T(8,128)(2,1)}), bf16[4,80,128]{2,1,0:T(8,128)(2,1)S(1)}, u32[]{:S(2)}, u32[]{:S(2)}) %all-to-all-start.2) | async-done | bytes 81952 | tf_op jit(solution)/shard_map/all_to_all | solution.py:480
  63.3 0.9 %unpack.1 = f32[12,1,3312]{2,1,0:T(1,128)} custom-call(bf16[4,80,128]{2,1,0:T(8,128)(2,1)S(1)} %all-to-all-done.2.grad_ref), custom_call_target="tpu_custom_call" | custom-call | tf_op jit(solution)/shard_map/unpack/pallas_call | solution.py:608
  (27 shorter events, 0.1 us)
Async XLA Ops:
  0.6 1.0 %copy-start = (bf16[4,6,24,192]{3,2,1,0:T(8,128)(2,1)S(1)}, bf16[4,6,24,192]{3,2,1,0:T(8,128)(2,1)}, u32[]{:S(2)}) copy-start(bf16[4,6,24,192]{3,2,1,0:T(8,128)(2,1)} %field_ref.5) | copy-start | bytes 663556
  1.6 1.0 %copy-start.2 = (bf16[4,6,24,192]{3,2,1,0:T(8,128)(2,1)S(1)}, bf16[4,6,24,192]{3,2,1,0:T(8,128)(2,1)}, u32[]{:S(2)}) copy-start(bf16[4,6,24,192]{3,2,1,0:T(8,128)(2,1)} %cot_ref.5) | copy-start | bytes 663556
  2.6 12.9 %copy-start.6 = (bf16[192,576]{1,0:T(8,128)(2,1)S(1)}, bf16[192,576]{1,0:T(8,128)(2,1)}, u32[]{:S(2)}) copy-start(bf16[192,576]{1,0:T(8,128)(2,1)} %wqkv_ref.1) | copy-start | bytes 663556
  2.6 12.9 %copy-start.7 = (f32[2,1,6,3312]{3,1,2,0:T(1,128)S(1)}, f32[2,1,6,3312]{3,1,2,0:T(1,128)}, u32[]{:S(2)}) copy-start(f32[2,1,6,3312]{3,1,2,0:T(1,128)} %param.19) | copy-start | bytes 476932
  2.6 15.6 %copy-start.8 = (bf16[192,192]{1,0:T(8,128)(2,1)S(1)}, bf16[192,192]{1,0:T(8,128)(2,1)}, u32[]{:S(2)}) copy-start(bf16[192,192]{1,0:T(8,128)(2,1)} %wproj_ref.1) | copy-start | bytes 221188
  2.6 15.6 %copy-start.12 = (s32[2,1,2]{2,1,0:T(1,128)S(1)}, s32[2,1,2]{2,1,0:T(1,128)}, u32[]{:S(2)}) copy-start(s32[2,1,2]{2,1,0:T(1,128)} %keep_ref.1) | copy-start | bytes 52
  2.8 12.7 %copy-start.9 = (s32[4,6,24]{2,0,1:T(4,128)S(1)}, s32[4,6,24]{2,0,1:T(4,128)}, u32[]{:S(2)}) copy-start(s32[4,6,24]{2,0,1:T(4,128)} %param.20) | copy-start | bytes 6916
  2.8 15.3 %collective-permute-start.1 = (bf16[648,128]{1,0:T(8,128)(2,1)S(1)}, bf16[648,128]{1,0:T(8,128)(2,1)S(1)}, u32[]{:S(2)}, u32[]{:S(2)}) collective-permute-start(bf16[648,128]{1,0:T(8,128)(2,1)S(1)} %pack_lat.1.after_ref), channel_id=1, source_target_pairs={{0,224},{1,225},{2,226},{3,227},{4,228},{5,229},{6,230},{7,231},{8... | collective-permute-start | bytes 497672 | tf_op jit(solution)/shard_map/ppermute | solution.py:44
  7.2 10.9 %copy-start.3 = (bf16[4,6,24,192]{3,2,1,0:T(8,128)(2,1)S(1)}, bf16[4,6,24,192]{3,2,1,0:T(8,128)(2,1)}, u32[]{:S(2)}) copy-start(bf16[4,6,24,192]{3,2,1,0:T(8,128)(2,1)} %cot_ref.5) | copy-start | bytes 663556
  7.2 10.9 %copy-start.4 = (bf16[192,768]{1,0:T(8,128)(2,1)S(1)}, bf16[192,768]{1,0:T(8,128)(2,1)}, u32[]{:S(2)}) copy-start(bf16[192,768]{1,0:T(8,128)(2,1)} %wup_ref.1) | copy-start | bytes 884740
  7.2 10.9 %copy-start.5 = (bf16[768,192]{0,1:T(8,128)(2,1)S(1)}, bf16[768,192]{0,1:T(8,128)(2,1)}, u32[]{:S(2)}) copy-start(bf16[768,192]{0,1:T(8,128)(2,1)} %param.18) | copy-start | bytes 884740
  7.3 10.9 %copy-start.1 = (bf16[4,6,24,192]{3,2,1,0:T(8,128)(2,1)S(1)}, bf16[4,6,24,192]{3,2,1,0:T(8,128)(2,1)}, u32[]{:S(2)}) copy-start(bf16[4,6,24,192]{3,2,1,0:T(8,128)(2,1)} %field_ref.5) | copy-start | bytes 663556
  7.3 10.8 %collective-permute-start = (bf16[216,128]{1,0:T(8,128)(2,1)S(1)}, bf16[216,128]{1,0:T(8,128)(2,1)S(1)}, u32[]{:S(2)}, u32[]{:S(2)}) collective-permute-start(bf16[216,128]{1,0:T(8,128)(2,1)S(1)} %get-tuple-element.24), channel_id=1, source_target_pairs={{0,31},{1,0},{2,1},{3,2},{4,3},{5,4},{6,5},{7,6},{8,7},{9,8},{10,9... | collective-permute-start | bytes 165896 | tf_op jit(solution)/shard_map/ppermute | solution.py:44
  8.4 9.7 %collective-permute-start.2 = (bf16[216,128]{1,0:T(8,128)(2,1)S(1)}, bf16[216,128]{1,0:T(8,128)(2,1)S(1)}, u32[]{:S(2)}, u32[]{:S(2)}) collective-permute-start(bf16[216,128]{1,0:T(8,128)(2,1)S(1)} %get-tuple-element.25), channel_id=1, source_target_pairs={{0,255},{1,224},{2,225},{3,226},{4,227},{5,228},{6,229},{7,230},{8... | collective-permute-start | bytes 165896 | tf_op jit(solution)/shard_map/ppermute | solution.py:44
  15.5 2.7 %copy-start.11 = (f32[192]{0:T(256)S(1)}, f32[192]{0:T(256)}, u32[]{:S(2)}) copy-start(f32[192]{0:T(256)} %param.16) | copy-start | bytes 2308
  18.1 0.7 %copy-start.10 = (f32[192]{0:T(256)S(1)}, f32[192]{0:T(256)}, u32[]{:S(2)}) copy-start(f32[192]{0:T(256)} %param.13) | copy-start | bytes 2308
  39.8 12.4 %all-to-all-start.1 = ((bf16[8,80,128]{2,1,0:T(8,128)(2,1)}), bf16[8,80,128]{2,1,0:T(8,128)(2,1)S(1)}, u32[]{:S(2)}, u32[]{:S(2)}) async-start(bf16[8,80,128]{2,1,0:T(8,128)(2,1)} %add.2), calls=%async_computation.1 | async-start | bytes 327680 | tf_op jit(solution)/shard_map/all_to_all | solution.py:480
  43.9 9.6 %collective-permute-start.3 = (bf16[648,128]{1,0:T(8,128)(2,1)S(1)}, bf16[648,128]{1,0:T(8,128)(2,1)S(1)}, u32[]{:S(2)}, u32[]{:S(2)}) collective-permute-start(bf16[648,128]{1,0:T(8,128)(2,1)S(1)} %get-tuple-element.36), channel_id=1, source_target_pairs={{0,32},{1,33},{2,34},{3,35},{4,36},{5,37},{6,38},{7,39},{8,40},{9,... | collective-permute-start | bytes 497672 | tf_op jit(solution)/shard_map/ppermute | solution.py:44
  43.9 9.5 %collective-permute-start.4 = (bf16[216,128]{1,0:T(8,128)(2,1)S(1)}, bf16[216,128]{1,0:T(8,128)(2,1)S(1)}, u32[]{:S(2)}, u32[]{:S(2)}) collective-permute-start(bf16[216,128]{1,0:T(8,128)(2,1)S(1)} %get-tuple-element.37), channel_id=1, source_target_pairs={{0,33},{1,34},{2,35},{3,36},{4,37},{5,38},{6,39},{7,40},{8,41},{9,... | collective-permute-start | bytes 165896 | tf_op jit(solution)/shard_map/ppermute | solution.py:44
  44.8 8.6 %collective-permute-start.5 = (bf16[216,128]{1,0:T(8,128)(2,1)S(1)}, bf16[216,128]{1,0:T(8,128)(2,1)S(1)}, u32[]{:S(2)}, u32[]{:S(2)}) collective-permute-start(bf16[216,128]{1,0:T(8,128)(2,1)S(1)} %get-tuple-element.38), channel_id=1, source_target_pairs={{0,1},{1,2},{2,3},{3,4},{4,5},{5,6},{6,7},{7,8},{8,9},{9,10},{10,1... | collective-permute-start | bytes 165896 | tf_op jit(solution)/shard_map/ppermute | solution.py:44
  53.4 9.9 %all-to-all-start.2 = ((bf16[4,80,128]{2,1,0:T(8,128)(2,1)}), bf16[4,80,128]{2,1,0:T(8,128)(2,1)S(1)}, u32[]{:S(2)}, u32[]{:S(2)}) async-start(bf16[4,80,128]{2,1,0:T(8,128)(2,1)} %add.3), calls=%async_computation.2 | async-start | bytes 163840 | tf_op jit(solution)/shard_map/all_to_all | solution.py:480

commit v8 on v7

--- a/solution.py
+++ b/solution.py
@@ -93,7 +93,7 @@
 
 
 def one_hot(rows, columns, target):
-    row = lax.broadcasted_iota(jnp.int32, (rows, columns), 0)
+    row = lax.broadcasted_iota(jnp.int32, (rows, 1), 0)
     column = lax.broadcasted_iota(jnp.int32, (rows, columns), 1)
     return (column == target(row)).astype(f32).astype(bf16)
 
@@ -331,7 +331,12 @@
             dense[QUARTER : 2 * QUARTER, :] = part[:, LANES : 2 * LANES]
             rest = [part[HEADS * g : HEADS * (g + 1), 2 * LANES :] for g in range(WLAT)]
             dense[2 * QUARTER : 2 * QUARTER + HEADS, : WLAT * REST] = jnp.concatenate(rest, axis=1)
-            fold_out[2 * n + k] = dense[...].astype(bf16)
+            count = fold_out.shape[0] // 4
+            size = DENSE // count
+            spare = jnp.zeros((fold_out.shape[1] - size, LANES), f32)
+            for j in range(count):
+                share = jnp.concatenate([dense[j * size : (j + 1) * size, :], spare], axis=0)
+                fold_out[(2 * n + k) * count + j] = share.astype(bf16)
         grad_h1 = jnp.concatenate(grad_h1, axis=0).astype(bf16).astype(f32)
         grad_field = (grad_sum + norm_back(grad_h1, gain1, normed1, inverse1)).astype(bf16)
         for t, value in enumerate((result, grad_field)):
@@ -424,7 +429,10 @@
     for n in range(2):
         halves = []
         for k in range(2):
-            dense = grad_ref[2 * n + k].astype(f32)
+            count = grad_ref.shape[0] // 4
+            size = DENSE // count
+            shares = [grad_ref[(2 * n + k) * count + j].astype(f32)[:size] for j in range(count)]
+            dense = jnp.concatenate(shares, axis=0)
             rest = dense[2 * QUARTER : 2 * QUARTER + HEADS]
             rest = [rest[:, g * REST : (g + 1) * REST] for g in range(WLAT)]
             rest = jnp.concatenate(rest, axis=0)
@@ -471,32 +479,23 @@
                 target[z, half + i] = jnp.concatenate([slab, own], axis=0).astype(bf16)
 
 
-def lon_sum(quarters, strips):
-    lons = lax.axis_size("lon")
-    near = [[4 * k + j for j in range(4)] for k in range(lons // 4)]
-    far = [[4 * k + j for k in range(lons // 4)] for j in range(4)]
-
-    def exchange(parts, groups):
-        return lax.all_to_all(parts, "lon", 0, 0, axis_index_groups=groups)
-
-    def added(parts, copies):
-        vmem = pl.BlockSpec(memory_space=pltpu.VMEM)
-        return pl.pallas_call(
-            add_kernel,
-            out_shape=jax.ShapeDtypeStruct((copies,) + parts.shape[1:], bf16),
-            in_specs=[vmem],
-            out_specs=vmem,
-            compiler_params=pltpu.CompilerParams(vmem_limit_bytes=VMEM_BYTES),
-            name="add",
-        )(parts)
-
-    parts = added(exchange(quarters, near), lons // 4)
+def lon_sum(shares, strips):
+    def exchange(parts):
+        return lax.all_to_all(parts, "lon", 0, 0)
+
+    vmem = pl.BlockSpec(memory_space=pltpu.VMEM)
+    parts = pl.pallas_call(
+        add_kernel,
+        out_shape=jax.ShapeDtypeStruct(shares.shape, bf16),
+        in_specs=[vmem],
+        out_specs=vmem,
+        compiler_params=pltpu.CompilerParams(vmem_limit_bytes=VMEM_BYTES),
+        name="add",
+    )(exchange(shares))
     parts, strips = lax.optimization_barrier((parts, strips))
     steps = ((1, 0), (1, 1), (0, 1))
     strips = [shifted(strip, *step) for strip, step in zip(strips, steps)]
-    parts = exchange(parts, far)
-    parts, strips = lax.optimization_barrier((added(parts, 4), strips))
-    return exchange(parts, near), strips
+    return exchange(parts), strips
 
 
 def body(
@@ -569,11 +568,13 @@
         w_qkv,
     )
     positions = levels * lat_rows * lon_cols
+    lons = lax.axis_size("lon")
+    share_rows = -(-4 * DENSE // lons // 16) * 16
     gain1 = ln1_gain.reshape(1, C)
     fold, own, *strips = pl.pallas_call(
         block_kernel,
         out_shape=(
-            jax.ShapeDtypeStruct((4, DENSE, LANES), bf16),
+            jax.ShapeDtypeStruct((lons, share_rows, LANES), bf16),
             jax.ShapeDtypeStruct((2, levels, half, inner, C), bf16),
         )
         + packed,

time: 64.6 us -> 64.4 us (level)
  blocking collectives: 8.35 us -> 17 us
  waiting for transfers between devices: 11.2 us -> 5.98 us
  starting transfers between devices: 23.3 us -> 20.4 us
  Pallas kernels: 18.1 us -> 17.4 us
    all_to_all x2 -> x1, waiting for transfers between devices: 10.7 us -> 0.41 us  [exchange(): return lax.all_to_all(parts, 'lon', 0, 0)]
    all_to_all x1, blocking collectives: 8.35 us -> 17 us  [exchange(): return lax.all_to_all(parts, 'lon', 0, 0)]
    all_to_all x2 -> x1, starting transfers between devices: 9.15 us -> 3.74 us  [exchange(): return lax.all_to_all(parts, 'lon', 0, 0)]
    ppermute x6, waiting for transfers between devices: 0.55 us -> 5.57 us  [shifted(): return lax.ppermute(block, ('lat', 'lon'), route)]
    ppermute x6, starting transfers between devices: 14.1 us -> 16.6 us  [shifted(): return lax.ppermute(block, ('lat', 'lon'), route)]
    pallas_call x3 -> x2, Pallas kernels: 13.3 us -> 12.7 us  [the longest x1 12 us: body(): pl.pallas_call(block_kernel, out_shape=(jax.ShapeDtypeStruct((lons, share...]
  transfers between devices with their start and end apart: 8 -> 7, of which waited for: 3 -> 2; matrix products, arithmetic and copies ran while one was open for 0% -> 0% of each run, Pallas kernels for 7% -> 6%
where the time goes in v8:
time: 64.4 us; the launch traced here: 64.1 us
  starting transfers between devices  20.4 us (32%)
  Pallas kernels  17.4 us (27%)
  blocking collectives  17 us (26%)
  waiting for transfers between devices  5.98 us (9%)
  local copies, waits for them, and re-layouts  2.56 us (4%)
  between operations  0.8 us (1%)
    all_to_all x1, blocking collectives, exchange(): return lax.all_to_all(parts, 'lon', 0, 0)  17 us
    ppermute x6, starting transfers between devices, shifted(): return lax.ppermute(block, ('lat', 'lon'), route)  16.6 us
    pallas_call x1, Pallas kernels, body(): pl.pallas_call(block_kernel, out_shape=(jax.ShapeDtypeStruct((lons, share...  12 us
    ppermute x6, waiting for transfers between devices, shifted(): return lax.ppermute(block, ('lat', 'lon'), route)  5.57 us
    all_to_all x1, starting transfers between devices, exchange(): return lax.all_to_all(parts, 'lon', 0, 0)  3.74 us
    pallas_call x1, Pallas kernels, body(): pl.pallas_call(prepare_kernel, out_shape=(jax.ShapeDtypeStruct((2, POS, R...  2.6 us
    unnamed x26, local copies, waits for them, and re-layouts  2.56 us
  transfers between devices with their start and end apart: 7, of which 2 were waited for; matrix products, arithmetic and copies ran while one was open for 0% of the time, Pallas kernels for 6%

profile of v8, /device:TPU:1, one launch (start us, length us, event | category | flops | bytes accessed | tf_op | source)
XLA Modules:
  0.0 64.1 jit_solution(14075725364515429796)
XLA Ops:
  0.6 0.0 copy-start
  0.6 1.0 %copy-done = bf16[4,6,24,192]{3,2,1,0:T(8,128)(2,1)S(1)} copy-done((bf16[4,6,24,192]{3,2,1,0:T(8,128)(2,1)S(1)}, bf16[4,6,24,192]{3,2,1,0:T(8,128)(2,1)}, u32[]{:S(2)}) %copy-start) | copy-done | bytes 221208
  1.6 1.0 %copy-done.2 = bf16[4,6,24,192]{3,2,1,0:T(8,128)(2,1)S(1)} copy-done((bf16[4,6,24,192]{3,2,1,0:T(8,128)(2,1)S(1)}, bf16[4,6,24,192]{3,2,1,0:T(8,128)(2,1)}, u32[]{:S(2)}) %copy-start.2) | copy-done | bytes 221208
  2.6 0.2 pack_lat.1.after_ref
  2.8 0.0 copy-start.9
  2.8 4.4 %collective-permute-start.1 = (bf16[648,128]{1,0:T(8,128)(2,1)S(1)}, bf16[648,128]{1,0:T(8,128)(2,1)S(1)}, u32[]{:S(2)}, u32[]{:S(2)}) collective-permute-start(bf16[648,128]{1,0:T(8,128)(2,1)S(1)} %pack_lat.1.after_ref), channel_id=1, source_target_pairs={{0,224},{1,225},{2,226},{3,227},{4,228},{5,229},{6,230},{7,231},{8... | collective-permute-start | bytes 497672 | tf_op jit(solution)/shard_map/ppermute | solution.py:44
  7.2 0.1 pack_edge.1
  7.3 0.0 copy-start.1
  7.3 1.0 %collective-permute-start = (bf16[216,128]{1,0:T(8,128)(2,1)S(1)}, bf16[216,128]{1,0:T(8,128)(2,1)S(1)}, u32[]{:S(2)}, u32[]{:S(2)}) collective-permute-start(bf16[216,128]{1,0:T(8,128)(2,1)S(1)} %get-tuple-element.20), channel_id=1, source_target_pairs={{0,31},{1,0},{2,1},{3,2},{4,3},{5,4},{6,5},{7,6},{8,7},{9,8},{10,9... | collective-permute-start | bytes 165896 | tf_op jit(solution)/shard_map/ppermute | solution.py:44
  8.4 7.1 %collective-permute-start.2 = (bf16[216,128]{1,0:T(8,128)(2,1)S(1)}, bf16[216,128]{1,0:T(8,128)(2,1)S(1)}, u32[]{:S(2)}, u32[]{:S(2)}) collective-permute-start(bf16[216,128]{1,0:T(8,128)(2,1)S(1)} %get-tuple-element.21), channel_id=1, source_target_pairs={{0,255},{1,224},{2,225},{3,226},{4,227},{5,228},{6,229},{7,230},{8... | collective-permute-start | bytes 165896 | tf_op jit(solution)/shard_map/ppermute | solution.py:44
  15.5 2.6 %prepare.1 = (f32[2,144,864]{2,1,0:T(8,128)S(1)}, f32[4,864]{1,0:T(4,128)S(1)}, f32[144,4]{1,0:T(8,128)S(1)}, bf16[576,192]{1,0:T(8,128)(2,1)S(1)}) custom-call(f32[12,1,3312]{2,1,0:T(1,128)S(1)} %bitcast.7, s32[6,4,24]{2,1,0:T(4,128)S(1)} %bitcast.8, bf16[192,576]{1,0:T(8,128)(2,1)S(1)} %copy-done.6), custom_call_target="tpu_custom_call" | custom-call | tf_op jit(solution)/shard_map/prepare/pallas_call | solution.py:547
  18.1 0.0 copy-start.10
  18.2 0.6 copy-done.10
  18.8 12.0 %block.1 = (bf16[32,16,128]{2,1,0:T(8,128)(2,1)S(1)}, bf16[2,4,3,18,192]{4,3,2,1,0:T(8,128)(2,1)S(1)}, bf16[648,128]{1,0:T(8,128)(2,1)S(1)}, bf16[216,128]{1,0:T(8,128)(2,1)S(1)}, bf16[216,128]{1,0:T(8,128)(2,1)S(1)}) custom-call(bf16[4,6,24,192]{3,2,1,0:T(8,128)(2,1)S(1)} %copy-done.1, bf16[4,6,24,192]{3,2,1,0:T(8,128)(2,1)S(1)} %copy-done.3, ...), custom_call_target="tpu_custom_call" | custom-call | tf_op jit(solution)/shard_map/block/pallas_call | solution.py:574
  30.8 17.0 %all_to_all.10.parts_ref = bf16[32,16,128]{2,1,0:T(8,128)(2,1)S(1)} all-to-all(bf16[32,16,128]{2,1,0:T(8,128)(2,1)S(1)} %get-tuple-element.27), channel_id=1, replica_groups=mesh['lat'=8,'lon'=32] {'lon'}, dimensions={0} | all-to-all | bytes 262144 | tf_op jit(solution)/shard_map/all_to_all | solution.py:484
  47.8 0.7 %add.1 = bf16[32,16,128]{2,1,0:T(8,128)(2,1)} custom-call(bf16[32,16,128]{2,1,0:T(8,128)(2,1)S(1)} %all_to_all.10.parts_ref), custom_call_target="tpu_custom_call" | custom-call | tf_op jit(solution)/shard_map/add/pallas_call | solution.py:487
  48.5 3.7 %all-to-all-start.1 = ((bf16[32,16,128]{2,1,0:T(8,128)(2,1)}), bf16[32,16,128]{2,1,0:T(8,128)(2,1)S(1)}, u32[]{:S(2)}, u32[]{:S(2)}) async-start(bf16[32,16,128]{2,1,0:T(8,128)(2,1)} %add.1), calls=%async_computation.1 | async-start | bytes 262144 | tf_op jit(solution)/shard_map/all_to_all | solution.py:484
  52.2 0.1 collective-permute-start.3
  52.3 3.1 %collective-permute-start.4 = (bf16[216,128]{1,0:T(8,128)(2,1)S(1)}, bf16[216,128]{1,0:T(8,128)(2,1)S(1)}, u32[]{:S(2)}, u32[]{:S(2)}) collective-permute-start(bf16[216,128]{1,0:T(8,128)(2,1)S(1)} %get-tuple-element.32), channel_id=1, source_target_pairs={{0,33},{1,34},{2,35},{3,36},{4,37},{5,38},{6,39},{7,40},{8,41},{9,... | collective-permute-start | bytes 165896 | tf_op jit(solution)/shard_map/ppermute | solution.py:44
  55.4 0.9 %collective-permute-start.5 = (bf16[216,128]{1,0:T(8,128)(2,1)S(1)}, bf16[216,128]{1,0:T(8,128)(2,1)S(1)}, u32[]{:S(2)}, u32[]{:S(2)}) collective-permute-start(bf16[216,128]{1,0:T(8,128)(2,1)S(1)} %get-tuple-element.33), channel_id=1, source_target_pairs={{0,1},{1,2},{2,3},{3,4},{4,5},{5,6},{6,7},{7,8},{8,9},{9,10},{10,1... | collective-permute-start | bytes 165896 | tf_op jit(solution)/shard_map/ppermute | solution.py:44
  56.3 5.6 %collective-permute-done.4.diag_ref = bf16[216,128]{1,0:T(8,128)(2,1)S(1)} collective-permute-done((bf16[216,128]{1,0:T(8,128)(2,1)S(1)}, bf16[216,128]{1,0:T(8,128)(2,1)S(1)}, u32[]{:S(2)}, u32[]{:S(2)}) %collective-permute-start.4) | collective-permute-done | bytes 55328 | tf_op jit(solution)/shard_map/ppermute | solution.py:44
  61.9 0.9 %finish.1 = (bf16[4,6,24,192]{3,2,1,0:T(8,128)(2,1)}, bf16[4,6,24,192]{3,2,1,0:T(8,128)(2,1)}) custom-call(bf16[2,4,3,18,192]{4,3,2,1,0:T(8,128)(2,1)S(1)} %get-tuple-element.26.own_ref, bf16[648,128]{1,0:T(8,128)(2,1)S(1)} %collective-permute-done.3.lat_ref, bf16[216,128]{1,0:T(8,128)(2,1)S(1)} %collective-permute-done.4.diag_ref, ...), custom_call_target="tpu_custom_call" | custom-call | tf_op jit(solution)/shard_map/finish/pallas_call | solution.py:619
  62.8 0.4 all-to-all-done.1.grad_ref
  63.2 0.9 %unpack.1 = f32[12,1,3312]{2,1,0:T(1,128)} custom-call(bf16[32,16,128]{2,1,0:T(8,128)(2,1)S(1)} %all-to-all-done.1.grad_ref), custom_call_target="tpu_custom_call" | custom-call | tf_op jit(solution)/shard_map/unpack/pallas_call | solution.py:609
  (24 shorter events, 0.0 us)
Async XLA Ops:
  0.6 1.0 %copy-start = (bf16[4,6,24,192]{3,2,1,0:T(8,128)(2,1)S(1)}, bf16[4,6,24,192]{3,2,1,0:T(8,128)(2,1)}, u32[]{:S(2)}) copy-start(bf16[4,6,24,192]{3,2,1,0:T(8,128)(2,1)} %field_ref.5) | copy-start | bytes 663556
  1.6 1.0 %copy-start.2 = (bf16[4,6,24,192]{3,2,1,0:T(8,128)(2,1)S(1)}, bf16[4,6,24,192]{3,2,1,0:T(8,128)(2,1)}, u32[]{:S(2)}) copy-start(bf16[4,6,24,192]{3,2,1,0:T(8,128)(2,1)} %cot_ref.5) | copy-start | bytes 663556
  2.6 12.9 %copy-start.6 = (bf16[192,576]{1,0:T(8,128)(2,1)S(1)}, bf16[192,576]{1,0:T(8,128)(2,1)}, u32[]{:S(2)}) copy-start(bf16[192,576]{1,0:T(8,128)(2,1)} %wqkv_ref.1) | copy-start | bytes 663556
  2.6 12.9 %copy-start.7 = (f32[2,1,6,3312]{3,1,2,0:T(1,128)S(1)}, f32[2,1,6,3312]{3,1,2,0:T(1,128)}, u32[]{:S(2)}) copy-start(f32[2,1,6,3312]{3,1,2,0:T(1,128)} %param.19) | copy-start | bytes 476932
  2.6 15.6 %copy-start.8 = (bf16[192,192]{1,0:T(8,128)(2,1)S(1)}, bf16[192,192]{1,0:T(8,128)(2,1)}, u32[]{:S(2)}) copy-start(bf16[192,192]{1,0:T(8,128)(2,1)} %wproj_ref.1) | copy-start | bytes 221188
  2.6 15.6 %copy-start.12 = (s32[2,1,2]{2,1,0:T(1,128)S(1)}, s32[2,1,2]{2,1,0:T(1,128)}, u32[]{:S(2)}) copy-start(s32[2,1,2]{2,1,0:T(1,128)} %keep_ref.1) | copy-start | bytes 52
  2.8 12.7 %copy-start.9 = (s32[4,6,24]{2,0,1:T(4,128)S(1)}, s32[4,6,24]{2,0,1:T(4,128)}, u32[]{:S(2)}) copy-start(s32[4,6,24]{2,0,1:T(4,128)} %param.20) | copy-start | bytes 6916
  2.8 15.3 %collective-permute-start.1 = (bf16[648,128]{1,0:T(8,128)(2,1)S(1)}, bf16[648,128]{1,0:T(8,128)(2,1)S(1)}, u32[]{:S(2)}, u32[]{:S(2)}) collective-permute-start(bf16[648,128]{1,0:T(8,128)(2,1)S(1)} %pack_lat.1.after_ref), channel_id=1, source_target_pairs={{0,224},{1,225},{2,226},{3,227},{4,228},{5,229},{6,230},{7,231},{8... | collective-permute-start | bytes 497672 | tf_op jit(solution)/shard_map/ppermute | solution.py:44
  7.2 10.9 %copy-start.3 = (bf16[4,6,24,192]{3,2,1,0:T(8,128)(2,1)S(1)}, bf16[4,6,24,192]{3,2,1,0:T(8,128)(2,1)}, u32[]{:S(2)}) copy-start(bf16[4,6,24,192]{3,2,1,0:T(8,128)(2,1)} %cot_ref.5) | copy-start | bytes 663556
  7.2 10.9 %copy-start.4 = (bf16[192,768]{1,0:T(8,128)(2,1)S(1)}, bf16[192,768]{1,0:T(8,128)(2,1)}, u32[]{:S(2)}) copy-start(bf16[192,768]{1,0:T(8,128)(2,1)} %wup_ref.1) | copy-start | bytes 884740
  7.2 10.9 %copy-start.5 = (bf16[768,192]{0,1:T(8,128)(2,1)S(1)}, bf16[768,192]{0,1:T(8,128)(2,1)}, u32[]{:S(2)}) copy-start(bf16[768,192]{0,1:T(8,128)(2,1)} %param.18) | copy-start | bytes 884740
  7.3 10.9 %copy-start.1 = (bf16[4,6,24,192]{3,2,1,0:T(8,128)(2,1)S(1)}, bf16[4,6,24,192]{3,2,1,0:T(8,128)(2,1)}, u32[]{:S(2)}) copy-start(bf16[4,6,24,192]{3,2,1,0:T(8,128)(2,1)} %field_ref.5) | copy-start | bytes 663556
  7.3 10.8 %collective-permute-start = (bf16[216,128]{1,0:T(8,128)(2,1)S(1)}, bf16[216,128]{1,0:T(8,128)(2,1)S(1)}, u32[]{:S(2)}, u32[]{:S(2)}) collective-permute-start(bf16[216,128]{1,0:T(8,128)(2,1)S(1)} %get-tuple-element.20), channel_id=1, source_target_pairs={{0,31},{1,0},{2,1},{3,2},{4,3},{5,4},{6,5},{7,6},{8,7},{9,8},{10,9... | collective-permute-start | bytes 165896 | tf_op jit(solution)/shard_map/ppermute | solution.py:44
  8.4 9.7 %collective-permute-start.2 = (bf16[216,128]{1,0:T(8,128)(2,1)S(1)}, bf16[216,128]{1,0:T(8,128)(2,1)S(1)}, u32[]{:S(2)}, u32[]{:S(2)}) collective-permute-start(bf16[216,128]{1,0:T(8,128)(2,1)S(1)} %get-tuple-element.21), channel_id=1, source_target_pairs={{0,255},{1,224},{2,225},{3,226},{4,227},{5,228},{6,229},{7,230},{8... | collective-permute-start | bytes 165896 | tf_op jit(solution)/shard_map/ppermute | solution.py:44
  15.5 2.7 %copy-start.11 = (f32[192]{0:T(256)S(1)}, f32[192]{0:T(256)}, u32[]{:S(2)}) copy-start(f32[192]{0:T(256)} %param.16) | copy-start | bytes 2308
  18.1 0.7 %copy-start.10 = (f32[192]{0:T(256)S(1)}, f32[192]{0:T(256)}, u32[]{:S(2)}) copy-start(f32[192]{0:T(256)} %param.13) | copy-start | bytes 2308
  48.5 14.7 %all-to-all-start.1 = ((bf16[32,16,128]{2,1,0:T(8,128)(2,1)}), bf16[32,16,128]{2,1,0:T(8,128)(2,1)S(1)}, u32[]{:S(2)}, u32[]{:S(2)}) async-start(bf16[32,16,128]{2,1,0:T(8,128)(2,1)} %add.1), calls=%async_computation.1 | async-start | bytes 262144 | tf_op jit(solution)/shard_map/all_to_all | solution.py:484
  52.2 9.7 %collective-permute-start.3 = (bf16[648,128]{1,0:T(8,128)(2,1)S(1)}, bf16[648,128]{1,0:T(8,128)(2,1)S(1)}, u32[]{:S(2)}, u32[]{:S(2)}) collective-permute-start(bf16[648,128]{1,0:T(8,128)(2,1)S(1)} %get-tuple-element.31), channel_id=1, source_target_pairs={{0,32},{1,33},{2,34},{3,35},{4,36},{5,37},{6,38},{7,39},{8,40},{9,... | collective-permute-start | bytes 497672 | tf_op jit(solution)/shard_map/ppermute | solution.py:44
  52.3 9.6 %collective-permute-start.4 = (bf16[216,128]{1,0:T(8,128)(2,1)S(1)}, bf16[216,128]{1,0:T(8,128)(2,1)S(1)}, u32[]{:S(2)}, u32[]{:S(2)}) collective-permute-start(bf16[216,128]{1,0:T(8,128)(2,1)S(1)} %get-tuple-element.32), channel_id=1, source_target_pairs={{0,33},{1,34},{2,35},{3,36},{4,37},{5,38},{6,39},{7,40},{8,41},{9,... | collective-permute-start | bytes 165896 | tf_op jit(solution)/shard_map/ppermute | solution.py:44
  55.4 6.5 %collective-permute-start.5 = (bf16[216,128]{1,0:T(8,128)(2,1)S(1)}, bf16[216,128]{1,0:T(8,128)(2,1)S(1)}, u32[]{:S(2)}, u32[]{:S(2)}) collective-permute-start(bf16[216,128]{1,0:T(8,128)(2,1)S(1)} %get-tuple-element.33), channel_id=1, source_target_pairs={{0,1},{1,2},{2,3},{3,4},{4,5},{5,6},{6,7},{7,8},{8,9},{9,10},{10,1... | collective-permute-start | bytes 165896 | tf_op jit(solution)/shard_map/ppermute | solution.py:44

commit v9 on v7

--- a/solution.py
+++ b/solution.py
@@ -93,7 +93,7 @@
 
 
 def one_hot(rows, columns, target):
-    row = lax.broadcasted_iota(jnp.int32, (rows, columns), 0)
+    row = lax.broadcasted_iota(jnp.int32, (rows, 1), 0)
     column = lax.broadcasted_iota(jnp.int32, (rows, columns), 1)
     return (column == target(row)).astype(f32).astype(bf16)
 
@@ -197,10 +197,9 @@
     lon_ref,
     lat_ref,
     diag_ref,
-    gain1_ref,
+    gains_ref,
     wqkv_t_ref,
     wproj_ref,
-    gain2_ref,
     wup_ref,
     wdown_t_ref,
     bias_ref,
@@ -244,8 +243,8 @@
                 main, rest = get(diag_part, t, k * edge, edge)
                 frame[t, row + inner : row + cols, :LANES] = main
                 frame[t, row + inner : row + cols, LANES:] = rest
-    gain1 = gain1_ref[...]
-    gain2 = gain2_ref[...]
+    gain1 = gains_ref[0:1, :]
+    gain2 = gains_ref[1:2, :]
     wq_t = wqkv_t_ref[0:C, :]
     wk_t = wqkv_t_ref[C : 2 * C, :]
     wv_t = wqkv_t_ref[2 * C : 3 * C, :]
@@ -357,16 +356,21 @@
     table_ref,
     region_ref,
     wqkv_ref,
+    gain1_ref,
+    gain2_ref,
     bias_out,
     label_row_out,
     label_col_out,
     wqkv_t_out,
+    gains_out,
     flat,
     rows,
     wide,
     marks,
 ):
     wqkv_t_out[...] = wqkv_ref[...].astype(f32).T.astype(bf16)
+    gains_out[0:1, :] = gain1_ref[...]
+    gains_out[1:2, :] = gain2_ref[...]
     last = lax.axis_index("lat") == lax.axis_size("lat") - 1
     level = lax.broadcasted_iota(jnp.int32, (4, 2 * WLON), 0)
     for i in range(WLAT):
@@ -419,12 +423,15 @@
         bias_out[n] = wide[n * HEADS : (n + 1) * HEADS].reshape(ROWS, POS).T * LOG2E
 
 
-def unpack_kernel(grad_ref, table_out, flat):
+def unpack_kernel(mine_ref, other_ref, table_out, flat):
+    odd = (lax.axis_index("lon") & 1) != 0
     part = PAIR // WZ * SPREAD
     for n in range(2):
         halves = []
         for k in range(2):
-            dense = grad_ref[2 * n + k].astype(f32)
+            mine = mine_ref[n].astype(f32)
+            other = other_ref[n].astype(f32)
+            dense = jnp.where(odd == (k == 1), mine, other)
             rest = dense[2 * QUARTER : 2 * QUARTER + HEADS]
             rest = [rest[:, g * REST : (g + 1) * REST] for g in range(WLAT)]
             rest = jnp.concatenate(rest, axis=0)
@@ -443,11 +450,12 @@
         table_out[k] = flat[k : k + 1, :]
 
 
-def add_kernel(parts_ref, copies_out):
-    total = parts_ref[0].astype(f32)
-    for k in range(1, parts_ref.shape[0]):
-        total = total + parts_ref[k].astype(f32)
-    total = total.astype(bf16)
+def add_kernel(*refs):
+    copies_out = refs[-1]
+    parts = [ref[k].astype(f32) for ref in refs[:-1] for k in range(ref.shape[0])]
+    while len(parts) > 1:
+        parts = [parts[k] + parts[k + 1] for k in range(0, len(parts), 2)]
+    total = parts[0].astype(bf16)
     for k in range(copies_out.shape[0]):
         copies_out[k] = total
 
@@ -473,30 +481,43 @@
 
 def lon_sum(quarters, strips):
     lons = lax.axis_size("lon")
-    near = [[4 * k + j for j in range(4)] for k in range(lons // 4)]
+    me = lax.axis_index("lon")
+    bits = [(me >> k) & 1 for k in range(2)]
     far = [[4 * k + j for k in range(lons // 4)] for j in range(4)]
 
-    def exchange(parts, groups):
-        return lax.all_to_all(parts, "lon", 0, 0, axis_index_groups=groups)
+    def swapped(block, distance):
+        return lax.ppermute(block, "lon", [(i, i ^ distance) for i in range(lons)])
+
+    def pick(value, bit, axis):
+        return lax.dynamic_index_in_dim(value, bit, axis, keepdims=False)
 
     def added(parts, copies):
         vmem = pl.BlockSpec(memory_space=pltpu.VMEM)
         return pl.pallas_call(
             add_kernel,
-            out_shape=jax.ShapeDtypeStruct((copies,) + parts.shape[1:], bf16),
-            in_specs=[vmem],
+            out_shape=jax.ShapeDtypeStruct((copies,) + parts[0].shape[1:], bf16),
+            in_specs=[vmem] * len(parts),
             out_specs=vmem,
             compiler_params=pltpu.CompilerParams(vmem_limit_bytes=VMEM_BYTES),
             name="add",
-        )(parts)
-
-    parts = added(exchange(quarters, near), lons // 4)
+        )(*parts)
+
+    value = quarters.reshape((2, 2) + quarters.shape[1:])
+    other = swapped(pick(value, 1 - bits[0], 1), 1)
+    value = pick(value, bits[0], 1).astype(f32) + other.astype(f32)
+    value = value.astype(bf16)
+    other = swapped(pick(value, 1 - bits[1], 0), 2)
+    parts = added((pick(value, bits[1], 0)[None], other[None]), lons // 4)
     parts, strips = lax.optimization_barrier((parts, strips))
     steps = ((1, 0), (1, 1), (0, 1))
     strips = [shifted(strip, *step) for strip, step in zip(strips, steps)]
-    parts = exchange(parts, far)
-    parts, strips = lax.optimization_barrier((added(parts, 4), strips))
-    return exchange(parts, near), strips
+    parts = lax.all_to_all(parts, "lon", 0, 0, axis_index_groups=far)
+    value, strips = lax.optimization_barrier((added((parts,), 1)[0], strips))
+    other = swapped(value, 2)
+    lower = jnp.where(bits[1] == 0, value, other)
+    upper = jnp.where(bits[1] == 0, other, value)
+    value = jnp.stack([lower, upper])
+    return (value, swapped(value, 1)), strips
 
 
 def body(
@@ -545,16 +566,17 @@
     diag_part = shifted(diag_part, -1, -1)
     lon_part = shifted(lon_part, 0, -1)
 
-    bias_wide, label_row, label_col, weights_t = pl.pallas_call(
+    bias_wide, label_row, label_col, weights_t, gains = pl.pallas_call(
         prepare_kernel,
         out_shape=(
             jax.ShapeDtypeStruct((2, POS, ROWS), f32),
             jax.ShapeDtypeStruct((4, ROWS), f32),
             jax.ShapeDtypeStruct((POS, 4), f32),
             jax.ShapeDtypeStruct((3 * C, C), bf16),
+            jax.ShapeDtypeStruct((2, C), f32),
         ),
-        in_specs=[vmem] * 3,
-        out_specs=(vmem,) * 4,
+        in_specs=[vmem] * 5,
+        out_specs=(vmem,) * 5,
         scratch_shapes=[
             pltpu.VMEM((2 * HEADS, PAIR * TAB), f32),
             pltpu.VMEM((PAIR * SLOTS, TAB), f32),
@@ -567,9 +589,10 @@
         bias_table.reshape(2 * HEADS, 1, PAIR * TAB),
         region_ids.transpose(1, 0, 2),
         w_qkv,
+        ln1_gain.reshape(1, C),
+        ln2_gain.reshape(1, C),
     )
     positions = levels * lat_rows * lon_cols
-    gain1 = ln1_gain.reshape(1, C)
     fold, own, *strips = pl.pallas_call(
         block_kernel,
         out_shape=(
@@ -577,7 +600,7 @@
             jax.ShapeDtypeStruct((2, levels, half, inner, C), bf16),
         )
         + packed,
-        in_specs=[vmem] * 14 + [smem],
+        in_specs=[vmem] * 13 + [smem],
         out_specs=(vmem,) * 5,
         scratch_shapes=[
             pltpu.VMEM((2, positions, C), f32),
@@ -593,10 +616,9 @@
         lon_part,
         lat_part,
         diag_part,
-        gain1,
+        gains,
         weights_t,
         w_proj,
-        ln2_gain.reshape(1, C),
         w_up,
         w_down.T,
         bias_wide,
@@ -604,16 +626,16 @@
         label_col,
         keep_flags,
     )
-    grads, (lat_back, diag_back, lon_back) = lon_sum(fold, strips)
+    halves, (lat_back, diag_back, lon_back) = lon_sum(fold, strips)
     grads = pl.pallas_call(
         unpack_kernel,
         out_shape=jax.ShapeDtypeStruct((2 * HEADS, 1, PAIR * TAB), f32),
-        in_specs=[vmem],
+        in_specs=[vmem] * 2,
         out_specs=vmem,
         scratch_shapes=[pltpu.VMEM((2 * HEADS, PAIR * TAB), f32)],
         compiler_params=params,
         name="unpack",
-    )(grads)
+    )(*halves)
     grads = grads.reshape(2, 1, HEADS, PAIR * TAB)
     result, grad_field = pl.pallas_call(
         finish_kernel,

time: 64.6 us -> 61.2 us (0.947)
  blocking collectives: 8.35 us -> 0 us
  starting transfers between devices: 23.3 us -> 26.6 us
  waiting for transfers between devices: 11.2 us -> 13.5 us
  Pallas kernels: 18.1 us -> 17.4 us
    all_to_all x1 -> x0, blocking collectives: 8.35 us -> none  [exchange(): return lax.all_to_all(parts, 'lon', 0, 0, axis_index_groups=groups)]
    ppermute x0 -> x4, waiting for transfers between devices: none -> 7.78 us  [swapped(): return lax.ppermute(block, 'lon', [(i, i ^ distance) for i in range(lons)])]
    ppermute x0 -> x4, starting transfers between devices: none -> 6.91 us  [swapped(): return lax.ppermute(block, 'lon', [(i, i ^ distance) for i in range(lons)])]
    all_to_all x2 -> x1, waiting for transfers between devices: 10.7 us -> 4.65 us  [lon_sum(): parts = lax.all_to_all(parts, 'lon', 0, 0, axis_index_groups=far)]
    all_to_all x2 -> x1, starting transfers between devices: 9.15 us -> 3.47 us  [lon_sum(): parts = lax.all_to_all(parts, 'lon', 0, 0, axis_index_groups=far)]
    ppermute x6, starting transfers between devices: 14.1 us -> 16.2 us  [shifted(): return lax.ppermute(block, ('lat', 'lon'), route)]
  transfers between devices with their start and end apart: 8 -> 11, of which waited for: 3 -> 5; matrix products, arithmetic and copies ran while one was open for 0% -> 0% of each run, Pallas kernels for 7% -> 6%
where the time goes in v9:
time: 61.2 us; the launch traced here: 61 us
  starting transfers between devices  26.6 us (43%)
  Pallas kernels  17.4 us (28%)
  waiting for transfers between devices  13.5 us (22%)
  local copies, waits for them, and re-layouts  2.61 us (4%)
  between operations  0.82 us (1%)
    ppermute x6, starting transfers between devices, shifted(): return lax.ppermute(block, ('lat', 'lon'), route)  16.2 us
    pallas_call x1, Pallas kernels, body(): pl.pallas_call(block_kernel, out_shape=(jax.ShapeDtypeStruct((4, DENSE, L...  11.9 us
    ppermute x4, waiting for transfers between devices, swapped(): return lax.ppermute(block, 'lon', [(i, i ^ distance) for i in range(lons)])  7.78 us
    ppermute x4, starting transfers between devices, swapped(): return lax.ppermute(block, 'lon', [(i, i ^ distance) for i in range(lons)])  6.91 us
    all_to_all x1, waiting for transfers between devices, lon_sum(): parts = lax.all_to_all(parts, 'lon', 0, 0, axis_index_groups=far)  4.65 us
    all_to_all x1, starting transfers between devices, lon_sum(): parts = lax.all_to_all(parts, 'lon', 0, 0, axis_index_groups=far)  3.47 us
    pallas_call x1, Pallas kernels, body(): pl.pallas_call(prepare_kernel, out_shape=(jax.ShapeDtypeStruct((2, POS, R...  2.61 us
    unnamed x26, local copies, waits for them, and re-layouts  2.58 us
  transfers between devices with their start and end apart: 11, of which 5 were waited for; matrix products, arithmetic and copies ran while one was open for 0% of the time, Pallas kernels for 6%

profile of v9, /device:TPU:1, one launch (start us, length us, event | category | flops | bytes accessed | tf_op | source)
XLA Modules:
  0.0 61.0 jit_solution(6170670573049959985)
XLA Ops:
  0.6 1.0 %copy-done = bf16[4,6,24,192]{3,2,1,0:T(8,128)(2,1)S(1)} copy-done((bf16[4,6,24,192]{3,2,1,0:T(8,128)(2,1)S(1)}, bf16[4,6,24,192]{3,2,1,0:T(8,128)(2,1)}, u32[]{:S(2)}) %copy-start) | copy-done | bytes 221208
  1.6 1.0 %copy-done.2 = bf16[4,6,24,192]{3,2,1,0:T(8,128)(2,1)S(1)} copy-done((bf16[4,6,24,192]{3,2,1,0:T(8,128)(2,1)S(1)}, bf16[4,6,24,192]{3,2,1,0:T(8,128)(2,1)}, u32[]{:S(2)}) %copy-start.2) | copy-done | bytes 221208
  2.6 0.2 pack_lat.1.after_ref
  2.8 4.4 %collective-permute-start.1 = (bf16[648,128]{1,0:T(8,128)(2,1)S(1)}, bf16[648,128]{1,0:T(8,128)(2,1)S(1)}, u32[]{:S(2)}, u32[]{:S(2)}) collective-permute-start(bf16[648,128]{1,0:T(8,128)(2,1)S(1)} %pack_lat.1.after_ref), channel_id=1, source_target_pairs={{0,224},{1,225},{2,226},{3,227},{4,228},{5,229},{6,230},{7,231},{8... | collective-permute-start | bytes 497672 | tf_op jit(solution)/shard_map/ppermute | solution.py:44
  7.4 1.0 %collective-permute-start = (bf16[216,128]{1,0:T(8,128)(2,1)S(1)}, bf16[216,128]{1,0:T(8,128)(2,1)S(1)}, u32[]{:S(2)}, u32[]{:S(2)}) collective-permute-start(bf16[216,128]{1,0:T(8,128)(2,1)S(1)} %get-tuple-element.25), channel_id=1, source_target_pairs={{0,31},{1,0},{2,1},{3,2},{4,3},{5,4},{6,5},{7,6},{8,7},{9,8},{10,9... | collective-permute-start | bytes 165896 | tf_op jit(solution)/shard_map/ppermute | solution.py:44
  8.4 7.1 %collective-permute-start.2 = (bf16[216,128]{1,0:T(8,128)(2,1)S(1)}, bf16[216,128]{1,0:T(8,128)(2,1)S(1)}, u32[]{:S(2)}, u32[]{:S(2)}) collective-permute-start(bf16[216,128]{1,0:T(8,128)(2,1)S(1)} %get-tuple-element.26), channel_id=1, source_target_pairs={{0,255},{1,224},{2,225},{3,226},{4,227},{5,228},{6,229},{7,230},{8... | collective-permute-start | bytes 165896 | tf_op jit(solution)/shard_map/ppermute | solution.py:44
  15.5 2.6 %prepare.1 = (f32[2,144,864]{2,1,0:T(8,128)S(1)}, f32[4,864]{1,0:T(4,128)S(1)}, f32[144,4]{1,0:T(8,128)S(1)}, bf16[576,192]{1,0:T(8,128)(2,1)S(1)}, f32[2,192]{1,0:T(2,128)S(1)}) custom-call(f32[12,1,3312]{2,1,0:T(1,128)S(1)} %bitcast.23, s32[6,4,24]{2,1,0:T(4,128)S(1)} %bitcast.29, bf16[192,576]{1,0:T(8,128)(2,1)S(1)} %copy-done.6, f32[1,192]{1,0:T(1,128)S(1)} %bitcast.30, ...), custom_call_target="tpu_custom_call" | custom-call | tf_op jit(solution)/shard_map/prepare/pallas_call | solution.py:569
  18.2 0.6 %copy-done.12 = s32[2,1,2]{2,1,0:T(1,128)S(1)} copy-done((s32[2,1,2]{2,1,0:T(1,128)S(1)}, s32[2,1,2]{2,1,0:T(1,128)}, u32[]{:S(2)}) %copy-start.12) | copy-done | bytes 40
  18.8 11.9 %block.1 = (bf16[4,80,128]{2,1,0:T(8,128)(2,1)S(1)}, bf16[2,4,3,18,192]{4,3,2,1,0:T(8,128)(2,1)S(1)}, bf16[648,128]{1,0:T(8,128)(2,1)S(1)}, bf16[216,128]{1,0:T(8,128)(2,1)S(1)}, bf16[216,128]{1,0:T(8,128)(2,1)S(1)}) custom-call(bf16[4,6,24,192]{3,2,1,0:T(8,128)(2,1)S(1)} %copy-done.1, bf16[4,6,24,192]{3,2,1,0:T(8,128)(2,1)S(1)} %copy-done.3, ...), custom_call_target="tpu_custom_call" | custom-call | tf_op jit(solution)/shard_map/block/pallas_call | solution.py:596
  30.8 1.5 %collective-permute-start.3 = (bf16[2,80,128]{2,1,0:T(8,128)(2,1)S(1)}, bf16[2,80,128]{2,1,0:T(8,128)(2,1)S(1)}, u32[]{:S(2)}, u32[]{:S(2)}) collective-permute-start(bf16[2,80,128]{2,1,0:T(8,128)(2,1)S(1)} %dynamic-slice_bitcast_fusion), channel_id=1, source_target_pairs={{0,1},{1,0},{2,3},{3,2},{4,5},{5,4},{6,7},{7,6},{8,9},{9,8},{10,11... | collective-permute-start | bytes 122888 | tf_op jit(solution)/shard_map/ppermute | solution.py:489
  32.3 0.9 %collective-permute-done.3 = bf16[2,80,128]{2,1,0:T(8,128)(2,1)S(1)} collective-permute-done((bf16[2,80,128]{2,1,0:T(8,128)(2,1)S(1)}, bf16[2,80,128]{2,1,0:T(8,128)(2,1)S(1)}, u32[]{:S(2)}, u32[]{:S(2)}) %collective-permute-start.3) | collective-permute-done | bytes 40992 | tf_op jit(solution)/shard_map/ppermute | solution.py:489
  33.3 4.1 %collective-permute-done.4 = bf16[80,128]{1,0:T(8,128)(2,1)S(1)} collective-permute-done((bf16[80,128]{1,0:T(8,128)(2,1)S(1)}, bf16[80,128]{1,0:T(8,128)(2,1)S(1)}, u32[]{:S(2)}, u32[]{:S(2)}) %collective-permute-start.4) | collective-permute-done | bytes 20512 | tf_op jit(solution)/shard_map/ppermute | solution.py:489
  37.4 0.7 %add.29 = bf16[8,80,128]{2,1,0:T(8,128)(2,1)} custom-call(bf16[1,80,128]{2,1,0:T(8,128)(2,1)S(1)} %get-tuple-element.50.refs_0_, bf16[1,80,128]{2,1,0:T(8,128)(2,1)S(1)} %bitcast.28), custom_call_target="tpu_custom_call" | custom-call | tf_op jit(solution)/shard_map/add/pallas_call | solution.py:496
  38.1 3.5 %all-to-all-start = ((bf16[8,80,128]{2,1,0:T(8,128)(2,1)}), bf16[8,80,128]{2,1,0:T(8,128)(2,1)S(1)}, u32[]{:S(2)}, u32[]{:S(2)}) async-start(bf16[8,80,128]{2,1,0:T(8,128)(2,1)} %add.29), calls=%async_computation | async-start | bytes 327680 | tf_op jit(solution)/shard_map/all_to_all | solution.py:514
  41.6 0.8 %collective-permute-start.5 = (bf16[648,128]{1,0:T(8,128)(2,1)S(1)}, bf16[648,128]{1,0:T(8,128)(2,1)S(1)}, u32[]{:S(2)}, u32[]{:S(2)}) collective-permute-start(bf16[648,128]{1,0:T(8,128)(2,1)S(1)} %get-tuple-element.38), channel_id=1, source_target_pairs={{0,32},{1,33},{2,34},{3,35},{4,36},{5,37},{6,38},{7,39},{8,40},{9,... | collective-permute-start | bytes 497672 | tf_op jit(solution)/shard_map/ppermute | solution.py:44
  42.4 2.3 %collective-permute-start.6 = (bf16[216,128]{1,0:T(8,128)(2,1)S(1)}, bf16[216,128]{1,0:T(8,128)(2,1)S(1)}, u32[]{:S(2)}, u32[]{:S(2)}) collective-permute-start(bf16[216,128]{1,0:T(8,128)(2,1)S(1)} %get-tuple-element.39), channel_id=1, source_target_pairs={{0,33},{1,34},{2,35},{3,36},{4,37},{5,38},{6,39},{7,40},{8,41},{9,... | collective-permute-start | bytes 165896 | tf_op jit(solution)/shard_map/ppermute | solution.py:44
  44.7 0.6 collective-permute-start.7
  45.3 4.7 %all-to-all-done.refs_0_ = bf16[8,80,128]{2,1,0:T(8,128)(2,1)S(1)} async-done(((bf16[8,80,128]{2,1,0:T(8,128)(2,1)}), bf16[8,80,128]{2,1,0:T(8,128)(2,1)S(1)}, u32[]{:S(2)}, u32[]{:S(2)}) %all-to-all-start) | async-done | bytes 163872 | tf_op jit(solution)/shard_map/all_to_all | solution.py:514
  50.0 1.0 %collective-permute-done.6.diag_ref = bf16[216,128]{1,0:T(8,128)(2,1)S(1)} collective-permute-done((bf16[216,128]{1,0:T(8,128)(2,1)S(1)}, bf16[216,128]{1,0:T(8,128)(2,1)S(1)}, u32[]{:S(2)}, u32[]{:S(2)}) %collective-permute-start.6) | collective-permute-done | bytes 55328 | tf_op jit(solution)/shard_map/ppermute | solution.py:44
  51.0 1.4 %collective-permute-start.8 = (bf16[80,128]{1,0:T(8,128)(2,1)S(1)}, bf16[80,128]{1,0:T(8,128)(2,1)S(1)}, u32[]{:S(2)}, u32[]{:S(2)}) collective-permute-start(bf16[80,128]{1,0:T(8,128)(2,1)S(1)} %bitcast.26), channel_id=1, source_target_pairs={{0,2},{1,3},{2,0},{3,1},{4,6},{5,7},{6,4},{7,5},{8,10},{9,11},{10,... | collective-permute-start | bytes 61448 | tf_op jit(solution)/shard_map/ppermute | solution.py:489
  52.4 2.8 %collective-permute-done.8 = bf16[80,128]{1,0:T(8,128)(2,1)S(1)} collective-permute-done((bf16[80,128]{1,0:T(8,128)(2,1)S(1)}, bf16[80,128]{1,0:T(8,128)(2,1)S(1)}, u32[]{:S(2)}, u32[]{:S(2)}) %collective-permute-start.8) | collective-permute-done | bytes 20512 | tf_op jit(solution)/shard_map/ppermute | solution.py:489
  55.2 4.0 %collective-permute-start.9 = (bf16[2,80,128]{2,1,0:T(8,128)(2,1)S(1)}, bf16[2,80,128]{2,1,0:T(8,128)(2,1)S(1)}, u32[]{:S(2)}, u32[]{:S(2)}) collective-permute-start(bf16[2,80,128]{2,1,0:T(8,128)(2,1)S(1)} %pad_maximum_fusion.mine_ref), channel_id=1, source_target_pairs={{0,1},{1,0},{2,3},{3,2},{4,5},{5,4},{6,7},{7,6},{8,9},{9,8},{10,11... | collective-permute-start | bytes 122888 | tf_op jit(solution)/shard_map/ppermute | solution.py:489
  59.1 0.9 %finish.1 = (bf16[4,6,24,192]{3,2,1,0:T(8,128)(2,1)}, bf16[4,6,24,192]{3,2,1,0:T(8,128)(2,1)}) custom-call(bf16[2,4,3,18,192]{4,3,2,1,0:T(8,128)(2,1)S(1)} %get-tuple-element.32.own_ref, bf16[648,128]{1,0:T(8,128)(2,1)S(1)} %collective-permute-done.5.lat_ref, bf16[216,128]{1,0:T(8,128)(2,1)S(1)} %collective-permute-done.6.diag_ref, ...), custom_call_target="tpu_custom_call" | custom-call | tf_op jit(solution)/shard_map/finish/pallas_call | solution.py:640
  60.0 0.9 %unpack.1 = f32[12,1,3312]{2,1,0:T(1,128)} custom-call(bf16[2,80,128]{2,1,0:T(8,128)(2,1)S(1)} %pad_maximum_fusion.mine_ref, bf16[2,80,128]{2,1,0:T(8,128)(2,1)S(1)} %collective-permute-done.9.other_ref), custom_call_target="tpu_custom_call" | custom-call | tf_op jit(solution)/shard_map/unpack/pallas_call | solution.py:630
  (37 shorter events, 0.3 us)
Async XLA Ops:
  0.6 1.0 %copy-start = (bf16[4,6,24,192]{3,2,1,0:T(8,128)(2,1)S(1)}, bf16[4,6,24,192]{3,2,1,0:T(8,128)(2,1)}, u32[]{:S(2)}) copy-start(bf16[4,6,24,192]{3,2,1,0:T(8,128)(2,1)} %field_ref.5) | copy-start | bytes 663556
  1.6 1.0 %copy-start.2 = (bf16[4,6,24,192]{3,2,1,0:T(8,128)(2,1)S(1)}, bf16[4,6,24,192]{3,2,1,0:T(8,128)(2,1)}, u32[]{:S(2)}) copy-start(bf16[4,6,24,192]{3,2,1,0:T(8,128)(2,1)} %cot_ref.5) | copy-start | bytes 663556
  2.6 12.9 %copy-start.6 = (bf16[192,576]{1,0:T(8,128)(2,1)S(1)}, bf16[192,576]{1,0:T(8,128)(2,1)}, u32[]{:S(2)}) copy-start(bf16[192,576]{1,0:T(8,128)(2,1)} %wqkv_ref.1) | copy-start | bytes 663556
  2.6 12.9 %copy-start.7 = (f32[2,1,6,3312]{3,1,2,0:T(1,128)S(1)}, f32[2,1,6,3312]{3,1,2,0:T(1,128)}, u32[]{:S(2)}) copy-start(f32[2,1,6,3312]{3,1,2,0:T(1,128)} %param.19) | copy-start | bytes 476932
  2.6 12.9 %copy-start.10 = (f32[192]{0:T(256)S(1)}, f32[192]{0:T(256)}, u32[]{:S(2)}) copy-start(f32[192]{0:T(256)} %param.13) | copy-start | bytes 2308
  2.6 12.9 %copy-start.11 = (f32[192]{0:T(256)S(1)}, f32[192]{0:T(256)}, u32[]{:S(2)}) copy-start(f32[192]{0:T(256)} %param.16) | copy-start | bytes 2308
  2.6 15.6 %copy-start.8 = (bf16[192,192]{1,0:T(8,128)(2,1)S(1)}, bf16[192,192]{1,0:T(8,128)(2,1)}, u32[]{:S(2)}) copy-start(bf16[192,192]{1,0:T(8,128)(2,1)} %wproj_ref.1) | copy-start | bytes 221188
  2.8 12.7 %copy-start.9 = (s32[4,6,24]{2,0,1:T(4,128)S(1)}, s32[4,6,24]{2,0,1:T(4,128)}, u32[]{:S(2)}) copy-start(s32[4,6,24]{2,0,1:T(4,128)} %param.20) | copy-start | bytes 6916
  2.8 15.3 %collective-permute-start.1 = (bf16[648,128]{1,0:T(8,128)(2,1)S(1)}, bf16[648,128]{1,0:T(8,128)(2,1)S(1)}, u32[]{:S(2)}, u32[]{:S(2)}) collective-permute-start(bf16[648,128]{1,0:T(8,128)(2,1)S(1)} %pack_lat.1.after_ref), channel_id=1, source_target_pairs={{0,224},{1,225},{2,226},{3,227},{4,228},{5,229},{6,230},{7,231},{8... | collective-permute-start | bytes 497672 | tf_op jit(solution)/shard_map/ppermute | solution.py:44
  7.2 10.9 %copy-start.3 = (bf16[4,6,24,192]{3,2,1,0:T(8,128)(2,1)S(1)}, bf16[4,6,24,192]{3,2,1,0:T(8,128)(2,1)}, u32[]{:S(2)}) copy-start(bf16[4,6,24,192]{3,2,1,0:T(8,128)(2,1)} %cot_ref.5) | copy-start | bytes 663556
  7.2 10.9 %copy-start.4 = (bf16[192,768]{1,0:T(8,128)(2,1)S(1)}, bf16[192,768]{1,0:T(8,128)(2,1)}, u32[]{:S(2)}) copy-start(bf16[192,768]{1,0:T(8,128)(2,1)} %wup_ref.1) | copy-start | bytes 884740
  7.2 11.0 %copy-start.5 = (bf16[768,192]{0,1:T(8,128)(2,1)S(1)}, bf16[768,192]{0,1:T(8,128)(2,1)}, u32[]{:S(2)}) copy-start(bf16[768,192]{0,1:T(8,128)(2,1)} %param.18) | copy-start | bytes 884740
  7.3 10.9 %copy-start.1 = (bf16[4,6,24,192]{3,2,1,0:T(8,128)(2,1)S(1)}, bf16[4,6,24,192]{3,2,1,0:T(8,128)(2,1)}, u32[]{:S(2)}) copy-start(bf16[4,6,24,192]{3,2,1,0:T(8,128)(2,1)} %field_ref.5) | copy-start | bytes 663556
  7.4 10.8 %collective-permute-start = (bf16[216,128]{1,0:T(8,128)(2,1)S(1)}, bf16[216,128]{1,0:T(8,128)(2,1)S(1)}, u32[]{:S(2)}, u32[]{:S(2)}) collective-permute-start(bf16[216,128]{1,0:T(8,128)(2,1)S(1)} %get-tuple-element.25), channel_id=1, source_target_pairs={{0,31},{1,0},{2,1},{3,2},{4,3},{5,4},{6,5},{7,6},{8,7},{9,8},{10,9... | collective-permute-start | bytes 165896 | tf_op jit(solution)/shard_map/ppermute | solution.py:44
  8.4 9.7 %collective-permute-start.2 = (bf16[216,128]{1,0:T(8,128)(2,1)S(1)}, bf16[216,128]{1,0:T(8,128)(2,1)S(1)}, u32[]{:S(2)}, u32[]{:S(2)}) collective-permute-start(bf16[216,128]{1,0:T(8,128)(2,1)S(1)} %get-tuple-element.26), channel_id=1, source_target_pairs={{0,255},{1,224},{2,225},{3,226},{4,227},{5,228},{6,229},{7,230},{8... | collective-permute-start | bytes 165896 | tf_op jit(solution)/shard_map/ppermute | solution.py:44
  18.2 0.7 %copy-start.12 = (s32[2,1,2]{2,1,0:T(1,128)S(1)}, s32[2,1,2]{2,1,0:T(1,128)}, u32[]{:S(2)}) copy-start(s32[2,1,2]{2,1,0:T(1,128)} %keep_ref.1) | copy-start | bytes 52
  30.8 2.3 %collective-permute-start.3 = (bf16[2,80,128]{2,1,0:T(8,128)(2,1)S(1)}, bf16[2,80,128]{2,1,0:T(8,128)(2,1)S(1)}, u32[]{:S(2)}, u32[]{:S(2)}) collective-permute-start(bf16[2,80,128]{2,1,0:T(8,128)(2,1)S(1)} %dynamic-slice_bitcast_fusion), channel_id=1, source_target_pairs={{0,1},{1,0},{2,3},{3,2},{4,5},{5,4},{6,7},{7,6},{8,9},{9,8},{10,11... | collective-permute-start | bytes 122888 | tf_op jit(solution)/shard_map/ppermute | solution.py:489
  33.2 4.2 %collective-permute-start.4 = (bf16[80,128]{1,0:T(8,128)(2,1)S(1)}, bf16[80,128]{1,0:T(8,128)(2,1)S(1)}, u32[]{:S(2)}, u32[]{:S(2)}) collective-permute-start(bf16[80,128]{1,0:T(8,128)(2,1)S(1)} %get-tuple-element.49), channel_id=1, source_target_pairs={{0,2},{1,3},{2,0},{3,1},{4,6},{5,7},{6,4},{7,5},{8,10},{9,11},{10,... | collective-permute-start | bytes 61448 | tf_op jit(solution)/shard_map/ppermute | solution.py:489
  38.1 11.9 %all-to-all-start = ((bf16[8,80,128]{2,1,0:T(8,128)(2,1)}), bf16[8,80,128]{2,1,0:T(8,128)(2,1)S(1)}, u32[]{:S(2)}, u32[]{:S(2)}) async-start(bf16[8,80,128]{2,1,0:T(8,128)(2,1)} %add.29), calls=%async_computation | async-start | bytes 327680 | tf_op jit(solution)/shard_map/all_to_all | solution.py:514
  41.6 9.4 %collective-permute-start.5 = (bf16[648,128]{1,0:T(8,128)(2,1)S(1)}, bf16[648,128]{1,0:T(8,128)(2,1)S(1)}, u32[]{:S(2)}, u32[]{:S(2)}) collective-permute-start(bf16[648,128]{1,0:T(8,128)(2,1)S(1)} %get-tuple-element.38), channel_id=1, source_target_pairs={{0,32},{1,33},{2,34},{3,35},{4,36},{5,37},{6,38},{7,39},{8,40},{9,... | collective-permute-start | bytes 497672 | tf_op jit(solution)/shard_map/ppermute | solution.py:44
  42.4 8.6 %collective-permute-start.6 = (bf16[216,128]{1,0:T(8,128)(2,1)S(1)}, bf16[216,128]{1,0:T(8,128)(2,1)S(1)}, u32[]{:S(2)}, u32[]{:S(2)}) collective-permute-start(bf16[216,128]{1,0:T(8,128)(2,1)S(1)} %get-tuple-element.39), channel_id=1, source_target_pairs={{0,33},{1,34},{2,35},{3,36},{4,37},{5,38},{6,39},{7,40},{8,41},{9,... | collective-permute-start | bytes 165896 | tf_op jit(solution)/shard_map/ppermute | solution.py:44
  44.7 6.3 %collective-permute-start.7 = (bf16[216,128]{1,0:T(8,128)(2,1)S(1)}, bf16[216,128]{1,0:T(8,128)(2,1)S(1)}, u32[]{:S(2)}, u32[]{:S(2)}) collective-permute-start(bf16[216,128]{1,0:T(8,128)(2,1)S(1)} %get-tuple-element.40), channel_id=1, source_target_pairs={{0,1},{1,2},{2,3},{3,4},{4,5},{5,6},{6,7},{7,8},{8,9},{9,10},{10,1... | collective-permute-start | bytes 165896 | tf_op jit(solution)/shard_map/ppermute | solution.py:44
  51.0 4.1 %collective-permute-start.8 = (bf16[80,128]{1,0:T(8,128)(2,1)S(1)}, bf16[80,128]{1,0:T(8,128)(2,1)S(1)}, u32[]{:S(2)}, u32[]{:S(2)}) collective-permute-start(bf16[80,128]{1,0:T(8,128)(2,1)S(1)} %bitcast.26), channel_id=1, source_target_pairs={{0,2},{1,3},{2,0},{3,1},{4,6},{5,7},{6,4},{7,5},{8,10},{9,11},{10,... | collective-permute-start | bytes 61448 | tf_op jit(solution)/shard_map/ppermute | solution.py:489
  55.2 4.9 %collective-permute-start.9 = (bf16[2,80,128]{2,1,0:T(8,128)(2,1)S(1)}, bf16[2,80,128]{2,1,0:T(8,128)(2,1)S(1)}, u32[]{:S(2)}, u32[]{:S(2)}) collective-permute-start(bf16[2,80,128]{2,1,0:T(8,128)(2,1)S(1)} %pad_maximum_fusion.mine_ref), channel_id=1, source_target_pairs={{0,1},{1,0},{2,3},{3,2},{4,5},{5,4},{6,7},{7,6},{8,9},{9,8},{10,11... | collective-permute-start | bytes 122888 | tf_op jit(solution)/shard_map/ppermute | solution.py:489

commit v10 on v9

--- a/solution.py
+++ b/solution.py
@@ -22,6 +22,9 @@
 SLOTS = 16
 QUARTER = PAIR * HEADS // 2
 REST = 20
+LN_ROWS = 96
+GELU_ROWS = 48
+LANE_CUTS = [(k, min(k + 256, ROWS)) for k in range(0, ROWS, 256)]
 DENSE = 80
 LANES = 128
 
@@ -75,7 +78,20 @@
     half = 0.5 + 0.5 * tangent
     result = values * half
     derivative = half + result * (1.0 - tangent) * (factor + (3.0 * gelu_coef * factor) * square)
-    return result, derivative
+    return result.astype(bf16), derivative
+
+
+def by_rows(function, size, *arrays):
+    rows = arrays[0].shape[0]
+    parts = [function(*(v[r : r + size] for v in arrays)) for r in range(0, rows, size)]
+    return tuple(jnp.concatenate(part, axis=0) for part in zip(*parts))
+
+
+def masked_softmax(scores, bias, allowed):
+    scores = scores * (LOG2E / math.sqrt(HD)) + bias
+    scores = jnp.where(allowed, scores, -1e30)
+    weights = jnp.exp2(scores - jnp.max(scores, axis=0, keepdims=True))
+    return weights * (1.0 / jnp.sum(weights, axis=0, keepdims=True))
 
 
 def head_blocks(wide):
@@ -205,7 +221,6 @@
     bias_ref,
     label_row_ref,
     label_col_ref,
-    keep_ref,
     fold_out,
     own_out,
     lat_out,
@@ -260,7 +275,7 @@
         both = slice(n * 2 * POS, (n + 1) * 2 * POS)
         x = mm(perm, frame[0, both, :].astype(bf16))
         cot = mm(perm, frame[1, both, :].astype(bf16))
-        scaled1, normed1, inverse1 = norm_parts(x, gain1)
+        scaled1, normed1, inverse1 = by_rows(lambda v: norm_parts(v, gain1), LN_ROWS, x)
         h1 = scaled1.astype(bf16)
         q_all = mm_nt(h1, wq_t).astype(bf16)
         k_all = mm_nt(h1, wk_t).astype(bf16)
@@ -272,43 +287,56 @@
             rows = slice(c * POS, (c + 1) * POS)
             v_t = mm_nt(wv_t, h1[rows]).astype(bf16)
             q_wide = spread_heads(q_all[rows], head_mask)
-            scores = mm_nt(k_all[rows], q_wide) * (root * LOG2E) + bias_ref[n]
-            allowed = label_col_ref[:, w : w + 1] == label_row_ref[w : w + 1, :]
-            scores = jnp.where(allowed, scores, -1e30)
-            weights = jnp.exp2(scores - jnp.max(scores, axis=0, keepdims=True))
-            probs = weights * (1.0 / jnp.sum(weights, axis=0, keepdims=True))
-            probs_low = probs.astype(bf16)
-            attended = head_blocks(mm(v_t, probs_low)).T.astype(bf16)
-            factor = keep_ref[n, 0, c].astype(f32) * (1.0 / keep_share)
+            label_col = label_col_ref[:, w : w + 1]
+            probs = []
+            for low, high in LANE_CUTS:
+                scores = mm_nt(k_all[rows], q_wide[low:high])
+                allowed = label_col == label_row_ref[w : w + 1, low:high]
+                probs.append(masked_softmax(scores, bias_ref[n, :, low:high], allowed))
+            probs_low = jnp.concatenate([part.astype(bf16) for part in probs], axis=1)
+            attended = head_blocks(mm(v_t, probs_low)).astype(bf16).T
+            factor = gains_ref[2 + w : 3 + w, :]
             branches.append((mm(attended, wproj_ref[...]) * factor).astype(bf16).astype(f32))
             saved.append((q_wide, probs, probs_low))
         y_sum = x + jnp.concatenate(branches, axis=0)
-        scaled2, normed2, inverse2 = norm_parts(y_sum, gain2)
-        act, slope = gelu_parts(mm(scaled2.astype(bf16), wup_ref[...]))
-        result = (y_sum + mm_nt(act.astype(bf16), wdown_t_ref[...])).astype(bf16)
+        scaled2, normed2, inverse2 = by_rows(lambda v: norm_parts(v, gain2), LN_ROWS, y_sum)
+        act, slope = by_rows(gelu_parts, GELU_ROWS, mm(scaled2.astype(bf16), wup_ref[...]))
+        result = (y_sum + mm_nt(act, wdown_t_ref[...])).astype(bf16)
         grad_up = (mm(cot.astype(bf16), wdown_t_ref[...]) * slope).astype(bf16)
-        grad_sum = cot + norm_back(mm_nt(grad_up, wup_ref[...]), gain2, normed2, inverse2)
+        grad_hidden = mm_nt(grad_up, wup_ref[...])
+        (grad_sum,) = by_rows(
+            lambda v, g, normed, inverse: (v + norm_back(g, gain2, normed, inverse),),
+            LN_ROWS,
+            cot,
+            grad_hidden,
+            normed2,
+            inverse2,
+        )
         grad_low_in = grad_sum.astype(bf16).astype(f32)
-        folded = None
+        folded = [None] * len(LANE_CUTS)
         grad_h1 = []
         for c in range(2):
             rows = slice(c * POS, (c + 1) * POS)
             q_wide, probs, probs_low = saved[c]
-            factor = keep_ref[n, 0, c].astype(f32) * (1.0 / keep_share)
+            factor = gains_ref[2 + 2 * n + c : 3 + 2 * n + c, :]
             grad_branch = (grad_low_in[rows] * factor).astype(bf16)
             grad_att = mm_nt(grad_branch, wproj_ref[...]).astype(bf16)
             g_wide = spread_heads(grad_att, head_mask)
-            grad_probs = mm_nt(v_all[rows], g_wide)
-            inner_sum = jnp.sum(probs * grad_probs, axis=0, keepdims=True)
-            grad_scores = probs * (grad_probs - inner_sum)
-            folded = grad_scores if folded is None else folded + grad_scores
-            grad_low = grad_scores.astype(bf16)
+            grad_low = []
+            for k, (low, high) in enumerate(LANE_CUTS):
+                grad_probs = mm_nt(v_all[rows], g_wide[low:high])
+                inner_sum = jnp.sum(probs[k] * grad_probs, axis=0, keepdims=True)
+                grad_scores = probs[k] * (grad_probs - inner_sum)
+                folded[k] = grad_scores if c == 0 else folded[k] + grad_scores
+                grad_low.append(grad_scores.astype(bf16))
+            grad_low = jnp.concatenate(grad_low, axis=1)
             k_t = mm_nt(wk_t, h1[rows]).astype(bf16)
-            grad_q = (head_blocks(mm(k_t, grad_low)).T * root).astype(bf16)
+            grad_q = (head_blocks(mm(k_t, grad_low)) * root).astype(bf16).T
             grad_k = (mm(grad_low, q_wide) * root).astype(bf16)
             grad_v = mm(probs_low, g_wide).astype(bf16)
             grad_h1.append(mm(grad_q, wq_t) + mm(grad_k, wk_t) + mm(grad_v, wv_t))
-        wide[...] = folded.T.reshape(HEADS, POS, POS)
+        folded = jnp.concatenate([part.astype(bf16) for part in folded], axis=1)
+        wide[...] = folded.T.astype(f32).reshape(HEADS, POS, POS)
         total = None
         for o in range(WLON):
             left = PAIR * (WLON - 1 - o)
@@ -332,7 +360,16 @@
             dense[2 * QUARTER : 2 * QUARTER + HEADS, : WLAT * REST] = jnp.concatenate(rest, axis=1)
             fold_out[2 * n + k] = dense[...].astype(bf16)
         grad_h1 = jnp.concatenate(grad_h1, axis=0).astype(bf16).astype(f32)
-        grad_field = (grad_sum + norm_back(grad_h1, gain1, normed1, inverse1)).astype(bf16)
+        (grad_field,) = by_rows(
+            lambda v, g, normed, inverse: (
+                (v + norm_back(g, gain1, normed, inverse)).astype(bf16),
+            ),
+            LN_ROWS,
+            grad_sum,
+            grad_h1,
+            normed1,
+            inverse1,
+        )
         for t, value in enumerate((result, grad_field)):
             natural = mm(perm_t, value)
             for dz in range(WZ):
@@ -358,6 +395,7 @@
     wqkv_ref,
     gain1_ref,
     gain2_ref,
+    keep_ref,
     bias_out,
     label_row_out,
     label_col_out,
@@ -371,6 +409,11 @@
     wqkv_t_out[...] = wqkv_ref[...].astype(f32).T.astype(bf16)
     gains_out[0:1, :] = gain1_ref[...]
     gains_out[1:2, :] = gain2_ref[...]
+    for n in range(2):
+        for c in range(2):
+            factor = keep_ref[n, 0, c].astype(f32) * (1.0 / keep_share)
+            row = 2 + 2 * n + c
+            gains_out[row : row + 1, :] = jnp.full((1, C), factor, f32)
     last = lax.axis_index("lat") == lax.axis_size("lat") - 1
     level = lax.broadcasted_iota(jnp.int32, (4, 2 * WLON), 0)
     for i in range(WLAT):
@@ -573,9 +616,9 @@
             jax.ShapeDtypeStruct((4, ROWS), f32),
             jax.ShapeDtypeStruct((POS, 4), f32),
             jax.ShapeDtypeStruct((3 * C, C), bf16),
-            jax.ShapeDtypeStruct((2, C), f32),
+            jax.ShapeDtypeStruct((6, C), f32),
         ),
-        in_specs=[vmem] * 5,
+        in_specs=[vmem] * 5 + [smem],
         out_specs=(vmem,) * 5,
         scratch_shapes=[
             pltpu.VMEM((2 * HEADS, PAIR * TAB), f32),
@@ -591,6 +634,7 @@
         w_qkv,
         ln1_gain.reshape(1, C),
         ln2_gain.reshape(1, C),
+        keep_flags,
     )
     positions = levels * lat_rows * lon_cols
     fold, own, *strips = pl.pallas_call(
@@ -600,7 +644,7 @@
             jax.ShapeDtypeStruct((2, levels, half, inner, C), bf16),
         )
         + packed,
-        in_specs=[vmem] * 13 + [smem],
+        in_specs=[vmem] * 13,
         out_specs=(vmem,) * 5,
         scratch_shapes=[
             pltpu.VMEM((2, positions, C), f32),
@@ -624,7 +668,6 @@
         bias_wide,
         label_row,
         label_col,
-        keep_flags,
     )
     halves, (lat_back, diag_back, lon_back) = lon_sum(fold, strips)
     grads = pl.pallas_call(

time: 61.2 us -> 60.5 us (0.989)
  local copies, waits for them, and re-layouts: 2.61 us -> 1.99 us
    pallas_call x1, Pallas kernels: 11.9 us -> 11 us  [body(): pl.pallas_call(block_kernel, out_shape=(jax.ShapeDtypeStruct((4, DENSE, L...]
    unnamed x26, local copies, waits for them, and re-layouts: 2.58 us -> 1.96 us
  transfers between devices with their start and end apart: 11 -> 11, of which waited for: 5 -> 5; matrix products, arithmetic and copies ran while one was open for 0% -> 0% of each run, Pallas kernels for 6% -> 7%
where the time goes in v10:
time: 60.5 us; the launch traced here: 60.2 us
  starting transfers between devices  27 us (45%)
  Pallas kernels  17 us (28%)
  waiting for transfers between devices  13.5 us (22%)
  local copies, waits for them, and re-layouts  1.99 us (3%)
  between operations  0.82 us (1%)
    ppermute x6, starting transfers between devices, shifted(): return lax.ppermute(block, ('lat', 'lon'), route)  16.2 us
    pallas_call x1, Pallas kernels, body(): pl.pallas_call(block_kernel, out_shape=(jax.ShapeDtypeStruct((4, DENSE, L...  11 us
    ppermute x4, waiting for transfers between devices, swapped(): return lax.ppermute(block, 'lon', [(i, i ^ distance) for i in range(lons)])  7.77 us
    ppermute x4, starting transfers between devices, swapped(): return lax.ppermute(block, 'lon', [(i, i ^ distance) for i in range(lons)])  7.24 us
    all_to_all x1, waiting for transfers between devices, lon_sum(): parts = lax.all_to_all(parts, 'lon', 0, 0, axis_index_groups=far)  4.66 us
    all_to_all x1, starting transfers between devices, lon_sum(): parts = lax.all_to_all(parts, 'lon', 0, 0, axis_index_groups=far)  3.48 us
    pallas_call x1, Pallas kernels, body(): pl.pallas_call(prepare_kernel, out_shape=(jax.ShapeDtypeStruct((2, POS, R...  3.16 us
    unnamed x26, local copies, waits for them, and re-layouts  1.96 us
  transfers between devices with their start and end apart: 11, of which 5 were waited for; matrix products, arithmetic and copies ran while one was open for 0% of the time, Pallas kernels for 7%

profile of v10, /device:TPU:1, one launch (start us, length us, event | category | flops | bytes accessed | tf_op | source)
XLA Modules:
  0.0 60.2 jit_solution(6133075323510340947)
XLA Ops:
  0.6 1.0 %copy-done = bf16[4,6,24,192]{3,2,1,0:T(8,128)(2,1)S(1)} copy-done((bf16[4,6,24,192]{3,2,1,0:T(8,128)(2,1)S(1)}, bf16[4,6,24,192]{3,2,1,0:T(8,128)(2,1)}, u32[]{:S(2)}) %copy-start) | copy-done | bytes 221208
  1.6 1.0 %copy-done.2 = bf16[4,6,24,192]{3,2,1,0:T(8,128)(2,1)S(1)} copy-done((bf16[4,6,24,192]{3,2,1,0:T(8,128)(2,1)S(1)}, bf16[4,6,24,192]{3,2,1,0:T(8,128)(2,1)}, u32[]{:S(2)}) %copy-start.2) | copy-done | bytes 221208
  2.6 0.2 pack_lat.1.after_ref
  2.9 4.4 %collective-permute-start.1 = (bf16[648,128]{1,0:T(8,128)(2,1)S(1)}, bf16[648,128]{1,0:T(8,128)(2,1)S(1)}, u32[]{:S(2)}, u32[]{:S(2)}) collective-permute-start(bf16[648,128]{1,0:T(8,128)(2,1)S(1)} %pack_lat.1.after_ref), channel_id=1, source_target_pairs={{0,224},{1,225},{2,226},{3,227},{4,228},{5,229},{6,230},{7,231},{8... | collective-permute-start | bytes 497672 | tf_op jit(solution)/shard_map/ppermute | solution.py:47
  7.4 1.0 %collective-permute-start = (bf16[216,128]{1,0:T(8,128)(2,1)S(1)}, bf16[216,128]{1,0:T(8,128)(2,1)S(1)}, u32[]{:S(2)}, u32[]{:S(2)}) collective-permute-start(bf16[216,128]{1,0:T(8,128)(2,1)S(1)} %get-tuple-element.25), channel_id=1, source_target_pairs={{0,31},{1,0},{2,1},{3,2},{4,3},{5,4},{6,5},{7,6},{8,7},{9,8},{10,9... | collective-permute-start | bytes 165896 | tf_op jit(solution)/shard_map/ppermute | solution.py:47
  8.4 7.1 %collective-permute-start.2 = (bf16[216,128]{1,0:T(8,128)(2,1)S(1)}, bf16[216,128]{1,0:T(8,128)(2,1)S(1)}, u32[]{:S(2)}, u32[]{:S(2)}) collective-permute-start(bf16[216,128]{1,0:T(8,128)(2,1)S(1)} %get-tuple-element.26), channel_id=1, source_target_pairs={{0,255},{1,224},{2,225},{3,226},{4,227},{5,228},{6,229},{7,230},{8... | collective-permute-start | bytes 165896 | tf_op jit(solution)/shard_map/ppermute | solution.py:47
  15.5 3.2 %prepare.1 = (f32[2,144,864]{2,1,0:T(8,128)S(1)}, f32[4,864]{1,0:T(4,128)S(1)}, f32[144,4]{1,0:T(8,128)S(1)}, bf16[576,192]{1,0:T(8,128)(2,1)S(1)}, f32[6,192]{1,0:T(8,128)S(1)}) custom-call(f32[12,1,3312]{2,1,0:T(1,128)S(1)} %bitcast.23, s32[6,4,24]{2,1,0:T(4,128)S(1)} %bitcast.29, bf16[192,576]{1,0:T(8,128)(2,1)S(1)} %copy-done.6, f32[1,192]{1,0:T(1,128)S(1)} %bitcast.30, ...), custom_call_target="tpu_custom_call" | custom-call | tf_op jit(solution)/shard_map/prepare/pallas_call | solution.py:612
  18.8 11.0 %block.1 = (bf16[4,80,128]{2,1,0:T(8,128)(2,1)S(1)}, bf16[2,4,3,18,192]{4,3,2,1,0:T(8,128)(2,1)S(1)}, bf16[648,128]{1,0:T(8,128)(2,1)S(1)}, bf16[216,128]{1,0:T(8,128)(2,1)S(1)}, bf16[216,128]{1,0:T(8,128)(2,1)S(1)}) custom-call(bf16[4,6,24,192]{3,2,1,0:T(8,128)(2,1)S(1)} %copy-done.1, bf16[4,6,24,192]{3,2,1,0:T(8,128)(2,1)S(1)} %copy-done.3, ...), custom_call_target="tpu_custom_call" | custom-call | tf_op jit(solution)/shard_map/block/pallas_call | solution.py:640
  29.8 0.7 %collective-permute-start.3 = (bf16[2,80,128]{2,1,0:T(8,128)(2,1)S(1)}, bf16[2,80,128]{2,1,0:T(8,128)(2,1)S(1)}, u32[]{:S(2)}, u32[]{:S(2)}) collective-permute-start(bf16[2,80,128]{2,1,0:T(8,128)(2,1)S(1)} %dynamic-slice_bitcast_fusion), channel_id=1, source_target_pairs={{0,1},{1,0},{2,3},{3,2},{4,5},{5,4},{6,7},{7,6},{8,9},{9,8},{10,11... | collective-permute-start | bytes 122888 | tf_op jit(solution)/shard_map/ppermute | solution.py:532
  30.5 0.9 %collective-permute-done.3 = bf16[2,80,128]{2,1,0:T(8,128)(2,1)S(1)} collective-permute-done((bf16[2,80,128]{2,1,0:T(8,128)(2,1)S(1)}, bf16[2,80,128]{2,1,0:T(8,128)(2,1)S(1)}, u32[]{:S(2)}, u32[]{:S(2)}) %collective-permute-start.3) | collective-permute-done | bytes 40992 | tf_op jit(solution)/shard_map/ppermute | solution.py:532
  31.4 0.3 collective-permute-start.4
  31.7 4.1 %collective-permute-done.4 = bf16[80,128]{1,0:T(8,128)(2,1)S(1)} collective-permute-done((bf16[80,128]{1,0:T(8,128)(2,1)S(1)}, bf16[80,128]{1,0:T(8,128)(2,1)S(1)}, u32[]{:S(2)}, u32[]{:S(2)}) %collective-permute-start.4) | collective-permute-done | bytes 20512 | tf_op jit(solution)/shard_map/ppermute | solution.py:532
  35.8 0.7 %add.29 = bf16[8,80,128]{2,1,0:T(8,128)(2,1)} custom-call(bf16[1,80,128]{2,1,0:T(8,128)(2,1)S(1)} %get-tuple-element.50.refs_0_, bf16[1,80,128]{2,1,0:T(8,128)(2,1)S(1)} %bitcast.28), custom_call_target="tpu_custom_call" | custom-call | tf_op jit(solution)/shard_map/add/pallas_call | solution.py:539
  36.5 3.5 %all-to-all-start = ((bf16[8,80,128]{2,1,0:T(8,128)(2,1)}), bf16[8,80,128]{2,1,0:T(8,128)(2,1)S(1)}, u32[]{:S(2)}, u32[]{:S(2)}) async-start(bf16[8,80,128]{2,1,0:T(8,128)(2,1)} %add.29), calls=%async_computation | async-start | bytes 327680 | tf_op jit(solution)/shard_map/all_to_all | solution.py:557
  40.0 1.4 %collective-permute-start.5 = (bf16[648,128]{1,0:T(8,128)(2,1)S(1)}, bf16[648,128]{1,0:T(8,128)(2,1)S(1)}, u32[]{:S(2)}, u32[]{:S(2)}) collective-permute-start(bf16[648,128]{1,0:T(8,128)(2,1)S(1)} %get-tuple-element.38), channel_id=1, source_target_pairs={{0,32},{1,33},{2,34},{3,35},{4,36},{5,37},{6,38},{7,39},{8,40},{9,... | collective-permute-start | bytes 497672 | tf_op jit(solution)/shard_map/ppermute | solution.py:47
  41.3 1.8 %collective-permute-start.6 = (bf16[216,128]{1,0:T(8,128)(2,1)S(1)}, bf16[216,128]{1,0:T(8,128)(2,1)S(1)}, u32[]{:S(2)}, u32[]{:S(2)}) collective-permute-start(bf16[216,128]{1,0:T(8,128)(2,1)S(1)} %get-tuple-element.39), channel_id=1, source_target_pairs={{0,33},{1,34},{2,35},{3,36},{4,37},{5,38},{6,39},{7,40},{8,41},{9,... | collective-permute-start | bytes 165896 | tf_op jit(solution)/shard_map/ppermute | solution.py:47
  43.1 0.6 collective-permute-start.7
  43.7 4.7 %all-to-all-done.refs_0_ = bf16[8,80,128]{2,1,0:T(8,128)(2,1)S(1)} async-done(((bf16[8,80,128]{2,1,0:T(8,128)(2,1)}), bf16[8,80,128]{2,1,0:T(8,128)(2,1)S(1)}, u32[]{:S(2)}, u32[]{:S(2)}) %all-to-all-start) | async-done | bytes 163872 | tf_op jit(solution)/shard_map/all_to_all | solution.py:557
  48.4 1.0 %collective-permute-done.6.diag_ref = bf16[216,128]{1,0:T(8,128)(2,1)S(1)} collective-permute-done((bf16[216,128]{1,0:T(8,128)(2,1)S(1)}, bf16[216,128]{1,0:T(8,128)(2,1)S(1)}, u32[]{:S(2)}, u32[]{:S(2)}) %collective-permute-start.6) | collective-permute-done | bytes 55328 | tf_op jit(solution)/shard_map/ppermute | solution.py:47
  49.4 1.4 %collective-permute-start.8 = (bf16[80,128]{1,0:T(8,128)(2,1)S(1)}, bf16[80,128]{1,0:T(8,128)(2,1)S(1)}, u32[]{:S(2)}, u32[]{:S(2)}) collective-permute-start(bf16[80,128]{1,0:T(8,128)(2,1)S(1)} %bitcast.26), channel_id=1, source_target_pairs={{0,2},{1,3},{2,0},{3,1},{4,6},{5,7},{6,4},{7,5},{8,10},{9,11},{10,... | collective-permute-start | bytes 61448 | tf_op jit(solution)/shard_map/ppermute | solution.py:532
  50.8 2.8 %collective-permute-done.8 = bf16[80,128]{1,0:T(8,128)(2,1)S(1)} collective-permute-done((bf16[80,128]{1,0:T(8,128)(2,1)S(1)}, bf16[80,128]{1,0:T(8,128)(2,1)S(1)}, u32[]{:S(2)}, u32[]{:S(2)}) %collective-permute-start.8) | collective-permute-done | bytes 20512 | tf_op jit(solution)/shard_map/ppermute | solution.py:532
  53.5 4.9 %collective-permute-start.9 = (bf16[2,80,128]{2,1,0:T(8,128)(2,1)S(1)}, bf16[2,80,128]{2,1,0:T(8,128)(2,1)S(1)}, u32[]{:S(2)}, u32[]{:S(2)}) collective-permute-start(bf16[2,80,128]{2,1,0:T(8,128)(2,1)S(1)} %pad_maximum_fusion.mine_ref), channel_id=1, source_target_pairs={{0,1},{1,0},{2,3},{3,2},{4,5},{5,4},{6,7},{7,6},{8,9},{9,8},{10,11... | collective-permute-start | bytes 122888 | tf_op jit(solution)/shard_map/ppermute | solution.py:532
  58.4 0.9 %finish.1 = (bf16[4,6,24,192]{3,2,1,0:T(8,128)(2,1)}, bf16[4,6,24,192]{3,2,1,0:T(8,128)(2,1)}) custom-call(bf16[2,4,3,18,192]{4,3,2,1,0:T(8,128)(2,1)S(1)} %get-tuple-element.32.own_ref, bf16[648,128]{1,0:T(8,128)(2,1)S(1)} %collective-permute-done.5.lat_ref, bf16[216,128]{1,0:T(8,128)(2,1)S(1)} %collective-permute-done.6.diag_ref, ...), custom_call_target="tpu_custom_call" | custom-call | tf_op jit(solution)/shard_map/finish/pallas_call | solution.py:683
  59.3 0.9 %unpack.1 = f32[12,1,3312]{2,1,0:T(1,128)} custom-call(bf16[2,80,128]{2,1,0:T(8,128)(2,1)S(1)} %pad_maximum_fusion.mine_ref, bf16[2,80,128]{2,1,0:T(8,128)(2,1)S(1)} %collective-permute-done.9.other_ref), custom_call_target="tpu_custom_call" | custom-call | tf_op jit(solution)/shard_map/unpack/pallas_call | solution.py:673
  (37 shorter events, 0.2 us)
Async XLA Ops:
  0.6 1.0 %copy-start = (bf16[4,6,24,192]{3,2,1,0:T(8,128)(2,1)S(1)}, bf16[4,6,24,192]{3,2,1,0:T(8,128)(2,1)}, u32[]{:S(2)}) copy-start(bf16[4,6,24,192]{3,2,1,0:T(8,128)(2,1)} %field_ref.5) | copy-start | bytes 663556
  1.6 1.0 %copy-start.2 = (bf16[4,6,24,192]{3,2,1,0:T(8,128)(2,1)S(1)}, bf16[4,6,24,192]{3,2,1,0:T(8,128)(2,1)}, u32[]{:S(2)}) copy-start(bf16[4,6,24,192]{3,2,1,0:T(8,128)(2,1)} %cot_ref.5) | copy-start | bytes 663556
  2.6 12.9 %copy-start.6 = (bf16[192,576]{1,0:T(8,128)(2,1)S(1)}, bf16[192,576]{1,0:T(8,128)(2,1)}, u32[]{:S(2)}) copy-start(bf16[192,576]{1,0:T(8,128)(2,1)} %wqkv_ref.1) | copy-start | bytes 663556
  2.6 12.9 %copy-start.7 = (f32[2,1,6,3312]{3,1,2,0:T(1,128)S(1)}, f32[2,1,6,3312]{3,1,2,0:T(1,128)}, u32[]{:S(2)}) copy-start(f32[2,1,6,3312]{3,1,2,0:T(1,128)} %param.19) | copy-start | bytes 476932
  2.6 12.9 %copy-start.10 = (f32[192]{0:T(256)S(1)}, f32[192]{0:T(256)}, u32[]{:S(2)}) copy-start(f32[192]{0:T(256)} %param.13) | copy-start | bytes 2308
  2.6 12.9 %copy-start.11 = (f32[192]{0:T(256)S(1)}, f32[192]{0:T(256)}, u32[]{:S(2)}) copy-start(f32[192]{0:T(256)} %param.16) | copy-start | bytes 2308
  2.6 12.9 %copy-start.12 = (s32[2,1,2]{2,1,0:T(1,128)S(1)}, s32[2,1,2]{2,1,0:T(1,128)}, u32[]{:S(2)}) copy-start(s32[2,1,2]{2,1,0:T(1,128)} %keep_ref.1) | copy-start | bytes 52
  2.6 16.2 %copy-start.8 = (bf16[192,192]{1,0:T(8,128)(2,1)S(1)}, bf16[192,192]{1,0:T(8,128)(2,1)}, u32[]{:S(2)}) copy-start(bf16[192,192]{1,0:T(8,128)(2,1)} %wproj_ref.1) | copy-start | bytes 221188
  2.8 12.7 %copy-start.9 = (s32[4,6,24]{2,0,1:T(4,128)S(1)}, s32[4,6,24]{2,0,1:T(4,128)}, u32[]{:S(2)}) copy-start(s32[4,6,24]{2,0,1:T(4,128)} %param.20) | copy-start | bytes 6916
  2.9 15.9 %collective-permute-start.1 = (bf16[648,128]{1,0:T(8,128)(2,1)S(1)}, bf16[648,128]{1,0:T(8,128)(2,1)S(1)}, u32[]{:S(2)}, u32[]{:S(2)}) collective-permute-start(bf16[648,128]{1,0:T(8,128)(2,1)S(1)} %pack_lat.1.after_ref), channel_id=1, source_target_pairs={{0,224},{1,225},{2,226},{3,227},{4,228},{5,229},{6,230},{7,231},{8... | collective-permute-start | bytes 497672 | tf_op jit(solution)/shard_map/ppermute | solution.py:47
  7.3 11.5 %copy-start.3 = (bf16[4,6,24,192]{3,2,1,0:T(8,128)(2,1)S(1)}, bf16[4,6,24,192]{3,2,1,0:T(8,128)(2,1)}, u32[]{:S(2)}) copy-start(bf16[4,6,24,192]{3,2,1,0:T(8,128)(2,1)} %cot_ref.5) | copy-start | bytes 663556
  7.3 11.5 %copy-start.4 = (bf16[192,768]{1,0:T(8,128)(2,1)S(1)}, bf16[192,768]{1,0:T(8,128)(2,1)}, u32[]{:S(2)}) copy-start(bf16[192,768]{1,0:T(8,128)(2,1)} %wup_ref.1) | copy-start | bytes 884740
  7.3 11.5 %copy-start.5 = (bf16[768,192]{0,1:T(8,128)(2,1)S(1)}, bf16[768,192]{0,1:T(8,128)(2,1)}, u32[]{:S(2)}) copy-start(bf16[768,192]{0,1:T(8,128)(2,1)} %param.18) | copy-start | bytes 884740
  7.4 11.4 %copy-start.1 = (bf16[4,6,24,192]{3,2,1,0:T(8,128)(2,1)S(1)}, bf16[4,6,24,192]{3,2,1,0:T(8,128)(2,1)}, u32[]{:S(2)}) copy-start(bf16[4,6,24,192]{3,2,1,0:T(8,128)(2,1)} %field_ref.5) | copy-start | bytes 663556
  7.4 11.3 %collective-permute-start = (bf16[216,128]{1,0:T(8,128)(2,1)S(1)}, bf16[216,128]{1,0:T(8,128)(2,1)S(1)}, u32[]{:S(2)}, u32[]{:S(2)}) collective-permute-start(bf16[216,128]{1,0:T(8,128)(2,1)S(1)} %get-tuple-element.25), channel_id=1, source_target_pairs={{0,31},{1,0},{2,1},{3,2},{4,3},{5,4},{6,5},{7,6},{8,7},{9,8},{10,9... | collective-permute-start | bytes 165896 | tf_op jit(solution)/shard_map/ppermute | solution.py:47
  8.4 10.3 %collective-permute-start.2 = (bf16[216,128]{1,0:T(8,128)(2,1)S(1)}, bf16[216,128]{1,0:T(8,128)(2,1)S(1)}, u32[]{:S(2)}, u32[]{:S(2)}) collective-permute-start(bf16[216,128]{1,0:T(8,128)(2,1)S(1)} %get-tuple-element.26), channel_id=1, source_target_pairs={{0,255},{1,224},{2,225},{3,226},{4,227},{5,228},{6,229},{7,230},{8... | collective-permute-start | bytes 165896 | tf_op jit(solution)/shard_map/ppermute | solution.py:47
  29.8 1.6 %collective-permute-start.3 = (bf16[2,80,128]{2,1,0:T(8,128)(2,1)S(1)}, bf16[2,80,128]{2,1,0:T(8,128)(2,1)S(1)}, u32[]{:S(2)}, u32[]{:S(2)}) collective-permute-start(bf16[2,80,128]{2,1,0:T(8,128)(2,1)S(1)} %dynamic-slice_bitcast_fusion), channel_id=1, source_target_pairs={{0,1},{1,0},{2,3},{3,2},{4,5},{5,4},{6,7},{7,6},{8,9},{9,8},{10,11... | collective-permute-start | bytes 122888 | tf_op jit(solution)/shard_map/ppermute | solution.py:532
  31.4 4.4 %collective-permute-start.4 = (bf16[80,128]{1,0:T(8,128)(2,1)S(1)}, bf16[80,128]{1,0:T(8,128)(2,1)S(1)}, u32[]{:S(2)}, u32[]{:S(2)}) collective-permute-start(bf16[80,128]{1,0:T(8,128)(2,1)S(1)} %get-tuple-element.49), channel_id=1, source_target_pairs={{0,2},{1,3},{2,0},{3,1},{4,6},{5,7},{6,4},{7,5},{8,10},{9,11},{10,... | collective-permute-start | bytes 61448 | tf_op jit(solution)/shard_map/ppermute | solution.py:532
  36.5 11.9 %all-to-all-start = ((bf16[8,80,128]{2,1,0:T(8,128)(2,1)}), bf16[8,80,128]{2,1,0:T(8,128)(2,1)S(1)}, u32[]{:S(2)}, u32[]{:S(2)}) async-start(bf16[8,80,128]{2,1,0:T(8,128)(2,1)} %add.29), calls=%async_computation | async-start | bytes 327680 | tf_op jit(solution)/shard_map/all_to_all | solution.py:557
  40.0 9.4 %collective-permute-start.5 = (bf16[648,128]{1,0:T(8,128)(2,1)S(1)}, bf16[648,128]{1,0:T(8,128)(2,1)S(1)}, u32[]{:S(2)}, u32[]{:S(2)}) collective-permute-start(bf16[648,128]{1,0:T(8,128)(2,1)S(1)} %get-tuple-element.38), channel_id=1, source_target_pairs={{0,32},{1,33},{2,34},{3,35},{4,36},{5,37},{6,38},{7,39},{8,40},{9,... | collective-permute-start | bytes 497672 | tf_op jit(solution)/shard_map/ppermute | solution.py:47
  41.3 8.1 %collective-permute-start.6 = (bf16[216,128]{1,0:T(8,128)(2,1)S(1)}, bf16[216,128]{1,0:T(8,128)(2,1)S(1)}, u32[]{:S(2)}, u32[]{:S(2)}) collective-permute-start(bf16[216,128]{1,0:T(8,128)(2,1)S(1)} %get-tuple-element.39), channel_id=1, source_target_pairs={{0,33},{1,34},{2,35},{3,36},{4,37},{5,38},{6,39},{7,40},{8,41},{9,... | collective-permute-start | bytes 165896 | tf_op jit(solution)/shard_map/ppermute | solution.py:47
  43.1 6.3 %collective-permute-start.7 = (bf16[216,128]{1,0:T(8,128)(2,1)S(1)}, bf16[216,128]{1,0:T(8,128)(2,1)S(1)}, u32[]{:S(2)}, u32[]{:S(2)}) collective-permute-start(bf16[216,128]{1,0:T(8,128)(2,1)S(1)} %get-tuple-element.40), channel_id=1, source_target_pairs={{0,1},{1,2},{2,3},{3,4},{4,5},{5,6},{6,7},{7,8},{8,9},{9,10},{10,1... | collective-permute-start | bytes 165896 | tf_op jit(solution)/shard_map/ppermute | solution.py:47
  49.4 4.1 %collective-permute-start.8 = (bf16[80,128]{1,0:T(8,128)(2,1)S(1)}, bf16[80,128]{1,0:T(8,128)(2,1)S(1)}, u32[]{:S(2)}, u32[]{:S(2)}) collective-permute-start(bf16[80,128]{1,0:T(8,128)(2,1)S(1)} %bitcast.26), channel_id=1, source_target_pairs={{0,2},{1,3},{2,0},{3,1},{4,6},{5,7},{6,4},{7,5},{8,10},{9,11},{10,... | collective-permute-start | bytes 61448 | tf_op jit(solution)/shard_map/ppermute | solution.py:532
  53.5 5.8 %collective-permute-start.9 = (bf16[2,80,128]{2,1,0:T(8,128)(2,1)S(1)}, bf16[2,80,128]{2,1,0:T(8,128)(2,1)S(1)}, u32[]{:S(2)}, u32[]{:S(2)}) collective-permute-start(bf16[2,80,128]{2,1,0:T(8,128)(2,1)S(1)} %pad_maximum_fusion.mine_ref), channel_id=1, source_target_pairs={{0,1},{1,0},{2,3},{3,2},{4,5},{5,4},{6,7},{7,6},{8,9},{9,8},{10,11... | collective-permute-start | bytes 122888 | tf_op jit(solution)/shard_map/ppermute | solution.py:532

commit v11 on v10

--- a/solution.py
+++ b/solution.py
@@ -114,24 +114,53 @@
     return (column == target(row)).astype(f32).astype(bf16)
 
 
-def window_order():
+def window_sources(n, from_strips):
+    half, edge = WLAT // 2, WLON // 2
+    inner = 2 * WLON - edge
+
     def target(row):
         c = (row >= POS).astype(jnp.int32)
         row = row - POS * c
         j = quotient(row, PAIR)
-        return (row - PAIR * j) * (2 * WLON) + c * WLON + j
-
-    return one_hot(2 * POS, 2 * POS, target)
-
-
-def natural_order():
+        pair = row - PAIR * j
+        dz = (pair >= WLAT).astype(jnp.int32)
+        i = pair - WLAT * dz
+        lon = c * WLON + j
+        upper = i < half
+        if not from_strips:
+            own = (half * dz + i) * (2 * WLON) + lon + edge
+            return jnp.where(upper & (lon < inner), own, -1)
+        slab = ((2 * n + dz + 1) & 3) * half + jnp.where(upper, i, i - half)
+        lat = slab * inner + lon
+        corner = 4 * half * inner + slab * edge + lon - inner
+        corner = jnp.where(upper, corner, corner + 4 * half * edge)
+        return jnp.where(lon < inner, jnp.where(upper, -1, lat), corner)
+
+    columns = 4 * half * (inner + 2 * edge) if from_strips else 2 * half * 2 * WLON
+    return one_hot(2 * POS, columns, target)
+
+
+def output_sources():
+    half, edge = WLAT // 2, WLON // 2
+    inner = 2 * WLON - edge
+    wide, narrow = 4 * half * inner, 4 * half * edge
+
     def target(row):
-        pair = quotient(row, 2 * WLON)
-        lon = row - 2 * WLON * pair
+        narrow_row = row >= 2 * wide
+        row = jnp.where(narrow_row, row - 2 * wide, row)
+        size = jnp.where(narrow_row, narrow, wide)
+        second = row >= size
+        row = jnp.where(second, row - size, row)
+        slab = jnp.where(narrow_row, quotient(row, edge), quotient(row, inner))
+        lon = jnp.where(narrow_row, row - slab * edge + inner, row - slab * inner)
+        z = quotient(slab, half)
+        i = slab - half * z + jnp.where(second, half, 0)
+        level = (z + 3) & 3
         c = (lon >= WLON).astype(jnp.int32)
-        return c * POS + (lon - WLON * c) * PAIR + pair
-
-    return one_hot(2 * POS, 2 * POS, target)
+        pair = (level & 1) * WLAT + i
+        return (level >> 1) * (2 * POS) + c * POS + (lon - WLON * c) * PAIR + pair
+
+    return one_hot(4 * POS, 4 * POS, target)
 
 
 def table_order():
@@ -226,38 +255,19 @@
     lat_out,
     diag_out,
     lon_out,
-    frame,
     wide,
     dense,
-    lat_buf,
-    diag_buf,
-    lon_buf,
 ):
     half = WLAT // 2
-    cols = 2 * WLON
-    edge = WLON // 2
-    inner = cols - edge
     root = 1.0 / math.sqrt(HD)
-    lon_part = lon_ref[...].astype(f32)
-    lat_part = lat_ref[...].astype(f32)
-    diag_part = diag_ref[...].astype(f32)
-    for t, own in enumerate((field_ref, cot_ref)):
-        for level in range(4):
-            z = (level + 1) % 4
-            for i in range(half):
-                k = z * half + i
-                row = (level * WLAT + i) * cols
-                frame[t, row : row + inner, :] = own[z, half + i].astype(f32)[edge:, :]
-                main, rest = get(lon_part, t, k * edge, edge)
-                frame[t, row + inner : row + cols, :LANES] = main
-                frame[t, row + inner : row + cols, LANES:] = rest
-                row = (level * WLAT + half + i) * cols
-                main, rest = get(lat_part, t, k * inner, inner)
-                frame[t, row : row + inner, :LANES] = main
-                frame[t, row : row + inner, LANES:] = rest
-                main, rest = get(diag_part, t, k * edge, edge)
-                frame[t, row + inner : row + cols, :LANES] = main
-                frame[t, row + inner : row + cols, LANES:] = rest
+    pieces = [ref[...].astype(f32) for ref in (lat_ref, lon_ref, diag_ref)]
+    thirds = []
+    for k in range(3):
+        sizes = [piece.shape[0] // 3 for piece in pieces]
+        third = [piece[k * size : (k + 1) * size] for piece, size in zip(pieces, sizes)]
+        thirds.append(jnp.concatenate(third, axis=0).astype(bf16))
+    strips = jnp.concatenate(thirds, axis=1)
+    narrow = C - LANES
     gain1 = gains_ref[0:1, :]
     gain2 = gains_ref[1:2, :]
     wq_t = wqkv_t_ref[0:C, :]
@@ -266,15 +276,22 @@
     head = lax.broadcasted_iota(jnp.int32, (HEADS, C), 0)
     head_mask = (lax.broadcasted_iota(jnp.int32, (HEADS, C), 1) >> 5) == head
     head_mask = head_mask.astype(f32).astype(bf16)
-    perm = window_order()
-    perm_t = natural_order()
     table_perm = table_order()
     chunk_perm = chunk_order()
     dense[...] = jnp.zeros_like(dense)
+    results = []
     for n in range(2):
-        both = slice(n * 2 * POS, (n + 1) * 2 * POS)
-        x = mm(perm, frame[0, both, :].astype(bf16))
-        cot = mm(perm, frame[1, both, :].astype(bf16))
+        moved = mm(window_sources(n, True), strips)
+        own_rows = window_sources(n, False)
+        inputs = []
+        for t, own in enumerate((field_ref, cot_ref)):
+            levels = [(2 * n + dz + 1) % 4 for dz in range(WZ)]
+            slabs = [own[z, half + i].astype(f32) for z in levels for i in range(half)]
+            slabs = mm(own_rows, jnp.concatenate(slabs, axis=0).astype(bf16))
+            main = moved[:, t * LANES : (t + 1) * LANES]
+            side = moved[:, 2 * LANES + t * narrow : 2 * LANES + (t + 1) * narrow]
+            inputs.append(slabs + jnp.concatenate([main, side], axis=1))
+        x, cot = inputs
         scaled1, normed1, inverse1 = by_rows(lambda v: norm_parts(v, gain1), LN_ROWS, x)
         h1 = scaled1.astype(bf16)
         q_all = mm_nt(h1, wq_t).astype(bf16)
@@ -370,23 +387,17 @@
             normed1,
             inverse1,
         )
-        for t, value in enumerate((result, grad_field)):
-            natural = mm(perm_t, value)
-            for dz in range(WZ):
-                z = (2 * n + dz + 1) % 4
-                for i in range(half):
-                    k = z * half + i
-                    row = (dz * WLAT + i) * cols
-                    slab = natural[row : row + cols]
-                    own_out[t, z, i] = slab[:inner].astype(bf16)
-                    put(lon_buf, t, k * edge, slab[inner:])
-                    row = (dz * WLAT + half + i) * cols
-                    slab = natural[row : row + cols]
-                    put(lat_buf, t, k * inner, slab[:inner])
-                    put(diag_buf, t, k * edge, slab[inner:])
-    lat_out[...] = lat_buf[...].astype(bf16)
-    diag_out[...] = diag_buf[...].astype(bf16)
-    lon_out[...] = lon_buf[...].astype(bf16)
+        results.append((result, grad_field))
+    order = output_sources()
+    outputs = [mm(order, jnp.concatenate(parts, axis=0)) for parts in zip(*results)]
+    row = 0
+    for out in (own_out, lat_out, lon_out, diag_out):
+        size = out.shape[0] // 3
+        cuts = [value[row : row + size] for value in outputs]
+        side = jnp.concatenate([cut[:, LANES:] for cut in cuts], axis=1)
+        cuts = [cut[:, :LANES] for cut in cuts] + [side]
+        out[...] = jnp.concatenate(cuts, axis=0).astype(bf16)
+        row += size
 
 
 def prepare_kernel(
@@ -510,6 +521,7 @@
     lat_part = lat_ref[...].astype(f32)
     diag_part = diag_ref[...].astype(f32)
     lon_part = lon_ref[...].astype(f32)
+    own_part = own_ref[...].astype(f32)
     for t, target in enumerate((out_ref, grad_ref)):
         for z in range(4):
             for i in range(half):
@@ -518,7 +530,7 @@
                 slab = [jnp.concatenate([parts[0][j], parts[1][j]], axis=0) for j in range(2)]
                 target[z, i] = jnp.concatenate(slab, axis=1).astype(bf16)
                 slab = jnp.concatenate(get(lon_part, t, k * edge, edge), axis=1)
-                own = own_ref[t, z, i].astype(f32)
+                own = jnp.concatenate(get(own_part, t, k * inner, inner), axis=1)
                 target[z, half + i] = jnp.concatenate([slab, own], axis=0).astype(bf16)
 
 
@@ -636,22 +648,19 @@
         ln2_gain.reshape(1, C),
         keep_flags,
     )
-    positions = levels * lat_rows * lon_cols
     fold, own, *strips = pl.pallas_call(
         block_kernel,
         out_shape=(
             jax.ShapeDtypeStruct((4, DENSE, LANES), bf16),
-            jax.ShapeDtypeStruct((2, levels, half, inner, C), bf16),
+            packed[0],
         )
         + packed,
         in_specs=[vmem] * 13,
         out_specs=(vmem,) * 5,
         scratch_shapes=[
-            pltpu.VMEM((2, positions, C), f32),
             pltpu.VMEM((HEADS, POS, POS), f32),
             pltpu.VMEM((DENSE, LANES), f32),
-        ]
-        + buffers,
+        ],
         compiler_params=params,
         name="block",
     )(

time: 60.5 us -> 60.9 us (level)
  no operation moved by 1% of the time
where the time goes in v11:
time: 60.9 us; the launch traced here: 60.7 us
  starting transfers between devices  26.9 us (44%)
  Pallas kernels  17.4 us (29%)
  waiting for transfers between devices  13.5 us (22%)
  local copies, waits for them, and re-layouts  1.99 us (3%)
  between operations  0.82 us (1%)
    ppermute x6, starting transfers between devices, shifted(): return lax.ppermute(block, ('lat', 'lon'), route)  16.2 us
    pallas_call x1, Pallas kernels, body(): pl.pallas_call(block_kernel, out_shape=(jax.ShapeDtypeStruct((4, DENSE, L...  11.4 us
    ppermute x4, waiting for transfers between devices, swapped(): return lax.ppermute(block, 'lon', [(i, i ^ distance) for i in range(lons)])  7.79 us
    ppermute x4, starting transfers between devices, swapped(): return lax.ppermute(block, 'lon', [(i, i ^ distance) for i in range(lons)])  7.21 us
    all_to_all x1, waiting for transfers between devices, lon_sum(): parts = lax.all_to_all(parts, 'lon', 0, 0, axis_index_groups=far)  4.66 us
    all_to_all x1, starting transfers between devices, lon_sum(): parts = lax.all_to_all(parts, 'lon', 0, 0, axis_index_groups=far)  3.48 us
    pallas_call x1, Pallas kernels, body(): pl.pallas_call(prepare_kernel, out_shape=(jax.ShapeDtypeStruct((2, POS, R...  3.16 us
    unnamed x26, local copies, waits for them, and re-layouts  1.96 us
  transfers between devices with their start and end apart: 11, of which 5 were waited for; matrix products, arithmetic and copies ran while one was open for 0% of the time, Pallas kernels for 7%

profile of v11, /device:TPU:1, one launch (start us, length us, event | category | flops | bytes accessed | tf_op | source)
XLA Modules:
  0.0 60.7 jit_solution(11561317894579915504)
XLA Ops:
  0.6 1.0 %copy-done = bf16[4,6,24,192]{3,2,1,0:T(8,128)(2,1)S(1)} copy-done((bf16[4,6,24,192]{3,2,1,0:T(8,128)(2,1)S(1)}, bf16[4,6,24,192]{3,2,1,0:T(8,128)(2,1)}, u32[]{:S(2)}) %copy-start) | copy-done | bytes 221208
  1.6 1.0 %copy-done.2 = bf16[4,6,24,192]{3,2,1,0:T(8,128)(2,1)S(1)} copy-done((bf16[4,6,24,192]{3,2,1,0:T(8,128)(2,1)S(1)}, bf16[4,6,24,192]{3,2,1,0:T(8,128)(2,1)}, u32[]{:S(2)}) %copy-start.2) | copy-done | bytes 221208
  2.6 0.2 pack_lat.1.after_ref
  2.9 4.4 %collective-permute-start.1 = (bf16[648,128]{1,0:T(8,128)(2,1)S(1)}, bf16[648,128]{1,0:T(8,128)(2,1)S(1)}, u32[]{:S(2)}, u32[]{:S(2)}) collective-permute-start(bf16[648,128]{1,0:T(8,128)(2,1)S(1)} %pack_lat.1.after_ref), channel_id=1, source_target_pairs={{0,224},{1,225},{2,226},{3,227},{4,228},{5,229},{6,230},{7,231},{8... | collective-permute-start | bytes 497672 | tf_op jit(solution)/shard_map/ppermute | solution.py:47
  7.3 0.1 pack_edge.1
  7.4 1.0 %collective-permute-start = (bf16[216,128]{1,0:T(8,128)(2,1)S(1)}, bf16[216,128]{1,0:T(8,128)(2,1)S(1)}, u32[]{:S(2)}, u32[]{:S(2)}) collective-permute-start(bf16[216,128]{1,0:T(8,128)(2,1)S(1)} %get-tuple-element.25), channel_id=1, source_target_pairs={{0,31},{1,0},{2,1},{3,2},{4,3},{5,4},{6,5},{7,6},{8,7},{9,8},{10,9... | collective-permute-start | bytes 165896 | tf_op jit(solution)/shard_map/ppermute | solution.py:47
  8.4 7.1 %collective-permute-start.2 = (bf16[216,128]{1,0:T(8,128)(2,1)S(1)}, bf16[216,128]{1,0:T(8,128)(2,1)S(1)}, u32[]{:S(2)}, u32[]{:S(2)}) collective-permute-start(bf16[216,128]{1,0:T(8,128)(2,1)S(1)} %get-tuple-element.26), channel_id=1, source_target_pairs={{0,255},{1,224},{2,225},{3,226},{4,227},{5,228},{6,229},{7,230},{8... | collective-permute-start | bytes 165896 | tf_op jit(solution)/shard_map/ppermute | solution.py:47
  15.5 3.2 %prepare.1 = (f32[2,144,864]{2,1,0:T(8,128)S(1)}, f32[4,864]{1,0:T(4,128)S(1)}, f32[144,4]{1,0:T(8,128)S(1)}, bf16[576,192]{1,0:T(8,128)(2,1)S(1)}, f32[6,192]{1,0:T(8,128)S(1)}) custom-call(f32[12,1,3312]{2,1,0:T(1,128)S(1)} %bitcast.23, s32[6,4,24]{2,1,0:T(4,128)S(1)} %bitcast.29, bf16[192,576]{1,0:T(8,128)(2,1)S(1)} %copy-done.6, f32[1,192]{1,0:T(1,128)S(1)} %bitcast.30, ...), custom_call_target="tpu_custom_call" | custom-call | tf_op jit(solution)/shard_map/prepare/pallas_call | solution.py:624
  18.8 11.4 %block.1 = (bf16[4,80,128]{2,1,0:T(8,128)(2,1)S(1)}, bf16[648,128]{1,0:T(8,128)(2,1)S(1)}, bf16[648,128]{1,0:T(8,128)(2,1)S(1)}, bf16[216,128]{1,0:T(8,128)(2,1)S(1)}, bf16[216,128]{1,0:T(8,128)(2,1)S(1)}) custom-call(bf16[4,6,24,192]{3,2,1,0:T(8,128)(2,1)S(1)} %copy-done.1, bf16[4,6,24,192]{3,2,1,0:T(8,128)(2,1)S(1)} %copy-done.3, ...), custom_call_target="tpu_custom_call" | custom-call | tf_op jit(solution)/shard_map/block/pallas_call | solution.py:651
  30.2 0.9 %collective-permute-start.3 = (bf16[2,80,128]{2,1,0:T(8,128)(2,1)S(1)}, bf16[2,80,128]{2,1,0:T(8,128)(2,1)S(1)}, u32[]{:S(2)}, u32[]{:S(2)}) collective-permute-start(bf16[2,80,128]{2,1,0:T(8,128)(2,1)S(1)} %dynamic-slice_bitcast_fusion), channel_id=1, source_target_pairs={{0,1},{1,0},{2,3},{3,2},{4,5},{5,4},{6,7},{7,6},{8,9},{9,8},{10,11... | collective-permute-start | bytes 122888 | tf_op jit(solution)/shard_map/ppermute | solution.py:544
  31.1 0.9 %collective-permute-done.3 = bf16[2,80,128]{2,1,0:T(8,128)(2,1)S(1)} collective-permute-done((bf16[2,80,128]{2,1,0:T(8,128)(2,1)S(1)}, bf16[2,80,128]{2,1,0:T(8,128)(2,1)S(1)}, u32[]{:S(2)}, u32[]{:S(2)}) %collective-permute-start.3) | collective-permute-done | bytes 40992 | tf_op jit(solution)/shard_map/ppermute | solution.py:544
  32.1 4.1 %collective-permute-done.4 = bf16[80,128]{1,0:T(8,128)(2,1)S(1)} collective-permute-done((bf16[80,128]{1,0:T(8,128)(2,1)S(1)}, bf16[80,128]{1,0:T(8,128)(2,1)S(1)}, u32[]{:S(2)}, u32[]{:S(2)}) %collective-permute-start.4) | collective-permute-done | bytes 20512 | tf_op jit(solution)/shard_map/ppermute | solution.py:544
  36.3 0.7 %add.29 = bf16[8,80,128]{2,1,0:T(8,128)(2,1)} custom-call(bf16[1,80,128]{2,1,0:T(8,128)(2,1)S(1)} %get-tuple-element.50.refs_0_, bf16[1,80,128]{2,1,0:T(8,128)(2,1)S(1)} %bitcast.28), custom_call_target="tpu_custom_call" | custom-call | tf_op jit(solution)/shard_map/add/pallas_call | solution.py:551
  36.9 3.5 %all-to-all-start = ((bf16[8,80,128]{2,1,0:T(8,128)(2,1)}), bf16[8,80,128]{2,1,0:T(8,128)(2,1)S(1)}, u32[]{:S(2)}, u32[]{:S(2)}) async-start(bf16[8,80,128]{2,1,0:T(8,128)(2,1)} %add.29), calls=%async_computation | async-start | bytes 327680 | tf_op jit(solution)/shard_map/all_to_all | solution.py:569
  40.4 1.3 %collective-permute-start.5 = (bf16[648,128]{1,0:T(8,128)(2,1)S(1)}, bf16[648,128]{1,0:T(8,128)(2,1)S(1)}, u32[]{:S(2)}, u32[]{:S(2)}) collective-permute-start(bf16[648,128]{1,0:T(8,128)(2,1)S(1)} %get-tuple-element.38), channel_id=1, source_target_pairs={{0,32},{1,33},{2,34},{3,35},{4,36},{5,37},{6,38},{7,39},{8,40},{9,... | collective-permute-start | bytes 497672 | tf_op jit(solution)/shard_map/ppermute | solution.py:47
  41.8 1.8 %collective-permute-start.6 = (bf16[216,128]{1,0:T(8,128)(2,1)S(1)}, bf16[216,128]{1,0:T(8,128)(2,1)S(1)}, u32[]{:S(2)}, u32[]{:S(2)}) collective-permute-start(bf16[216,128]{1,0:T(8,128)(2,1)S(1)} %get-tuple-element.39), channel_id=1, source_target_pairs={{0,33},{1,34},{2,35},{3,36},{4,37},{5,38},{6,39},{7,40},{8,41},{9,... | collective-permute-start | bytes 165896 | tf_op jit(solution)/shard_map/ppermute | solution.py:47
  43.5 0.6 collective-permute-start.7
  44.1 4.7 %all-to-all-done.refs_0_ = bf16[8,80,128]{2,1,0:T(8,128)(2,1)S(1)} async-done(((bf16[8,80,128]{2,1,0:T(8,128)(2,1)}), bf16[8,80,128]{2,1,0:T(8,128)(2,1)S(1)}, u32[]{:S(2)}, u32[]{:S(2)}) %all-to-all-start) | async-done | bytes 163872 | tf_op jit(solution)/shard_map/all_to_all | solution.py:569
  48.8 1.0 %collective-permute-done.6.diag_ref = bf16[216,128]{1,0:T(8,128)(2,1)S(1)} collective-permute-done((bf16[216,128]{1,0:T(8,128)(2,1)S(1)}, bf16[216,128]{1,0:T(8,128)(2,1)S(1)}, u32[]{:S(2)}, u32[]{:S(2)}) %collective-permute-start.6) | collective-permute-done | bytes 55328 | tf_op jit(solution)/shard_map/ppermute | solution.py:47
  49.8 1.3 %collective-permute-start.8 = (bf16[80,128]{1,0:T(8,128)(2,1)S(1)}, bf16[80,128]{1,0:T(8,128)(2,1)S(1)}, u32[]{:S(2)}, u32[]{:S(2)}) collective-permute-start(bf16[80,128]{1,0:T(8,128)(2,1)S(1)} %bitcast.26), channel_id=1, source_target_pairs={{0,2},{1,3},{2,0},{3,1},{4,6},{5,7},{6,4},{7,5},{8,10},{9,11},{10,... | collective-permute-start | bytes 61448 | tf_op jit(solution)/shard_map/ppermute | solution.py:544
  51.2 2.8 %collective-permute-done.8 = bf16[80,128]{1,0:T(8,128)(2,1)S(1)} collective-permute-done((bf16[80,128]{1,0:T(8,128)(2,1)S(1)}, bf16[80,128]{1,0:T(8,128)(2,1)S(1)}, u32[]{:S(2)}, u32[]{:S(2)}) %collective-permute-start.8) | collective-permute-done | bytes 20512 | tf_op jit(solution)/shard_map/ppermute | solution.py:544
  54.0 4.9 %collective-permute-start.9 = (bf16[2,80,128]{2,1,0:T(8,128)(2,1)S(1)}, bf16[2,80,128]{2,1,0:T(8,128)(2,1)S(1)}, u32[]{:S(2)}, u32[]{:S(2)}) collective-permute-start(bf16[2,80,128]{2,1,0:T(8,128)(2,1)S(1)} %pad_maximum_fusion.mine_ref), channel_id=1, source_target_pairs={{0,1},{1,0},{2,3},{3,2},{4,5},{5,4},{6,7},{7,6},{8,9},{9,8},{10,11... | collective-permute-start | bytes 122888 | tf_op jit(solution)/shard_map/ppermute | solution.py:544
  58.9 0.9 %finish.1 = (bf16[4,6,24,192]{3,2,1,0:T(8,128)(2,1)}, bf16[4,6,24,192]{3,2,1,0:T(8,128)(2,1)}) custom-call(bf16[648,128]{1,0:T(8,128)(2,1)S(1)} %get-tuple-element.32.own_ref, bf16[648,128]{1,0:T(8,128)(2,1)S(1)} %collective-permute-done.5.lat_ref, bf16[216,128]{1,0:T(8,128)(2,1)S(1)} %collective-permute-done.6.diag_ref, ...), custom_call_target="tpu_custom_call" | custom-call | tf_op jit(solution)/shard_map/finish/pallas_call | solution.py:692
  59.8 0.9 %unpack.1 = f32[12,1,3312]{2,1,0:T(1,128)} custom-call(bf16[2,80,128]{2,1,0:T(8,128)(2,1)S(1)} %pad_maximum_fusion.mine_ref, bf16[2,80,128]{2,1,0:T(8,128)(2,1)S(1)} %collective-permute-done.9.other_ref), custom_call_target="tpu_custom_call" | custom-call | tf_op jit(solution)/shard_map/unpack/pallas_call | solution.py:682
  (37 shorter events, 0.2 us)
Async XLA Ops:
  0.6 1.0 %copy-start = (bf16[4,6,24,192]{3,2,1,0:T(8,128)(2,1)S(1)}, bf16[4,6,24,192]{3,2,1,0:T(8,128)(2,1)}, u32[]{:S(2)}) copy-start(bf16[4,6,24,192]{3,2,1,0:T(8,128)(2,1)} %field_ref.5) | copy-start | bytes 663556
  1.6 1.0 %copy-start.2 = (bf16[4,6,24,192]{3,2,1,0:T(8,128)(2,1)S(1)}, bf16[4,6,24,192]{3,2,1,0:T(8,128)(2,1)}, u32[]{:S(2)}) copy-start(bf16[4,6,24,192]{3,2,1,0:T(8,128)(2,1)} %cot_ref.5) | copy-start | bytes 663556
  2.6 12.9 %copy-start.6 = (bf16[192,576]{1,0:T(8,128)(2,1)S(1)}, bf16[192,576]{1,0:T(8,128)(2,1)}, u32[]{:S(2)}) copy-start(bf16[192,576]{1,0:T(8,128)(2,1)} %wqkv_ref.1) | copy-start | bytes 663556
  2.6 12.9 %copy-start.7 = (f32[2,1,6,3312]{3,1,2,0:T(1,128)S(1)}, f32[2,1,6,3312]{3,1,2,0:T(1,128)}, u32[]{:S(2)}) copy-start(f32[2,1,6,3312]{3,1,2,0:T(1,128)} %param.19) | copy-start | bytes 476932
  2.6 12.9 %copy-start.10 = (f32[192]{0:T(256)S(1)}, f32[192]{0:T(256)}, u32[]{:S(2)}) copy-start(f32[192]{0:T(256)} %param.13) | copy-start | bytes 2308
  2.6 12.9 %copy-start.11 = (f32[192]{0:T(256)S(1)}, f32[192]{0:T(256)}, u32[]{:S(2)}) copy-start(f32[192]{0:T(256)} %param.16) | copy-start | bytes 2308
  2.6 12.9 %copy-start.12 = (s32[2,1,2]{2,1,0:T(1,128)S(1)}, s32[2,1,2]{2,1,0:T(1,128)}, u32[]{:S(2)}) copy-start(s32[2,1,2]{2,1,0:T(1,128)} %keep_ref.1) | copy-start | bytes 52
  2.6 16.2 %copy-start.8 = (bf16[192,192]{1,0:T(8,128)(2,1)S(1)}, bf16[192,192]{1,0:T(8,128)(2,1)}, u32[]{:S(2)}) copy-start(bf16[192,192]{1,0:T(8,128)(2,1)} %wproj_ref.1) | copy-start | bytes 221188
  2.8 12.7 %copy-start.9 = (s32[4,6,24]{2,0,1:T(4,128)S(1)}, s32[4,6,24]{2,0,1:T(4,128)}, u32[]{:S(2)}) copy-start(s32[4,6,24]{2,0,1:T(4,128)} %param.20) | copy-start | bytes 6916
  2.9 15.9 %collective-permute-start.1 = (bf16[648,128]{1,0:T(8,128)(2,1)S(1)}, bf16[648,128]{1,0:T(8,128)(2,1)S(1)}, u32[]{:S(2)}, u32[]{:S(2)}) collective-permute-start(bf16[648,128]{1,0:T(8,128)(2,1)S(1)} %pack_lat.1.after_ref), channel_id=1, source_target_pairs={{0,224},{1,225},{2,226},{3,227},{4,228},{5,229},{6,230},{7,231},{8... | collective-permute-start | bytes 497672 | tf_op jit(solution)/shard_map/ppermute | solution.py:47
  7.3 11.5 %copy-start.3 = (bf16[4,6,24,192]{3,2,1,0:T(8,128)(2,1)S(1)}, bf16[4,6,24,192]{3,2,1,0:T(8,128)(2,1)}, u32[]{:S(2)}) copy-start(bf16[4,6,24,192]{3,2,1,0:T(8,128)(2,1)} %cot_ref.5) | copy-start | bytes 663556
  7.3 11.5 %copy-start.4 = (bf16[192,768]{1,0:T(8,128)(2,1)S(1)}, bf16[192,768]{1,0:T(8,128)(2,1)}, u32[]{:S(2)}) copy-start(bf16[192,768]{1,0:T(8,128)(2,1)} %wup_ref.1) | copy-start | bytes 884740
  7.3 11.5 %copy-start.5 = (bf16[768,192]{0,1:T(8,128)(2,1)S(1)}, bf16[768,192]{0,1:T(8,128)(2,1)}, u32[]{:S(2)}) copy-start(bf16[768,192]{0,1:T(8,128)(2,1)} %param.18) | copy-start | bytes 884740
  7.4 11.4 %copy-start.1 = (bf16[4,6,24,192]{3,2,1,0:T(8,128)(2,1)S(1)}, bf16[4,6,24,192]{3,2,1,0:T(8,128)(2,1)}, u32[]{:S(2)}) copy-start(bf16[4,6,24,192]{3,2,1,0:T(8,128)(2,1)} %field_ref.5) | copy-start | bytes 663556
  7.4 11.3 %collective-permute-start = (bf16[216,128]{1,0:T(8,128)(2,1)S(1)}, bf16[216,128]{1,0:T(8,128)(2,1)S(1)}, u32[]{:S(2)}, u32[]{:S(2)}) collective-permute-start(bf16[216,128]{1,0:T(8,128)(2,1)S(1)} %get-tuple-element.25), channel_id=1, source_target_pairs={{0,31},{1,0},{2,1},{3,2},{4,3},{5,4},{6,5},{7,6},{8,7},{9,8},{10,9... | collective-permute-start | bytes 165896 | tf_op jit(solution)/shard_map/ppermute | solution.py:47
  8.4 10.3 %collective-permute-start.2 = (bf16[216,128]{1,0:T(8,128)(2,1)S(1)}, bf16[216,128]{1,0:T(8,128)(2,1)S(1)}, u32[]{:S(2)}, u32[]{:S(2)}) collective-permute-start(bf16[216,128]{1,0:T(8,128)(2,1)S(1)} %get-tuple-element.26), channel_id=1, source_target_pairs={{0,255},{1,224},{2,225},{3,226},{4,227},{5,228},{6,229},{7,230},{8... | collective-permute-start | bytes 165896 | tf_op jit(solution)/shard_map/ppermute | solution.py:47
  30.2 1.8 %collective-permute-start.3 = (bf16[2,80,128]{2,1,0:T(8,128)(2,1)S(1)}, bf16[2,80,128]{2,1,0:T(8,128)(2,1)S(1)}, u32[]{:S(2)}, u32[]{:S(2)}) collective-permute-start(bf16[2,80,128]{2,1,0:T(8,128)(2,1)S(1)} %dynamic-slice_bitcast_fusion), channel_id=1, source_target_pairs={{0,1},{1,0},{2,3},{3,2},{4,5},{5,4},{6,7},{7,6},{8,9},{9,8},{10,11... | collective-permute-start | bytes 122888 | tf_op jit(solution)/shard_map/ppermute | solution.py:544
  32.0 4.2 %collective-permute-start.4 = (bf16[80,128]{1,0:T(8,128)(2,1)S(1)}, bf16[80,128]{1,0:T(8,128)(2,1)S(1)}, u32[]{:S(2)}, u32[]{:S(2)}) collective-permute-start(bf16[80,128]{1,0:T(8,128)(2,1)S(1)} %get-tuple-element.49), channel_id=1, source_target_pairs={{0,2},{1,3},{2,0},{3,1},{4,6},{5,7},{6,4},{7,5},{8,10},{9,11},{10,... | collective-permute-start | bytes 61448 | tf_op jit(solution)/shard_map/ppermute | solution.py:544
  36.9 11.9 %all-to-all-start = ((bf16[8,80,128]{2,1,0:T(8,128)(2,1)}), bf16[8,80,128]{2,1,0:T(8,128)(2,1)S(1)}, u32[]{:S(2)}, u32[]{:S(2)}) async-start(bf16[8,80,128]{2,1,0:T(8,128)(2,1)} %add.29), calls=%async_computation | async-start | bytes 327680 | tf_op jit(solution)/shard_map/all_to_all | solution.py:569
  40.4 9.4 %collective-permute-start.5 = (bf16[648,128]{1,0:T(8,128)(2,1)S(1)}, bf16[648,128]{1,0:T(8,128)(2,1)S(1)}, u32[]{:S(2)}, u32[]{:S(2)}) collective-permute-start(bf16[648,128]{1,0:T(8,128)(2,1)S(1)} %get-tuple-element.38), channel_id=1, source_target_pairs={{0,32},{1,33},{2,34},{3,35},{4,36},{5,37},{6,38},{7,39},{8,40},{9,... | collective-permute-start | bytes 497672 | tf_op jit(solution)/shard_map/ppermute | solution.py:47
  41.8 8.1 %collective-permute-start.6 = (bf16[216,128]{1,0:T(8,128)(2,1)S(1)}, bf16[216,128]{1,0:T(8,128)(2,1)S(1)}, u32[]{:S(2)}, u32[]{:S(2)}) collective-permute-start(bf16[216,128]{1,0:T(8,128)(2,1)S(1)} %get-tuple-element.39), channel_id=1, source_target_pairs={{0,33},{1,34},{2,35},{3,36},{4,37},{5,38},{6,39},{7,40},{8,41},{9,... | collective-permute-start | bytes 165896 | tf_op jit(solution)/shard_map/ppermute | solution.py:47
  43.5 6.3 %collective-permute-start.7 = (bf16[216,128]{1,0:T(8,128)(2,1)S(1)}, bf16[216,128]{1,0:T(8,128)(2,1)S(1)}, u32[]{:S(2)}, u32[]{:S(2)}) collective-permute-start(bf16[216,128]{1,0:T(8,128)(2,1)S(1)} %get-tuple-element.40), channel_id=1, source_target_pairs={{0,1},{1,2},{2,3},{3,4},{4,5},{5,6},{6,7},{7,8},{8,9},{9,10},{10,1... | collective-permute-start | bytes 165896 | tf_op jit(solution)/shard_map/ppermute | solution.py:47
  49.8 4.1 %collective-permute-start.8 = (bf16[80,128]{1,0:T(8,128)(2,1)S(1)}, bf16[80,128]{1,0:T(8,128)(2,1)S(1)}, u32[]{:S(2)}, u32[]{:S(2)}) collective-permute-start(bf16[80,128]{1,0:T(8,128)(2,1)S(1)} %bitcast.26), channel_id=1, source_target_pairs={{0,2},{1,3},{2,0},{3,1},{4,6},{5,7},{6,4},{7,5},{8,10},{9,11},{10,... | collective-permute-start | bytes 61448 | tf_op jit(solution)/shard_map/ppermute | solution.py:544
  54.0 5.8 %collective-permute-start.9 = (bf16[2,80,128]{2,1,0:T(8,128)(2,1)S(1)}, bf16[2,80,128]{2,1,0:T(8,128)(2,1)S(1)}, u32[]{:S(2)}, u32[]{:S(2)}) collective-permute-start(bf16[2,80,128]{2,1,0:T(8,128)(2,1)S(1)} %pad_maximum_fusion.mine_ref), channel_id=1, source_target_pairs={{0,1},{1,0},{2,3},{3,2},{4,5},{5,4},{6,7},{7,6},{8,9},{9,8},{10,11... | collective-permute-start | bytes 122888 | tf_op jit(solution)/shard_map/ppermute | solution.py:544

commit v12 on v10

--- a/solution.py
+++ b/solution.py
@@ -207,7 +207,7 @@
     lon_out[...] = lon_buf[...].astype(bf16)
 
 
-def block_kernel(
+def scores_kernel(
     field_ref,
     cot_ref,
     lon_ref,
@@ -222,16 +222,14 @@
     label_row_ref,
     label_col_ref,
     fold_out,
-    own_out,
-    lat_out,
-    diag_out,
-    lon_out,
+    x_out,
+    probs_out,
+    grad_low_out,
+    grad_sum_out,
+    result_out,
     frame,
     wide,
     dense,
-    lat_buf,
-    diag_buf,
-    lon_buf,
 ):
     half = WLAT // 2
     cols = 2 * WLON
@@ -267,7 +265,6 @@
     head_mask = (lax.broadcasted_iota(jnp.int32, (HEADS, C), 1) >> 5) == head
     head_mask = head_mask.astype(f32).astype(bf16)
     perm = window_order()
-    perm_t = natural_order()
     table_perm = table_order()
     chunk_perm = chunk_order()
     dense[...] = jnp.zeros_like(dense)
@@ -275,7 +272,8 @@
         both = slice(n * 2 * POS, (n + 1) * 2 * POS)
         x = mm(perm, frame[0, both, :].astype(bf16))
         cot = mm(perm, frame[1, both, :].astype(bf16))
-        scaled1, normed1, inverse1 = by_rows(lambda v: norm_parts(v, gain1), LN_ROWS, x)
+        x_out[both, :] = x.astype(bf16)
+        (scaled1,) = by_rows(lambda v: norm_parts(v, gain1)[:1], LN_ROWS, x)
         h1 = scaled1.astype(bf16)
         q_all = mm_nt(h1, wq_t).astype(bf16)
         k_all = mm_nt(h1, wk_t).astype(bf16)
@@ -294,14 +292,15 @@
                 allowed = label_col == label_row_ref[w : w + 1, low:high]
                 probs.append(masked_softmax(scores, bias_ref[n, :, low:high], allowed))
             probs_low = jnp.concatenate([part.astype(bf16) for part in probs], axis=1)
+            probs_out[w] = probs_low
             attended = head_blocks(mm(v_t, probs_low)).astype(bf16).T
             factor = gains_ref[2 + w : 3 + w, :]
             branches.append((mm(attended, wproj_ref[...]) * factor).astype(bf16).astype(f32))
-            saved.append((q_wide, probs, probs_low))
+            saved.append(probs)
         y_sum = x + jnp.concatenate(branches, axis=0)
         scaled2, normed2, inverse2 = by_rows(lambda v: norm_parts(v, gain2), LN_ROWS, y_sum)
         act, slope = by_rows(gelu_parts, GELU_ROWS, mm(scaled2.astype(bf16), wup_ref[...]))
-        result = (y_sum + mm_nt(act, wdown_t_ref[...])).astype(bf16)
+        result_out[both, :] = (y_sum + mm_nt(act, wdown_t_ref[...])).astype(bf16)
         grad_up = (mm(cot.astype(bf16), wdown_t_ref[...]) * slope).astype(bf16)
         grad_hidden = mm_nt(grad_up, wup_ref[...])
         (grad_sum,) = by_rows(
@@ -312,12 +311,13 @@
             normed2,
             inverse2,
         )
-        grad_low_in = grad_sum.astype(bf16).astype(f32)
+        grad_sum_low = grad_sum.astype(bf16)
+        grad_sum_out[both, :] = grad_sum_low
+        grad_low_in = grad_sum_low.astype(f32)
         folded = [None] * len(LANE_CUTS)
-        grad_h1 = []
         for c in range(2):
             rows = slice(c * POS, (c + 1) * POS)
-            q_wide, probs, probs_low = saved[c]
+            probs = saved[c]
             factor = gains_ref[2 + 2 * n + c : 3 + 2 * n + c, :]
             grad_branch = (grad_low_in[rows] * factor).astype(bf16)
             grad_att = mm_nt(grad_branch, wproj_ref[...]).astype(bf16)
@@ -329,12 +329,7 @@
                 grad_scores = probs[k] * (grad_probs - inner_sum)
                 folded[k] = grad_scores if c == 0 else folded[k] + grad_scores
                 grad_low.append(grad_scores.astype(bf16))
-            grad_low = jnp.concatenate(grad_low, axis=1)
-            k_t = mm_nt(wk_t, h1[rows]).astype(bf16)
-            grad_q = (head_blocks(mm(k_t, grad_low)) * root).astype(bf16).T
-            grad_k = (mm(grad_low, q_wide) * root).astype(bf16)
-            grad_v = mm(probs_low, g_wide).astype(bf16)
-            grad_h1.append(mm(grad_q, wq_t) + mm(grad_k, wk_t) + mm(grad_v, wv_t))
+            grad_low_out[2 * n + c] = jnp.concatenate(grad_low, axis=1)
         folded = jnp.concatenate([part.astype(bf16) for part in folded], axis=1)
         wide[...] = folded.T.astype(f32).reshape(HEADS, POS, POS)
         total = None
@@ -359,6 +354,59 @@
             rest = [part[HEADS * g : HEADS * (g + 1), 2 * LANES :] for g in range(WLAT)]
             dense[2 * QUARTER : 2 * QUARTER + HEADS, : WLAT * REST] = jnp.concatenate(rest, axis=1)
             fold_out[2 * n + k] = dense[...].astype(bf16)
+
+
+def rest_kernel(
+    x_ref,
+    probs_ref,
+    grad_low_ref,
+    grad_sum_ref,
+    result_ref,
+    gains_ref,
+    wqkv_t_ref,
+    wproj_ref,
+    own_out,
+    lat_out,
+    diag_out,
+    lon_out,
+    lat_buf,
+    diag_buf,
+    lon_buf,
+):
+    half = WLAT // 2
+    cols = 2 * WLON
+    edge = WLON // 2
+    inner = cols - edge
+    root = 1.0 / math.sqrt(HD)
+    gain1 = gains_ref[0:1, :]
+    wq_t = wqkv_t_ref[0:C, :]
+    wk_t = wqkv_t_ref[C : 2 * C, :]
+    wv_t = wqkv_t_ref[2 * C : 3 * C, :]
+    head = lax.broadcasted_iota(jnp.int32, (HEADS, C), 0)
+    head_mask = (lax.broadcasted_iota(jnp.int32, (HEADS, C), 1) >> 5) == head
+    head_mask = head_mask.astype(f32).astype(bf16)
+    perm_t = natural_order()
+    for n in range(2):
+        both = slice(n * 2 * POS, (n + 1) * 2 * POS)
+        x = x_ref[both, :].astype(f32)
+        scaled1, normed1, inverse1 = by_rows(lambda v: norm_parts(v, gain1), LN_ROWS, x)
+        h1 = scaled1.astype(bf16)
+        q_all = mm_nt(h1, wq_t).astype(bf16)
+        grad_sum = grad_sum_ref[both, :].astype(f32)
+        grad_h1 = []
+        for c in range(2):
+            w = 2 * n + c
+            rows = slice(c * POS, (c + 1) * POS)
+            q_wide = spread_heads(q_all[rows], head_mask)
+            grad_branch = (grad_sum[rows] * gains_ref[2 + w : 3 + w, :]).astype(bf16)
+            grad_att = mm_nt(grad_branch, wproj_ref[...]).astype(bf16)
+            g_wide = spread_heads(grad_att, head_mask)
+            grad_low = grad_low_ref[w]
+            k_t = mm_nt(wk_t, h1[rows]).astype(bf16)
+            grad_q = (head_blocks(mm(k_t, grad_low)) * root).astype(bf16).T
+            grad_k = (mm(grad_low, q_wide) * root).astype(bf16)
+            grad_v = mm(probs_ref[w], g_wide).astype(bf16)
+            grad_h1.append(mm(grad_q, wq_t) + mm(grad_k, wk_t) + mm(grad_v, wv_t))
         grad_h1 = jnp.concatenate(grad_h1, axis=0).astype(bf16).astype(f32)
         (grad_field,) = by_rows(
             lambda v, g, normed, inverse: (
@@ -370,7 +418,7 @@
             normed1,
             inverse1,
         )
-        for t, value in enumerate((result, grad_field)):
+        for t, value in enumerate((result_ref[both, :], grad_field)):
             natural = mm(perm_t, value)
             for dz in range(WZ):
                 z = (2 * n + dz + 1) % 4
@@ -522,7 +570,7 @@
                 target[z, half + i] = jnp.concatenate([slab, own], axis=0).astype(bf16)
 
 
-def lon_sum(quarters, strips):
+def lon_sum(quarters, saved, rest_of_backward):
     lons = lax.axis_size("lon")
     me = lax.axis_index("lon")
     bits = [(me >> k) & 1 for k in range(2)]
@@ -548,8 +596,9 @@
     value = quarters.reshape((2, 2) + quarters.shape[1:])
     other = swapped(pick(value, 1 - bits[0], 1), 1)
     value = pick(value, bits[0], 1).astype(f32) + other.astype(f32)
-    value = value.astype(bf16)
+    value, saved = lax.optimization_barrier((value.astype(bf16), saved))
     other = swapped(pick(value, 1 - bits[1], 0), 2)
+    own, *strips = rest_of_backward(saved)
     parts = added((pick(value, bits[1], 0)[None], other[None]), lons // 4)
     parts, strips = lax.optimization_barrier((parts, strips))
     steps = ((1, 0), (1, 1), (0, 1))
@@ -560,7 +609,7 @@
     lower = jnp.where(bits[1] == 0, value, other)
     upper = jnp.where(bits[1] == 0, other, value)
     value = jnp.stack([lower, upper])
-    return (value, swapped(value, 1)), strips
+    return (value, swapped(value, 1)), own, strips
 
 
 def body(
@@ -637,23 +686,25 @@
         keep_flags,
     )
     positions = levels * lat_rows * lon_cols
-    fold, own, *strips = pl.pallas_call(
-        block_kernel,
+    fold, *saved = pl.pallas_call(
+        scores_kernel,
         out_shape=(
             jax.ShapeDtypeStruct((4, DENSE, LANES), bf16),
-            jax.ShapeDtypeStruct((2, levels, half, inner, C), bf16),
-        )
-        + packed,
+            jax.ShapeDtypeStruct((positions, C), bf16),
+            jax.ShapeDtypeStruct((4, POS, ROWS), bf16),
+            jax.ShapeDtypeStruct((4, POS, ROWS), bf16),
+            jax.ShapeDtypeStruct((positions, C), bf16),
+            jax.ShapeDtypeStruct((positions, C), bf16),
+        ),
         in_specs=[vmem] * 13,
-        out_specs=(vmem,) * 5,
+        out_specs=(vmem,) * 6,
         scratch_shapes=[
             pltpu.VMEM((2, positions, C), f32),
             pltpu.VMEM((HEADS, POS, POS), f32),
             pltpu.VMEM((DENSE, LANES), f32),
-        ]
-        + buffers,
+        ],
         compiler_params=params,
-        name="block",
+        name="scores",
     )(
         field_in,
         cotangent,
@@ -669,7 +720,22 @@
         label_row,
         label_col,
     )
-    halves, (lat_back, diag_back, lon_back) = lon_sum(fold, strips)
+
+    def rest_of_backward(saved):
+        return pl.pallas_call(
+            rest_kernel,
+            out_shape=(jax.ShapeDtypeStruct((2, levels, half, inner, C), bf16),) + packed,
+            in_specs=[vmem] * 8,
+            out_specs=(vmem,) * 4,
+            scratch_shapes=buffers,
+            compiler_params=params,
+            cost_estimate=pl.CostEstimate(
+                flops=1_000_000_000, bytes_accessed=8_000_000, transcendentals=0
+            ),
+            name="rest",
+        )(*saved, gains, weights_t, w_proj)
+
+    halves, own, (lat_back, diag_back, lon_back) = lon_sum(fold, saved, rest_of_backward)
     grads = pl.pallas_call(
         unpack_kernel,
         out_shape=jax.ShapeDtypeStruct((2 * HEADS, 1, PAIR * TAB), f32),

time: 60.5 us -> 64.6 us (1.068)
  local copies, waits for them, and re-layouts: 1.99 us -> 8.21 us
  waiting for transfers between devices: 13.5 us -> 10.1 us
  Pallas kernels: 17 us -> 18.8 us
  starting transfers between devices: 27 us -> 26.2 us
    unnamed x26 -> x42, local copies, waits for them, and re-layouts: 1.96 us -> 8.19 us
    ppermute x4, waiting for transfers between devices: 7.77 us -> 4.43 us  [swapped(): return lax.ppermute(block, 'lon', [(i, i ^ distance) for i in range(lons)])]
    ppermute x4, starting transfers between devices: 7.24 us -> 4.57 us  [swapped(): return lax.ppermute(block, 'lon', [(i, i ^ distance) for i in range(lons)])]
    pallas_call x1 -> x2, Pallas kernels: 11 us -> 12.8 us  [the longest x1 9.36 us: body(): pl.pallas_call(scores_kernel, out_shape=(jax.ShapeDtypeStruct((4, DENSE,...]
    all_to_all x1, starting transfers between devices: 3.48 us -> 5.28 us  [lon_sum(): parts = lax.all_to_all(parts, 'lon', 0, 0, axis_index_groups=far)]
  transfers between devices with their start and end apart: 11 -> 11, of which waited for: 5 -> 4; matrix products, arithmetic and copies ran while one was open for 0% -> 0% of each run, Pallas kernels for 7% -> 12%
where the time goes in v12:
time: 64.6 us; the launch traced here: 64.2 us
  starting transfers between devices  26.2 us (41%)
  Pallas kernels  18.8 us (29%)
  waiting for transfers between devices  10.1 us (16%)
  local copies, waits for them, and re-layouts  8.21 us (13%)
  between operations  0.86 us (1%)
    ppermute x6, starting transfers between devices, shifted(): return lax.ppermute(block, ('lat', 'lon'), route)  16.3 us
    pallas_call x1, Pallas kernels, body(): pl.pallas_call(scores_kernel, out_shape=(jax.ShapeDtypeStruct((4, DENSE,...  9.36 us
    unnamed x42, local copies, waits for them, and re-layouts  8.19 us
    all_to_all x1, starting transfers between devices, lon_sum(): parts = lax.all_to_all(parts, 'lon', 0, 0, axis_index_groups=far)  5.28 us
    all_to_all x1, waiting for transfers between devices, lon_sum(): parts = lax.all_to_all(parts, 'lon', 0, 0, axis_index_groups=far)  4.65 us
    ppermute x4, starting transfers between devices, swapped(): return lax.ppermute(block, 'lon', [(i, i ^ distance) for i in range(lons)])  4.57 us
    ppermute x4, waiting for transfers between devices, swapped(): return lax.ppermute(block, 'lon', [(i, i ^ distance) for i in range(lons)])  4.43 us
    pallas_call x1, Pallas kernels, rest_of_backward(): pl.pallas_call(rest_kernel, out_shape=(jax.ShapeDtypeStruct((2, levels, h...  3.4 us
  transfers between devices with their start and end apart: 11, of which 4 were waited for; matrix products, arithmetic and copies ran while one was open for 0% of the time, Pallas kernels for 12%

profile of v12, /device:TPU:1, one launch (start us, length us, event | category | flops | bytes accessed | tf_op | source)
XLA Modules:
  0.0 64.2 jit_solution(51921547767692282)
XLA Ops:
  0.6 1.0 %copy-done = bf16[4,6,24,192]{3,2,1,0:T(8,128)(2,1)S(1)} copy-done((bf16[4,6,24,192]{3,2,1,0:T(8,128)(2,1)S(1)}, bf16[4,6,24,192]{3,2,1,0:T(8,128)(2,1)}, u32[]{:S(2)}) %copy-start) | copy-done | bytes 221208
  1.6 1.0 %copy-done.2 = bf16[4,6,24,192]{3,2,1,0:T(8,128)(2,1)S(1)} copy-done((bf16[4,6,24,192]{3,2,1,0:T(8,128)(2,1)S(1)}, bf16[4,6,24,192]{3,2,1,0:T(8,128)(2,1)}, u32[]{:S(2)}) %copy-start.2) | copy-done | bytes 221208
  2.9 4.4 %collective-permute-start.1 = (bf16[648,128]{1,0:T(8,128)(2,1)S(1)}, bf16[648,128]{1,0:T(8,128)(2,1)S(1)}, u32[]{:S(2)}, u32[]{:S(2)}) collective-permute-start(bf16[648,128]{1,0:T(8,128)(2,1)S(1)} %pack_lat.1.after_ref), channel_id=1, source_target_pairs={{0,224},{1,225},{2,226},{3,227},{4,228},{5,229},{6,230},{7,231},{8... | collective-permute-start | bytes 497672 | tf_op jit(solution)/shard_map/ppermute | solution.py:47
  7.4 1.0 %collective-permute-start = (bf16[216,128]{1,0:T(8,128)(2,1)S(1)}, bf16[216,128]{1,0:T(8,128)(2,1)S(1)}, u32[]{:S(2)}, u32[]{:S(2)}) collective-permute-start(bf16[216,128]{1,0:T(8,128)(2,1)S(1)} %get-tuple-element.36), channel_id=1, source_target_pairs={{0,31},{1,0},{2,1},{3,2},{4,3},{5,4},{6,5},{7,6},{8,7},{9,8},{10,9... | collective-permute-start | bytes 165896 | tf_op jit(solution)/shard_map/ppermute | solution.py:47
  8.4 7.1 %collective-permute-start.2 = (bf16[216,128]{1,0:T(8,128)(2,1)S(1)}, bf16[216,128]{1,0:T(8,128)(2,1)S(1)}, u32[]{:S(2)}, u32[]{:S(2)}) collective-permute-start(bf16[216,128]{1,0:T(8,128)(2,1)S(1)} %get-tuple-element.37), channel_id=1, source_target_pairs={{0,255},{1,224},{2,225},{3,226},{4,227},{5,228},{6,229},{7,230},{8... | collective-permute-start | bytes 165896 | tf_op jit(solution)/shard_map/ppermute | solution.py:47
  15.5 3.2 %prepare.1 = (f32[2,144,864]{2,1,0:T(8,128)S(1)}, f32[4,864]{1,0:T(4,128)S(1)}, f32[144,4]{1,0:T(8,128)S(1)}, bf16[576,192]{1,0:T(8,128)(2,1)S(1)}, f32[6,192]{1,0:T(8,128)S(1)}) custom-call(f32[12,1,3312]{2,1,0:T(1,128)S(1)} %bitcast.23, s32[6,4,24]{2,1,0:T(4,128)S(1)} %bitcast.29, bf16[192,576]{1,0:T(8,128)(2,1)S(1)} %copy-done.6, f32[1,192]{1,0:T(1,128)S(1)} %bitcast.30, ...), custom_call_target="tpu_custom_call" | custom-call | tf_op jit(solution)/shard_map/prepare/pallas_call | solution.py:661
  18.8 9.4 %scores.1 = (bf16[4,80,128]{2,1,0:T(8,128)(2,1)S(1)}, bf16[576,192]{1,0:T(8,128)(2,1)S(1)}, bf16[4,144,864]{2,1,0:T(8,128)(2,1)S(1)}, bf16[4,144,864]{2,1,0:T(8,...) custom-call(bf16[4,6,24,192]{3,2,1,0:T(8,128)(2,1)S(1)} %copy-done.1, ...), custom_call_target="tpu_custom_call" | custom-call | tf_op jit(solution)/shard_map/scores/pallas_call | solution.py:689
  28.2 1.0 %copy-done.13 = bf16[4,144,864]{2,1,0:T(8,128)(2,1)} copy-done((bf16[4,144,864]{2,1,0:T(8,128)(2,1)}, bf16[4,144,864]{2,1,0:T(8,128)(2,1)S(1)}, u32[]{:S(2)}) %copy-start.13) | copy-done | bytes 995352
  29.1 0.7 %copy-done.15 = bf16[576,192]{1,0:T(8,128)(2,1)} copy-done((bf16[576,192]{1,0:T(8,128)(2,1)}, bf16[576,192]{1,0:T(8,128)(2,1)S(1)}, u32[]{:S(2)}) %copy-start.15) | copy-done | bytes 221208
  29.8 0.7 %copy-done.17 = bf16[576,192]{1,0:T(8,128)(2,1)} copy-done((bf16[576,192]{1,0:T(8,128)(2,1)}, bf16[576,192]{1,0:T(8,128)(2,1)S(1)}, u32[]{:S(2)}) %copy-start.17) | copy-done | bytes 221208
  30.5 0.7 %copy-done.19 = bf16[576,192]{1,0:T(8,128)(2,1)} copy-done((bf16[576,192]{1,0:T(8,128)(2,1)}, bf16[576,192]{1,0:T(8,128)(2,1)S(1)}, u32[]{:S(2)}) %copy-start.19) | copy-done | bytes 221208
  31.8 0.9 %collective-permute-done.3 = bf16[2,80,128]{2,1,0:T(8,128)(2,1)S(1)} collective-permute-done((bf16[2,80,128]{2,1,0:T(8,128)(2,1)S(1)}, bf16[2,80,128]{2,1,0:T(8,128)(2,1)S(1)}, u32[]{:S(2)}, u32[]{:S(2)}) %collective-permute-start.3) | collective-permute-done | bytes 40992 | tf_op jit(solution)/shard_map/ppermute | solution.py:580
  33.1 1.2 %copy-done.14 = bf16[4,144,864]{2,1,0:T(8,128)(2,1)S(1)} copy-done((bf16[4,144,864]{2,1,0:T(8,128)(2,1)S(1)}, bf16[4,144,864]{2,1,0:T(8,128)(2,1)}, u32[]{:S(2)}) %copy-start.14) | copy-done | bytes 995352
  34.3 1.0 %copy-done.18 = bf16[576,192]{1,0:T(8,128)(2,1)S(1)} copy-done((bf16[576,192]{1,0:T(8,128)(2,1)S(1)}, bf16[576,192]{1,0:T(8,128)(2,1)}, u32[]{:S(2)}) %copy-start.18) | copy-done | bytes 221208
  35.3 1.0 %copy-done.20 = bf16[576,192]{1,0:T(8,128)(2,1)S(1)} copy-done((bf16[576,192]{1,0:T(8,128)(2,1)S(1)}, bf16[576,192]{1,0:T(8,128)(2,1)}, u32[]{:S(2)}) %copy-start.20) | copy-done | bytes 221208
  36.2 3.4 %rest.1 = (bf16[2,4,3,18,192]{4,3,2,1,0:T(8,128)(2,1)S(1)}, bf16[648,128]{1,0:T(8,128)(2,1)S(1)}, bf16[216,128]{1,0:T(8,128)(2,1)S(1)}, bf16[216,128]{1,0:T(8,128)(2,1)S(1)}) custom-call(bf16[576,192]{1,0:T(8,128)(2,1)S(1)} %copy-done.16, bf16[4,144,864]{2,1,0:T(8,128)(2,1)S(1)} %get-tuple-element.50.probs_ref, bf16[4,144,864]{2,1,0:T(8,128)(2,1)S(1)} %copy-done.14, ...), custom_call_target="tpu_custom_call" | custom-call | flops 1000000000 | bytes 8000000 | tf_op jit(solution)/shard_map/rest/pallas_call | solution.py:725
  40.3 5.3 %all-to-all-start = ((bf16[8,80,128]{2,1,0:T(8,128)(2,1)}), bf16[8,80,128]{2,1,0:T(8,128)(2,1)S(1)}, u32[]{:S(2)}, u32[]{:S(2)}) async-start(bf16[8,80,128]{2,1,0:T(8,128)(2,1)} %add.29), calls=%async_computation | async-start | bytes 327680 | tf_op jit(solution)/shard_map/all_to_all | solution.py:606
  45.6 3.2 %collective-permute-start.6 = (bf16[216,128]{1,0:T(8,128)(2,1)S(1)}, bf16[216,128]{1,0:T(8,128)(2,1)S(1)}, u32[]{:S(2)}, u32[]{:S(2)}) collective-permute-start(bf16[216,128]{1,0:T(8,128)(2,1)S(1)} %get-tuple-element.61), channel_id=1, source_target_pairs={{0,33},{1,34},{2,35},{3,36},{4,37},{5,38},{6,39},{7,40},{8,41},{9,... | collective-permute-start | bytes 165896 | tf_op jit(solution)/shard_map/ppermute | solution.py:47
  49.4 4.6 %all-to-all-done.refs_0_ = bf16[8,80,128]{2,1,0:T(8,128)(2,1)S(1)} async-done(((bf16[8,80,128]{2,1,0:T(8,128)(2,1)}), bf16[8,80,128]{2,1,0:T(8,128)(2,1)S(1)}, u32[]{:S(2)}, u32[]{:S(2)}) %all-to-all-start) | async-done | bytes 163872 | tf_op jit(solution)/shard_map/all_to_all | solution.py:606
  54.1 1.1 %collective-permute-done.6.diag_ref = bf16[216,128]{1,0:T(8,128)(2,1)S(1)} collective-permute-done((bf16[216,128]{1,0:T(8,128)(2,1)S(1)}, bf16[216,128]{1,0:T(8,128)(2,1)S(1)}, u32[]{:S(2)}, u32[]{:S(2)}) %collective-permute-start.6) | collective-permute-done | bytes 55328 | tf_op jit(solution)/shard_map/ppermute | solution.py:47
  55.8 3.5 %collective-permute-done.8 = bf16[80,128]{1,0:T(8,128)(2,1)S(1)} collective-permute-done((bf16[80,128]{1,0:T(8,128)(2,1)S(1)}, bf16[80,128]{1,0:T(8,128)(2,1)S(1)}, u32[]{:S(2)}, u32[]{:S(2)}) %collective-permute-start.8) | collective-permute-done | bytes 20512 | tf_op jit(solution)/shard_map/ppermute | solution.py:580
  59.3 3.1 %collective-permute-start.9 = (bf16[2,80,128]{2,1,0:T(8,128)(2,1)S(1)}, bf16[2,80,128]{2,1,0:T(8,128)(2,1)S(1)}, u32[]{:S(2)}, u32[]{:S(2)}) collective-permute-start(bf16[2,80,128]{2,1,0:T(8,128)(2,1)S(1)} %pad_maximum_fusion.mine_ref), channel_id=1, source_target_pairs={{0,1},{1,0},{2,3},{3,2},{4,5},{5,4},{6,7},{7,6},{8,9},{9,8},{10,11... | collective-permute-start | bytes 122888 | tf_op jit(solution)/shard_map/ppermute | solution.py:580
  62.4 0.9 %finish.1 = (bf16[4,6,24,192]{3,2,1,0:T(8,128)(2,1)}, bf16[4,6,24,192]{3,2,1,0:T(8,128)(2,1)}) custom-call(bf16[2,4,3,18,192]{4,3,2,1,0:T(8,128)(2,1)S(1)} %get-tuple-element.54.own_ref, bf16[648,128]{1,0:T(8,128)(2,1)S(1)} %collective-permute-done.5.lat_ref, bf16[216,128]{1,0:T(8,128)(2,1)S(1)} %collective-permute-done.6.diag_ref, ...), custom_call_target="tpu_custom_call" | custom-call | tf_op jit(solution)/shard_map/finish/pallas_call | solution.py:749
  63.3 0.9 %unpack.1 = f32[12,1,3312]{2,1,0:T(1,128)} custom-call(bf16[2,80,128]{2,1,0:T(8,128)(2,1)S(1)} %pad_maximum_fusion.mine_ref, bf16[2,80,128]{2,1,0:T(8,128)(2,1)S(1)} %collective-permute-done.9.other_ref), custom_call_target="tpu_custom_call" | custom-call | tf_op jit(solution)/shard_map/unpack/pallas_call | solution.py:739
  (54 shorter events, 3.3 us)
Async XLA Ops:
  2.6 12.9 %copy-start.6 = (bf16[192,576]{1,0:T(8,128)(2,1)S(1)}, bf16[192,576]{1,0:T(8,128)(2,1)}, u32[]{:S(2)}) copy-start(bf16[192,576]{1,0:T(8,128)(2,1)} %wqkv_ref.1) | copy-start | bytes 663556
  2.6 12.9 %copy-start.7 = (f32[2,1,6,3312]{3,1,2,0:T(1,128)S(1)}, f32[2,1,6,3312]{3,1,2,0:T(1,128)}, u32[]{:S(2)}) copy-start(f32[2,1,6,3312]{3,1,2,0:T(1,128)} %param.19) | copy-start | bytes 476932
  2.6 12.9 %copy-start.10 = (f32[192]{0:T(256)S(1)}, f32[192]{0:T(256)}, u32[]{:S(2)}) copy-start(f32[192]{0:T(256)} %param.13) | copy-start | bytes 2308
  2.6 12.9 %copy-start.11 = (f32[192]{0:T(256)S(1)}, f32[192]{0:T(256)}, u32[]{:S(2)}) copy-start(f32[192]{0:T(256)} %param.16) | copy-start | bytes 2308
  2.6 12.9 %copy-start.12 = (s32[2,1,2]{2,1,0:T(1,128)S(1)}, s32[2,1,2]{2,1,0:T(1,128)}, u32[]{:S(2)}) copy-start(s32[2,1,2]{2,1,0:T(1,128)} %keep_ref.1) | copy-start | bytes 52
  2.6 16.2 %copy-start.8 = (bf16[192,192]{1,0:T(8,128)(2,1)S(1)}, bf16[192,192]{1,0:T(8,128)(2,1)}, u32[]{:S(2)}) copy-start(bf16[192,192]{1,0:T(8,128)(2,1)} %wproj_ref.3) | copy-start | bytes 221188
  2.8 12.7 %copy-start.9 = (s32[4,6,24]{2,0,1:T(4,128)S(1)}, s32[4,6,24]{2,0,1:T(4,128)}, u32[]{:S(2)}) copy-start(s32[4,6,24]{2,0,1:T(4,128)} %param.20) | copy-start | bytes 6916
  2.9 15.9 %collective-permute-start.1 = (bf16[648,128]{1,0:T(8,128)(2,1)S(1)}, bf16[648,128]{1,0:T(8,128)(2,1)S(1)}, u32[]{:S(2)}, u32[]{:S(2)}) collective-permute-start(bf16[648,128]{1,0:T(8,128)(2,1)S(1)} %pack_lat.1.after_ref), channel_id=1, source_target_pairs={{0,224},{1,225},{2,226},{3,227},{4,228},{5,229},{6,230},{7,231},{8... | collective-permute-start | bytes 497672 | tf_op jit(solution)/shard_map/ppermute | solution.py:47
  7.3 11.5 %copy-start.3 = (bf16[4,6,24,192]{3,2,1,0:T(8,128)(2,1)S(1)}, bf16[4,6,24,192]{3,2,1,0:T(8,128)(2,1)}, u32[]{:S(2)}) copy-start(bf16[4,6,24,192]{3,2,1,0:T(8,128)(2,1)} %cot_ref.5) | copy-start | bytes 663556
  7.3 11.5 %copy-start.4 = (bf16[192,768]{1,0:T(8,128)(2,1)S(1)}, bf16[192,768]{1,0:T(8,128)(2,1)}, u32[]{:S(2)}) copy-start(bf16[192,768]{1,0:T(8,128)(2,1)} %wup_ref.1) | copy-start | bytes 884740
  7.3 11.5 %copy-start.5 = (bf16[768,192]{0,1:T(8,128)(2,1)S(1)}, bf16[768,192]{0,1:T(8,128)(2,1)}, u32[]{:S(2)}) copy-start(bf16[768,192]{0,1:T(8,128)(2,1)} %param.18) | copy-start | bytes 884740
  7.4 11.4 %copy-start.1 = (bf16[4,6,24,192]{3,2,1,0:T(8,128)(2,1)S(1)}, bf16[4,6,24,192]{3,2,1,0:T(8,128)(2,1)}, u32[]{:S(2)}) copy-start(bf16[4,6,24,192]{3,2,1,0:T(8,128)(2,1)} %field_ref.5) | copy-start | bytes 663556
  7.4 11.3 %collective-permute-start = (bf16[216,128]{1,0:T(8,128)(2,1)S(1)}, bf16[216,128]{1,0:T(8,128)(2,1)S(1)}, u32[]{:S(2)}, u32[]{:S(2)}) collective-permute-start(bf16[216,128]{1,0:T(8,128)(2,1)S(1)} %get-tuple-element.36), channel_id=1, source_target_pairs={{0,31},{1,0},{2,1},{3,2},{4,3},{5,4},{6,5},{7,6},{8,7},{9,8},{10,9... | collective-permute-start | bytes 165896 | tf_op jit(solution)/shard_map/ppermute | solution.py:47
  8.4 10.3 %collective-permute-start.2 = (bf16[216,128]{1,0:T(8,128)(2,1)S(1)}, bf16[216,128]{1,0:T(8,128)(2,1)S(1)}, u32[]{:S(2)}, u32[]{:S(2)}) collective-permute-start(bf16[216,128]{1,0:T(8,128)(2,1)S(1)} %get-tuple-element.37), channel_id=1, source_target_pairs={{0,255},{1,224},{2,225},{3,226},{4,227},{5,228},{6,229},{7,230},{8... | collective-permute-start | bytes 165896 | tf_op jit(solution)/shard_map/ppermute | solution.py:47
  31.2 1.8 %copy-start.16 = (bf16[576,192]{1,0:T(8,128)(2,1)S(1)}, bf16[576,192]{1,0:T(8,128)(2,1)}, u32[]{:S(2)}) copy-start(bf16[576,192]{1,0:T(8,128)(2,1)} %copy-done.15) | copy-start | bytes 663556
  31.2 1.5 %collective-permute-start.3 = (bf16[2,80,128]{2,1,0:T(8,128)(2,1)S(1)}, bf16[2,80,128]{2,1,0:T(8,128)(2,1)S(1)}, u32[]{:S(2)}, u32[]{:S(2)}) collective-permute-start(bf16[2,80,128]{2,1,0:T(8,128)(2,1)S(1)} %dynamic-slice_bitcast_fusion), channel_id=1, source_target_pairs={{0,1},{1,0},{2,3},{3,2},{4,5},{5,4},{6,7},{7,6},{8,9},{9,8},{10,11... | collective-permute-start | bytes 122888 | tf_op jit(solution)/shard_map/ppermute | solution.py:580
  32.7 6.9 %collective-permute-start.4 = (bf16[80,128]{1,0:T(8,128)(2,1)S(1)}, bf16[80,128]{1,0:T(8,128)(2,1)S(1)}, u32[]{:S(2)}, u32[]{:S(2)}) collective-permute-start(bf16[80,128]{1,0:T(8,128)(2,1)S(1)} %get-tuple-element.71), channel_id=1, source_target_pairs={{0,2},{1,3},{2,0},{3,1},{4,6},{5,7},{6,4},{7,5},{8,10},{9,11},{10,... | collective-permute-start | bytes 61448 | tf_op jit(solution)/shard_map/ppermute | solution.py:580
  33.1 1.2 %copy-start.14 = (bf16[4,144,864]{2,1,0:T(8,128)(2,1)S(1)}, bf16[4,144,864]{2,1,0:T(8,128)(2,1)}, u32[]{:S(2)}) copy-start(bf16[4,144,864]{2,1,0:T(8,128)(2,1)} %copy-done.13) | copy-start | bytes 2985988
  40.3 13.8 %all-to-all-start = ((bf16[8,80,128]{2,1,0:T(8,128)(2,1)}), bf16[8,80,128]{2,1,0:T(8,128)(2,1)S(1)}, u32[]{:S(2)}, u32[]{:S(2)}) async-start(bf16[8,80,128]{2,1,0:T(8,128)(2,1)} %add.29), calls=%async_computation | async-start | bytes 327680 | tf_op jit(solution)/shard_map/all_to_all | solution.py:606
  45.6 9.6 %collective-permute-start.5 = (bf16[648,128]{1,0:T(8,128)(2,1)S(1)}, bf16[648,128]{1,0:T(8,128)(2,1)S(1)}, u32[]{:S(2)}, u32[]{:S(2)}) collective-permute-start(bf16[648,128]{1,0:T(8,128)(2,1)S(1)} %get-tuple-element.60), channel_id=1, source_target_pairs={{0,32},{1,33},{2,34},{3,35},{4,36},{5,37},{6,38},{7,39},{8,40},{9,... | collective-permute-start | bytes 497672 | tf_op jit(solution)/shard_map/ppermute | solution.py:47
  45.6 9.5 %collective-permute-start.6 = (bf16[216,128]{1,0:T(8,128)(2,1)S(1)}, bf16[216,128]{1,0:T(8,128)(2,1)S(1)}, u32[]{:S(2)}, u32[]{:S(2)}) collective-permute-start(bf16[216,128]{1,0:T(8,128)(2,1)S(1)} %get-tuple-element.61), channel_id=1, source_target_pairs={{0,33},{1,34},{2,35},{3,36},{4,37},{5,38},{6,39},{7,40},{8,41},{9,... | collective-permute-start | bytes 165896 | tf_op jit(solution)/shard_map/ppermute | solution.py:47
  48.9 6.3 %collective-permute-start.7 = (bf16[216,128]{1,0:T(8,128)(2,1)S(1)}, bf16[216,128]{1,0:T(8,128)(2,1)S(1)}, u32[]{:S(2)}, u32[]{:S(2)}) collective-permute-start(bf16[216,128]{1,0:T(8,128)(2,1)S(1)} %get-tuple-element.62), channel_id=1, source_target_pairs={{0,1},{1,2},{2,3},{3,4},{4,5},{5,6},{6,7},{7,8},{8,9},{9,10},{10,1... | collective-permute-start | bytes 165896 | tf_op jit(solution)/shard_map/ppermute | solution.py:47
  55.2 4.1 %collective-permute-start.8 = (bf16[80,128]{1,0:T(8,128)(2,1)S(1)}, bf16[80,128]{1,0:T(8,128)(2,1)S(1)}, u32[]{:S(2)}, u32[]{:S(2)}) collective-permute-start(bf16[80,128]{1,0:T(8,128)(2,1)S(1)} %bitcast.26), channel_id=1, source_target_pairs={{0,2},{1,3},{2,0},{3,1},{4,6},{5,7},{6,4},{7,5},{8,10},{9,11},{10,... | collective-permute-start | bytes 61448 | tf_op jit(solution)/shard_map/ppermute | solution.py:580
  59.3 4.0 %collective-permute-start.9 = (bf16[2,80,128]{2,1,0:T(8,128)(2,1)S(1)}, bf16[2,80,128]{2,1,0:T(8,128)(2,1)S(1)}, u32[]{:S(2)}, u32[]{:S(2)}) collective-permute-start(bf16[2,80,128]{2,1,0:T(8,128)(2,1)S(1)} %pad_maximum_fusion.mine_ref), channel_id=1, source_target_pairs={{0,1},{1,0},{2,3},{3,2},{4,5},{5,4},{6,7},{7,6},{8,9},{9,8},{10,11... | collective-permute-start | bytes 122888 | tf_op jit(solution)/shard_map/ppermute | solution.py:580
  (8 other events, 6.9 us)

commit v13 on v12

--- a/solution.py
+++ b/solution.py
@@ -221,7 +221,8 @@
     bias_ref,
     label_row_ref,
     label_col_ref,
-    fold_out,
+    keep_out,
+    send_out,
     x_out,
     probs_out,
     grad_low_out,
@@ -268,6 +269,7 @@
     table_perm = table_order()
     chunk_perm = chunk_order()
     dense[...] = jnp.zeros_like(dense)
+    odd = jnp.broadcast_to(gains_ref[6:7, :LANES], (DENSE, LANES)) > 0.5
     for n in range(2):
         both = slice(n * 2 * POS, (n + 1) * 2 * POS)
         x = mm(perm, frame[0, both, :].astype(bf16))
@@ -347,13 +349,16 @@
         total = total.reshape(HEADS * SLOTS, TAB).astype(bf16)
         total = mm_nt(total, table_perm).astype(bf16)
         total = mm(chunk_perm, total)
+        quarters = []
         for k in range(2):
             part = total[k * QUARTER : (k + 1) * QUARTER]
             dense[:QUARTER, :] = part[:, :LANES]
             dense[QUARTER : 2 * QUARTER, :] = part[:, LANES : 2 * LANES]
             rest = [part[HEADS * g : HEADS * (g + 1), 2 * LANES :] for g in range(WLAT)]
             dense[2 * QUARTER : 2 * QUARTER + HEADS, : WLAT * REST] = jnp.concatenate(rest, axis=1)
-            fold_out[2 * n + k] = dense[...].astype(bf16)
+            quarters.append(dense[...])
+        keep_out[n] = jnp.where(odd, quarters[1], quarters[0]).astype(bf16)
+        send_out[n] = jnp.where(odd, quarters[0], quarters[1]).astype(bf16)
 
 
 def rest_kernel(
@@ -462,6 +467,10 @@
             factor = keep_ref[n, 0, c].astype(f32) * (1.0 / keep_share)
             row = 2 + 2 * n + c
             gains_out[row : row + 1, :] = jnp.full((1, C), factor, f32)
+    lon_index = lax.axis_index("lon")
+    for k in range(2):
+        bit = ((lon_index >> k) & 1).astype(f32)
+        gains_out[6 + k : 7 + k, :] = jnp.full((1, C), bit, f32)
     last = lax.axis_index("lat") == lax.axis_size("lat") - 1
     level = lax.broadcasted_iota(jnp.int32, (4, 2 * WLON), 0)
     for i in range(WLAT):
@@ -541,6 +550,13 @@
         table_out[k] = flat[k : k + 1, :]
 
 
+def halve_kernel(mine_ref, other_ref, gains_ref, keep_out, send_out):
+    upper = jnp.broadcast_to(gains_ref[7:8, :LANES], (DENSE, LANES)) > 0.5
+    sums = [mine_ref[k].astype(f32) + other_ref[k].astype(f32) for k in range(2)]
+    keep_out[0] = jnp.where(upper, sums[1], sums[0]).astype(bf16)
+    send_out[0] = jnp.where(upper, sums[0], sums[1]).astype(bf16)
+
+
 def add_kernel(*refs):
     copies_out = refs[-1]
     parts = [ref[k].astype(f32) for ref in refs[:-1] for k in range(ref.shape[0])]
@@ -570,20 +586,15 @@
                 target[z, half + i] = jnp.concatenate([slab, own], axis=0).astype(bf16)
 
 
-def lon_sum(quarters, saved, rest_of_backward):
+def lon_sum(keep, send, gains, saved, rest_of_backward):
     lons = lax.axis_size("lon")
-    me = lax.axis_index("lon")
-    bits = [(me >> k) & 1 for k in range(2)]
     far = [[4 * k + j for k in range(lons // 4)] for j in range(4)]
+    vmem = pl.BlockSpec(memory_space=pltpu.VMEM)
 
     def swapped(block, distance):
         return lax.ppermute(block, "lon", [(i, i ^ distance) for i in range(lons)])
 
-    def pick(value, bit, axis):
-        return lax.dynamic_index_in_dim(value, bit, axis, keepdims=False)
-
     def added(parts, copies):
-        vmem = pl.BlockSpec(memory_space=pltpu.VMEM)
         return pl.pallas_call(
             add_kernel,
             out_shape=jax.ShapeDtypeStruct((copies,) + parts[0].shape[1:], bf16),
@@ -593,21 +604,28 @@
             name="add",
         )(*parts)
 
-    value = quarters.reshape((2, 2) + quarters.shape[1:])
-    other = swapped(pick(value, 1 - bits[0], 1), 1)
-    value = pick(value, bits[0], 1).astype(f32) + other.astype(f32)
-    value, saved = lax.optimization_barrier((value.astype(bf16), saved))
-    other = swapped(pick(value, 1 - bits[1], 0), 2)
+    other, saved = lax.optimization_barrier((swapped(send, 1), saved))
+    quarter = jax.ShapeDtypeStruct((1,) + keep.shape[1:], bf16)
+    keep, send = pl.pallas_call(
+        halve_kernel,
+        out_shape=(quarter,) * 2,
+        in_specs=[vmem] * 3,
+        out_specs=(vmem,) * 2,
+        compiler_params=pltpu.CompilerParams(vmem_limit_bytes=VMEM_BYTES),
+        name="halve",
+    )(keep, other, gains)
+    other = swapped(send, 2)
     own, *strips = rest_of_backward(saved)
-    parts = added((pick(value, bits[1], 0)[None], other[None]), lons // 4)
+    parts = added((keep, other), lons // 4)
     parts, strips = lax.optimization_barrier((parts, strips))
     steps = ((1, 0), (1, 1), (0, 1))
     strips = [shifted(strip, *step) for strip, step in zip(strips, steps)]
     parts = lax.all_to_all(parts, "lon", 0, 0, axis_index_groups=far)
     value, strips = lax.optimization_barrier((added((parts,), 1)[0], strips))
     other = swapped(value, 2)
-    lower = jnp.where(bits[1] == 0, value, other)
-    upper = jnp.where(bits[1] == 0, other, value)
+    second = gains[7:8, :LANES] > 0.5
+    lower = jnp.where(second, other, value)
+    upper = jnp.where(second, value, other)
     value = jnp.stack([lower, upper])
     return (value, swapped(value, 1)), own, strips
 
@@ -665,7 +683,7 @@
             jax.ShapeDtypeStruct((4, ROWS), f32),
             jax.ShapeDtypeStruct((POS, 4), f32),
             jax.ShapeDtypeStruct((3 * C, C), bf16),
-            jax.ShapeDtypeStruct((6, C), f32),
+            jax.ShapeDtypeStruct((8, C), f32),
         ),
         in_specs=[vmem] * 5 + [smem],
         out_specs=(vmem,) * 5,
@@ -686,10 +704,11 @@
         keep_flags,
     )
     positions = levels * lat_rows * lon_cols
-    fold, *saved = pl.pallas_call(
+    keep, send, *saved = pl.pallas_call(
         scores_kernel,
         out_shape=(
-            jax.ShapeDtypeStruct((4, DENSE, LANES), bf16),
+            jax.ShapeDtypeStruct((2, DENSE, LANES), bf16),
+            jax.ShapeDtypeStruct((2, DENSE, LANES), bf16),
             jax.ShapeDtypeStruct((positions, C), bf16),
             jax.ShapeDtypeStruct((4, POS, ROWS), bf16),
             jax.ShapeDtypeStruct((4, POS, ROWS), bf16),
@@ -697,7 +716,7 @@
             jax.ShapeDtypeStruct((positions, C), bf16),
         ),
         in_specs=[vmem] * 13,
-        out_specs=(vmem,) * 6,
+        out_specs=(vmem,) * 7,
         scratch_shapes=[
             pltpu.VMEM((2, positions, C), f32),
             pltpu.VMEM((HEADS, POS, POS), f32),
@@ -735,7 +754,7 @@
             name="rest",
         )(*saved, gains, weights_t, w_proj)
 
-    halves, own, (lat_back, diag_back, lon_back) = lon_sum(fold, saved, rest_of_backward)
+    halves, own, (lat_back, diag_back, lon_back) = lon_sum(keep, send, gains, saved, rest_of_backward)
     grads = pl.pallas_call(
         unpack_kernel,
         out_shape=jax.ShapeDtypeStruct((2 * HEADS, 1, PAIR * TAB), f32),

time: 64.6 us -> 59 us (0.913)
  local copies, waits for them, and re-layouts: 8.21 us -> 1.96 us
  waiting for transfers between devices: 10.1 us -> 10.9 us
    unnamed x42 -> x26, local copies, waits for them, and re-layouts: 8.19 us -> 1.96 us
    ppermute x4, starting transfers between devices: 4.57 us -> 5.32 us  [swapped(): return lax.ppermute(block, 'lon', [(i, i ^ distance) for i in range(lons)])]
    ppermute x4, waiting for transfers between devices: 4.43 us -> 5.13 us  [swapped(): return lax.ppermute(block, 'lon', [(i, i ^ distance) for i in range(lons)])]
    all_to_all x1, starting transfers between devices: 5.28 us -> 4.6 us  [lon_sum(): parts = lax.all_to_all(parts, 'lon', 0, 0, axis_index_groups=far)]
    pallas_call x1 -> x2, Pallas kernels: 9.36 us -> 9.35 us  [the longest x1 9.34 us: body(): pl.pallas_call(scores_kernel, out_shape=(jax.ShapeDtypeStruct((2, DENSE,...]
  transfers between devices with their start and end apart: 11 -> 11, of which waited for: 4 -> 5; matrix products, arithmetic and copies ran while one was open for 0% -> 0% of each run, Pallas kernels for 12% -> 13%
where the time goes in v13:
time: 59 us; the launch traced here: 58.7 us
  starting transfers between devices  26.3 us (45%)
  Pallas kernels  18.8 us (32%)
  waiting for transfers between devices  10.9 us (18%)
  local copies, waits for them, and re-layouts  1.96 us (3%)
  between operations  0.82 us (1%)
    ppermute x6, starting transfers between devices, shifted(): return lax.ppermute(block, ('lat', 'lon'), route)  16.3 us
    pallas_call x1, Pallas kernels, body(): pl.pallas_call(scores_kernel, out_shape=(jax.ShapeDtypeStruct((2, DENSE,...  9.34 us
    ppermute x4, starting transfers between devices, swapped(): return lax.ppermute(block, 'lon', [(i, i ^ distance) for i in range(lons)])  5.32 us
    ppermute x4, waiting for transfers between devices, swapped(): return lax.ppermute(block, 'lon', [(i, i ^ distance) for i in range(lons)])  5.13 us
    all_to_all x1, waiting for transfers between devices, lon_sum(): parts = lax.all_to_all(parts, 'lon', 0, 0, axis_index_groups=far)  4.65 us
    all_to_all x1, starting transfers between devices, lon_sum(): parts = lax.all_to_all(parts, 'lon', 0, 0, axis_index_groups=far)  4.6 us
    pallas_call x1, Pallas kernels, rest_of_backward(): pl.pallas_call(rest_kernel, out_shape=(jax.ShapeDtypeStruct((2, levels, h...  3.41 us
    pallas_call x1, Pallas kernels, body(): pl.pallas_call(prepare_kernel, out_shape=(jax.ShapeDtypeStruct((2, POS, R...  3.17 us
  transfers between devices with their start and end apart: 11, of which 5 were waited for; matrix products, arithmetic and copies ran while one was open for 0% of the time, Pallas kernels for 13%

profile of v13, /device:TPU:1, one launch (start us, length us, event | category | flops | bytes accessed | tf_op | source)
XLA Modules:
  0.0 58.7 jit_solution(532912037009364343)
XLA Ops:
  0.6 1.0 %copy-done = bf16[4,6,24,192]{3,2,1,0:T(8,128)(2,1)S(1)} copy-done((bf16[4,6,24,192]{3,2,1,0:T(8,128)(2,1)S(1)}, bf16[4,6,24,192]{3,2,1,0:T(8,128)(2,1)}, u32[]{:S(2)}) %copy-start) | copy-done | bytes 221208
  1.6 1.0 %copy-done.2 = bf16[4,6,24,192]{3,2,1,0:T(8,128)(2,1)S(1)} copy-done((bf16[4,6,24,192]{3,2,1,0:T(8,128)(2,1)S(1)}, bf16[4,6,24,192]{3,2,1,0:T(8,128)(2,1)}, u32[]{:S(2)}) %copy-start.2) | copy-done | bytes 221208
  2.6 0.2 pack_lat.1.after_ref
  2.9 4.4 %collective-permute-start.1 = (bf16[648,128]{1,0:T(8,128)(2,1)S(1)}, bf16[648,128]{1,0:T(8,128)(2,1)S(1)}, u32[]{:S(2)}, u32[]{:S(2)}) collective-permute-start(bf16[648,128]{1,0:T(8,128)(2,1)S(1)} %pack_lat.1.after_ref), channel_id=1, source_target_pairs={{0,224},{1,225},{2,226},{3,227},{4,228},{5,229},{6,230},{7,231},{8... | collective-permute-start | bytes 497672 | tf_op jit(solution)/shard_map/ppermute | solution.py:47
  7.4 1.0 %collective-permute-start = (bf16[216,128]{1,0:T(8,128)(2,1)S(1)}, bf16[216,128]{1,0:T(8,128)(2,1)S(1)}, u32[]{:S(2)}, u32[]{:S(2)}) collective-permute-start(bf16[216,128]{1,0:T(8,128)(2,1)S(1)} %get-tuple-element.39), channel_id=1, source_target_pairs={{0,31},{1,0},{2,1},{3,2},{4,3},{5,4},{6,5},{7,6},{8,7},{9,8},{10,9... | collective-permute-start | bytes 165896 | tf_op jit(solution)/shard_map/ppermute | solution.py:47
  8.4 7.1 %collective-permute-start.2 = (bf16[216,128]{1,0:T(8,128)(2,1)S(1)}, bf16[216,128]{1,0:T(8,128)(2,1)S(1)}, u32[]{:S(2)}, u32[]{:S(2)}) collective-permute-start(bf16[216,128]{1,0:T(8,128)(2,1)S(1)} %get-tuple-element.40), channel_id=1, source_target_pairs={{0,255},{1,224},{2,225},{3,226},{4,227},{5,228},{6,229},{7,230},{8... | collective-permute-start | bytes 165896 | tf_op jit(solution)/shard_map/ppermute | solution.py:47
  15.5 3.2 %prepare.1 = (f32[2,144,864]{2,1,0:T(8,128)S(1)}, f32[4,864]{1,0:T(4,128)S(1)}, f32[144,4]{1,0:T(8,128)S(1)}, bf16[576,192]{1,0:T(8,128)(2,1)S(1)}, f32[8,192]{1,0:T(8,128)S(1)}) custom-call(f32[12,1,3312]{2,1,0:T(1,128)S(1)} %bitcast.14, s32[6,4,24]{2,1,0:T(4,128)S(1)} %bitcast.17, bf16[192,576]{1,0:T(8,128)(2,1)S(1)} %copy-done.6, f32[1,192]{1,0:T(1,128)S(1)} %bitcast.18, ...), custom_call_target="tpu_custom_call" | custom-call | tf_op jit(solution)/shard_map/prepare/pallas_call | solution.py:679
  18.8 9.3 %scores.1 = (bf16[2,80,128]{2,1,0:T(8,128)(2,1)S(1)}, bf16[2,80,128]{2,1,0:T(8,128)(2,1)S(1)}, bf16[576,192]{1,0:T(8,128)(2,1)S(1)}, bf16[4,144,864]{2,1,0:T(8,1...) custom-call(bf16[4,6,24,192]{3,2,1,0:T(8,128)(2,1)S(1)} %copy-done.1, ...), custom_call_target="tpu_custom_call" | custom-call | tf_op jit(solution)/shard_map/scores/pallas_call | solution.py:707
  28.1 0.7 %collective-permute-start.3 = (bf16[2,80,128]{2,1,0:T(8,128)(2,1)S(1)}, bf16[2,80,128]{2,1,0:T(8,128)(2,1)S(1)}, u32[]{:S(2)}, u32[]{:S(2)}) collective-permute-start(bf16[2,80,128]{2,1,0:T(8,128)(2,1)S(1)} %get-tuple-element.46), channel_id=1, source_target_pairs={{0,1},{1,0},{2,3},{3,2},{4,5},{5,4},{6,7},{7,6},{8,9},{9,8},{10,11... | collective-permute-start | bytes 122888 | tf_op jit(solution)/shard_map/ppermute | solution.py:595
  28.8 0.9 %collective-permute-done.3.other_ref = bf16[2,80,128]{2,1,0:T(8,128)(2,1)S(1)} collective-permute-done((bf16[2,80,128]{2,1,0:T(8,128)(2,1)S(1)}, bf16[2,80,128]{2,1,0:T(8,128)(2,1)S(1)}, u32[]{:S(2)}, u32[]{:S(2)}) %collective-permute-start.3) | collective-permute-done | bytes 40992 | tf_op jit(solution)/shard_map/ppermute | solution.py:595
  29.7 0.3 collective-permute-start.4
  30.0 3.4 %rest.1 = (bf16[2,4,3,18,192]{4,3,2,1,0:T(8,128)(2,1)S(1)}, bf16[648,128]{1,0:T(8,128)(2,1)S(1)}, bf16[216,128]{1,0:T(8,128)(2,1)S(1)}, bf16[216,128]{1,0:T(8,128)(2,1)S(1)}) custom-call(bf16[576,192]{1,0:T(8,128)(2,1)S(1)} %get-tuple-element.52.x_ref, bf16[4,144,864]{2,1,0:T(8,128)(2,1)S(1)} %get-tuple-element.53.probs_ref, ...), custom_call_target="tpu_custom_call" | custom-call | flops 1000000000 | bytes 8000000 | tf_op jit(solution)/shard_map/rest/pallas_call | solution.py:744
  33.4 0.7 %collective-permute-done.4.refs_1_ = bf16[1,80,128]{2,1,0:T(8,128)(2,1)S(1)} collective-permute-done((bf16[1,80,128]{2,1,0:T(8,128)(2,1)S(1)}, bf16[1,80,128]{2,1,0:T(8,128)(2,1)S(1)}, u32[]{:S(2)}, u32[]{:S(2)}) %collective-permute-start.4) | collective-permute-done | bytes 20512 | tf_op jit(solution)/shard_map/ppermute | solution.py:595
  34.1 0.7 %add.2 = bf16[8,80,128]{2,1,0:T(8,128)(2,1)} custom-call(bf16[1,80,128]{2,1,0:T(8,128)(2,1)S(1)} %get-tuple-element.60.refs_0_, bf16[1,80,128]{2,1,0:T(8,128)(2,1)S(1)} %collective-permute-done.4.refs_1_), custom_call_target="tpu_custom_call" | custom-call | tf_op jit(solution)/shard_map/add/pallas_call | solution.py:598
  34.8 4.6 %all-to-all-start = ((bf16[8,80,128]{2,1,0:T(8,128)(2,1)}), bf16[8,80,128]{2,1,0:T(8,128)(2,1)S(1)}, u32[]{:S(2)}, u32[]{:S(2)}) async-start(bf16[8,80,128]{2,1,0:T(8,128)(2,1)} %add.2), calls=%async_computation | async-start | bytes 327680 | tf_op jit(solution)/shard_map/all_to_all | solution.py:623
  39.7 3.0 %collective-permute-start.6 = (bf16[216,128]{1,0:T(8,128)(2,1)S(1)}, bf16[216,128]{1,0:T(8,128)(2,1)S(1)}, u32[]{:S(2)}, u32[]{:S(2)}) collective-permute-start(bf16[216,128]{1,0:T(8,128)(2,1)S(1)} %get-tuple-element.67), channel_id=1, source_target_pairs={{0,33},{1,34},{2,35},{3,36},{4,37},{5,38},{6,39},{7,40},{8,41},{9,... | collective-permute-start | bytes 165896 | tf_op jit(solution)/shard_map/ppermute | solution.py:47
  42.7 0.6 collective-permute-start.7
  43.2 4.7 %all-to-all-done.refs_0_ = bf16[8,80,128]{2,1,0:T(8,128)(2,1)S(1)} async-done(((bf16[8,80,128]{2,1,0:T(8,128)(2,1)}), bf16[8,80,128]{2,1,0:T(8,128)(2,1)S(1)}, u32[]{:S(2)}, u32[]{:S(2)}) %all-to-all-start) | async-done | bytes 163872 | tf_op jit(solution)/shard_map/all_to_all | solution.py:623
  47.9 1.1 %collective-permute-done.6.diag_ref = bf16[216,128]{1,0:T(8,128)(2,1)S(1)} collective-permute-done((bf16[216,128]{1,0:T(8,128)(2,1)S(1)}, bf16[216,128]{1,0:T(8,128)(2,1)S(1)}, u32[]{:S(2)}, u32[]{:S(2)}) %collective-permute-start.6) | collective-permute-done | bytes 55328 | tf_op jit(solution)/shard_map/ppermute | solution.py:47
  49.0 0.6 collective-permute-start.8
  49.6 3.5 %collective-permute-done.8 = bf16[80,128]{1,0:T(8,128)(2,1)S(1)} collective-permute-done((bf16[80,128]{1,0:T(8,128)(2,1)S(1)}, bf16[80,128]{1,0:T(8,128)(2,1)S(1)}, u32[]{:S(2)}, u32[]{:S(2)}) %collective-permute-start.8) | collective-permute-done | bytes 20512 | tf_op jit(solution)/shard_map/ppermute | solution.py:595
  53.2 3.7 %collective-permute-start.9 = (bf16[2,80,128]{2,1,0:T(8,128)(2,1)S(1)}, bf16[2,80,128]{2,1,0:T(8,128)(2,1)S(1)}, u32[]{:S(2)}, u32[]{:S(2)}) collective-permute-start(bf16[2,80,128]{2,1,0:T(8,128)(2,1)S(1)} %pad_maximum_fusion.mine_ref), channel_id=1, source_target_pairs={{0,1},{1,0},{2,3},{3,2},{4,5},{5,4},{6,7},{7,6},{8,9},{9,8},{10,11... | collective-permute-start | bytes 122888 | tf_op jit(solution)/shard_map/ppermute | solution.py:595
  56.9 0.9 %finish.1 = (bf16[4,6,24,192]{3,2,1,0:T(8,128)(2,1)}, bf16[4,6,24,192]{3,2,1,0:T(8,128)(2,1)}) custom-call(bf16[2,4,3,18,192]{4,3,2,1,0:T(8,128)(2,1)S(1)} %get-tuple-element.57.own_ref, bf16[648,128]{1,0:T(8,128)(2,1)S(1)} %collective-permute-done.5.lat_ref, bf16[216,128]{1,0:T(8,128)(2,1)S(1)} %collective-permute-done.6.diag_ref, ...), custom_call_target="tpu_custom_call" | custom-call | tf_op jit(solution)/shard_map/finish/pallas_call | solution.py:768
  57.8 0.9 %unpack.1 = f32[12,1,3312]{2,1,0:T(1,128)} custom-call(bf16[2,80,128]{2,1,0:T(8,128)(2,1)S(1)} %pad_maximum_fusion.mine_ref, bf16[2,80,128]{2,1,0:T(8,128)(2,1)S(1)} %collective-permute-done.9.other_ref), custom_call_target="tpu_custom_call" | custom-call | tf_op jit(solution)/shard_map/unpack/pallas_call | solution.py:758
  (37 shorter events, 0.5 us)
Async XLA Ops:
  0.6 1.0 %copy-start = (bf16[4,6,24,192]{3,2,1,0:T(8,128)(2,1)S(1)}, bf16[4,6,24,192]{3,2,1,0:T(8,128)(2,1)}, u32[]{:S(2)}) copy-start(bf16[4,6,24,192]{3,2,1,0:T(8,128)(2,1)} %field_ref.5) | copy-start | bytes 663556
  1.6 1.0 %copy-start.2 = (bf16[4,6,24,192]{3,2,1,0:T(8,128)(2,1)S(1)}, bf16[4,6,24,192]{3,2,1,0:T(8,128)(2,1)}, u32[]{:S(2)}) copy-start(bf16[4,6,24,192]{3,2,1,0:T(8,128)(2,1)} %cot_ref.5) | copy-start | bytes 663556
  2.6 12.9 %copy-start.6 = (bf16[192,576]{1,0:T(8,128)(2,1)S(1)}, bf16[192,576]{1,0:T(8,128)(2,1)}, u32[]{:S(2)}) copy-start(bf16[192,576]{1,0:T(8,128)(2,1)} %wqkv_ref.1) | copy-start | bytes 663556
  2.6 12.9 %copy-start.7 = (f32[2,1,6,3312]{3,1,2,0:T(1,128)S(1)}, f32[2,1,6,3312]{3,1,2,0:T(1,128)}, u32[]{:S(2)}) copy-start(f32[2,1,6,3312]{3,1,2,0:T(1,128)} %param.19) | copy-start | bytes 476932
  2.6 12.9 %copy-start.10 = (f32[192]{0:T(256)S(1)}, f32[192]{0:T(256)}, u32[]{:S(2)}) copy-start(f32[192]{0:T(256)} %param.13) | copy-start | bytes 2308
  2.6 12.9 %copy-start.11 = (f32[192]{0:T(256)S(1)}, f32[192]{0:T(256)}, u32[]{:S(2)}) copy-start(f32[192]{0:T(256)} %param.16) | copy-start | bytes 2308
  2.6 12.9 %copy-start.12 = (s32[2,1,2]{2,1,0:T(1,128)S(1)}, s32[2,1,2]{2,1,0:T(1,128)}, u32[]{:S(2)}) copy-start(s32[2,1,2]{2,1,0:T(1,128)} %keep_ref.1) | copy-start | bytes 52
  2.6 16.2 %copy-start.8 = (bf16[192,192]{1,0:T(8,128)(2,1)S(1)}, bf16[192,192]{1,0:T(8,128)(2,1)}, u32[]{:S(2)}) copy-start(bf16[192,192]{1,0:T(8,128)(2,1)} %wproj_ref.3) | copy-start | bytes 221188
  2.8 12.7 %copy-start.9 = (s32[4,6,24]{2,0,1:T(4,128)S(1)}, s32[4,6,24]{2,0,1:T(4,128)}, u32[]{:S(2)}) copy-start(s32[4,6,24]{2,0,1:T(4,128)} %param.20) | copy-start | bytes 6916
  2.9 15.9 %collective-permute-start.1 = (bf16[648,128]{1,0:T(8,128)(2,1)S(1)}, bf16[648,128]{1,0:T(8,128)(2,1)S(1)}, u32[]{:S(2)}, u32[]{:S(2)}) collective-permute-start(bf16[648,128]{1,0:T(8,128)(2,1)S(1)} %pack_lat.1.after_ref), channel_id=1, source_target_pairs={{0,224},{1,225},{2,226},{3,227},{4,228},{5,229},{6,230},{7,231},{8... | collective-permute-start | bytes 497672 | tf_op jit(solution)/shard_map/ppermute | solution.py:47
  7.3 11.5 %copy-start.3 = (bf16[4,6,24,192]{3,2,1,0:T(8,128)(2,1)S(1)}, bf16[4,6,24,192]{3,2,1,0:T(8,128)(2,1)}, u32[]{:S(2)}) copy-start(bf16[4,6,24,192]{3,2,1,0:T(8,128)(2,1)} %cot_ref.5) | copy-start | bytes 663556
  7.3 11.5 %copy-start.4 = (bf16[192,768]{1,0:T(8,128)(2,1)S(1)}, bf16[192,768]{1,0:T(8,128)(2,1)}, u32[]{:S(2)}) copy-start(bf16[192,768]{1,0:T(8,128)(2,1)} %wup_ref.1) | copy-start | bytes 884740
  7.3 11.5 %copy-start.5 = (bf16[768,192]{0,1:T(8,128)(2,1)S(1)}, bf16[768,192]{0,1:T(8,128)(2,1)}, u32[]{:S(2)}) copy-start(bf16[768,192]{0,1:T(8,128)(2,1)} %param.18) | copy-start | bytes 884740
  7.4 11.4 %copy-start.1 = (bf16[4,6,24,192]{3,2,1,0:T(8,128)(2,1)S(1)}, bf16[4,6,24,192]{3,2,1,0:T(8,128)(2,1)}, u32[]{:S(2)}) copy-start(bf16[4,6,24,192]{3,2,1,0:T(8,128)(2,1)} %field_ref.5) | copy-start | bytes 663556
  7.4 11.3 %collective-permute-start = (bf16[216,128]{1,0:T(8,128)(2,1)S(1)}, bf16[216,128]{1,0:T(8,128)(2,1)S(1)}, u32[]{:S(2)}, u32[]{:S(2)}) collective-permute-start(bf16[216,128]{1,0:T(8,128)(2,1)S(1)} %get-tuple-element.39), channel_id=1, source_target_pairs={{0,31},{1,0},{2,1},{3,2},{4,3},{5,4},{6,5},{7,6},{8,7},{9,8},{10,9... | collective-permute-start | bytes 165896 | tf_op jit(solution)/shard_map/ppermute | solution.py:47
  8.4 10.3 %collective-permute-start.2 = (bf16[216,128]{1,0:T(8,128)(2,1)S(1)}, bf16[216,128]{1,0:T(8,128)(2,1)S(1)}, u32[]{:S(2)}, u32[]{:S(2)}) collective-permute-start(bf16[216,128]{1,0:T(8,128)(2,1)S(1)} %get-tuple-element.40), channel_id=1, source_target_pairs={{0,255},{1,224},{2,225},{3,226},{4,227},{5,228},{6,229},{7,230},{8... | collective-permute-start | bytes 165896 | tf_op jit(solution)/shard_map/ppermute | solution.py:47
  28.1 1.6 %collective-permute-start.3 = (bf16[2,80,128]{2,1,0:T(8,128)(2,1)S(1)}, bf16[2,80,128]{2,1,0:T(8,128)(2,1)S(1)}, u32[]{:S(2)}, u32[]{:S(2)}) collective-permute-start(bf16[2,80,128]{2,1,0:T(8,128)(2,1)S(1)} %get-tuple-element.46), channel_id=1, source_target_pairs={{0,1},{1,0},{2,3},{3,2},{4,5},{5,4},{6,7},{7,6},{8,9},{9,8},{10,11... | collective-permute-start | bytes 122888 | tf_op jit(solution)/shard_map/ppermute | solution.py:595
  29.7 4.4 %collective-permute-start.4 = (bf16[1,80,128]{2,1,0:T(8,128)(2,1)S(1)}, bf16[1,80,128]{2,1,0:T(8,128)(2,1)S(1)}, u32[]{:S(2)}, u32[]{:S(2)}) collective-permute-start(bf16[1,80,128]{2,1,0:T(8,128)(2,1)S(1)} %get-tuple-element.61), channel_id=1, source_target_pairs={{0,2},{1,3},{2,0},{3,1},{4,6},{5,7},{6,4},{7,5},{8,10},{9,11},{10,... | collective-permute-start | bytes 61448 | tf_op jit(solution)/shard_map/ppermute | solution.py:595
  34.8 13.1 %all-to-all-start = ((bf16[8,80,128]{2,1,0:T(8,128)(2,1)}), bf16[8,80,128]{2,1,0:T(8,128)(2,1)S(1)}, u32[]{:S(2)}, u32[]{:S(2)}) async-start(bf16[8,80,128]{2,1,0:T(8,128)(2,1)} %add.2), calls=%async_computation | async-start | bytes 327680 | tf_op jit(solution)/shard_map/all_to_all | solution.py:623
  39.4 9.6 %collective-permute-start.5 = (bf16[648,128]{1,0:T(8,128)(2,1)S(1)}, bf16[648,128]{1,0:T(8,128)(2,1)S(1)}, u32[]{:S(2)}, u32[]{:S(2)}) collective-permute-start(bf16[648,128]{1,0:T(8,128)(2,1)S(1)} %get-tuple-element.66), channel_id=1, source_target_pairs={{0,32},{1,33},{2,34},{3,35},{4,36},{5,37},{6,38},{7,39},{8,40},{9,... | collective-permute-start | bytes 497672 | tf_op jit(solution)/shard_map/ppermute | solution.py:47
  39.7 9.3 %collective-permute-start.6 = (bf16[216,128]{1,0:T(8,128)(2,1)S(1)}, bf16[216,128]{1,0:T(8,128)(2,1)S(1)}, u32[]{:S(2)}, u32[]{:S(2)}) collective-permute-start(bf16[216,128]{1,0:T(8,128)(2,1)S(1)} %get-tuple-element.67), channel_id=1, source_target_pairs={{0,33},{1,34},{2,35},{3,36},{4,37},{5,38},{6,39},{7,40},{8,41},{9,... | collective-permute-start | bytes 165896 | tf_op jit(solution)/shard_map/ppermute | solution.py:47
  42.7 6.3 %collective-permute-start.7 = (bf16[216,128]{1,0:T(8,128)(2,1)S(1)}, bf16[216,128]{1,0:T(8,128)(2,1)S(1)}, u32[]{:S(2)}, u32[]{:S(2)}) collective-permute-start(bf16[216,128]{1,0:T(8,128)(2,1)S(1)} %get-tuple-element.68), channel_id=1, source_target_pairs={{0,1},{1,2},{2,3},{3,4},{4,5},{5,6},{6,7},{7,8},{8,9},{9,10},{10,1... | collective-permute-start | bytes 165896 | tf_op jit(solution)/shard_map/ppermute | solution.py:47
  49.0 4.1 %collective-permute-start.8 = (bf16[80,128]{1,0:T(8,128)(2,1)S(1)}, bf16[80,128]{1,0:T(8,128)(2,1)S(1)}, u32[]{:S(2)}, u32[]{:S(2)}) collective-permute-start(bf16[80,128]{1,0:T(8,128)(2,1)S(1)} %bitcast.15), channel_id=1, source_target_pairs={{0,2},{1,3},{2,0},{3,1},{4,6},{5,7},{6,4},{7,5},{8,10},{9,11},{10,... | collective-permute-start | bytes 61448 | tf_op jit(solution)/shard_map/ppermute | solution.py:595
  53.2 4.6 %collective-permute-start.9 = (bf16[2,80,128]{2,1,0:T(8,128)(2,1)S(1)}, bf16[2,80,128]{2,1,0:T(8,128)(2,1)S(1)}, u32[]{:S(2)}, u32[]{:S(2)}) collective-permute-start(bf16[2,80,128]{2,1,0:T(8,128)(2,1)S(1)} %pad_maximum_fusion.mine_ref), channel_id=1, source_target_pairs={{0,1},{1,0},{2,3},{3,2},{4,5},{5,4},{6,7},{7,6},{8,9},{9,8},{10,11... | collective-permute-start | bytes 122888 | tf_op jit(solution)/shard_map/ppermute | solution.py:595

commit v14 on v13

--- a/solution.py
+++ b/solution.py
@@ -22,8 +22,8 @@
 SLOTS = 16
 QUARTER = PAIR * HEADS // 2
 REST = 20
-LN_ROWS = 96
-GELU_ROWS = 48
+LN_ROWS = 48
+GELU_ROWS = 16
 LANE_CUTS = [(k, min(k + 256, ROWS)) for k in range(0, ROWS, 256)]
 DENSE = 80
 LANES = 128
@@ -291,8 +291,11 @@
             probs = []
             for low, high in LANE_CUTS:
                 scores = mm_nt(k_all[rows], q_wide[low:high])
-                allowed = label_col == label_row_ref[w : w + 1, low:high]
-                probs.append(masked_softmax(scores, bias_ref[n, :, low:high], allowed))
+                for start in range(low, high, LANES):
+                    stop = min(start + LANES, high)
+                    allowed = label_col == label_row_ref[w : w + 1, start:stop]
+                    part = scores[:, start - low : stop - low]
+                    probs.append(masked_softmax(part, bias_ref[n, :, start:stop], allowed))
             probs_low = jnp.concatenate([part.astype(bf16) for part in probs], axis=1)
             probs_out[w] = probs_low
             attended = head_blocks(mm(v_t, probs_low)).astype(bf16).T
@@ -316,7 +319,7 @@
         grad_sum_low = grad_sum.astype(bf16)
         grad_sum_out[both, :] = grad_sum_low
         grad_low_in = grad_sum_low.astype(f32)
-        folded = [None] * len(LANE_CUTS)
+        folded = [None] * -(-ROWS // LANES)
         for c in range(2):
             rows = slice(c * POS, (c + 1) * POS)
             probs = saved[c]
@@ -325,12 +328,15 @@
             grad_att = mm_nt(grad_branch, wproj_ref[...]).astype(bf16)
             g_wide = spread_heads(grad_att, head_mask)
             grad_low = []
-            for k, (low, high) in enumerate(LANE_CUTS):
-                grad_probs = mm_nt(v_all[rows], g_wide[low:high])
-                inner_sum = jnp.sum(probs[k] * grad_probs, axis=0, keepdims=True)
-                grad_scores = probs[k] * (grad_probs - inner_sum)
-                folded[k] = grad_scores if c == 0 else folded[k] + grad_scores
-                grad_low.append(grad_scores.astype(bf16))
+            for low, high in LANE_CUTS:
+                products = mm_nt(v_all[rows], g_wide[low:high])
+                for start in range(low, high, LANES):
+                    k = start // LANES
+                    grad_probs = products[:, start - low : min(start + LANES, high) - low]
+                    inner_sum = jnp.sum(probs[k] * grad_probs, axis=0, keepdims=True)
+                    grad_scores = probs[k] * (grad_probs - inner_sum)
+                    folded[k] = grad_scores if c == 0 else folded[k] + grad_scores
+                    grad_low.append(grad_scores.astype(bf16))
             grad_low_out[2 * n + c] = jnp.concatenate(grad_low, axis=1)
         folded = jnp.concatenate([part.astype(bf16) for part in folded], axis=1)
         wide[...] = folded.T.astype(f32).reshape(HEADS, POS, POS)

time: 59 us -> 59 us (level)
  no operation moved by 1% of the time
where the time goes in v14:
time: 59 us; the launch traced here: 58.7 us
  starting transfers between devices  26.3 us (45%)
  Pallas kernels  18.8 us (32%)
  waiting for transfers between devices  10.8 us (18%)
  local copies, waits for them, and re-layouts  1.96 us (3%)
  between operations  0.82 us (1%)
    ppermute x6, starting transfers between devices, shifted(): return lax.ppermute(block, ('lat', 'lon'), route)  16.3 us
    pallas_call x1, Pallas kernels, body(): pl.pallas_call(scores_kernel, out_shape=(jax.ShapeDtypeStruct((2, DENSE,...  9.34 us
    ppermute x4, starting transfers between devices, swapped(): return lax.ppermute(block, 'lon', [(i, i ^ distance) for i in range(lons)])  5.32 us
    ppermute x4, waiting for transfers between devices, swapped(): return lax.ppermute(block, 'lon', [(i, i ^ distance) for i in range(lons)])  5.12 us
    all_to_all x1, waiting for transfers between devices, lon_sum(): parts = lax.all_to_all(parts, 'lon', 0, 0, axis_index_groups=far)  4.66 us
    all_to_all x1, starting transfers between devices, lon_sum(): parts = lax.all_to_all(parts, 'lon', 0, 0, axis_index_groups=far)  4.61 us
    pallas_call x1, Pallas kernels, rest_of_backward(): pl.pallas_call(rest_kernel, out_shape=(jax.ShapeDtypeStruct((2, levels, h...  3.41 us
    pallas_call x1, Pallas kernels, body(): pl.pallas_call(prepare_kernel, out_shape=(jax.ShapeDtypeStruct((2, POS, R...  3.17 us
  transfers between devices with their start and end apart: 11, of which 5 were waited for; matrix products, arithmetic and copies ran while one was open for 0% of the time, Pallas kernels for 13%

profile of v14, /device:TPU:1, one launch (start us, length us, event | category | flops | bytes accessed | tf_op | source)
XLA Modules:
  0.0 58.7 jit_solution(5219474941650807806)
XLA Ops:
  0.6 1.0 %copy-done = bf16[4,6,24,192]{3,2,1,0:T(8,128)(2,1)S(1)} copy-done((bf16[4,6,24,192]{3,2,1,0:T(8,128)(2,1)S(1)}, bf16[4,6,24,192]{3,2,1,0:T(8,128)(2,1)}, u32[]{:S(2)}) %copy-start) | copy-done | bytes 221208
  1.6 1.0 %copy-done.2 = bf16[4,6,24,192]{3,2,1,0:T(8,128)(2,1)S(1)} copy-done((bf16[4,6,24,192]{3,2,1,0:T(8,128)(2,1)S(1)}, bf16[4,6,24,192]{3,2,1,0:T(8,128)(2,1)}, u32[]{:S(2)}) %copy-start.2) | copy-done | bytes 221208
  2.6 0.2 pack_lat.1.after_ref
  2.9 4.4 %collective-permute-start.1 = (bf16[648,128]{1,0:T(8,128)(2,1)S(1)}, bf16[648,128]{1,0:T(8,128)(2,1)S(1)}, u32[]{:S(2)}, u32[]{:S(2)}) collective-permute-start(bf16[648,128]{1,0:T(8,128)(2,1)S(1)} %pack_lat.1.after_ref), channel_id=1, source_target_pairs={{0,224},{1,225},{2,226},{3,227},{4,228},{5,229},{6,230},{7,231},{8... | collective-permute-start | bytes 497672 | tf_op jit(solution)/shard_map/ppermute | solution.py:47
  7.4 1.0 %collective-permute-start = (bf16[216,128]{1,0:T(8,128)(2,1)S(1)}, bf16[216,128]{1,0:T(8,128)(2,1)S(1)}, u32[]{:S(2)}, u32[]{:S(2)}) collective-permute-start(bf16[216,128]{1,0:T(8,128)(2,1)S(1)} %get-tuple-element.39), channel_id=1, source_target_pairs={{0,31},{1,0},{2,1},{3,2},{4,3},{5,4},{6,5},{7,6},{8,7},{9,8},{10,9... | collective-permute-start | bytes 165896 | tf_op jit(solution)/shard_map/ppermute | solution.py:47
  8.4 7.1 %collective-permute-start.2 = (bf16[216,128]{1,0:T(8,128)(2,1)S(1)}, bf16[216,128]{1,0:T(8,128)(2,1)S(1)}, u32[]{:S(2)}, u32[]{:S(2)}) collective-permute-start(bf16[216,128]{1,0:T(8,128)(2,1)S(1)} %get-tuple-element.40), channel_id=1, source_target_pairs={{0,255},{1,224},{2,225},{3,226},{4,227},{5,228},{6,229},{7,230},{8... | collective-permute-start | bytes 165896 | tf_op jit(solution)/shard_map/ppermute | solution.py:47
  15.5 3.2 %prepare.1 = (f32[2,144,864]{2,1,0:T(8,128)S(1)}, f32[4,864]{1,0:T(4,128)S(1)}, f32[144,4]{1,0:T(8,128)S(1)}, bf16[576,192]{1,0:T(8,128)(2,1)S(1)}, f32[8,192]{1,0:T(8,128)S(1)}) custom-call(f32[12,1,3312]{2,1,0:T(1,128)S(1)} %bitcast.14, s32[6,4,24]{2,1,0:T(4,128)S(1)} %bitcast.17, bf16[192,576]{1,0:T(8,128)(2,1)S(1)} %copy-done.6, f32[1,192]{1,0:T(1,128)S(1)} %bitcast.18, ...), custom_call_target="tpu_custom_call" | custom-call | tf_op jit(solution)/shard_map/prepare/pallas_call | solution.py:685
  18.8 9.3 %scores.1 = (bf16[2,80,128]{2,1,0:T(8,128)(2,1)S(1)}, bf16[2,80,128]{2,1,0:T(8,128)(2,1)S(1)}, bf16[576,192]{1,0:T(8,128)(2,1)S(1)}, bf16[4,144,864]{2,1,0:T(8,1...) custom-call(bf16[4,6,24,192]{3,2,1,0:T(8,128)(2,1)S(1)} %copy-done.1, ...), custom_call_target="tpu_custom_call" | custom-call | tf_op jit(solution)/shard_map/scores/pallas_call | solution.py:713
  28.1 0.7 %collective-permute-start.3 = (bf16[2,80,128]{2,1,0:T(8,128)(2,1)S(1)}, bf16[2,80,128]{2,1,0:T(8,128)(2,1)S(1)}, u32[]{:S(2)}, u32[]{:S(2)}) collective-permute-start(bf16[2,80,128]{2,1,0:T(8,128)(2,1)S(1)} %get-tuple-element.46), channel_id=1, source_target_pairs={{0,1},{1,0},{2,3},{3,2},{4,5},{5,4},{6,7},{7,6},{8,9},{9,8},{10,11... | collective-permute-start | bytes 122888 | tf_op jit(solution)/shard_map/ppermute | solution.py:601
  28.8 0.9 %collective-permute-done.3.other_ref = bf16[2,80,128]{2,1,0:T(8,128)(2,1)S(1)} collective-permute-done((bf16[2,80,128]{2,1,0:T(8,128)(2,1)S(1)}, bf16[2,80,128]{2,1,0:T(8,128)(2,1)S(1)}, u32[]{:S(2)}, u32[]{:S(2)}) %collective-permute-start.3) | collective-permute-done | bytes 40992 | tf_op jit(solution)/shard_map/ppermute | solution.py:601
  29.7 0.3 collective-permute-start.4
  30.0 3.4 %rest.1 = (bf16[2,4,3,18,192]{4,3,2,1,0:T(8,128)(2,1)S(1)}, bf16[648,128]{1,0:T(8,128)(2,1)S(1)}, bf16[216,128]{1,0:T(8,128)(2,1)S(1)}, bf16[216,128]{1,0:T(8,128)(2,1)S(1)}) custom-call(bf16[576,192]{1,0:T(8,128)(2,1)S(1)} %get-tuple-element.52.x_ref, bf16[4,144,864]{2,1,0:T(8,128)(2,1)S(1)} %get-tuple-element.53.probs_ref, ...), custom_call_target="tpu_custom_call" | custom-call | flops 1000000000 | bytes 8000000 | tf_op jit(solution)/shard_map/rest/pallas_call | solution.py:750
  33.4 0.7 %collective-permute-done.4.refs_1_ = bf16[1,80,128]{2,1,0:T(8,128)(2,1)S(1)} collective-permute-done((bf16[1,80,128]{2,1,0:T(8,128)(2,1)S(1)}, bf16[1,80,128]{2,1,0:T(8,128)(2,1)S(1)}, u32[]{:S(2)}, u32[]{:S(2)}) %collective-permute-start.4) | collective-permute-done | bytes 20512 | tf_op jit(solution)/shard_map/ppermute | solution.py:601
  34.1 0.7 %add.2 = bf16[8,80,128]{2,1,0:T(8,128)(2,1)} custom-call(bf16[1,80,128]{2,1,0:T(8,128)(2,1)S(1)} %get-tuple-element.60.refs_0_, bf16[1,80,128]{2,1,0:T(8,128)(2,1)S(1)} %collective-permute-done.4.refs_1_), custom_call_target="tpu_custom_call" | custom-call | tf_op jit(solution)/shard_map/add/pallas_call | solution.py:604
  34.8 4.6 %all-to-all-start = ((bf16[8,80,128]{2,1,0:T(8,128)(2,1)}), bf16[8,80,128]{2,1,0:T(8,128)(2,1)S(1)}, u32[]{:S(2)}, u32[]{:S(2)}) async-start(bf16[8,80,128]{2,1,0:T(8,128)(2,1)} %add.2), calls=%async_computation | async-start | bytes 327680 | tf_op jit(solution)/shard_map/all_to_all | solution.py:629
  39.7 3.0 %collective-permute-start.6 = (bf16[216,128]{1,0:T(8,128)(2,1)S(1)}, bf16[216,128]{1,0:T(8,128)(2,1)S(1)}, u32[]{:S(2)}, u32[]{:S(2)}) collective-permute-start(bf16[216,128]{1,0:T(8,128)(2,1)S(1)} %get-tuple-element.67), channel_id=1, source_target_pairs={{0,33},{1,34},{2,35},{3,36},{4,37},{5,38},{6,39},{7,40},{8,41},{9,... | collective-permute-start | bytes 165896 | tf_op jit(solution)/shard_map/ppermute | solution.py:47
  42.7 0.6 collective-permute-start.7
  43.2 4.7 %all-to-all-done.refs_0_ = bf16[8,80,128]{2,1,0:T(8,128)(2,1)S(1)} async-done(((bf16[8,80,128]{2,1,0:T(8,128)(2,1)}), bf16[8,80,128]{2,1,0:T(8,128)(2,1)S(1)}, u32[]{:S(2)}, u32[]{:S(2)}) %all-to-all-start) | async-done | bytes 163872 | tf_op jit(solution)/shard_map/all_to_all | solution.py:629
  47.9 1.1 %collective-permute-done.6.diag_ref = bf16[216,128]{1,0:T(8,128)(2,1)S(1)} collective-permute-done((bf16[216,128]{1,0:T(8,128)(2,1)S(1)}, bf16[216,128]{1,0:T(8,128)(2,1)S(1)}, u32[]{:S(2)}, u32[]{:S(2)}) %collective-permute-start.6) | collective-permute-done | bytes 55328 | tf_op jit(solution)/shard_map/ppermute | solution.py:47
  49.0 0.6 %collective-permute-start.8 = (bf16[80,128]{1,0:T(8,128)(2,1)S(1)}, bf16[80,128]{1,0:T(8,128)(2,1)S(1)}, u32[]{:S(2)}, u32[]{:S(2)}) collective-permute-start(bf16[80,128]{1,0:T(8,128)(2,1)S(1)} %bitcast.15), channel_id=1, source_target_pairs={{0,2},{1,3},{2,0},{3,1},{4,6},{5,7},{6,4},{7,5},{8,10},{9,11},{10,... | collective-permute-start | bytes 61448 | tf_op jit(solution)/shard_map/ppermute | solution.py:601
  49.6 3.5 %collective-permute-done.8 = bf16[80,128]{1,0:T(8,128)(2,1)S(1)} collective-permute-done((bf16[80,128]{1,0:T(8,128)(2,1)S(1)}, bf16[80,128]{1,0:T(8,128)(2,1)S(1)}, u32[]{:S(2)}, u32[]{:S(2)}) %collective-permute-start.8) | collective-permute-done | bytes 20512 | tf_op jit(solution)/shard_map/ppermute | solution.py:601
  53.2 3.7 %collective-permute-start.9 = (bf16[2,80,128]{2,1,0:T(8,128)(2,1)S(1)}, bf16[2,80,128]{2,1,0:T(8,128)(2,1)S(1)}, u32[]{:S(2)}, u32[]{:S(2)}) collective-permute-start(bf16[2,80,128]{2,1,0:T(8,128)(2,1)S(1)} %pad_maximum_fusion.mine_ref), channel_id=1, source_target_pairs={{0,1},{1,0},{2,3},{3,2},{4,5},{5,4},{6,7},{7,6},{8,9},{9,8},{10,11... | collective-permute-start | bytes 122888 | tf_op jit(solution)/shard_map/ppermute | solution.py:601
  56.9 0.9 %finish.1 = (bf16[4,6,24,192]{3,2,1,0:T(8,128)(2,1)}, bf16[4,6,24,192]{3,2,1,0:T(8,128)(2,1)}) custom-call(bf16[2,4,3,18,192]{4,3,2,1,0:T(8,128)(2,1)S(1)} %get-tuple-element.57.own_ref, bf16[648,128]{1,0:T(8,128)(2,1)S(1)} %collective-permute-done.5.lat_ref, bf16[216,128]{1,0:T(8,128)(2,1)S(1)} %collective-permute-done.6.diag_ref, ...), custom_call_target="tpu_custom_call" | custom-call | tf_op jit(solution)/shard_map/finish/pallas_call | solution.py:774
  57.8 0.9 %unpack.1 = f32[12,1,3312]{2,1,0:T(1,128)} custom-call(bf16[2,80,128]{2,1,0:T(8,128)(2,1)S(1)} %pad_maximum_fusion.mine_ref, bf16[2,80,128]{2,1,0:T(8,128)(2,1)S(1)} %collective-permute-done.9.other_ref), custom_call_target="tpu_custom_call" | custom-call | tf_op jit(solution)/shard_map/unpack/pallas_call | solution.py:764
  (37 shorter events, 0.5 us)
Async XLA Ops:
  0.6 1.0 %copy-start = (bf16[4,6,24,192]{3,2,1,0:T(8,128)(2,1)S(1)}, bf16[4,6,24,192]{3,2,1,0:T(8,128)(2,1)}, u32[]{:S(2)}) copy-start(bf16[4,6,24,192]{3,2,1,0:T(8,128)(2,1)} %field_ref.5) | copy-start | bytes 663556
  1.6 1.0 %copy-start.2 = (bf16[4,6,24,192]{3,2,1,0:T(8,128)(2,1)S(1)}, bf16[4,6,24,192]{3,2,1,0:T(8,128)(2,1)}, u32[]{:S(2)}) copy-start(bf16[4,6,24,192]{3,2,1,0:T(8,128)(2,1)} %cot_ref.5) | copy-start | bytes 663556
  2.6 12.9 %copy-start.6 = (bf16[192,576]{1,0:T(8,128)(2,1)S(1)}, bf16[192,576]{1,0:T(8,128)(2,1)}, u32[]{:S(2)}) copy-start(bf16[192,576]{1,0:T(8,128)(2,1)} %wqkv_ref.1) | copy-start | bytes 663556
  2.6 12.9 %copy-start.7 = (f32[2,1,6,3312]{3,1,2,0:T(1,128)S(1)}, f32[2,1,6,3312]{3,1,2,0:T(1,128)}, u32[]{:S(2)}) copy-start(f32[2,1,6,3312]{3,1,2,0:T(1,128)} %param.19) | copy-start | bytes 476932
  2.6 12.9 %copy-start.10 = (f32[192]{0:T(256)S(1)}, f32[192]{0:T(256)}, u32[]{:S(2)}) copy-start(f32[192]{0:T(256)} %param.13) | copy-start | bytes 2308
  2.6 12.9 %copy-start.11 = (f32[192]{0:T(256)S(1)}, f32[192]{0:T(256)}, u32[]{:S(2)}) copy-start(f32[192]{0:T(256)} %param.16) | copy-start | bytes 2308
  2.6 12.9 %copy-start.12 = (s32[2,1,2]{2,1,0:T(1,128)S(1)}, s32[2,1,2]{2,1,0:T(1,128)}, u32[]{:S(2)}) copy-start(s32[2,1,2]{2,1,0:T(1,128)} %keep_ref.1) | copy-start | bytes 52
  2.6 16.2 %copy-start.8 = (bf16[192,192]{1,0:T(8,128)(2,1)S(1)}, bf16[192,192]{1,0:T(8,128)(2,1)}, u32[]{:S(2)}) copy-start(bf16[192,192]{1,0:T(8,128)(2,1)} %wproj_ref.3) | copy-start | bytes 221188
  2.8 12.7 %copy-start.9 = (s32[4,6,24]{2,0,1:T(4,128)S(1)}, s32[4,6,24]{2,0,1:T(4,128)}, u32[]{:S(2)}) copy-start(s32[4,6,24]{2,0,1:T(4,128)} %param.20) | copy-start | bytes 6916
  2.9 15.9 %collective-permute-start.1 = (bf16[648,128]{1,0:T(8,128)(2,1)S(1)}, bf16[648,128]{1,0:T(8,128)(2,1)S(1)}, u32[]{:S(2)}, u32[]{:S(2)}) collective-permute-start(bf16[648,128]{1,0:T(8,128)(2,1)S(1)} %pack_lat.1.after_ref), channel_id=1, source_target_pairs={{0,224},{1,225},{2,226},{3,227},{4,228},{5,229},{6,230},{7,231},{8... | collective-permute-start | bytes 497672 | tf_op jit(solution)/shard_map/ppermute | solution.py:47
  7.3 11.5 %copy-start.3 = (bf16[4,6,24,192]{3,2,1,0:T(8,128)(2,1)S(1)}, bf16[4,6,24,192]{3,2,1,0:T(8,128)(2,1)}, u32[]{:S(2)}) copy-start(bf16[4,6,24,192]{3,2,1,0:T(8,128)(2,1)} %cot_ref.5) | copy-start | bytes 663556
  7.3 11.5 %copy-start.4 = (bf16[192,768]{1,0:T(8,128)(2,1)S(1)}, bf16[192,768]{1,0:T(8,128)(2,1)}, u32[]{:S(2)}) copy-start(bf16[192,768]{1,0:T(8,128)(2,1)} %wup_ref.1) | copy-start | bytes 884740
  7.3 11.5 %copy-start.5 = (bf16[768,192]{0,1:T(8,128)(2,1)S(1)}, bf16[768,192]{0,1:T(8,128)(2,1)}, u32[]{:S(2)}) copy-start(bf16[768,192]{0,1:T(8,128)(2,1)} %param.18) | copy-start | bytes 884740
  7.4 11.4 %copy-start.1 = (bf16[4,6,24,192]{3,2,1,0:T(8,128)(2,1)S(1)}, bf16[4,6,24,192]{3,2,1,0:T(8,128)(2,1)}, u32[]{:S(2)}) copy-start(bf16[4,6,24,192]{3,2,1,0:T(8,128)(2,1)} %field_ref.5) | copy-start | bytes 663556
  7.4 11.3 %collective-permute-start = (bf16[216,128]{1,0:T(8,128)(2,1)S(1)}, bf16[216,128]{1,0:T(8,128)(2,1)S(1)}, u32[]{:S(2)}, u32[]{:S(2)}) collective-permute-start(bf16[216,128]{1,0:T(8,128)(2,1)S(1)} %get-tuple-element.39), channel_id=1, source_target_pairs={{0,31},{1,0},{2,1},{3,2},{4,3},{5,4},{6,5},{7,6},{8,7},{9,8},{10,9... | collective-permute-start | bytes 165896 | tf_op jit(solution)/shard_map/ppermute | solution.py:47
  8.4 10.3 %collective-permute-start.2 = (bf16[216,128]{1,0:T(8,128)(2,1)S(1)}, bf16[216,128]{1,0:T(8,128)(2,1)S(1)}, u32[]{:S(2)}, u32[]{:S(2)}) collective-permute-start(bf16[216,128]{1,0:T(8,128)(2,1)S(1)} %get-tuple-element.40), channel_id=1, source_target_pairs={{0,255},{1,224},{2,225},{3,226},{4,227},{5,228},{6,229},{7,230},{8... | collective-permute-start | bytes 165896 | tf_op jit(solution)/shard_map/ppermute | solution.py:47
  28.1 1.5 %collective-permute-start.3 = (bf16[2,80,128]{2,1,0:T(8,128)(2,1)S(1)}, bf16[2,80,128]{2,1,0:T(8,128)(2,1)S(1)}, u32[]{:S(2)}, u32[]{:S(2)}) collective-permute-start(bf16[2,80,128]{2,1,0:T(8,128)(2,1)S(1)} %get-tuple-element.46), channel_id=1, source_target_pairs={{0,1},{1,0},{2,3},{3,2},{4,5},{5,4},{6,7},{7,6},{8,9},{9,8},{10,11... | collective-permute-start | bytes 122888 | tf_op jit(solution)/shard_map/ppermute | solution.py:601
  29.7 4.4 %collective-permute-start.4 = (bf16[1,80,128]{2,1,0:T(8,128)(2,1)S(1)}, bf16[1,80,128]{2,1,0:T(8,128)(2,1)S(1)}, u32[]{:S(2)}, u32[]{:S(2)}) collective-permute-start(bf16[1,80,128]{2,1,0:T(8,128)(2,1)S(1)} %get-tuple-element.61), channel_id=1, source_target_pairs={{0,2},{1,3},{2,0},{3,1},{4,6},{5,7},{6,4},{7,5},{8,10},{9,11},{10,... | collective-permute-start | bytes 61448 | tf_op jit(solution)/shard_map/ppermute | solution.py:601
  34.8 13.1 %all-to-all-start = ((bf16[8,80,128]{2,1,0:T(8,128)(2,1)}), bf16[8,80,128]{2,1,0:T(8,128)(2,1)S(1)}, u32[]{:S(2)}, u32[]{:S(2)}) async-start(bf16[8,80,128]{2,1,0:T(8,128)(2,1)} %add.2), calls=%async_computation | async-start | bytes 327680 | tf_op jit(solution)/shard_map/all_to_all | solution.py:629
  39.4 9.6 %collective-permute-start.5 = (bf16[648,128]{1,0:T(8,128)(2,1)S(1)}, bf16[648,128]{1,0:T(8,128)(2,1)S(1)}, u32[]{:S(2)}, u32[]{:S(2)}) collective-permute-start(bf16[648,128]{1,0:T(8,128)(2,1)S(1)} %get-tuple-element.66), channel_id=1, source_target_pairs={{0,32},{1,33},{2,34},{3,35},{4,36},{5,37},{6,38},{7,39},{8,40},{9,... | collective-permute-start | bytes 497672 | tf_op jit(solution)/shard_map/ppermute | solution.py:47
  39.7 9.3 %collective-permute-start.6 = (bf16[216,128]{1,0:T(8,128)(2,1)S(1)}, bf16[216,128]{1,0:T(8,128)(2,1)S(1)}, u32[]{:S(2)}, u32[]{:S(2)}) collective-permute-start(bf16[216,128]{1,0:T(8,128)(2,1)S(1)} %get-tuple-element.67), channel_id=1, source_target_pairs={{0,33},{1,34},{2,35},{3,36},{4,37},{5,38},{6,39},{7,40},{8,41},{9,... | collective-permute-start | bytes 165896 | tf_op jit(solution)/shard_map/ppermute | solution.py:47
  42.7 6.3 %collective-permute-start.7 = (bf16[216,128]{1,0:T(8,128)(2,1)S(1)}, bf16[216,128]{1,0:T(8,128)(2,1)S(1)}, u32[]{:S(2)}, u32[]{:S(2)}) collective-permute-start(bf16[216,128]{1,0:T(8,128)(2,1)S(1)} %get-tuple-element.68), channel_id=1, source_target_pairs={{0,1},{1,2},{2,3},{3,4},{4,5},{5,6},{6,7},{7,8},{8,9},{9,10},{10,1... | collective-permute-start | bytes 165896 | tf_op jit(solution)/shard_map/ppermute | solution.py:47
  49.0 4.1 %collective-permute-start.8 = (bf16[80,128]{1,0:T(8,128)(2,1)S(1)}, bf16[80,128]{1,0:T(8,128)(2,1)S(1)}, u32[]{:S(2)}, u32[]{:S(2)}) collective-permute-start(bf16[80,128]{1,0:T(8,128)(2,1)S(1)} %bitcast.15), channel_id=1, source_target_pairs={{0,2},{1,3},{2,0},{3,1},{4,6},{5,7},{6,4},{7,5},{8,10},{9,11},{10,... | collective-permute-start | bytes 61448 | tf_op jit(solution)/shard_map/ppermute | solution.py:601
  53.2 4.6 %collective-permute-start.9 = (bf16[2,80,128]{2,1,0:T(8,128)(2,1)S(1)}, bf16[2,80,128]{2,1,0:T(8,128)(2,1)S(1)}, u32[]{:S(2)}, u32[]{:S(2)}) collective-permute-start(bf16[2,80,128]{2,1,0:T(8,128)(2,1)S(1)} %pad_maximum_fusion.mine_ref), channel_id=1, source_target_pairs={{0,1},{1,0},{2,3},{3,2},{4,5},{5,4},{6,7},{7,6},{8,9},{9,8},{10,11... | collective-permute-start | bytes 122888 | tf_op jit(solution)/shard_map/ppermute | solution.py:601

commit v15 on v13

--- a/solution.py
+++ b/solution.py
@@ -617,7 +617,6 @@
     other = swapped(send, 2)
     own, *strips = rest_of_backward(saved)
     parts = added((keep, other), lons // 4)
-    parts, strips = lax.optimization_barrier((parts, strips))
     steps = ((1, 0), (1, 1), (0, 1))
     strips = [shifted(strip, *step) for strip, step in zip(strips, steps)]
     parts = lax.all_to_all(parts, "lon", 0, 0, axis_index_groups=far)

time: 59 us -> 63.6 us (1.078)
  waiting for transfers between devices: 10.9 us -> 14.2 us
  local copies, waits for them, and re-layouts: 1.96 us -> 3.63 us
  starting transfers between devices: 26.3 us -> 25.1 us
  Pallas kernels: 18.8 us -> 19.5 us
    ppermute x6, waiting for transfers between devices: 1.07 us -> 6.18 us  [shifted(): return lax.ppermute(block, ('lat', 'lon'), route)]
    all_to_all x1, waiting for transfers between devices: 4.65 us -> 0.01 us  [lon_sum(): parts = lax.all_to_all(parts, 'lon', 0, 0, axis_index_groups=far)]
    ppermute x4, waiting for transfers between devices: 5.13 us -> 8.04 us  [swapped(): return lax.ppermute(block, 'lon', [(i, i ^ distance) for i in range(lons)])]
    unnamed x26 -> x30, local copies, waits for them, and re-layouts: 1.96 us -> 3.63 us
    all_to_all x1, starting transfers between devices: 4.6 us -> 3.6 us  [lon_sum(): parts = lax.all_to_all(parts, 'lon', 0, 0, axis_index_groups=far)]
    pallas_call x1, Pallas kernels: 3.41 us -> 4.12 us  [rest_of_backward(): pl.pallas_call(rest_kernel, out_shape=(jax.ShapeDtypeStruct((2, levels, h...]
  transfers between devices with their start and end apart: 11 -> 11, of which waited for: 5 -> 4; matrix products, arithmetic and copies ran while one was open for 0% -> 0% of each run, Pallas kernels for 13% -> 13%
where the time goes in v15:
time: 63.6 us; the launch traced here: 63.3 us
  starting transfers between devices  25.1 us (39%)
  Pallas kernels  19.5 us (31%)
  waiting for transfers between devices  14.2 us (22%)
  local copies, waits for them, and re-layouts  3.63 us (6%)
  between operations  0.84 us (1%)
    ppermute x6, starting transfers between devices, shifted(): return lax.ppermute(block, ('lat', 'lon'), route)  16.1 us
    pallas_call x1, Pallas kernels, body(): pl.pallas_call(scores_kernel, out_shape=(jax.ShapeDtypeStruct((2, DENSE,...  9.33 us
    ppermute x4, waiting for transfers between devices, swapped(): return lax.ppermute(block, 'lon', [(i, i ^ distance) for i in range(lons)])  8.04 us
    ppermute x6, waiting for transfers between devices, shifted(): return lax.ppermute(block, ('lat', 'lon'), route)  6.18 us
    ppermute x4, starting transfers between devices, swapped(): return lax.ppermute(block, 'lon', [(i, i ^ distance) for i in range(lons)])  5.39 us
    pallas_call x1, Pallas kernels, rest_of_backward(): pl.pallas_call(rest_kernel, out_shape=(jax.ShapeDtypeStruct((2, levels, h...  4.12 us
    unnamed x30, local copies, waits for them, and re-layouts  3.63 us
    all_to_all x1, starting transfers between devices, lon_sum(): parts = lax.all_to_all(parts, 'lon', 0, 0, axis_index_groups=far)  3.6 us
  transfers between devices with their start and end apart: 11, of which 4 were waited for; matrix products, arithmetic and copies ran while one was open for 0% of the time, Pallas kernels for 13%

profile of v15, /device:TPU:1, one launch (start us, length us, event | category | flops | bytes accessed | tf_op | source)
XLA Modules:
  0.0 63.3 jit_solution(3073779885227559041)
XLA Ops:
  0.6 1.0 %copy-done = bf16[4,6,24,192]{3,2,1,0:T(8,128)(2,1)S(1)} copy-done((bf16[4,6,24,192]{3,2,1,0:T(8,128)(2,1)S(1)}, bf16[4,6,24,192]{3,2,1,0:T(8,128)(2,1)}, u32[]{:S(2)}) %copy-start) | copy-done | bytes 221208
  1.6 1.0 %copy-done.2 = bf16[4,6,24,192]{3,2,1,0:T(8,128)(2,1)S(1)} copy-done((bf16[4,6,24,192]{3,2,1,0:T(8,128)(2,1)S(1)}, bf16[4,6,24,192]{3,2,1,0:T(8,128)(2,1)}, u32[]{:S(2)}) %copy-start.2) | copy-done | bytes 221208
  2.9 4.4 %collective-permute-start.1 = (bf16[648,128]{1,0:T(8,128)(2,1)S(1)}, bf16[648,128]{1,0:T(8,128)(2,1)S(1)}, u32[]{:S(2)}, u32[]{:S(2)}) collective-permute-start(bf16[648,128]{1,0:T(8,128)(2,1)S(1)} %pack_lat.1.after_ref), channel_id=1, source_target_pairs={{0,224},{1,225},{2,226},{3,227},{4,228},{5,229},{6,230},{7,231},{8... | collective-permute-start | bytes 497672 | tf_op jit(solution)/shard_map/ppermute | solution.py:47
  7.4 1.0 %collective-permute-start = (bf16[216,128]{1,0:T(8,128)(2,1)S(1)}, bf16[216,128]{1,0:T(8,128)(2,1)S(1)}, u32[]{:S(2)}, u32[]{:S(2)}) collective-permute-start(bf16[216,128]{1,0:T(8,128)(2,1)S(1)} %get-tuple-element.35), channel_id=1, source_target_pairs={{0,31},{1,0},{2,1},{3,2},{4,3},{5,4},{6,5},{7,6},{8,7},{9,8},{10,9... | collective-permute-start | bytes 165896 | tf_op jit(solution)/shard_map/ppermute | solution.py:47
  8.4 7.1 %collective-permute-start.2 = (bf16[216,128]{1,0:T(8,128)(2,1)S(1)}, bf16[216,128]{1,0:T(8,128)(2,1)S(1)}, u32[]{:S(2)}, u32[]{:S(2)}) collective-permute-start(bf16[216,128]{1,0:T(8,128)(2,1)S(1)} %get-tuple-element.36), channel_id=1, source_target_pairs={{0,255},{1,224},{2,225},{3,226},{4,227},{5,228},{6,229},{7,230},{8... | collective-permute-start | bytes 165896 | tf_op jit(solution)/shard_map/ppermute | solution.py:47
  15.5 3.2 %prepare.1 = (f32[2,144,864]{2,1,0:T(8,128)S(1)}, f32[4,864]{1,0:T(4,128)S(1)}, f32[144,4]{1,0:T(8,128)S(1)}, bf16[576,192]{1,0:T(8,128)(2,1)S(1)}, f32[8,192]{1,0:T(8,128)S(1)}) custom-call(f32[12,1,3312]{2,1,0:T(1,128)S(1)} %bitcast.14, s32[6,4,24]{2,1,0:T(4,128)S(1)} %bitcast.17, bf16[192,576]{1,0:T(8,128)(2,1)S(1)} %copy-done.6, f32[1,192]{1,0:T(1,128)S(1)} %bitcast.18, ...), custom_call_target="tpu_custom_call" | custom-call | tf_op jit(solution)/shard_map/prepare/pallas_call | solution.py:678
  18.8 9.3 %scores.1 = (bf16[2,80,128]{2,1,0:T(8,128)(2,1)S(1)}, bf16[2,80,128]{2,1,0:T(8,128)(2,1)S(1)}, bf16[576,192]{1,0:T(8,128)(2,1)S(1)}, bf16[4,144,864]{2,1,0:T(8,1...) custom-call(bf16[4,6,24,192]{3,2,1,0:T(8,128)(2,1)S(1)} %copy-done.1, ...), custom_call_target="tpu_custom_call" | custom-call | tf_op jit(solution)/shard_map/scores/pallas_call | solution.py:706
  28.1 0.7 %copy-done.13 = bf16[576,192]{1,0:T(8,128)(2,1)} copy-done((bf16[576,192]{1,0:T(8,128)(2,1)}, bf16[576,192]{1,0:T(8,128)(2,1)S(1)}, u32[]{:S(2)}) %copy-start.13) | copy-done | bytes 221208
  28.8 0.6 collective-permute-start.3
  29.4 0.9 %collective-permute-done.3.other_ref = bf16[2,80,128]{2,1,0:T(8,128)(2,1)S(1)} collective-permute-done((bf16[2,80,128]{2,1,0:T(8,128)(2,1)S(1)}, bf16[2,80,128]{2,1,0:T(8,128)(2,1)S(1)}, u32[]{:S(2)}, u32[]{:S(2)}) %collective-permute-start.3) | collective-permute-done | bytes 40992 | tf_op jit(solution)/shard_map/ppermute | solution.py:595
  30.4 4.1 %collective-permute-done.4.refs_1_ = bf16[1,80,128]{2,1,0:T(8,128)(2,1)S(1)} collective-permute-done((bf16[1,80,128]{2,1,0:T(8,128)(2,1)S(1)}, bf16[1,80,128]{2,1,0:T(8,128)(2,1)S(1)}, u32[]{:S(2)}, u32[]{:S(2)}) %collective-permute-start.4) | collective-permute-done | bytes 20512 | tf_op jit(solution)/shard_map/ppermute | solution.py:595
  34.5 0.7 %add.2 = bf16[8,80,128]{2,1,0:T(8,128)(2,1)} custom-call(bf16[1,80,128]{2,1,0:T(8,128)(2,1)S(1)} %get-tuple-element.56.refs_0_, bf16[1,80,128]{2,1,0:T(8,128)(2,1)S(1)} %collective-permute-done.4.refs_1_), custom_call_target="tpu_custom_call" | custom-call | tf_op jit(solution)/shard_map/add/pallas_call | solution.py:598
  35.2 3.6 %all-to-all-start = ((bf16[8,80,128]{2,1,0:T(8,128)(2,1)}), bf16[8,80,128]{2,1,0:T(8,128)(2,1)S(1)}, u32[]{:S(2)}, u32[]{:S(2)}) async-start(bf16[8,80,128]{2,1,0:T(8,128)(2,1)} %add.2), calls=%async_computation | async-start | bytes 327680 | tf_op jit(solution)/shard_map/all_to_all | solution.py:622
  38.8 1.0 %copy-done.14 = bf16[576,192]{1,0:T(8,128)(2,1)S(1)} copy-done((bf16[576,192]{1,0:T(8,128)(2,1)S(1)}, bf16[576,192]{1,0:T(8,128)(2,1)}, u32[]{:S(2)}) %copy-start.14) | copy-done | bytes 221208
  39.8 4.1 %rest.1 = (bf16[2,4,3,18,192]{4,3,2,1,0:T(8,128)(2,1)S(1)}, bf16[648,128]{1,0:T(8,128)(2,1)}, bf16[216,128]{1,0:T(8,128)(2,1)}, bf16[216,128]{1,0:T(8,128)(2,1)}) custom-call(bf16[576,192]{1,0:T(8,128)(2,1)S(1)} %get-tuple-element.48.x_ref, bf16[4,144,864]{2,1,0:T(8,128)(2,1)S(1)} %get-tuple-element.49.probs_ref, ...), custom_call_target="tpu_custom_call" | custom-call | flops 1000000000 | bytes 8000000 | tf_op jit(solution)/shard_map/rest/pallas_call | solution.py:743
  43.9 1.4 %collective-permute-start.5 = (bf16[648,128]{1,0:T(8,128)(2,1)}, bf16[648,128]{1,0:T(8,128)(2,1)S(1)}, u32[]{:S(2)}, u32[]{:S(2)}) collective-permute-start(bf16[648,128]{1,0:T(8,128)(2,1)} %get-tuple-element.58), channel_id=1, source_target_pairs={{0,32},{1,33},{2,34},{3,35},{4,36},{5,37},{6,38},{7,39},{8,40},{9,... | collective-permute-start | bytes 497672 | tf_op jit(solution)/shard_map/ppermute | solution.py:47
  45.3 1.6 %collective-permute-start.6 = (bf16[216,128]{1,0:T(8,128)(2,1)}, bf16[216,128]{1,0:T(8,128)(2,1)S(1)}, u32[]{:S(2)}, u32[]{:S(2)}) collective-permute-start(bf16[216,128]{1,0:T(8,128)(2,1)} %get-tuple-element.59), channel_id=1, source_target_pairs={{0,33},{1,34},{2,35},{3,36},{4,37},{5,38},{6,39},{7,40},{8,41},{9,... | collective-permute-start | bytes 165896 | tf_op jit(solution)/shard_map/ppermute | solution.py:47
  46.9 0.6 collective-permute-start.7
  47.5 6.2 %collective-permute-done.6.diag_ref = bf16[216,128]{1,0:T(8,128)(2,1)S(1)} collective-permute-done((bf16[216,128]{1,0:T(8,128)(2,1)}, bf16[216,128]{1,0:T(8,128)(2,1)S(1)}, u32[]{:S(2)}, u32[]{:S(2)}) %collective-permute-start.6) | collective-permute-done | bytes 55328 | tf_op jit(solution)/shard_map/ppermute | solution.py:47
  53.7 1.1 %collective-permute-start.8 = (bf16[80,128]{1,0:T(8,128)(2,1)S(1)}, bf16[80,128]{1,0:T(8,128)(2,1)S(1)}, u32[]{:S(2)}, u32[]{:S(2)}) collective-permute-start(bf16[80,128]{1,0:T(8,128)(2,1)S(1)} %bitcast.15), channel_id=1, source_target_pairs={{0,2},{1,3},{2,0},{3,1},{4,6},{5,7},{6,4},{7,5},{8,10},{9,11},{10,... | collective-permute-start | bytes 61448 | tf_op jit(solution)/shard_map/ppermute | solution.py:595
  54.8 3.0 %collective-permute-done.8 = bf16[80,128]{1,0:T(8,128)(2,1)S(1)} collective-permute-done((bf16[80,128]{1,0:T(8,128)(2,1)S(1)}, bf16[80,128]{1,0:T(8,128)(2,1)S(1)}, u32[]{:S(2)}, u32[]{:S(2)}) %collective-permute-start.8) | collective-permute-done | bytes 20512 | tf_op jit(solution)/shard_map/ppermute | solution.py:595
  57.9 3.6 %collective-permute-start.9 = (bf16[2,80,128]{2,1,0:T(8,128)(2,1)S(1)}, bf16[2,80,128]{2,1,0:T(8,128)(2,1)S(1)}, u32[]{:S(2)}, u32[]{:S(2)}) collective-permute-start(bf16[2,80,128]{2,1,0:T(8,128)(2,1)S(1)} %pad_maximum_fusion.mine_ref), channel_id=1, source_target_pairs={{0,1},{1,0},{2,3},{3,2},{4,5},{5,4},{6,7},{7,6},{8,9},{9,8},{10,11... | collective-permute-start | bytes 122888 | tf_op jit(solution)/shard_map/ppermute | solution.py:595
  61.5 0.9 %finish.1 = (bf16[4,6,24,192]{3,2,1,0:T(8,128)(2,1)}, bf16[4,6,24,192]{3,2,1,0:T(8,128)(2,1)}) custom-call(bf16[2,4,3,18,192]{4,3,2,1,0:T(8,128)(2,1)S(1)} %get-tuple-element.53.own_ref, bf16[648,128]{1,0:T(8,128)(2,1)S(1)} %collective-permute-done.5.lat_ref, bf16[216,128]{1,0:T(8,128)(2,1)S(1)} %collective-permute-done.6.diag_ref, ...), custom_call_target="tpu_custom_call" | custom-call | tf_op jit(solution)/shard_map/finish/pallas_call | solution.py:767
  62.4 0.9 %unpack.1 = f32[12,1,3312]{2,1,0:T(1,128)} custom-call(bf16[2,80,128]{2,1,0:T(8,128)(2,1)S(1)} %pad_maximum_fusion.mine_ref, bf16[2,80,128]{2,1,0:T(8,128)(2,1)S(1)} %collective-permute-done.9.other_ref), custom_call_target="tpu_custom_call" | custom-call | tf_op jit(solution)/shard_map/unpack/pallas_call | solution.py:757
  (41 shorter events, 0.6 us)
Async XLA Ops:
  0.6 1.0 %copy-start = (bf16[4,6,24,192]{3,2,1,0:T(8,128)(2,1)S(1)}, bf16[4,6,24,192]{3,2,1,0:T(8,128)(2,1)}, u32[]{:S(2)}) copy-start(bf16[4,6,24,192]{3,2,1,0:T(8,128)(2,1)} %field_ref.5) | copy-start | bytes 663556
  2.6 12.9 %copy-start.6 = (bf16[192,576]{1,0:T(8,128)(2,1)S(1)}, bf16[192,576]{1,0:T(8,128)(2,1)}, u32[]{:S(2)}) copy-start(bf16[192,576]{1,0:T(8,128)(2,1)} %wqkv_ref.1) | copy-start | bytes 663556
  2.6 12.9 %copy-start.7 = (f32[2,1,6,3312]{3,1,2,0:T(1,128)S(1)}, f32[2,1,6,3312]{3,1,2,0:T(1,128)}, u32[]{:S(2)}) copy-start(f32[2,1,6,3312]{3,1,2,0:T(1,128)} %param.19) | copy-start | bytes 476932
  2.6 12.9 %copy-start.10 = (f32[192]{0:T(256)S(1)}, f32[192]{0:T(256)}, u32[]{:S(2)}) copy-start(f32[192]{0:T(256)} %param.13) | copy-start | bytes 2308
  2.6 12.9 %copy-start.11 = (f32[192]{0:T(256)S(1)}, f32[192]{0:T(256)}, u32[]{:S(2)}) copy-start(f32[192]{0:T(256)} %param.16) | copy-start | bytes 2308
  2.6 12.9 %copy-start.12 = (s32[2,1,2]{2,1,0:T(1,128)S(1)}, s32[2,1,2]{2,1,0:T(1,128)}, u32[]{:S(2)}) copy-start(s32[2,1,2]{2,1,0:T(1,128)} %keep_ref.1) | copy-start | bytes 52
  2.6 16.2 %copy-start.8 = (bf16[192,192]{1,0:T(8,128)(2,1)S(1)}, bf16[192,192]{1,0:T(8,128)(2,1)}, u32[]{:S(2)}) copy-start(bf16[192,192]{1,0:T(8,128)(2,1)} %wproj_ref.3) | copy-start | bytes 221188
  2.8 12.7 %copy-start.9 = (s32[4,6,24]{2,0,1:T(4,128)S(1)}, s32[4,6,24]{2,0,1:T(4,128)}, u32[]{:S(2)}) copy-start(s32[4,6,24]{2,0,1:T(4,128)} %param.20) | copy-start | bytes 6916
  2.9 15.9 %collective-permute-start.1 = (bf16[648,128]{1,0:T(8,128)(2,1)S(1)}, bf16[648,128]{1,0:T(8,128)(2,1)S(1)}, u32[]{:S(2)}, u32[]{:S(2)}) collective-permute-start(bf16[648,128]{1,0:T(8,128)(2,1)S(1)} %pack_lat.1.after_ref), channel_id=1, source_target_pairs={{0,224},{1,225},{2,226},{3,227},{4,228},{5,229},{6,230},{7,231},{8... | collective-permute-start | bytes 497672 | tf_op jit(solution)/shard_map/ppermute | solution.py:47
  7.3 11.5 %copy-start.3 = (bf16[4,6,24,192]{3,2,1,0:T(8,128)(2,1)S(1)}, bf16[4,6,24,192]{3,2,1,0:T(8,128)(2,1)}, u32[]{:S(2)}) copy-start(bf16[4,6,24,192]{3,2,1,0:T(8,128)(2,1)} %cot_ref.5) | copy-start | bytes 663556
  7.3 11.5 %copy-start.4 = (bf16[192,768]{1,0:T(8,128)(2,1)S(1)}, bf16[192,768]{1,0:T(8,128)(2,1)}, u32[]{:S(2)}) copy-start(bf16[192,768]{1,0:T(8,128)(2,1)} %wup_ref.1) | copy-start | bytes 884740
  7.3 11.5 %copy-start.5 = (bf16[768,192]{0,1:T(8,128)(2,1)S(1)}, bf16[768,192]{0,1:T(8,128)(2,1)}, u32[]{:S(2)}) copy-start(bf16[768,192]{0,1:T(8,128)(2,1)} %param.18) | copy-start | bytes 884740
  7.4 11.4 %copy-start.1 = (bf16[4,6,24,192]{3,2,1,0:T(8,128)(2,1)S(1)}, bf16[4,6,24,192]{3,2,1,0:T(8,128)(2,1)}, u32[]{:S(2)}) copy-start(bf16[4,6,24,192]{3,2,1,0:T(8,128)(2,1)} %field_ref.5) | copy-start | bytes 663556
  7.4 11.3 %collective-permute-start = (bf16[216,128]{1,0:T(8,128)(2,1)S(1)}, bf16[216,128]{1,0:T(8,128)(2,1)S(1)}, u32[]{:S(2)}, u32[]{:S(2)}) collective-permute-start(bf16[216,128]{1,0:T(8,128)(2,1)S(1)} %get-tuple-element.35), channel_id=1, source_target_pairs={{0,31},{1,0},{2,1},{3,2},{4,3},{5,4},{6,5},{7,6},{8,7},{9,8},{10,9... | collective-permute-start | bytes 165896 | tf_op jit(solution)/shard_map/ppermute | solution.py:47
  8.4 10.3 %collective-permute-start.2 = (bf16[216,128]{1,0:T(8,128)(2,1)S(1)}, bf16[216,128]{1,0:T(8,128)(2,1)S(1)}, u32[]{:S(2)}, u32[]{:S(2)}) collective-permute-start(bf16[216,128]{1,0:T(8,128)(2,1)S(1)} %get-tuple-element.36), channel_id=1, source_target_pairs={{0,255},{1,224},{2,225},{3,226},{4,227},{5,228},{6,229},{7,230},{8... | collective-permute-start | bytes 165896 | tf_op jit(solution)/shard_map/ppermute | solution.py:47
  28.8 1.5 %collective-permute-start.3 = (bf16[2,80,128]{2,1,0:T(8,128)(2,1)S(1)}, bf16[2,80,128]{2,1,0:T(8,128)(2,1)S(1)}, u32[]{:S(2)}, u32[]{:S(2)}) collective-permute-start(bf16[2,80,128]{2,1,0:T(8,128)(2,1)S(1)} %get-tuple-element.42), channel_id=1, source_target_pairs={{0,1},{1,0},{2,3},{3,2},{4,5},{5,4},{6,7},{7,6},{8,9},{9,8},{10,11... | collective-permute-start | bytes 122888 | tf_op jit(solution)/shard_map/ppermute | solution.py:595
  30.3 4.2 %collective-permute-start.4 = (bf16[1,80,128]{2,1,0:T(8,128)(2,1)S(1)}, bf16[1,80,128]{2,1,0:T(8,128)(2,1)S(1)}, u32[]{:S(2)}, u32[]{:S(2)}) collective-permute-start(bf16[1,80,128]{2,1,0:T(8,128)(2,1)S(1)} %get-tuple-element.57), channel_id=1, source_target_pairs={{0,2},{1,3},{2,0},{3,1},{4,6},{5,7},{6,4},{7,5},{8,10},{9,11},{10,... | collective-permute-start | bytes 61448 | tf_op jit(solution)/shard_map/ppermute | solution.py:595
  35.2 12.3 %all-to-all-start = ((bf16[8,80,128]{2,1,0:T(8,128)(2,1)}), bf16[8,80,128]{2,1,0:T(8,128)(2,1)S(1)}, u32[]{:S(2)}, u32[]{:S(2)}) async-start(bf16[8,80,128]{2,1,0:T(8,128)(2,1)} %add.2), calls=%async_computation | async-start | bytes 327680 | tf_op jit(solution)/shard_map/all_to_all | solution.py:622
  38.8 1.0 %copy-start.14 = (bf16[576,192]{1,0:T(8,128)(2,1)S(1)}, bf16[576,192]{1,0:T(8,128)(2,1)}, u32[]{:S(2)}) copy-start(bf16[576,192]{1,0:T(8,128)(2,1)} %copy-done.13) | copy-start | bytes 663556
  43.9 9.8 %collective-permute-start.5 = (bf16[648,128]{1,0:T(8,128)(2,1)}, bf16[648,128]{1,0:T(8,128)(2,1)S(1)}, u32[]{:S(2)}, u32[]{:S(2)}) collective-permute-start(bf16[648,128]{1,0:T(8,128)(2,1)} %get-tuple-element.58), channel_id=1, source_target_pairs={{0,32},{1,33},{2,34},{3,35},{4,36},{5,37},{6,38},{7,39},{8,40},{9,... | collective-permute-start | bytes 497672 | tf_op jit(solution)/shard_map/ppermute | solution.py:47
  45.3 8.4 %collective-permute-start.6 = (bf16[216,128]{1,0:T(8,128)(2,1)}, bf16[216,128]{1,0:T(8,128)(2,1)S(1)}, u32[]{:S(2)}, u32[]{:S(2)}) collective-permute-start(bf16[216,128]{1,0:T(8,128)(2,1)} %get-tuple-element.59), channel_id=1, source_target_pairs={{0,33},{1,34},{2,35},{3,36},{4,37},{5,38},{6,39},{7,40},{8,41},{9,... | collective-permute-start | bytes 165896 | tf_op jit(solution)/shard_map/ppermute | solution.py:47
  46.9 6.8 %collective-permute-start.7 = (bf16[216,128]{1,0:T(8,128)(2,1)}, bf16[216,128]{1,0:T(8,128)(2,1)S(1)}, u32[]{:S(2)}, u32[]{:S(2)}) collective-permute-start(bf16[216,128]{1,0:T(8,128)(2,1)} %get-tuple-element.60), channel_id=1, source_target_pairs={{0,1},{1,2},{2,3},{3,4},{4,5},{5,6},{6,7},{7,8},{8,9},{9,10},{10,1... | collective-permute-start | bytes 165896 | tf_op jit(solution)/shard_map/ppermute | solution.py:47
  53.7 4.1 %collective-permute-start.8 = (bf16[80,128]{1,0:T(8,128)(2,1)S(1)}, bf16[80,128]{1,0:T(8,128)(2,1)S(1)}, u32[]{:S(2)}, u32[]{:S(2)}) collective-permute-start(bf16[80,128]{1,0:T(8,128)(2,1)S(1)} %bitcast.15), channel_id=1, source_target_pairs={{0,2},{1,3},{2,0},{3,1},{4,6},{5,7},{6,4},{7,5},{8,10},{9,11},{10,... | collective-permute-start | bytes 61448 | tf_op jit(solution)/shard_map/ppermute | solution.py:595
  57.9 4.5 %collective-permute-start.9 = (bf16[2,80,128]{2,1,0:T(8,128)(2,1)S(1)}, bf16[2,80,128]{2,1,0:T(8,128)(2,1)S(1)}, u32[]{:S(2)}, u32[]{:S(2)}) collective-permute-start(bf16[2,80,128]{2,1,0:T(8,128)(2,1)S(1)} %pad_maximum_fusion.mine_ref), channel_id=1, source_target_pairs={{0,1},{1,0},{2,3},{3,2},{4,5},{5,4},{6,7},{7,6},{8,9},{9,8},{10,11... | collective-permute-start | bytes 122888 | tf_op jit(solution)/shard_map/ppermute | solution.py:595
  (2 other events, 1.7 us)
